TPU v7x, 32 devices: a whole 2x2x4 slice. The times are simulated.
32 devices in a mesh: rep: 16 (over z, y, core), shard: 2 (over x).
Axes of the slice: x: 2, y: 2, z: 4, core: 2. Of those that a mesh axis runs over, the one named last changes fastest.
Arguments:
- prompt_in: bfloat16 [2, 16, 1024, 1024], P(None, 'rep', 'shard'), may hold values from -6 to 6
- cont_in: bfloat16 [2, 16, 2, 128, 1024], P(None, 'rep', 'shard'), may hold values from -6 to 6
- prompt_cot: bfloat16 [2, 16, 1024, 1024], P(None, 'rep', 'shard'), may hold values from -6 to 6
- cont_cot: bfloat16 [2, 16, 2, 128, 1024], P(None, 'rep', 'shard'), may hold values from -6 to 6
- ln1_gain: bfloat16 [1024], P('shard'), may hold values from 0.099609375 to 1.8984375
- ln1_bias: bfloat16 [1024], P('shard'), may hold values from -3 to 3
- ln2_gain: bfloat16 [1024], P('shard'), may hold values from 0.099609375 to 1.8984375
- ln2_bias: bfloat16 [1024], P('shard'), may hold values from -3 to 3
- qkv_weight: bfloat16 [1024, 3072], P('shard'), may hold values from -0.25 to 0.25
- qkv_bias: bfloat16 [3072], P('shard'), may hold values from -3 to 3
- out_weight: bfloat16 [1024, 1024], P('shard'), may hold values from -0.75 to 0.75
- out_bias: bfloat16 [1024], P('shard'), may hold values from -3 to 3
- up_weight: bfloat16 [1024, 4096], P('shard'), may hold values from -0.1875 to 0.1875
- up_bias: bfloat16 [4096], P('shard'), may hold values from -3 to 3
- down_weight: bfloat16 [4096, 1024], P('shard'), may hold values from -0.09375 to 0.09375
- down_bias: bfloat16 [1024], P('shard'), may hold values from -3 to 3
Outputs:
- prompt_out: bfloat16 [2, 16, 1024, 1024], P(None, 'rep', 'shard')
- cont_out: bfloat16 [2, 16, 2, 128, 1024], P(None, 'rep', 'shard')
- prompt_grad: float32 [2, 16, 1024, 1024], P(None, 'rep', 'shard')
- cont_grad: float32 [2, 16, 2, 128, 1024], P(None, 'rep', 'shard')
- ln1_gain_grad: float32 [1024], P('shard')
- ln1_bias_grad: float32 [1024], P('shard')
- ln2_gain_grad: float32 [1024], P('shard')
- ln2_bias_grad: float32 [1024], P('shard')
- qkv_weight_grad: float32 [1024, 3072], P('shard')
- qkv_bias_grad: float32 [3072], P('shard')
- out_weight_grad: float32 [1024, 1024], P('shard')
- out_bias_grad: float32 [1024], P('shard')
- up_weight_grad: float32 [1024, 4096], P('shard')
- up_bias_grad: float32 [4096], P('shard')
- down_weight_grad: float32 [4096, 1024], P('shard')
- down_bias_grad: float32 [1024], P('shard')
All inputs are finite; a program needn't handle non-finite values.
Results may differ from a plain program's by a relative error of at most 0.018.
Values may be sent and summed in bfloat16 or wider, within the bound.
No kernel may reach another device: no remote copies, remote signals or barrier semaphores. Data moves between devices by JAX's collectives and lax.ppermute only.
A program may use at most 448 MiB of HBM per device.

v0:
```python
import math

import jax
import jax.numpy as jnp
from jax import lax
from jax.sharding import PartitionSpec as P

H = 16
HD = 64
ROT = 16


epsilon = 1e-05


def layer_stats(tokens):
    mean_val = jnp.mean(tokens, axis=-1, keepdims=True)
    centred = tokens - mean_val
    inverse = lax.rsqrt(jnp.mean(centred * centred, axis=-1, keepdims=True) + epsilon)
    return (centred * inverse, inverse)


def norm_back(grad_norm, normed, inverse, norm_gain):
    scaled = grad_norm * norm_gain
    centred = (
        scaled
        - jnp.mean(scaled, axis=-1, keepdims=True)
        - normed * jnp.mean(scaled * normed, axis=-1, keepdims=True)
    )
    return (centred * inverse, jnp.sum(grad_norm * normed, axis=0), jnp.sum(grad_norm, axis=0))


def rotary_tables(positions):
    half_rot = ROT // 2
    inverse_freq = jnp.exp(
        jnp.arange(half_rot, dtype=jnp.float32) * (-2.0 * math.log(10000.0) / ROT)
    )
    angles = positions[:, None] * inverse_freq[None, :]
    return (jnp.cos(angles), jnp.sin(angles))


def rotate(head_vals, cosine_table, sine_table):
    half_rot = ROT // 2
    front_half = head_vals[..., :half_rot]
    back_half = head_vals[..., half_rot:ROT]
    cos_part = cosine_table[:, None, :]
    sin_part = sine_table[:, None, :]
    return jnp.concatenate(
        [
            front_half * cos_part - back_half * sin_part,
            back_half * cos_part + front_half * sin_part,
            head_vals[..., ROT:],
        ],
        axis=-1,
    )


def inner_rows(left_mat, right_mat):
    return lax.dot_general(
        left_mat, right_mat, (((0,), (0,)), ((), ())), preferred_element_type=jnp.float32
    )


def inner_cols(left_mat, right_mat):
    return lax.dot_general(
        left_mat, right_mat, (((1,), (1,)), ((), ())), preferred_element_type=jnp.float32
    )


def gelu_slope(values):
    return (
        0.5 * (1.0 + lax.erf(values * 0.7071067811865476))
        + values * jnp.exp(-0.5 * values * values) * 0.3989422804014327
    )


def add_tuples(left_tuple, right_tuple):
    return tuple(
        (jnp.add(left_val, right_val) for left_val, right_val in zip(left_tuple, right_tuple))
    )


def per_device(
    prompt_in,
    cont_in,
    prompt_cot,
    cont_cot,
    ln1_gain,
    ln1_bias,
    ln2_gain,
    ln2_bias,
    qkv_weight,
    qkv_bias,
    out_weight,
    out_bias,
    up_weight,
    up_bias,
    down_weight,
    down_bias,
):
    micro = prompt_in.shape[0]
    prompt_dev = prompt_in.shape[2]
    width = prompt_in.shape[3]
    cont_dev = cont_in.shape[2]
    cont_len = cont_in.shape[3]
    prompt_len = prompt_dev * lax.axis_size("shard")
    count = prompt_dev + cont_dev * cont_len
    key_count = prompt_len + cont_dev * cont_len
    shard_pos = lax.axis_index("shard")
    score_scale = HD ** (-0.5)
    local_pos = jnp.arange(count, dtype=jnp.int32)
    is_prompt = local_pos < prompt_dev
    cont_pos = local_pos - prompt_dev
    query_cont = jnp.where(is_prompt, -1, cont_pos // cont_len)
    query_step = jnp.where(
        is_prompt, shard_pos * prompt_dev + local_pos, prompt_len + cont_pos % cont_len
    )
    key_pos = jnp.arange(key_count, dtype=jnp.int32)
    key_prompt = key_pos < prompt_len
    key_cont = jnp.where(key_prompt, -2, (key_pos - prompt_len) // cont_len)
    key_step = jnp.where(key_prompt, key_pos, prompt_len + (key_pos - prompt_len) % cont_len)
    earlier = key_step[None, :] <= query_step[:, None]
    allowed = (
        key_prompt[None, :] & (jnp.logical_not(is_prompt)[:, None] | earlier)
        | (query_cont[:, None] == key_cont[None, :]) & earlier
    )
    cosine_table, sine_table = rotary_tables(query_step.astype(jnp.float32))
    prompt_outs = []
    cont_outs = []
    prompt_grads = []
    cont_grads = []
    totals = ()
    for micro_step in range(micro):
        forward_set = (
            lax.all_gather(ln1_gain, "shard", axis=0, tiled=True),
            lax.all_gather(ln1_bias, "shard", axis=0, tiled=True),
            lax.all_gather(ln2_gain, "shard", axis=0, tiled=True),
            lax.all_gather(ln2_bias, "shard", axis=0, tiled=True),
            lax.all_gather(qkv_weight, "shard", axis=0, tiled=True),
            lax.all_gather(qkv_bias, "shard", axis=0, tiled=True),
            lax.all_gather(out_weight, "shard", axis=0, tiled=True),
            lax.all_gather(out_bias, "shard", axis=0, tiled=True),
            lax.all_gather(up_weight, "shard", axis=0, tiled=True),
            lax.all_gather(up_bias, "shard", axis=0, tiled=True),
            lax.all_gather(down_weight, "shard", axis=0, tiled=True),
            lax.all_gather(down_bias, "shard", axis=0, tiled=True),
        )
        (
            gain_one,
            bias_one,
            gain_two,
            bias_two,
            w_qkv,
            b_qkv,
            w_out,
            b_out,
            w_up,
            b_up,
            w_down,
            b_down,
        ) = forward_set
        tokens = jnp.concatenate(
            [prompt_in[micro_step, 0], cont_in[micro_step, 0].reshape(cont_dev * cont_len, width)],
            axis=0,
        ).astype(jnp.float32)
        normed, inverse = layer_stats(tokens)
        hidden_one = (normed * gain_one.astype(jnp.float32) + bias_one.astype(jnp.float32)).astype(
            jnp.bfloat16
        )
        hidden_two = (normed * gain_two.astype(jnp.float32) + bias_two.astype(jnp.float32)).astype(
            jnp.bfloat16
        )
        linear = jnp.dot(hidden_one, w_qkv, preferred_element_type=jnp.float32) + b_qkv.astype(
            jnp.float32
        )
        queries = rotate(linear[:, :width].reshape(count, H, HD), cosine_table, sine_table).astype(
            jnp.bfloat16
        )
        local_keys = (
            rotate(linear[:, width : 2 * width].reshape(count, H, HD), cosine_table, sine_table)
            .astype(jnp.bfloat16)
            .reshape(count, width)
        )
        local_values = linear[:, 2 * width :].astype(jnp.bfloat16)
        prompt_keys, prompt_values = (
            lax.all_gather(local_keys[:prompt_dev], "shard", axis=0, tiled=True),
            lax.all_gather(local_values[:prompt_dev], "shard", axis=0, tiled=True),
        )
        all_keys = jnp.concatenate([prompt_keys, local_keys[prompt_dev:]], axis=0).reshape(
            key_count, H, HD
        )
        all_values = jnp.concatenate([prompt_values, local_values[prompt_dev:]], axis=0).reshape(
            key_count, H, HD
        )
        scores = jnp.where(
            allowed[None],
            jnp.einsum("qhd,khd->hqk", queries, all_keys, preferred_element_type=jnp.float32)
            * score_scale,
            -1e30,
        )
        top_score = jnp.max(scores, axis=-1, keepdims=True)
        exponent = jnp.exp(scores - top_score)
        total_exp = jnp.sum(exponent, axis=-1, keepdims=True)
        probs_low = (exponent / total_exp).astype(jnp.bfloat16)
        log_total = top_score + jnp.log(total_exp)
        context = (
            jnp.einsum("hqk,khd->qhd", probs_low, all_values, preferred_element_type=jnp.float32)
            .reshape(count, width)
            .astype(jnp.bfloat16)
        )
        attended = jnp.dot(context, w_out, preferred_element_type=jnp.float32) + b_out.astype(
            jnp.float32
        )
        pre_act = jnp.dot(hidden_two, w_up, preferred_element_type=jnp.float32) + b_up.astype(
            jnp.float32
        )
        activated = jax.nn.gelu(pre_act, approximate=False).astype(jnp.bfloat16)
        result = (
            tokens
            + attended
            + jnp.dot(activated, w_down, preferred_element_type=jnp.float32)
            + b_down.astype(jnp.float32)
        )
        result_low = result.astype(jnp.bfloat16)
        prompt_outs.append(result_low[:prompt_dev])
        cont_outs.append(result_low[prompt_dev:].reshape(cont_dev, cont_len, width))
        back_set = (
            lax.all_gather(ln1_gain, "shard", axis=0, tiled=True),
            lax.all_gather(ln1_bias, "shard", axis=0, tiled=True),
            lax.all_gather(ln2_gain, "shard", axis=0, tiled=True),
            lax.all_gather(ln2_bias, "shard", axis=0, tiled=True),
            lax.all_gather(qkv_weight, "shard", axis=0, tiled=True),
            lax.all_gather(qkv_bias, "shard", axis=0, tiled=True),
            lax.all_gather(out_weight, "shard", axis=0, tiled=True),
            lax.all_gather(out_bias, "shard", axis=0, tiled=True),
            lax.all_gather(up_weight, "shard", axis=0, tiled=True),
            lax.all_gather(up_bias, "shard", axis=0, tiled=True),
            lax.all_gather(down_weight, "shard", axis=0, tiled=True),
            lax.all_gather(down_bias, "shard", axis=0, tiled=True),
        )
        gain_back_one = back_set[0].astype(jnp.float32)
        gain_back_two = back_set[2].astype(jnp.float32)
        w_qkv_back = back_set[4]
        w_out_back = back_set[6]
        w_up_back = back_set[8]
        w_down_back = back_set[10]
        grad_out = jnp.concatenate(
            [
                prompt_cot[micro_step, 0],
                cont_cot[micro_step, 0].reshape(cont_dev * cont_len, width),
            ],
            axis=0,
        )
        grad_float = grad_out.astype(jnp.float32)
        out_weight_step = inner_rows(context, grad_out)
        down_weight_step = inner_rows(activated, grad_out)
        bias_step = jnp.sum(grad_float, axis=0)
        d_act = inner_cols(grad_out, w_down_back)
        d_pre = (d_act * gelu_slope(pre_act)).astype(jnp.bfloat16)
        up_weight_step = inner_rows(hidden_two, d_pre)
        up_bias_step = jnp.sum(d_pre.astype(jnp.float32), axis=0)
        d_two = inner_cols(d_pre, w_up_back)
        d_context = inner_cols(grad_out, w_out_back).astype(jnp.bfloat16).reshape(count, H, HD)
        scores_again = jnp.where(
            allowed[None],
            jnp.einsum("qhd,khd->hqk", queries, all_keys, preferred_element_type=jnp.float32)
            * score_scale,
            -1e30,
        )
        probs = jnp.exp(scores_again - log_total)
        d_probs = jnp.einsum(
            "qhd,khd->hqk", d_context, all_values, preferred_element_type=jnp.float32
        )
        delta = jnp.sum(probs * d_probs, axis=-1, keepdims=True)
        d_scores = (probs * (d_probs - delta)).astype(jnp.bfloat16)
        d_queries = (
            jnp.einsum("hqk,khd->qhd", d_scores, all_keys, preferred_element_type=jnp.float32)
            * score_scale
        )
        d_keys = (
            jnp.einsum("hqk,qhd->khd", d_scores, queries, preferred_element_type=jnp.float32)
            * score_scale
        ).reshape(key_count, width)
        d_values = jnp.einsum(
            "hqk,qhd->khd",
            probs.astype(jnp.bfloat16),
            d_context,
            preferred_element_type=jnp.float32,
        ).reshape(key_count, width)
        own_keys, own_values = (
            lax.psum_scatter(
                d_keys[:prompt_len].astype(jnp.bfloat16), "shard", scatter_dimension=0, tiled=True
            ).astype(jnp.float32),
            lax.psum_scatter(
                d_values[:prompt_len].astype(jnp.bfloat16), "shard", scatter_dimension=0, tiled=True
            ).astype(jnp.float32),
        )
        key_grads = jnp.concatenate([own_keys, d_keys[prompt_len:]], axis=0).reshape(count, H, HD)
        value_grads = jnp.concatenate([own_values, d_values[prompt_len:]], axis=0)
        d_linear = jnp.concatenate(
            [
                rotate(d_queries, cosine_table, -sine_table).reshape(count, width),
                rotate(key_grads, cosine_table, -sine_table).reshape(count, width),
                value_grads,
            ],
            axis=1,
        ).astype(jnp.bfloat16)
        qkv_weight_step = inner_rows(hidden_one, d_linear)
        qkv_bias_step = jnp.sum(d_linear.astype(jnp.float32), axis=0)
        d_one = inner_cols(d_linear, w_qkv_back)
        token_one, gain_one_step, bias_one_step = norm_back(d_one, normed, inverse, gain_back_one)
        token_two, gain_two_step, bias_two_step = norm_back(d_two, normed, inverse, gain_back_two)
        input_grad = grad_float + token_one + token_two
        prompt_grads.append(input_grad[:prompt_dev])
        cont_grads.append(input_grad[prompt_dev:].reshape(cont_dev, cont_len, width))
        step_grads = (
            gain_one_step,
            bias_one_step,
            gain_two_step,
            bias_two_step,
            qkv_weight_step,
            qkv_bias_step,
            out_weight_step,
            bias_step,
            up_weight_step,
            up_bias_step,
            down_weight_step,
            bias_step,
        )
        totals = step_grads if micro_step == 0 else add_tuples(totals, step_grads)
    owned = (
        lax.psum_scatter(
            totals[0].astype(jnp.bfloat16), "shard", scatter_dimension=0, tiled=True
        ).astype(jnp.float32),
        lax.psum_scatter(
            totals[1].astype(jnp.bfloat16), "shard", scatter_dimension=0, tiled=True
        ).astype(jnp.float32),
        lax.psum_scatter(
            totals[2].astype(jnp.bfloat16), "shard", scatter_dimension=0, tiled=True
        ).astype(jnp.float32),
        lax.psum_scatter(
            totals[3].astype(jnp.bfloat16), "shard", scatter_dimension=0, tiled=True
        ).astype(jnp.float32),
        lax.psum_scatter(
            totals[4].astype(jnp.bfloat16), "shard", scatter_dimension=0, tiled=True
        ).astype(jnp.float32),
        lax.psum_scatter(
            totals[5].astype(jnp.bfloat16), "shard", scatter_dimension=0, tiled=True
        ).astype(jnp.float32),
        lax.psum_scatter(
            totals[6].astype(jnp.bfloat16), "shard", scatter_dimension=0, tiled=True
        ).astype(jnp.float32),
        lax.psum_scatter(
            totals[7].astype(jnp.bfloat16), "shard", scatter_dimension=0, tiled=True
        ).astype(jnp.float32),
        lax.psum_scatter(
            totals[8].astype(jnp.bfloat16), "shard", scatter_dimension=0, tiled=True
        ).astype(jnp.float32),
        lax.psum_scatter(
            totals[9].astype(jnp.bfloat16), "shard", scatter_dimension=0, tiled=True
        ).astype(jnp.float32),
        lax.psum_scatter(
            totals[10].astype(jnp.bfloat16), "shard", scatter_dimension=0, tiled=True
        ).astype(jnp.float32),
        lax.psum_scatter(
            totals[11].astype(jnp.bfloat16), "shard", scatter_dimension=0, tiled=True
        ).astype(jnp.float32),
    )
    summed = (
        lax.psum(owned[0].astype(jnp.bfloat16), "rep").astype(jnp.float32),
        lax.psum(owned[1].astype(jnp.bfloat16), "rep").astype(jnp.float32),
        lax.psum(owned[2].astype(jnp.bfloat16), "rep").astype(jnp.float32),
        lax.psum(owned[3].astype(jnp.bfloat16), "rep").astype(jnp.float32),
        lax.psum(owned[4].astype(jnp.bfloat16), "rep").astype(jnp.float32),
        lax.psum(owned[5].astype(jnp.bfloat16), "rep").astype(jnp.float32),
        lax.psum(owned[6].astype(jnp.bfloat16), "rep").astype(jnp.float32),
        lax.psum(owned[7].astype(jnp.bfloat16), "rep").astype(jnp.float32),
        lax.psum(owned[8].astype(jnp.bfloat16), "rep").astype(jnp.float32),
        lax.psum(owned[9].astype(jnp.bfloat16), "rep").astype(jnp.float32),
        lax.psum(owned[10].astype(jnp.bfloat16), "rep").astype(jnp.float32),
        lax.psum(owned[11].astype(jnp.bfloat16), "rep").astype(jnp.float32),
    )
    prompt_out = jnp.stack(prompt_outs, axis=0)[:, None]
    cont_out = jnp.stack(cont_outs, axis=0)[:, None]
    prompt_grad = jnp.stack(prompt_grads, axis=0)[:, None]
    cont_grad = jnp.stack(cont_grads, axis=0)[:, None]
    return (
        prompt_out,
        cont_out,
        prompt_grad,
        cont_grad,
        summed[0],
        summed[1],
        summed[2],
        summed[3],
        summed[4],
        summed[5],
        summed[6],
        summed[7],
        summed[8],
        summed[9],
        summed[10],
        summed[11],
    )


def solution(mesh):
    in_specs = (
        P(None, "rep", "shard", None),
        P(None, "rep", "shard", None, None),
        P(None, "rep", "shard", None),
        P(None, "rep", "shard", None, None),
        P("shard"),
        P("shard"),
        P("shard"),
        P("shard"),
        P("shard", None),
        P("shard"),
        P("shard", None),
        P("shard"),
        P("shard", None),
        P("shard"),
        P("shard", None),
        P("shard"),
    )
    out_specs = (
        P(None, "rep", "shard", None),
        P(None, "rep", "shard", None, None),
        P(None, "rep", "shard", None),
        P(None, "rep", "shard", None, None),
        P("shard"),
        P("shard"),
        P("shard"),
        P("shard"),
        P("shard", None),
        P("shard"),
        P("shard", None),
        P("shard"),
        P("shard", None),
        P("shard"),
        P("shard", None),
        P("shard"),
    )
    return jax.shard_map(
        per_device, mesh=mesh, in_specs=in_specs, out_specs=out_specs, check_vma=False
    )
```

profile of v0, /device:TPU:0, one launch (start us, length us, event | category | flops | bytes accessed | tf_op | source)
XLA Modules:
  0.0 1209.7 jit_solution(6251305691100553650)
XLA Ops:
  11.7 5.2 all-gather
  27.0 65.7 %all-gather.16.cloned.1.call-done = bf16[1024,3072]{1,0:T(8,128)(2,1)} async-done(((bf16[512,3072]{1,0:T(8,128)(2,1)}), bf16[1024,3072]{1,0:T(8,128)(2,1)}) %all-gather.16.cloned.1.call-update) | async-done | bytes 6291472 | tf_op jit(solution)/shard_map/all_gather | solution.py:139
  92.7 10.0 fusion.180
  105.7 5.7 fusion.179
  120.6 9.1 fusion.182
  193.3 4.6 all-gather.30.cloned.1.call-done
  198.0 21.2 %fusion.181 = (f32[16,640]{1,0:T(8,128)S(1)}, f32[16,640,1152]{2,1,0:T(8,128)}) fusion(bf16[640,16,48]{0,2,1:T(8,128)(2,1)S(1)} %copy-done.46, bf16[640,16,8]{0,2,1:T(8,128)(2,1)S(1)} %copy-done.77, bf16[640,16,8]{0,2,1:T(8,128)(2,1)} %copy-done.78, bf16[1024,16,64]{0,2,1:T(8,128)(2,1)} %bitcast.221, bf16[640,16,48]{0,2,1:T(8,128)(2,1)} %slice.447, ...), kind=kOutput, calls=%fused_computation.334 | convolution fusion | flops 1563416576 | bytes 52682752 | tf_op jit(solution)/shard_map/qhd,khd->hqk/dot_general | solution.py:197
  219.2 20.6 %fusion.1 = f32[16,640]{1,0:T(8,128)S(1)} fusion(f32[16,640,1152]{2,1,0:T(8,128)} %get-tuple-element.166, f32[16,640]{1,0:T(8,128)S(1)} %get-tuple-element.165), kind=kLoop, calls=%fused_computation.13 | loop fusion | flops 23582720 | bytes 47267840 | tf_op jit(solution)/shard_map/reduce_sum | solution.py:203
  240.4 30.7 %multiply_reduce_fusion = (f32[16,640]{1,0:T(8,128)S(1)}, f32[16,640,1152]{2,1,0:T(8,128)}) fusion(f32[16,640,1152]{2,1,0:T(8,128)} %get-tuple-element.166, f32[16,640]{1,0:T(8,128)S(1)} %log_add_fusion, bf16[640,16,64]{0,2,1:T(8,128)(2,1)S(1)} %bitcast.143, bf16[1152,16,64]{0,2,1:T(8,128)(2,1)S(1)} %bitcast.145), kind=kOutput, calls=%fused_computation.1 | convolution fusion | flops 1545328640 | bytes 98123776 | tf_op jit(solution)/shard_map/qhd,khd->hqk/dot_general | solution.py:271
  271.1 41.6 %multiply_convert_fusion = bf16[16,640,1152]{2,1,0:T(8,128)(2,1)} fusion(f32[16,640,1152]{2,1,0:T(8,128)} %get-tuple-element.175, f32[16,640,1152]{2,1,0:T(8,128)} %get-tuple-element.166, f32[16,640]{1,0:T(8,128)S(1)} %get-tuple-element.174, f32[16,640]{1,0:T(8,128)S(1)} %log_add_fusion), kind=kLoop, calls=%fused_computation | loop fusion | flops 47185920 | bytes 118046720 | tf_op jit(solution)/shard_map/convert_element_type | solution.py:275
  317.0 9.8 multiply_bitcast_fusion
  331.4 20.6 %fusion.183 = (f32[16,640]{1,0:T(8,128)S(1)}, f32[16,640,1152]{2,1,0:T(8,128)}) fusion(bf16[640,16,48]{0,2,1:T(8,128)(2,1)S(1)} %copy-done.49, bf16[640,16,8]{0,2,1:T(8,128)(2,1)S(1)} %copy-done.75, bf16[640,16,8]{0,2,1:T(8,128)(2,1)S(1)} %copy-done.73, bf16[1024,16,64]{0,2,1:T(8,128)(2,1)} %bitcast.223, bf16[640,16,48]{0,2,1:T(8,128)(2,1)S(1)} %slice.449, ...), kind=kOutput, calls=%fused_computation.336 | convolution fusion | flops 1563416576 | bytes 52682752 | tf_op jit(solution)/shard_map/qhd,khd->hqk/dot_general | solution.py:197
  352.0 20.5 %fusion = f32[16,640]{1,0:T(8,128)S(1)} fusion(f32[16,640,1152]{2,1,0:T(8,128)} %get-tuple-element.171, f32[16,640]{1,0:T(8,128)S(1)} %get-tuple-element.170), kind=kLoop, calls=%fused_computation.12 | loop fusion | flops 23582720 | bytes 47267840 | tf_op jit(solution)/shard_map/reduce_sum | solution.py:203
  373.8 36.1 %multiply_reduce_fusion.1 = (f32[16,640]{1,0:T(8,128)S(1)}, f32[16,640,1152]{2,1,0:T(8,128)}) fusion(f32[16,640,1152]{2,1,0:T(8,128)} %get-tuple-element.171, f32[16,640]{1,0:T(8,128)S(1)} %log_add_fusion.1, bf16[640,16,64]{0,2,1:T(8,128)(2,1)S(1)} %bitcast.141, bf16[1152,16,64]{0,2,1:T(8,128)(2,1)} %bitcast.147), kind=kOutput, calls=%fused_computation.4 | convolution fusion | flops 1545328640 | bytes 98123776 | tf_op jit(solution)/shard_map/qhd,khd->hqk/dot_general | solution.py:271
  409.9 37.9 %multiply_convert_fusion.1 = bf16[16,640,1152]{2,1,0:T(8,128)(2,1)} fusion(f32[16,640,1152]{2,1,0:T(8,128)} %get-tuple-element.173, f32[16,640,1152]{2,1,0:T(8,128)} %get-tuple-element.171, f32[16,640]{1,0:T(8,128)S(1)} %get-tuple-element.172, f32[16,640]{1,0:T(8,128)S(1)} %log_add_fusion.1), kind=kLoop, calls=%fused_computation.3 | loop fusion | flops 47185920 | bytes 118046720 | tf_op jit(solution)/shard_map/convert_element_type | solution.py:275
  447.8 9.8 multiply_bitcast_fusion.1
  461.5 17.4 %fusion.56 = bf16[1152,16,64]{0,2,1:T(8,128)(2,1)S(1)} fusion(bf16[640,16,64]{0,2,1:T(8,128)(2,1)S(1)} %bitcast.144, f32[16,640,1152]{2,1,0:T(8,128)} %get-tuple-element.166, f32[16,640]{1,0:T(8,128)S(1)} %log_add_fusion), kind=kOutput, calls=%fused_computation.116 | convolution fusion | flops 1534722048 | bytes 50896896 | tf_op jit(solution)/shard_map/hqk,qhd->khd/dot_general | solution.py:284
  480.8 19.4 %fusion.59 = bf16[1152,16,64]{0,2,1:T(8,128)(2,1)} fusion(bf16[640,16,64]{0,2,1:T(8,128)(2,1)S(1)} %bitcast.142, f32[16,640,1152]{2,1,0:T(8,128)} %get-tuple-element.171, f32[16,640]{1,0:T(8,128)S(1)} %log_add_fusion.1), kind=kOutput, calls=%fused_computation.117 | convolution fusion | flops 1534722048 | bytes 50896896 | tf_op jit(solution)/shard_map/hqk,qhd->khd/dot_general | solution.py:284
  503.6 18.1 %fusion.126 = bf16[16,64,640]{2,1,0:T(8,128)(2,1)} fusion(bf16[1152,16,64]{0,2,1:T(8,128)(2,1)S(1)} %bitcast.146, f32[16,640,1152]{2,1,0:T(8,128)} %get-tuple-element.166, f32[16,640]{1,0:T(8,128)S(1)} %copy-done.98, f32[16,640]{1,0:T(8,128)S(1)} %copy-done.96), kind=kOutput, calls=%fused_computation.207 | convolution fusion | flops 1545994240 | bytes 50937856 | tf_op jit(solution)/shard_map/hqk,khd->qhd/dot_general | solution.py:207
  521.9 18.8 %fusion.127 = bf16[16,64,640]{2,1,0:T(8,128)(2,1)S(1)} fusion(bf16[1152,16,64]{0,2,1:T(8,128)(2,1)} %bitcast.148, f32[16,640,1152]{2,1,0:T(8,128)} %get-tuple-element.171, f32[16,640]{1,0:T(8,128)S(1)} %copy-done.102, f32[16,640]{1,0:T(8,128)S(1)} %copy-done.100), kind=kOutput, calls=%fused_computation.208 | convolution fusion | flops 1545994240 | bytes 50937856 | tf_op jit(solution)/shard_map/hqk,khd->qhd/dot_general | solution.py:207
  546.2 8.5 fusion.166
  558.8 53.8 %fusion.14 = (bf16[640,4096]{1,0:T(8,128)(2,1)}, bf16[640,4096]{1,0:T(8,128)(2,1)}, f32[640,4096]{1,0:T(8,128)}) fusion(f32[4096]{0:T(1024)S(1)} %copy-done.112, f32[640,4096]{1,0:T(8,128)S(1)} %fusion.166, bf16[1024,4096]{1,0:T(8,128)(2,1)S(1)} %copy-done.125, f32[1024]{0:T(1024)S(1)} %bitcast.197, f32[1024]{0:T(1024)S(1)} %bitcast.190, ...), kind=kOutput, calls=%fused_computation.31 | convolution fusion | flops 5720637440 | bytes 41186304 | tf_op jit(solution)/shard_map/dot_general | solution.py:214
  612.5 13.7 %convert_reduce_fusion.1 = (f32[4096]{0:T(1024)}, bf16[640,4096]{1,0:T(8,128)(2,1)S(1)}) fusion(f32[640,4096]{1,0:T(8,128)} %get-tuple-element.167, f32[4096]{0:T(1024)S(1)} %copy-done.112, bf16[4096,1024]{1,0:T(8,128)(2,1)} %all-gather.26.cloned.1.call-done, bf16[128,1024]{1,0:T(8,128)(2,1)S(1)} %copy-done.66, bf16[512,1024]{1,0:T(8,128)(2,1)S(1)} %copy-done.39), kind=kOutput, calls=%fused_computation.48 | convolution fusion | flops 5405405184 | bytes 25460736 | tf_op jit(solution)/shard_map/dot_general | solution.py:65
  626.2 10.6 fusion.158
  636.9 12.2 %convert_reduce_fusion = (f32[4096]{0:T(1024)S(1)}, bf16[640,4096]{1,0:T(8,128)(2,1)S(1)}) fusion(f32[640,4096]{1,0:T(8,128)} %copy-done.128, f32[4096]{0:T(1024)S(1)} %copy-done.112, bf16[4096,1024]{1,0:T(8,128)(2,1)S(1)} %copy-done.126, bf16[128,1024]{1,0:T(8,128)(2,1)S(1)} %copy-done.70, bf16[512,1024]{1,0:T(8,128)(2,1)S(1)} %copy-done.43), kind=kOutput, calls=%fused_computation.47 | convolution fusion | flops 5405405184 | bytes 25460736 | tf_op jit(solution)/shard_map/dot_general | solution.py:65
  651.5 13.1 %add_convert_fusion.1 = bf16[1024,4096]{1,0:T(8,128)(2,1)} fusion(f32[1024,4096]{1,0:T(8,128)} %fusion.158, bf16[640,4096]{1,0:T(8,128)(2,1)S(1)} %get-tuple-element.180, f32[640]{0:T(1024)S(1)} %copy-done.111, f32[640]{0:T(1024)S(1)} %copy-done.108, f32[1024]{0:T(1024)S(1)} %bitcast.199, f32[1024]{0:T(1024)S(1)} %bitcast.192, ...), kind=kOutput, calls=%fused_computation.23 | convolution fusion | flops 5382995968 | bytes 31732736 | tf_op jit(solution)/shard_map/dot_general | solution.py:59
  664.6 12.9 %fusion.170 = f32[4096,1024]{1,0:T(8,128)} fusion(bf16[640,4096]{1,0:T(8,128)(2,1)} %get-tuple-element.150, bf16[128,1024]{1,0:T(8,128)(2,1)S(1)} %copy-done.66, bf16[512,1024]{1,0:T(8,128)(2,1)S(1)} %copy-done.39), kind=kOutput, calls=%fused_computation.327 | convolution fusion | flops 5371330560 | bytes 23330816 | tf_op jit(solution)/shard_map/dot_general | solution.py:59
  677.5 14.1 %add_convert_fusion = bf16[4096,1024]{1,0:T(8,128)(2,1)} fusion(f32[4096,1024]{1,0:T(8,128)} %fusion.170, bf16[640,4096]{1,0:T(8,128)(2,1)} %get-tuple-element.151, bf16[128,1024]{1,0:T(8,128)(2,1)S(1)} %copy-done.70, bf16[512,1024]{1,0:T(8,128)(2,1)S(1)} %copy-done.44), kind=kOutput, calls=%fused_computation.22 | convolution fusion | flops 5379719168 | bytes 31719424 | tf_op jit(solution)/shard_map/dot_general | solution.py:59
  699.0 14.0 %multiply_bitcast_fusion.2 = f32[640,16,64]{0,2,1:T(8,128)} fusion(bf16[16,640,1152]{2,1,0:T(8,128)(2,1)} %multiply_convert_fusion, bf16[640,16,48]{0,2,1:T(8,128)(2,1)S(1)} %copy-done.47, bf16[640,16,8]{0,2,1:T(8,128)(2,1)} %copy-done.76, bf16[640,16,8]{0,2,1:T(8,128)(2,1)} %copy-done.78, bf16[1024,16,64]{0,2,1:T(8,128)(2,1)} %bitcast.222), kind=kOutput, calls=%fused_computation.178 | convolution fusion | flops 1524760576 | bytes 29622272 | tf_op jit(solution)/shard_map/hqk,khd->qhd/dot_general | solution.py:277
  715.6 13.6 %multiply_bitcast_fusion.3 = f32[640,16,64]{0,2,1:T(8,128)} fusion(bf16[16,640,1152]{2,1,0:T(8,128)(2,1)} %multiply_convert_fusion.1, bf16[640,16,48]{0,2,1:T(8,128)(2,1)S(1)} %copy-done.50, bf16[640,16,8]{0,2,1:T(8,128)(2,1)} %copy-done.74, bf16[640,16,8]{0,2,1:T(8,128)(2,1)} %copy-done.72, bf16[1024,16,64]{0,2,1:T(8,128)(2,1)} %bitcast.224), kind=kOutput, calls=%fused_computation.179 | convolution fusion | flops 1524760576 | bytes 29622272 | tf_op jit(solution)/shard_map/hqk,khd->qhd/dot_general | solution.py:277
  742.6 12.2 %fusion.162 = f32[1024,3072]{1,0:T(8,128)} fusion(f32[1024]{0:T(1024)S(1)} %bitcast.211, f32[1024]{0:T(1024)S(1)} %bitcast.202, f32[640]{0:T(1024)S(1)} %copy-done.91, f32[640]{0:T(1024)S(1)} %copy-done.86, bf16[128,1024]{0,1:T(8,128)(2,1)S(1)} %bitcast.186, bf16[512,1024]{0,1:T(8,128)(2,1)} %reduce-scatter.11.cloned.1.call-done, ...), kind=kOutput, calls=%fused_computation.325 | convolution fusion | flops 4048158720 | bytes 17839104 | tf_op jit(solution)/shard_map/dot_general | solution.py:59
  754.9 11.6 add_convert_fusion.2
  782.1 10.0 fusion.117
  793.8 5.8 fusion.114
  802.2 9.8 fusion.187
  812.1 7.2 fusion.186
  819.3 8.9 fusion.176
  828.2 14.5 %fusion.109 = (f32[1024]{0:T(1024)S(1)}, f32[640]{0:T(1024)S(1)}, f32[640]{0:T(1024)S(1)}, f32[1024]{0:T(1024)S(1)}, f32[1024]{0:T(1024)S(1)}, /*index=5*/f32[64...) fusion(f32[640]{0:T(1024)S(1)} %copy-done.91, ...), kind=kOutput, calls=%fused_computation.169 | convolution fusion | flops 4068462592 | bytes 23402496 | tf_op jit(solution)/shard_map/dot_general | solution.py:65
  842.8 24.3 %reduce-scatter.23.cloned.1.call-done = bf16[2048,1024]{1,0:T(8,128)(2,1)} async-done(((bf16[4096,1024]{1,0:T(8,128)(2,1)}), bf16[2048,1024]{1,0:T(8,128)(2,1)}) %reduce-scatter.23.cloned.1.call-update) | async-done | bytes 4194320 | tf_op jit(solution)/shard_map/reduce_scatter | solution.py:362
  867.1 79.9 %reduce-scatter.17.cloned.1.call-done = bf16[512,3072]{1,0:T(8,128)(2,1)} async-done(((bf16[1024,3072]{1,0:T(8,128)(2,1)}), bf16[512,3072]{1,0:T(8,128)(2,1)}) %reduce-scatter.17.cloned.1.call-update) | async-done | bytes 3145744 | tf_op jit(solution)/shard_map/reduce_scatter | solution.py:344
  947.2 5.4 convert_reduce_fusion.6
  956.2 4.4 convert_reduce_fusion.3
  960.7 4.4 convert_reduce_fusion.2
  965.2 7.1 all-reduce.9
  972.8 64.4 %all-reduce.7 = (bf16[512]{0:T(512)(128)(2,1)S(1)}, bf16[512]{0:T(512)(128)(2,1)S(1)}, bf16[512]{0:T(512)(128)(2,1)S(1)}, bf16[512]{0:T(512)(128)(2,1)S(1)}, bf1...) all-reduce(bf16[512]{0:T(512)(128)(2,1)S(1)} %dynamic-slice.1, ...), channel_id=1, replica_groups=mesh['rep'=16,'shard'=2] {'rep'}, use_global_device_ids=true, to_apply=%region_25.26 | all-reduce | flops 6144 | bytes 24576 | tf_op jit(solution)/shard_map/psum | solution.py:370
  1046.5 140.5 %all-reduce.12.cloned.1.call-done = (bf16[512,3072]{1,0:T(8,128)(2,1)}, bf16[512,1024]{1,0:T(8,128)(2,1)}, bf16[512,4096]{1,0:T(8,128)(2,1)}, bf16[2048,1024]{1,0:T(8,128)(2,1)}) async-done(((bf16[512,3072]{1,0:T(8,128)(2,1)}, bf16[512,1024]{1,0:T(8,128)(2,1)}, bf16[512,4096]{1,0:T(8,128)(2,1)}, bf16[2048,1024]{1,0:T(8,128)(2,1)}), (bf16[512,3072]{1,0:T(8,128)(2,1)}, bf16[512,1024]{1,0:T(8,128)(2,1)}, ...) | async-done | bytes 12582928 | tf_op jit(solution)/shard_map/psum | solution.py:374
  1193.5 4.5 convert_element_type.319
  1198.0 4.4 convert_element_type.325
  (464 shorter events, 183.1 us)
Async XLA Ops:
  7.2 85.6 %all-gather.16.cloned.1.call-start = ((), (), s32[]{:S(2)}) async-start(), calls=%async_computation.8 | async-start | bytes 9437184 | tf_op jit(solution)/shard_map/all_gather | solution.py:139
  7.9 159.5 %all-gather.22.cloned.1.call-start = ((), (), s32[]{:S(2)}) async-start(), calls=%async_computation.11 | async-start | bytes 3145728 | tf_op jit(solution)/shard_map/all_gather | solution.py:141
  8.7 177.1 %all-gather.28.cloned.1.call-start = ((), (), s32[]{:S(2)}) async-start(), calls=%async_computation.14 | async-start | bytes 3145728 | tf_op jit(solution)/shard_map/all_gather | solution.py:187
  8.8 84.0 %copy-start.33 = (bf16[128,1024]{1,0:T(8,128)(2,1)}, bf16[128,1024]{1,0:T(8,128)(2,1)S(1)}, u32[]{:S(2)}) copy-start(bf16[128,1024]{1,0:T(8,128)(2,1)S(1)} %get-tuple-element.137) | copy-start | bytes 786436
  8.8 111.8 %copy-start.18 = (bf16[128,1024]{1,0:T(8,128)(2,1)}, bf16[128,1024]{1,0:T(8,128)(2,1)S(1)}, u32[]{:S(2)}) copy-start(bf16[128,1024]{1,0:T(8,128)(2,1)S(1)} %get-tuple-element.136) | copy-start | bytes 786436
  10.7 82.0 %copy-start.2 = (bf16[512,1024]{1,0:T(8,128)(2,1)}, bf16[512,1024]{1,0:T(8,128)(2,1)S(1)}, u32[]{:S(2)}) copy-start(bf16[512,1024]{1,0:T(8,128)(2,1)S(1)} %get-tuple-element.129) | copy-start | bytes 3145732
  10.7 109.8 %copy-start = (bf16[512,1024]{1,0:T(8,128)(2,1)}, bf16[512,1024]{1,0:T(8,128)(2,1)S(1)}, u32[]{:S(2)}) copy-start(bf16[512,1024]{1,0:T(8,128)(2,1)S(1)} %get-tuple-element.128) | copy-start | bytes 3145732
  11.2 91.5 %copy-start.106 = (f32[640]{0:T(1024)}, f32[640]{0:T(1024)S(1)}, u32[]{:S(2)}) copy-start(f32[640]{0:T(1024)S(1)} %broadcast_multiply_fusion.8) | copy-start | bytes 7684
  11.2 109.3 %copy-start.85 = (f32[640]{0:T(1024)}, f32[640]{0:T(1024)S(1)}, u32[]{:S(2)}) copy-start(f32[640]{0:T(1024)S(1)} %broadcast_multiply_fusion.9) | copy-start | bytes 7684
  17.0 103.6 %copy-start.104 = (f32[2,1,512]{2,1,0:T(1,128)}, f32[2,1,512]{2,1,0:T(1,128)S(1)}, u32[]{:S(2)}) copy-start(f32[2,1,512]{2,1,0:T(1,128)S(1)} %convert_element_type.326) | copy-start | bytes 12292
  21.3 99.2 %copy-start.117 = (f32[2,1,512]{2,1,0:T(1,128)}, f32[2,1,512]{2,1,0:T(1,128)S(1)}, u32[]{:S(2)}) copy-start(f32[2,1,512]{2,1,0:T(1,128)S(1)} %convert_element_type.327) | copy-start | bytes 12292
  26.2 94.3 %copy-start.90 = (f32[640]{0:T(1024)}, f32[640]{0:T(1024)S(1)}, u32[]{:S(2)}) copy-start(f32[640]{0:T(1024)S(1)} %add_rsqrt_fusion.1) | copy-start | bytes 7684
  26.3 76.4 %copy-start.109 = (f32[640]{0:T(1024)}, f32[640]{0:T(1024)S(1)}, u32[]{:S(2)}) copy-start(f32[640]{0:T(1024)S(1)} %add_rsqrt_fusion) | copy-start | bytes 7684
  27.0 109.9 %copy-start.93 = (f32[640,8]{0,1:T(8,128)}, f32[640,8]{0,1:T(8,128)S(1)}, u32[]{:S(2)}) copy-start(f32[640,8]{0,1:T(8,128)S(1)} %get-tuple-element.162) | copy-start | bytes 61444
  105.7 92.3 %all-gather.30.cloned.1.call-start = ((), (), s32[]{:S(2)}) async-start(), calls=%async_computation.15 | async-start | bytes 3145728 | tf_op jit(solution)/shard_map/all_gather | solution.py:186
  141.2 171.4 %all-gather.18.cloned.1.call-start = ((), (), s32[]{:S(2)}) async-start(), calls=%async_computation.9 | async-start | bytes 3145728 | tf_op jit(solution)/shard_map/all_gather | solution.py:187
  143.7 187.1 %all-gather.20.cloned.1.call-start = ((), (), s32[]{:S(2)}) async-start(), calls=%async_computation.10 | async-start | bytes 3145728 | tf_op jit(solution)/shard_map/all_gather | solution.py:186
  146.8 399.3 %all-gather.24.cloned.1.call-start = ((), (), s32[]{:S(2)}) async-start(), calls=%async_computation.12 | async-start | bytes 12582912 | tf_op jit(solution)/shard_map/all_gather | solution.py:143
  147.6 15.8 %copy-start.84 = (bf16[2,1,1,128,1024]{4,3,2,1,0:T(8,128)(2,1)S(1)}, bf16[2,1,1,128,1024]{4,3,2,1,0:T(8,128)(2,1)}, u32[]{:S(2)}) copy-start(bf16[2,1,1,128,1024]{4,3,2,1,0:T(8,128)(2,1)} %param.19) | copy-start | bytes 1572868
  147.6 465.0 %all-gather.26.cloned.1.call-start = ((), (), s32[]{:S(2)}) async-start(), calls=%async_computation.13 | async-start | bytes 12582912 | tf_op jit(solution)/shard_map/all_gather | solution.py:145
  148.3 583.4 %reduce-scatter.13.cloned.1.call-start = ((), (), s32[]{:S(2)}) async-start(), calls=%async_computation.18 | async-start | bytes 3145728 | tf_op jit(solution)/shard_map/reduce_scatter | solution.py:291
  178.6 61.8 %copy-start.7 = (bf16[640,1024]{0,1:T(8,128)(2,1)}, bf16[640,1024]{0,1:T(8,128)(2,1)S(1)}, u32[]{:S(2)}) copy-start(bf16[640,1024]{0,1:T(8,128)(2,1)S(1)} %copy.75) | copy-start | bytes 3932164
  219.2 20.6 %copy-start.95 = (f32[16,640]{1,0:T(8,128)}, f32[16,640]{1,0:T(8,128)S(1)}, u32[]{:S(2)}) copy-start(f32[16,640]{1,0:T(8,128)S(1)} %get-tuple-element.165) | copy-start | bytes 122884
  219.2 21.2 %copy-start.14 = (bf16[1152,1024]{0,1:T(8,128)(2,1)S(1)}, bf16[1152,1024]{0,1:T(8,128)(2,1)}, u32[]{:S(2)}) copy-start(bf16[1152,1024]{0,1:T(8,128)(2,1)} %copy.71) | copy-start | bytes 7077892
  352.0 20.5 %copy-start.99 = (f32[16,640]{1,0:T(8,128)}, f32[16,640]{1,0:T(8,128)S(1)}, u32[]{:S(2)}) copy-start(f32[16,640]{1,0:T(8,128)S(1)} %get-tuple-element.170) | copy-start | bytes 122884
  372.5 37.5 %copy-start.101 = (f32[16,640]{1,0:T(8,128)}, f32[16,640]{1,0:T(8,128)S(1)}, u32[]{:S(2)}) copy-start(f32[16,640]{1,0:T(8,128)S(1)} %fusion) | copy-start | bytes 122884
  372.5 360.8 %reduce-scatter.9.cloned.1.call-start = ((), (), s32[]{:S(2)}) async-start(), calls=%async_computation.16 | async-start | bytes 3145728 | tf_op jit(solution)/shard_map/reduce_scatter | solution.py:291
  409.9 37.9 %copy-start.81 = (bf16[640,16,8]{0,2,1:T(8,128)(2,1)S(1)}, bf16[640,16,8]{0,2,1:T(8,128)(2,1)}, u32[]{:S(2)}) copy-start(bf16[640,16,8]{0,2,1:T(8,128)(2,1)} %get-tuple-element.149) | copy-start | bytes 491524
  461.5 281.1 %reduce-scatter.11.cloned.1.call-start = ((), (), s32[]{:S(2)}) async-start(), calls=%async_computation.17 | async-start | bytes 3145728 | tf_op jit(solution)/shard_map/reduce_scatter | solution.py:294
  479.0 21.2 %copy-start.9 = (bf16[1152,16,64]{0,2,1:T(8,128)(2,1)}, bf16[1152,16,64]{0,2,1:T(8,128)(2,1)S(1)}, u32[]{:S(2)}) copy-start(bf16[1152,16,64]{0,2,1:T(8,128)(2,1)S(1)} %fusion.56) | copy-start | bytes 7077892
  503.5 18.3 %copy-start.100 = (f32[16,640]{1,0:T(8,128)S(1)}, f32[16,640]{1,0:T(8,128)}, u32[]{:S(2)}) copy-start(f32[16,640]{1,0:T(8,128)} %copy-done.99) | copy-start | bytes 122884
  503.5 18.3 %copy-start.102 = (f32[16,640]{1,0:T(8,128)S(1)}, f32[16,640]{1,0:T(8,128)}, u32[]{:S(2)}) copy-start(f32[16,640]{1,0:T(8,128)} %copy-done.101) | copy-start | bytes 122884
  503.6 251.3 %reduce-scatter.15.cloned.1.call-start = ((), (), s32[]{:S(2)}) async-start(), calls=%async_computation.19 | async-start | bytes 3145728 | tf_op jit(solution)/shard_map/reduce_scatter | solution.py:294
  521.8 18.9 %copy-start.38 = (bf16[512,1024]{1,0:T(8,128)(2,1)S(1)}, bf16[512,1024]{1,0:T(8,128)(2,1)}, u32[]{:S(2)}) copy-start(bf16[512,1024]{1,0:T(8,128)(2,1)} %copy-done.37) | copy-start | bytes 3145732
  521.8 18.9 %copy-start.65 = (bf16[128,1024]{1,0:T(8,128)(2,1)S(1)}, bf16[128,1024]{1,0:T(8,128)(2,1)}, u32[]{:S(2)}) copy-start(bf16[128,1024]{1,0:T(8,128)(2,1)} %copy-done.64) | copy-start | bytes 786436
  521.8 321.0 %reduce-scatter.19.cloned.1.call-start = ((), (), s32[]{:S(2)}) async-start(), calls=%async_computation.21 | async-start | bytes 3145728 | tf_op jit(solution)/shard_map/reduce_scatter | solution.py:350
  546.0 296.7 %reduce-scatter.21.cloned.1.call-start = ((), (), s32[]{:S(2)}) async-start(), calls=%async_computation.22 | async-start | bytes 12582912 | tf_op jit(solution)/shard_map/reduce_scatter | solution.py:356
  558.7 53.8 %copy-start.39 = (bf16[512,1024]{1,0:T(8,128)(2,1)S(1)}, bf16[512,1024]{1,0:T(8,128)(2,1)}, u32[]{:S(2)}) copy-start(bf16[512,1024]{1,0:T(8,128)(2,1)} %copy-done.37) | copy-start | bytes 3145732
  558.7 53.8 %copy-start.66 = (bf16[128,1024]{1,0:T(8,128)(2,1)S(1)}, bf16[128,1024]{1,0:T(8,128)(2,1)}, u32[]{:S(2)}) copy-start(bf16[128,1024]{1,0:T(8,128)(2,1)} %copy-done.64) | copy-start | bytes 786436
  636.9 14.6 %copy-start.4 = (bf16[512,1024]{1,0:T(8,128)(2,1)S(1)}, bf16[512,1024]{1,0:T(8,128)(2,1)}, u32[]{:S(2)}) copy-start(bf16[512,1024]{1,0:T(8,128)(2,1)} %copy-done.2) | copy-start | bytes 3145732
  664.6 202.6 %reduce-scatter.23.cloned.1.call-start = ((), (), s32[]{:S(2)}) async-start(), calls=%async_computation.23 | async-start | bytes 12582912 | tf_op jit(solution)/shard_map/reduce_scatter | solution.py:362
  691.6 255.4 %reduce-scatter.17.cloned.1.call-start = ((), (), s32[]{:S(2)}) async-start(), calls=%async_computation.20 | async-start | bytes 9437184 | tf_op jit(solution)/shard_map/reduce_scatter | solution.py:344
  699.0 16.6 %copy-start.50 = (bf16[640,16,48]{0,2,1:T(8,128)(2,1)S(1)}, bf16[640,16,48]{0,2,1:T(8,128)(2,1)}, u32[]{:S(2)}) copy-start(bf16[640,16,48]{0,2,1:T(8,128)(2,1)} %copy-done.48) | copy-start | bytes 2949124
  766.5 420.5 %all-reduce.12.cloned.1.call-start = ((), (), s32[]{:S(2)}) async-start(), calls=%async_computation.24 | async-start | bytes 25165824 | tf_op jit(solution)/shard_map/psum | solution.py:374
  778.4 15.4 %slice-start.4 = ((s8[8388608]{0:T(1024)(128)(4,1)}), s8[4194304]{0:T(1024)(128)(4,1)S(1)}, s32[]{:S(2)}) async-start(s8[8388608]{0:T(1024)(128)(4,1)} %bitcast.219), calls=%async_computation.29 | async-start | bytes 8388608
  778.4 15.4 %slice-start.6 = ((s8[5242880]{0:T(1024)(128)(4,1)}), s8[4194304]{0:T(1024)(128)(4,1)S(1)}, s32[]{:S(2)}) async-start(s8[5242880]{0:T(1024)(128)(4,1)} %bitcast.225), calls=%async_computation.31 | async-start | bytes 8388608
  960.7 80.0 %copy-start.12 = (f32[640,1024]{1,0:T(8,128)S(1)}, f32[640,1024]{1,0:T(8,128)}, u32[]{:S(2)}) copy-start(f32[640,1024]{1,0:T(8,128)} %get-tuple-element.131) | copy-start | bytes 7864324
  1037.7 164.7 %copy-start.114 = (f32[512]{0:T(512)}, f32[512]{0:T(512)S(1)}, u32[]{:S(2)}) copy-start(f32[512]{0:T(512)S(1)} %convert_element_type.317) | copy-start | bytes 6148
  (107 other events, 608.7 us)
Sparse Core Ops, SparseCore 0:
  9.6 83.1 all-gather.15
  94.3 33.1 all-gather.21
  129.6 33.2 all-gather.27
  164.9 33.0 all-gather.29
  199.4 33.1 all-gather.17
  233.9 33.1 all-gather.19
  268.6 104.0 all-gather.23
  374.2 103.9 all-gather.25
  481.1 31.8 reduce-scatter.12
  515.1 31.8 reduce-scatter.8
  549.3 31.8 reduce-scatter.10
  583.9 31.8 reduce-scatter.14
  618.0 31.8 reduce-scatter.18
  664.7 100.3 reduce-scatter.20
  767.8 99.2 reduce-scatter.22
  869.9 77.0 reduce-scatter.16
  951.4 235.5 all-reduce.11
where the time goes:
time: 1220 us; the launch traced here: 1210 us
  matrix products  484 us (40%)
  waiting for transfers between devices  318 us (26%)
  other arithmetic  188 us (15%)
  blocking collectives  107 us (9%)
  local copies, waits for them, and re-layouts  93.6 us (8%)
  between operations  18 us (1%)
    psum x1, waiting for transfers between devices, per_device(): lax.psum(owned[4].astype(jnp.bfloat16), 'rep').astype(jnp.float32)  141 us
    reduce_scatter x1, waiting for transfers between devices, per_device(): lax.psum_scatter(totals[4].astype(jnp.bfloat16), 'shard', scatter_dimensi...  79.9 us
    convert_element_type x2, other arithmetic, per_device(): d_scores = (probs * (d_probs - delta)).astype(jnp.bfloat16)  79.5 us
    dot_general x8, matrix products, inner_rows(): lax.dot_general(left_mat, right_mat, (((0,), (0,)), ((), ())), preferred_...  79.5 us
    dot_general x8, matrix products, inner_cols(): lax.dot_general(left_mat, right_mat, (((1,), (1,)), ((), ())), preferred_...  73.1 us
    dot_general x2, matrix products, per_device(): jnp.einsum('qhd,khd->hqk', d_context, all_values, preferred_element_type=...  66.8 us
    all_gather x1, waiting for transfers between devices, per_device(): lax.all_gather(qkv_weight, 'shard', axis=0, tiled=True)  65.7 us
    psum x1, blocking collectives, per_device(): lax.psum(owned[0].astype(jnp.bfloat16), 'rep').astype(jnp.float32)  64.4 us
  transfers between devices with their start and end apart: 17, of which 5 were waited for; matrix products, arithmetic and copies ran while one was open for 61% of the time, Pallas kernels for 0%

commit v1 on v0

v1 whole, which is shorter than its diff:
```python
import functools
import math

import jax
import jax.numpy as jnp
import numpy as np
from jax import lax
from jax.experimental import pallas as pl
from jax.experimental.pallas import tpu as pltpu
from jax.sharding import PartitionSpec as P

H = 16
HD = 64
ROT = 16
EPS = 1e-05
F32 = jnp.float32
BF = jnp.bfloat16
MIB = 1024 * 1024
SD = jax.ShapeDtypeStruct


def dnn(a, b):
    return lax.dot_general(a, b, (((1,), (0,)), ((), ())), preferred_element_type=F32)


def dnt(a, b):
    return lax.dot_general(a, b, (((1,), (1,)), ((), ())), preferred_element_type=F32)


def dtn(a, b):
    return lax.dot_general(a, b, (((0,), (0,)), ((), ())), preferred_element_type=F32)


def normed(rows):
    x = rows.astype(F32)
    c = x - jnp.mean(x, axis=-1, keepdims=True)
    inv = lax.rsqrt(jnp.mean(c * c, axis=-1, keepdims=True) + EPS)
    return c * inv, inv


def tile(i, n):
    return pl.ds(pl.multiple_of(i * n, n), n)


def rows_tile(n, most):
    t = most
    while n % t:
        t -= 8
    return t


def mlp_kernel(rt, x_ref, dy_ref, wu_ref, bu_ref, wd_ref, gb_ref, act_ref, dpre_ref, h_ref, yp_ref, g2_ref, ln_ref, bu_out, yacc, dacc):
    f = pl.program_id(0)
    last = pl.num_programs(0) - 1
    rows = x_ref.shape[0]

    @pl.when(f == 0)
    def _():
        @pl.loop(0, rows // 128)
        def _(i):
            r = tile(i, 128)
            xh, _ = normed(x_ref[r, :])
            h_ref[r, :] = (xh * gb_ref[0:1, :] + gb_ref[1:2, :]).astype(BF)
            yacc[r, :] = jnp.zeros((128, yacc.shape[1]), F32)
            dacc[r, :] = jnp.zeros((128, dacc.shape[1]), F32)

    def step(i, bsum):
        r = tile(i, rt)
        pre = dnn(h_ref[r, :], wu_ref[...]) + bu_ref[...]
        da = dnt(dy_ref[r, :], wd_ref[...])
        cdf = 0.5 * (1.0 + lax.erf(pre * 0.7071067811865476))
        act = (pre * cdf).astype(BF)
        dpre = (da * (cdf + pre * jnp.exp(-0.5 * pre * pre) * 0.3989422804014327)).astype(BF)
        act_ref[r, :] = act
        dpre_ref[r, :] = dpre
        yacc[r, :] += dnn(act, wd_ref[...])
        dacc[r, :] += dnt(dpre, wu_ref[...])
        return bsum + jnp.sum(dpre.astype(F32), axis=0, keepdims=True)

    bu_out[...] = lax.fori_loop(0, rows // rt, step, jnp.zeros(bu_out.shape, F32))

    @pl.when(f == last)
    def _():
        ln_ref[...] = jnp.zeros_like(ln_ref)

        @pl.loop(0, rows // 128)
        def _(i):
            r = tile(i, 128)
            xh, _ = normed(x_ref[r, :])
            dh = dacc[r, :]
            yp_ref[r, :] = yacc[r, :].astype(BF)
            g2_ref[r, :] = (dh * gb_ref[0:1, :]).astype(BF)
            ln_ref[0:1, :] += jnp.sum(dh * xh, axis=0, keepdims=True)
            ln_ref[1:2, :] += jnp.sum(dh, axis=0, keepdims=True)


def mlp_rows(x, dy, wu, bu, wd, gb):
    rows, width = x.shape
    hidden = wu.shape[1]
    fb = min(512, hidden)
    full = lambda s: pl.BlockSpec(s, lambda f: (0,) * len(s))
    return pl.pallas_call(
        functools.partial(mlp_kernel, rows_tile(rows, 640)),
        grid=(hidden // fb,),
        in_specs=[
            full((rows, width)),
            full((rows, width)),
            pl.BlockSpec((width, fb), lambda f: (0, f)),
            pl.BlockSpec((1, fb), lambda f: (0, f)),
            pl.BlockSpec((fb, width), lambda f: (f, 0)),
            full((2, width)),
        ],
        out_specs=[
            pl.BlockSpec((rows, fb), lambda f: (0, f)),
            pl.BlockSpec((rows, fb), lambda f: (0, f)),
            full((rows, width)),
            full((rows, width)),
            full((rows, width)),
            full((2, width)),
            pl.BlockSpec((1, fb), lambda f: (0, f)),
        ],
        out_shape=[
            SD((rows, hidden), BF),
            SD((rows, hidden), BF),
            SD((rows, width), BF),
            SD((rows, width), BF),
            SD((rows, width), BF),
            SD((2, width), F32),
            SD((1, hidden), F32),
        ],
        scratch_shapes=[pltpu.VMEM((rows, width), F32)] * 2,
        compiler_params=pltpu.CompilerParams(vmem_limit_bytes=60 * MIB),
        cost_estimate=pl.CostEstimate(
            flops=8 * rows * width * hidden,
            bytes_accessed=4 * (width * hidden + rows * hidden) + 10 * rows * width,
            transcendentals=2 * rows * hidden,
        ),
    )(x, dy, wu, bu, wd, gb)


def roll8(x, left):
    w = x.shape[-1]
    return pltpu.roll(x, (w - 8) if left else 8, 1)


def attn_kernel(S, PD, CL, QB, HG, adding, me_ref, *refs):
    it = iter(refs)
    take = lambda n: [next(it) for _ in range(n)]
    xs = take(S)
    dys = take(S)
    yps = take(S * adding)
    g2s = take(S * adding)
    wq, wk, wv = take(3)
    bq, bk, bv = take(3)
    wo, gb = take(2)
    cr, s1r, s2r = take(3)
    ys = take(S)
    gs = take(S)
    dl, ctx, h1, dyc, ln, db = take(6)
    yacc, dacc, q_s, k_s, v_s, dc_s, kT, vT, dk_s, dv_s = take(10)
    g = pl.program_id(0)
    last = pl.num_programs(0) - 1
    me = me_ref[0]
    N, _ = xs[0].shape
    T = N * S
    PR = PD * S
    CR = N - PD
    W = HG * HD

    def each_slot(fn):
        for s in range(S):
            for j in range(S):

                @pl.when(lax.rem(me + j, S) == s)
                def _():
                    fn(s, j)

    def spans(s):
        return ((0, PD, s * PD), (PD, CR, PR + s * CR))

    @pl.when(g == 0)
    def _():
        def load(s, j):
            for a, n, c in spans(s):
                xh, _ = normed(xs[j][a : a + n, :])
                h1[c : c + n, :] = (xh * gb[0:1, :] + gb[1:2, :]).astype(BF)
                dyc[c : c + n, :] = dys[j][a : a + n, :]

        each_slot(load)

    RT = T // 2

    def proj(i, _):
        r = tile(i, RT)
        c = cr[r, :]
        s1 = s1r[r, :]
        s2 = s2r[r, :]

        def rot(y, scale):
            out = []
            for p in range(W // 128):
                z = y[:, p * 128 : (p + 1) * 128]
                z = (z * c + roll8(z, True) * s1 + roll8(z, False) * s2).astype(BF)
                out.append(z * jnp.asarray(scale, BF))
            return jnp.concatenate(out, axis=1) if len(out) > 1 else out[0]

        hh = h1[r, :]
        q_s[r, :] = rot(dnn(hh, wq[...]) + bq[...], HD**-0.5)
        k_s[r, :] = rot(dnn(hh, wk[...]) + bk[...], 1.0)
        v_s[r, :] = (dnn(hh, wv[...]) + bv[...]).astype(BF)
        dc_s[r, :] = dnt(dyc[r, :], wo[...]).astype(BF)
        return 0

    lax.fori_loop(0, 2, proj, 0)
    lane = lax.broadcasted_iota(jnp.int32, (1, 128), 1)
    row_i = lax.broadcasted_iota(jnp.int32, (QB, QB), 0)
    col_i = lax.broadcasted_iota(jnp.int32, (QB, QB), 1)
    causal = row_i <= col_i
    cmask = causal & ((row_i // CL) == (col_i // CL))
    blocks = []
    for i in range(PR // QB):
        blocks.append((i * QB, [(0, i * QB, None)] * (i > 0) + [(i * QB, QB, causal)]))
    for c in range((T - PR) // QB):
        blocks.append((PR + c * QB, [(0, PR, None), (PR + c * QB, QB, cmask)]))

    @pl.loop(0, W // 128)
    def _(p):
        lanes = tile(p, 128)
        kT[...] = k_s[:, lanes].T
        vT[...] = v_s[:, lanes].T
        dk_s[...] = jnp.zeros_like(dk_s)
        dv_s[...] = jnp.zeros_like(dv_s)
        for q0, parts in blocks:
            rq = pl.ds(q0, QB)
            qb = q_s[rq, lanes]
            dcb = dc_s[rq, lanes]
            P_, DS, qh, dch, cT, dqT = [], [], [], [], [], []
            for h in range(2):
                sel = (lane >= HD * h) & (lane < HD * h + HD)
                qm = jnp.where(sel, qb, jnp.zeros_like(qb))
                dm = jnp.where(sel, dcb, jnp.zeros_like(dcb))
                qh.append(qm)
                dch.append(dm)
                ss = []
                for k0, n, mask in parts:
                    s = dnt(k_s[k0 : k0 + n, lanes], qm)
                    if mask is not None:
                        s = jnp.where(mask, s, -1e30)
                    ss.append(s)
                m = functools.reduce(jnp.maximum, [jnp.max(s, axis=0, keepdims=True) for s in ss])
                es = [jnp.exp(s - m) for s in ss]
                rl = 1.0 / sum(jnp.sum(e, axis=0, keepdims=True) for e in es)
                ps = [e * rl for e in es]
                dps = [dnt(v_s[k0 : k0 + n, lanes], dm) for k0, n, _ in parts]
                delta = sum(jnp.sum(a * b, axis=0, keepdims=True) for a, b in zip(ps, dps))
                P_.append([a.astype(BF) for a in ps])
                DS.append([(a * (b - delta)).astype(BF) for a, b in zip(ps, dps)])
                hr = slice(HD * h, HD * h + HD)
                cT.append(sum(dnn(vT[hr, k0 : k0 + n], a) for (k0, n, _), a in zip(parts, P_[h])))
                dqT.append(sum(dnn(kT[hr, k0 : k0 + n], a) for (k0, n, _), a in zip(parts, DS[h])))
            q2 = jnp.concatenate(qh, axis=0)
            dc2 = jnp.concatenate(dch, axis=0)
            for i, (k0, n, _) in enumerate(parts):
                dv_s[k0 : k0 + n, :] += dnn(jnp.concatenate([P_[0][i], P_[1][i]], axis=1), dc2)
                dk_s[k0 : k0 + n, :] += dnn(jnp.concatenate([DS[0][i], DS[1][i]], axis=1), q2)
            ctx[rq, lanes] = jnp.concatenate(cT, axis=0).T.astype(BF)
            z = jnp.concatenate(dqT, axis=0).T * (HD**-0.5)
            z = z * cr[rq, :] - roll8(z, True) * s1r[rq, :] - roll8(z, False) * s2r[rq, :]
            dl[0, rq, lanes] = z.astype(BF)
        z = dk_s[...]
        z = z * cr[...] - roll8(z, True) * s1r[...] - roll8(z, False) * s2r[...]
        dl[1, :, lanes] = z.astype(BF)
        dl[2, :, lanes] = dv_s[...].astype(BF)

    for c in range(3):
        db[c : c + 1, :] = jnp.sum(dl[c].astype(F32), axis=0, keepdims=True)

    def post(i, first):
        r = tile(i, RT)
        y = dnn(ctx[r, :], wo[...])
        d = dnt(dl[0, r, :], wq[...]) + dnt(dl[1, r, :], wk[...]) + dnt(dl[2, r, :], wv[...])
        if first:
            yacc[r, :] = y
            dacc[r, :] = d
        else:
            yacc[r, :] += y
            dacc[r, :] += d

    @pl.when(g == 0)
    def _():
        @pl.loop(0, 2)
        def _(i):
            post(i, True)

    @pl.when(g > 0)
    def _():
        @pl.loop(0, 2)
        def _(i):
            post(i, False)

    @pl.when(g == last)
    def _():
        ln[...] = jnp.zeros_like(ln)

        def store(s, j):
            for a, n, c in spans(s):
                xh, _ = normed(xs[j][a : a + n, :])
                d = dacc[c : c + n, :]
                y = yacc[c : c + n, :]
                gg = d * gb[0:1, :]
                if adding:
                    y = y + yps[j][a : a + n, :].astype(F32)
                    gg = gg + g2s[j][a : a + n, :].astype(F32)
                ys[j][a : a + n, :] = y.astype(BF)
                gs[j][a : a + n, :] = gg.astype(BF)
                ln[0:1, :] += jnp.sum(d * xh, axis=0, keepdims=True)
                ln[1:2, :] += jnp.sum(d, axis=0, keepdims=True)

        each_slot(store)


def attn_group(S, PD, CL, me, xs, dys, yps, g2s, wqkv, bqkv, wo, gb, tabs):
    N, D = xs[0].shape
    CW = wo.shape[0]
    T = N * S
    HG = 4 if CW % 256 == 0 else 2
    QB = 256
    W = HG * HD
    G = CW // W
    full = lambda s: pl.BlockSpec(s, lambda g, m: (0,) * len(s), pipeline_mode=pl.Buffered(1))
    keep = lambda s: pl.BlockSpec(s, lambda g, m: (0,) * len(s))
    tok = full((N, D))
    adding = int(T * D <= 1536 * 1024)
    if not adding:
        others = (yps, g2s)
        yps, g2s = [], []
    wspec = lambda c: pl.BlockSpec((D, W), lambda g, m: (0, c * G + g))
    bspec = lambda c: pl.BlockSpec((1, W), lambda g, m: (0, c * G + g))
    outs = pl.pallas_call(
        functools.partial(attn_kernel, S, PD, CL, QB, HG, adding),
        grid_spec=pltpu.PrefetchScalarGridSpec(
            num_scalar_prefetch=1,
            grid=(G,),
            in_specs=[tok] * ((2 + 2 * adding) * S)
            + [wspec(0), wspec(1), wspec(2), bspec(0), bspec(1), bspec(2)]
            + [pl.BlockSpec((W, D), lambda g, m: (g, 0)), full((2, D))]
            + [full((T, 128))] * 3,
            out_specs=[keep((N, D))] * (2 * S)
            + [
                pl.BlockSpec((3, T, W), lambda g, m: (0, 0, g)),
                pl.BlockSpec((T, W), lambda g, m: (0, g)),
                keep((T, D)),
                keep((T, D)),
                keep((2, D)),
                pl.BlockSpec((3, W), lambda g, m: (0, g)),
            ],
            scratch_shapes=[pltpu.VMEM((T, D), F32)] * 2
            + [pltpu.VMEM((T, W), BF)] * 4
            + [pltpu.VMEM((128, T), BF)] * 2
            + [pltpu.VMEM((T, 128), F32)] * 2,
        ),
        out_shape=[SD((N, D), BF)] * (2 * S)
        + [SD((3, T, CW), BF), SD((T, CW), BF), SD((T, D), BF), SD((T, D), BF), SD((2, D), F32), SD((3, CW), F32)],
        compiler_params=pltpu.CompilerParams(vmem_limit_bytes=62 * MIB),
        cost_estimate=pl.CostEstimate(
            flops=16 * T * D * CW + 48 * T * T * CW, bytes_accessed=16 * T * D + 12 * T * CW + 8 * D * CW, transcendentals=T * T * CW // HD
        ),
    )(me, *xs, *dys, *yps, *g2s, wqkv, wqkv, wqkv, bqkv, bqkv, bqkv, wo, gb, *tabs)
    ys, gs = outs[:S], outs[S : 2 * S]
    if not adding:
        ys, gs = [[a + b for a, b in zip(p, q)] for p, q in zip((ys, gs), others)]
    return ys, gs, outs[2 * S :]


def tn_kernel(n, wide, *refs):
    a = refs[:n]
    b = refs[n : 2 * n]
    o = refs[2 * n]
    if wide == 0:
        o[...] = sum(dtn(x[...], y[...]) for x, y in zip(a, b)).astype(BF)
    else:
        w = b[0].shape[2]
        for c in range(wide):
            o[:, c * w : (c + 1) * w] = sum(dtn(x[...], y[c]) for x, y in zip(a, b)).astype(BF)


def tn_sum(a, b, block):
    n = len(a)
    rows, da = a[0].shape
    block = min(block, da)
    wide = b[0].shape[0] if b[0].ndim == 3 else 0
    db = b[0].shape[-1] * max(wide, 1)
    keep = lambda s: pl.BlockSpec(s, lambda i: (0,) * len(s), pipeline_mode=pl.Buffered(1))
    return pl.pallas_call(
        functools.partial(tn_kernel, n, wide),
        grid=(da // block,),
        in_specs=[pl.BlockSpec((rows, block), lambda i: (0, i))] * n + [keep(b[0].shape)] * n,
        out_specs=pl.BlockSpec((block, db), lambda i: (i, 0)),
        out_shape=SD((da, db), BF),
        compiler_params=pltpu.CompilerParams(vmem_limit_bytes=60 * MIB),
        cost_estimate=pl.CostEstimate(flops=2 * n * rows * da * db, bytes_accessed=2 * (n * rows * (da + db) + da * db), transcendentals=0),
    )(*a, *b)


def final_kernel(S, first, PT, *refs):
    it = iter(refs)
    take = lambda n: [next(it) for _ in range(n)]
    x, dy = take(2)
    ys = take(S)
    gs = take(S)
    (vb,) = take(1)
    if not first:
        take(4)
    po, co, pg, cg = take(4)
    i = pl.program_id(0)
    xv = x[...].astype(F32)
    xh, inv = normed(xv)
    y = xv + vb[0:1, :] + sum(r[...].astype(F32) for r in ys) + vb[1:2, :]
    gsum = sum(r[...].astype(F32) for r in gs)
    dx = (gsum - jnp.mean(gsum, axis=-1, keepdims=True) - xh * jnp.mean(gsum * xh, axis=-1, keepdims=True)) * inv
    out = y.astype(BF)
    grad = dy[...].astype(F32) + dx

    @pl.when(i < PT)
    def _():
        po[0] = out
        pg[0] = grad

    @pl.when(i >= PT)
    def _():
        co[0] = out
        cg[0] = grad


def final_rows(m, MB, PD, x, dy, ys, gs, vb, prior):
    S = len(ys)
    N, D = x.shape
    CR = N - PD
    RT = 128
    PT = PD // RT
    first = prior is None
    row = pl.BlockSpec((RT, D), lambda i: (i, 0))
    pspec = pl.BlockSpec((1, RT, D), lambda i: (m, jnp.minimum(i, PT - 1), 0))
    cspec = pl.BlockSpec((1, RT, D), lambda i: (m, jnp.maximum(i - PT, 0), 0))
    hbm = pl.BlockSpec(memory_space=pl.ANY)
    n_in = 2 * S + 3
    return pl.pallas_call(
        functools.partial(final_kernel, S, first, PT),
        grid=(N // RT,),
        in_specs=[row] * (2 * S + 2) + [pl.BlockSpec((2, D), lambda i: (0, 0))] + ([] if first else [hbm] * 4),
        out_specs=[pspec, cspec, pspec, cspec],
        out_shape=[SD((MB, PD, D), BF), SD((MB, CR, D), BF), SD((MB, PD, D), F32), SD((MB, CR, D), F32)],
        input_output_aliases={} if first else {n_in + k: k for k in range(4)},
        compiler_params=pltpu.CompilerParams(vmem_limit_bytes=32 * MIB),
        cost_estimate=pl.CostEstimate(flops=20 * N * D, bytes_accessed=(4 * S + 10) * N * D, transcendentals=0),
    )(x, dy, *ys, *gs, vb, *(() if first else prior))


def shifted(value, S, j):
    return lax.ppermute(value, "shard", [(i, (i + j) % S) for i in range(S)])


def canonical(slots, me, S, back):
    if S == 1:
        return slots
    stacked = jnp.stack(slots, axis=0)
    return [
        lax.dynamic_index_in_dim(stacked, lax.rem((me - s if back else s - me) + S, S), 0, keepdims=False) for s in range(S)
    ]


def columns_for(weight, me, S, j, parts):
    rows, cols = weight.shape
    w = weight.reshape(rows, parts, S, cols // (parts * S))
    w = lax.dynamic_index_in_dim(w, lax.rem(me + j, S), 2, keepdims=False)
    return w.reshape(rows, cols // S)


def my_columns(weight, me, S, R, parts):
    rows = weight.shape[0]
    own = columns_for(weight, me, S, 0, parts)
    if S == 1:
        return own
    rep = lax.axis_index("rep")
    chunk = rows // R
    got = []
    for j in range(1, S):
        piece = columns_for(weight, me, S, j, parts)
        piece = lax.dynamic_slice_in_dim(piece, rep * chunk, chunk, 0)
        got.append(shifted(piece, S, j))
    others = lax.all_gather(jnp.stack(got, axis=0), "rep", axis=1, tiled=True)
    return jnp.concatenate(canonical([own] + [others[j] for j in range(S - 1)], me, S, True), axis=0)


def reduce_rows(grad):
    part = lax.psum_scatter(grad, "rep", scatter_dimension=0, tiled=True)
    return lax.all_gather(part, "rep", axis=0, tiled=True).astype(F32)


def reduce_columns(grad, me, S, parts):
    rows, cols = grad.shape
    part = lax.psum_scatter(grad.reshape(S, rows // S, cols), "rep", scatter_dimension=1, tiled=True)
    slots = [lax.dynamic_index_in_dim(part, me, 0, keepdims=False)]
    for j in range(1, S):
        slots.append(shifted(lax.dynamic_index_in_dim(part, lax.rem(me + j, S), 0, keepdims=False), S, j))
    slots = [s.reshape(s.shape[0], parts, cols // parts) for s in slots]
    whole = jnp.stack(canonical(slots, me, S, True), axis=2).reshape(-1, S * cols)
    return lax.all_gather(whole, "rep", axis=0, tiled=True).astype(F32)


def rotary_tables(PR, CR, CL):
    pos = np.concatenate([np.arange(PR), PR + np.arange(CR) % CL]).astype(np.float32)
    half = ROT // 2
    freq = np.exp(np.arange(half, dtype=np.float32) * np.float32(-2.0 * math.log(10000.0) / ROT)).astype(np.float32)
    ang = (pos[:, None] * freq[None, :]).astype(np.float32)
    c = np.cos(ang)
    s = np.sin(ang)
    n = pos.shape[0]
    one = np.ones((n, HD - ROT), np.float32)
    zero = np.zeros((n, HD - ROT), np.float32)
    z8 = np.zeros((n, half), np.float32)
    tabs = ([c, c, one], [-s, z8, zero], [z8, s, zero])
    return [jnp.asarray(np.tile(np.concatenate(t, axis=1), (1, 128 // HD)), F32) for t in tabs]


def per_device(
    prompt_in,
    cont_in,
    prompt_cot,
    cont_cot,
    ln1_gain,
    ln1_bias,
    ln2_gain,
    ln2_bias,
    qkv_weight,
    qkv_bias,
    out_weight,
    out_bias,
    up_weight,
    up_bias,
    down_weight,
    down_bias,
):
    S = lax.axis_size("shard")
    R = lax.axis_size("rep")
    me = lax.axis_index("shard")
    MB, _, PD, D = prompt_in.shape
    CD, CL = cont_in.shape[2:4]
    CR = CD * CL
    N = PD + CR
    CW = D // S
    FL = up_weight.shape[1] // S
    me_arr = jnp.reshape(me, (1,)).astype(jnp.int32)

    small = jnp.concatenate([ln1_gain, ln1_bias, ln2_gain, ln2_bias, out_bias, down_bias, qkv_bias])
    slots = [small] + [shifted(small, S, j) for j in range(1, S)]
    whole = jnp.stack(canonical(slots, me, S, True), axis=0).astype(F32)
    vec = whole[:, : 6 * CW].reshape(S, 6, CW).transpose(1, 0, 2).reshape(6, D)
    gb1 = vec[0:2]
    gb2 = vec[2:4]
    vb = vec[4:6]
    bqkv = whole[:, 6 * CW :].reshape(3, S, CW)
    bqkv = lax.dynamic_index_in_dim(bqkv, me, 1, keepdims=False).reshape(1, 3 * CW)
    bup = up_bias.astype(F32).reshape(1, FL)

    w_up = my_columns(up_weight, me, S, R, 1)
    w_qkv = my_columns(qkv_weight, me, S, R, 3)

    X = [[jnp.concatenate([prompt_in[m, 0], cont_in[m, 0].reshape(CR, D)], axis=0)] for m in range(MB)]
    DY = [[jnp.concatenate([prompt_cot[m, 0], cont_cot[m, 0].reshape(CR, D)], axis=0)] for m in range(MB)]
    for m in range(MB):
        for j in range(1, S):
            X[m].append(shifted(X[m][0], S, S - j))
            DY[m].append(shifted(DY[m][0], S, S - j))

    tabs = rotary_tables(PD * S, CR * S, CL)
    ff = [[None] * S for _ in range(MB)]
    for m in range(MB):
        ff[m][0] = mlp_rows(X[m][0], DY[m][0], w_up, bup, down_weight, gb2)
    y_own, g_own, rest = [], [], []
    y_got, g_got = [], []
    for m in range(MB):
        for j in range(1, S):
            ff[m][j] = mlp_rows(X[m][j], DY[m][j], w_up, bup, down_weight, gb2)
        ys, gs, more = attn_group(
            S, PD, CL, me_arr, X[m], DY[m], [f[3] for f in ff[m]], [f[4] for f in ff[m]], w_qkv, bqkv, out_weight, gb1, tabs
        )
        rest.append(more)
        y_got.append([ys[0]] + [shifted(ys[j], S, j) for j in range(1, S)])
        g_got.append([gs[0]] + [shifted(gs[j], S, j) for j in range(1, S)])

    every = [ff[m][j] for m in range(MB) for j in range(S)]
    dys = [DY[m][j] for m in range(MB) for j in range(S)]
    d_down = tn_sum([f[0] for f in every], dys, 256)
    d_up = tn_sum([f[2] for f in every], [f[1] for f in every], 256)
    d_qkv = tn_sum([r[2] for r in rest], [r[0] for r in rest], 256)
    d_out = tn_sum([r[1] for r in rest], [r[3] for r in rest], 256)

    g_down = reduce_rows(d_down)
    g_up = reduce_columns(d_up, me, S, 1)
    g_out = reduce_rows(d_out)
    g_qkv = reduce_columns(d_qkv, me, S, 3)

    ln1 = sum(r[4] for r in rest).reshape(2 * D)
    ln2 = sum(f[5] for f in every).reshape(2 * D)
    db_out = sum(jnp.sum(DY[m][0].astype(F32), axis=0) for m in range(MB))
    mine = (jnp.arange(S) == me).astype(F32)
    db_qkv = (sum(r[5] for r in rest)[:, None, :] * mine[None, :, None]).reshape(3 * D)
    db_up = (sum(f[6] for f in every) * mine[:, None]).reshape(S * FL)
    tot = lax.psum(jnp.concatenate([ln1, ln2, db_out, db_qkv, db_up]), ("rep", "shard"))
    own = lambda a, n: lax.dynamic_slice_in_dim(tot, a + me * n, n, 0)
    v_ln1g, v_ln1b, v_ln2g, v_ln2b, v_out = [own(k * D, CW) for k in range(5)]
    v_qkv = own(5 * D, 3 * CW)
    v_up = own(8 * D, FL)

    prior = None
    for m in range(MB):
        prior = final_rows(m, MB, PD, X[m][0], DY[m][0], y_got[m], g_got[m], vb, prior)
    po, co, pg, cg = prior
    return (
        po.reshape(MB, 1, PD, D),
        co.reshape(MB, 1, CD, CL, D),
        pg.reshape(MB, 1, PD, D),
        cg.reshape(MB, 1, CD, CL, D),
        v_ln1g,
        v_ln1b,
        v_ln2g,
        v_ln2b,
        g_qkv,
        v_qkv,
        g_out,
        v_out,
        g_up,
        v_up,
        g_down,
        v_out,
    )


def solution(mesh):
    tokens = (
        P(None, "rep", "shard", None),
        P(None, "rep", "shard", None, None),
        P(None, "rep", "shard", None),
        P(None, "rep", "shard", None, None),
    )
    vec = P("shard")
    mat = P("shard", None)
    params = (vec, vec, vec, vec, mat, vec, mat, vec, mat, vec, mat, vec)
    return jax.shard_map(
        per_device, mesh=mesh, in_specs=tokens + params, out_specs=tokens + params, check_vma=False
    )
```

time: 1220 us -> 850 us (0.70)
  matrix products: 484 us -> 0 us
  Pallas kernels: 0 us -> 302 us
  other arithmetic: 188 us -> 39.7 us
  local copies, waits for them, and re-layouts: 93.6 us -> 50.6 us
  waiting for transfers between devices: 318 us -> 280 us
  blocking collectives: 107 us -> 142 us
  starting transfers between devices: 0.69 us -> 17.3 us
    dot_general x36 -> x0, matrix products: 484 us -> none  [the longest x8 79.5 us: inner_rows(): lax.dot_general(left_mat, right_mat, (((0,), (0,)), ((), ())), preferred_...]
    pallas_call x0 -> x12, Pallas kernels: none -> 302 us  [the longest x2 150 us: attn_group(): pl.pallas_call(functools.partial(attn_kernel, S, PD, CL, QB, HG, adding),...]
    psum x1 -> x0, waiting for transfers between devices: 141 us -> none  [per_device(): lax.psum(owned[4].astype(jnp.bfloat16), 'rep').astype(jnp.float32)]
    reduce_scatter x8 -> x4, waiting for transfers between devices: 104 us -> 220 us  [the longest x2 146 us: reduce_columns(): lax.psum_scatter(grad.reshape(S, rows // S, cols), 'rep', scatter_dimensi...]
    convert_element_type x29 -> x6, other arithmetic: 100 us -> 21.6 us  [the longest x2 12.1 us: reduce_columns(): return lax.all_gather(whole, 'rep', axis=0, tiled=True).astype(F32)]
    psum x1, blocking collectives: 64.4 us -> 142 us  [per_device(): lax.psum(jnp.concatenate([ln1, ln2, db_out, db_qkv, db_up]), ('rep', 'sha...]
    reduce_sum x9 -> x1, other arithmetic: 60.2 us -> 0.43 us  [per_device(): db_out = sum((jnp.sum(DY[m][0].astype(F32), axis=0) for m in range(MB)))]
    slice x26 -> x2, local copies, waits for them, and re-layouts: 57.4 us -> 0.61 us  [the longest x1 0.6 us: per_device(): vb = vec[4:6]]
  transfers between devices with their start and end apart: 17 -> 23, of which waited for: 5 -> 12; matrix products, arithmetic and copies ran while one was open for 61% -> 9% of each run, Pallas kernels for 0% -> 15%
where the time goes in v1:
time: 850 us; the launch traced here: 846 us
  Pallas kernels  302 us (36%)
  waiting for transfers between devices  280 us (33%)
  blocking collectives  142 us (17%)
  local copies, waits for them, and re-layouts  50.6 us (6%)
  other arithmetic  39.7 us (5%)
  starting transfers between devices  17.3 us (2%)
  between operations  15.2 us (2%)
    pallas_call x2, Pallas kernels, attn_group(): pl.pallas_call(functools.partial(attn_kernel, S, PD, CL, QB, HG, adding),...  150 us
    reduce_scatter x2, waiting for transfers between devices, reduce_columns(): lax.psum_scatter(grad.reshape(S, rows // S, cols), 'rep', scatter_dimensi...  146 us
    psum x1, blocking collectives, per_device(): lax.psum(jnp.concatenate([ln1, ln2, db_out, db_qkv, db_up]), ('rep', 'sha...  142 us
    pallas_call x4, Pallas kernels, mlp_rows(): pl.pallas_call(functools.partial(mlp_kernel, rows_tile(rows, 640)), grid=...  80.8 us
    reduce_scatter x2, waiting for transfers between devices, reduce_rows(): part = lax.psum_scatter(grad, 'rep', scatter_dimension=0, tiled=True)  74.7 us
    pallas_call x4, Pallas kernels, tn_sum(): pl.pallas_call(functools.partial(tn_kernel, n, wide), grid=(da // block,)...  58.7 us
    all_gather x2, waiting for transfers between devices, my_columns(): others = lax.all_gather(jnp.stack(got, axis=0), 'rep', axis=1, tiled=True)  27.2 us
    ppermute x13, waiting for transfers between devices, shifted(): return lax.ppermute(value, 'shard', [(i, (i + j) % S) for i in range(S)])  26.2 us
  transfers between devices with their start and end apart: 23, of which 12 were waited for; matrix products, arithmetic and copies ran while one was open for 9% of the time, Pallas kernels for 15%

profile of v1, /device:TPU:0, one launch (start us, length us, event | category | flops | bytes accessed | tf_op | source)
XLA Modules:
  0.0 845.7 jit_solution(15831468683467502485)
XLA Ops:
  7.2 3.2 copy.69
  12.1 3.0 collective-permute-start.4
  15.1 9.1 %collective-permute-done.4 = bf16[32,1536]{0,1:T(8,128)(2,1)S(1)} collective-permute-done((bf16[32,1536]{0,1:T(8,128)(2,1)S(1)}, bf16[32,1536]{0,1:T(8,128)(2,1)S(1)}, u32[]{:S(2)}, u32[]{:S(2)}) %collective-permute-start.4) | collective-permute-done | bytes 98336 | tf_op jit(solution)/shard_map/ppermute | solution.py:460
  34.2 1.7 collective-permute-start.3
  35.9 6.4 copy.66
  44.3 1.7 slice_bitcast_fusion.1
  46.1 3.0 collective-permute-done.2
  51.8 1.7 collective-permute-start.7
  55.9 1.7 collective-permute-start.8
  57.7 1.5 constant_dynamic-slice_fusion.8
  60.4 3.9 copy.67
  66.3 2.6 copy.71
  68.9 4.7 fusion.5
  73.6 2.6 copy.72
  76.2 2.6 copy.73
  78.7 3.8 pad_maximum_fusion.1.refs_8_.refs_9_.refs_10_
  82.5 26.8 %all-gather.17.cloned.1.call-done = bf16[512,2048]{1,0:T(8,128)(2,1)} async-done(((bf16[32,2048]{1,0:T(8,128)(2,1)}), bf16[512,2048]{1,0:T(8,128)(2,1)}) %all-gather.17.cloned.1.call-update) | async-done | bytes 2097168 | tf_op jit(solution)/shard_map/all_gather | solution.py:491
  109.3 3.1 fusion.3
  112.3 2.6 pad_maximum_fusion.wu_ref
  114.9 20.1 %shard_map.309 = (bf16[640,2048]{1,0:T(8,128)(2,1)}, bf16[640,2048]{1,0:T(8,128)(2,1)}, bf16[640,1024]{1,0:T(8,128)(2,1)}, bf16[640,1024]{1,0:T(8,128)(2,1)}, bf...) custom-call(bf16[640,1024]{1,0:T(8,128)(2,1)} %pad_maximum_fusion.4.x_ref.refs_0_, ...), custom_call_target="tpu_custom_call" | custom-call | flops 10737418240 | bytes 20185088 | tf_op jit(solution)/shard_map/pallas_call | solution.py:102
  135.1 20.1 %shard_map.306 = (bf16[640,2048]{1,0:T(8,128)(2,1)}, bf16[640,2048]{1,0:T(8,128)(2,1)}, bf16[640,1024]{1,0:T(8,128)(2,1)}, bf16[640,1024]{1,0:T(8,128)(2,1)}, bf...) custom-call(bf16[640,1024]{1,0:T(8,128)(2,1)} %copy-done, bf16[640,1024]{1,0:T(8,128)(2,1)} %copy-done.2, ...), custom_call_target="tpu_custom_call" | custom-call | flops 10737418240 | bytes 20185088 | tf_op jit(solution)/shard_map/pallas_call | solution.py:102
  155.2 7.7 collective-permute-done.8.dy_ref.refs_3_.refs_5_
  162.9 20.6 %shard_map.310 = (bf16[640,2048]{1,0:T(8,128)(2,1)}, bf16[640,2048]{1,0:T(8,128)(2,1)}, bf16[640,1024]{1,0:T(8,128)(2,1)}, bf16[640,1024]{1,0:T(8,128)(2,1)}, bf...) custom-call(bf16[640,1024]{1,0:T(8,128)(2,1)} %collective-permute-done.7.x_ref.refs_1_, ...), custom_call_target="tpu_custom_call" | custom-call | flops 10737418240 | bytes 20185088 | tf_op jit(solution)/shard_map/pallas_call | solution.py:102
  183.5 20.0 %shard_map.307 = (bf16[640,2048]{1,0:T(8,128)(2,1)}, bf16[640,2048]{1,0:T(8,128)(2,1)}, bf16[640,1024]{1,0:T(8,128)(2,1)}, bf16[640,1024]{1,0:T(8,128)(2,1)}, bf...) custom-call(bf16[640,1024]{1,0:T(8,128)(2,1)} %collective-permute-done.x_ref.refs_1_, ...), custom_call_target="tpu_custom_call" | custom-call | flops 10737418240 | bytes 20185088 | tf_op jit(solution)/shard_map/pallas_call | solution.py:102
  203.5 66.7 %shard_map.308 = (bf16[640,1024]{1,0:T(8,128)(2,1)}, bf16[640,1024]{1,0:T(8,128)(2,1)}, bf16[640,1024]{1,0:T(8,128)(2,1)}, bf16[640,1024]{1,0:T(8,128)(2,1)}, bf...) custom-call(s32[1]{0:T(128)} %bitcast.4.me_ref, ...), custom_call_target="tpu_custom_call" | custom-call | flops 51002736640 | bytes 33030144 | tf_op jit(solution)/shard_map/pallas_call | solution.py:339
  270.2 83.3 %shard_map.311 = (bf16[640,1024]{1,0:T(8,128)(2,1)}, bf16[640,1024]{1,0:T(8,128)(2,1)}, bf16[640,1024]{1,0:T(8,128)(2,1)}, bf16[640,1024]{1,0:T(8,128)(2,1)}, bf...) custom-call(s32[1]{0:T(128)} %bitcast.4.me_ref, ...), custom_call_target="tpu_custom_call" | custom-call | flops 51002736640 | bytes 33030144 | tf_op jit(solution)/shard_map/pallas_call | solution.py:339
  353.5 6.9 shard_map.315
  360.5 13.6 %shard_map.314 = bf16[1024,1536]{1,0:T(8,128)(2,1)} custom-call(bf16[1280,1024]{1,0:T(8,128)(2,1)} %get-tuple-element.108.refs_0_, bf16[1280,1024]{1,0:T(8,128)(2,1)} %get-tuple-element.109.refs_1_, bf16[3,1280,512]{2,1,0:T(8,128)(2,1)} %get-tuple-element.110.refs_2_, bf16[3,1280,512]{2,1,0:T(8,128)(2,1)} %get-tuple-element.111.refs_3_), custom_call_target="tpu_custom_call" | custom-call | flops 8053063680 | bytes 16252928 | tf_op jit(solution)/shard_map/pallas_call | solution.py:394
  374.1 18.7 %shard_map.317 = bf16[2048,1024]{1,0:T(8,128)(2,1)} custom-call(bf16[640,2048]{1,0:T(8,128)(2,1)} %get-tuple-element.124.refs_0_, bf16[640,2048]{1,0:T(8,128)(2,1)} %get-tuple-element.125.refs_1_, bf16[640,2048]{1,0:T(8,128)(2,1)} %get-tuple-element.126.refs_2_, bf16[640,2048]{1,0:T(8,128)(2,1)} %get-tuple-element.127.refs_3_, ...), custom_call_target="tpu_custom_call" | custom-call | flops 10737418240 | bytes 19922944 | tf_op jit(solution)/shard_map/pallas_call | solution.py:394
  392.9 19.5 %shard_map.316 = bf16[1024,2048]{1,0:T(8,128)(2,1)} custom-call(bf16[640,1024]{1,0:T(8,128)(2,1)} %get-tuple-element.116.refs_0_, bf16[640,1024]{1,0:T(8,128)(2,1)} %get-tuple-element.117.refs_1_, bf16[640,1024]{1,0:T(8,128)(2,1)} %get-tuple-element.118.refs_2_, bf16[640,1024]{1,0:T(8,128)(2,1)} %get-tuple-element.119.refs_3_, ...), custom_call_target="tpu_custom_call" | custom-call | flops 10737418240 | bytes 19922944 | tf_op jit(solution)/shard_map/pallas_call | solution.py:394
  412.5 5.7 reduce-scatter.7.cloned.1.call-done
  418.2 69.8 %reduce-scatter.5.cloned.1.call-done = bf16[2,32,1536]{2,1,0:T(8,128)(2,1)} async-done(((bf16[2,512,1536]{2,1,0:T(8,128)(2,1)}), bf16[2,32,1536]{2,1,0:T(8,128)(2,1)}) %reduce-scatter.5.cloned.1.call-update) | async-done | bytes 196624 | tf_op jit(solution)/shard_map/reduce_scatter | solution.py:502
  489.0 1.5 collective-permute-start.11
  490.7 3.0 collective-permute-done.11
  495.2 69.0 %reduce-scatter.11.cloned.1.call-done = bf16[128,1024]{1,0:T(8,128)(2,1)} async-done(((bf16[2048,1024]{1,0:T(8,128)(2,1)}), bf16[128,1024]{1,0:T(8,128)(2,1)}) %reduce-scatter.11.cloned.1.call-update) | async-done | bytes 262160 | tf_op jit(solution)/shard_map/reduce_scatter | solution.py:496
  564.3 75.7 %reduce-scatter.9.cloned.1.call-done = bf16[2,32,2048]{2,1,0:T(8,128)(2,1)} async-done(((bf16[2,512,2048]{2,1,0:T(8,128)(2,1)}), bf16[2,32,2048]{2,1,0:T(8,128)(2,1)}) %reduce-scatter.9.cloned.1.call-update) | async-done | bytes 262160 | tf_op jit(solution)/shard_map/reduce_scatter | solution.py:502
  640.9 1.6 collective-permute-start.12
  642.6 3.4 collective-permute-done.12
  647.8 1.6 collective-permute-start.5
  649.9 1.6 collective-permute-start.9
  652.3 141.7 %psum.7 = f32[12288]{0:T(1024)S(1)} all-reduce(f32[12288]{0:T(1024)S(1)} %constant_dynamic-update-slice_fusion.3), channel_id=1, replica_groups=mesh['rep'=16,'shard'=2] {'rep','shard'}, use_global_device_ids=true, to_apply=%region_2.3 | all-reduce | flops 12288 | bytes 98304 | tf_op jit(solution)/shard_map/psum | solution.py:610
  798.7 7.6 shard_map.312
  806.3 4.5 shard_map.313
  810.8 2.8 convert_element_type.38
  813.7 5.4 convert_element_type.37
  819.1 6.6 convert_element_type.40
  825.7 5.8 all-gather.13.cloned.1.call-done
  831.5 6.7 convert_element_type.39
  (186 shorter events, 33.6 us)
Async XLA Ops:
  7.2 59.2 %all-gather.19.cloned.1.call-start = ((), (), s32[]{:S(2)}) async-start(), calls=%async_computation.13 | async-start | bytes 1671168 | tf_op jit(solution)/shard_map/all_gather | solution.py:491
  10.4 14.6 %copy-start.36 = (bf16[512]{0:T(512)(128)(2,1)S(1)}, bf16[512]{0:T(512)(128)(2,1)}, u32[]{:S(2)}) copy-start(bf16[512]{0:T(512)(128)(2,1)} %param.23) | copy-start | bytes 3076
  10.5 16.1 %copy-start.37 = (bf16[512]{0:T(512)(128)(2,1)S(1)}, bf16[512]{0:T(512)(128)(2,1)}, u32[]{:S(2)}) copy-start(bf16[512]{0:T(512)(128)(2,1)} %param.24) | copy-start | bytes 3076
  10.5 17.5 %copy-start.38 = (bf16[512]{0:T(512)(128)(2,1)S(1)}, bf16[512]{0:T(512)(128)(2,1)}, u32[]{:S(2)}) copy-start(bf16[512]{0:T(512)(128)(2,1)} %param.25) | copy-start | bytes 3076
  10.5 18.9 %copy-start.39 = (bf16[512]{0:T(512)(128)(2,1)S(1)}, bf16[512]{0:T(512)(128)(2,1)}, u32[]{:S(2)}) copy-start(bf16[512]{0:T(512)(128)(2,1)} %param.26) | copy-start | bytes 3076
  10.5 20.3 %copy-start.40 = (bf16[512]{0:T(512)(128)(2,1)S(1)}, bf16[512]{0:T(512)(128)(2,1)}, u32[]{:S(2)}) copy-start(bf16[512]{0:T(512)(128)(2,1)} %param.30) | copy-start | bytes 3076
  10.5 21.7 %copy-start.41 = (bf16[512]{0:T(512)(128)(2,1)S(1)}, bf16[512]{0:T(512)(128)(2,1)}, u32[]{:S(2)}) copy-start(bf16[512]{0:T(512)(128)(2,1)} %param.34) | copy-start | bytes 3076
  10.5 23.1 %copy-start.35 = (bf16[1536]{0:T(1024)(128)(2,1)S(1)}, bf16[1536]{0:T(1024)(128)(2,1)}, u32[]{:S(2)}) copy-start(bf16[1536]{0:T(1024)(128)(2,1)} %param.28) | copy-start | bytes 9220
  12.1 12.1 %collective-permute-start.4 = (bf16[32,1536]{0,1:T(8,128)(2,1)S(1)}, bf16[32,1536]{0,1:T(8,128)(2,1)S(1)}, u32[]{:S(2)}, u32[]{:S(2)}) collective-permute-start(bf16[32,1536]{0,1:T(8,128)(2,1)S(1)} %constant_dynamic-slice_fusion.4), channel_id=1, source_target_pairs={{0,1},{1,0},{2,3},{3,2},{4,5},{5,4},{6,7},{7,6},{8,9},{9,8},{10,11... | collective-permute-start | bytes 294920 | tf_op jit(solution)/shard_map/ppermute | solution.py:460
  25.0 84.3 %all-gather.17.cloned.1.call-start = ((), (), s32[]{:S(2)}) async-start(), calls=%async_computation.12 | async-start | bytes 2228224 | tf_op jit(solution)/shard_map/all_gather | solution.py:491
  34.2 30.2 %collective-permute-start.3 = (bf16[4608]{0:T(1024)(128)(2,1)}, bf16[4608]{0:T(1024)(128)(2,1)S(1)}, u32[]{:S(2)}, u32[]{:S(2)}) collective-permute-start(bf16[4608]{0:T(1024)(128)(2,1)} %constant_dynamic-update-slice_fusion.2), channel_id=1, source_target_pairs={{0,1},{1,0},{2,3},{3,2},{4,5},{5,4},{6,7},{7,6},{8,9},{9,8},{10,11... | collective-permute-start | bytes 27656 | tf_op jit(solution)/shard_map/ppermute | solution.py:460
  44.0 6.1 copy-start.18
  44.0 5.0 collective-permute-start.2
  49.7 368.4 %reduce-scatter.7.cloned.1.call-start = ((), (), s32[]{:S(2)}) async-start(), calls=%async_computation.6 | async-start | bytes 1114112 | tf_op jit(solution)/shard_map/reduce_scatter | solution.py:496
  50.2 133.3 %collective-permute-start = (bf16[640,1024]{1,0:T(8,128)(2,1)S(1)}, bf16[640,1024]{1,0:T(8,128)(2,1)}, u32[]{:S(2)}, u32[]{:S(2)}) collective-permute-start(bf16[640,1024]{1,0:T(8,128)(2,1)S(1)} %pad_maximum_fusion.2.x_ref.refs_0_), channel_id=1, source_target_pairs={{0,1},{1,0},{2,3},{3,2},{4,5},{5,4},{6,7},{7,6},{8,9},{9,8},{10,11... | collective-permute-start | bytes 3932168 | tf_op jit(solution)/shard_map/ppermute | solution.py:460
  51.8 103.4 %collective-permute-start.7 = (bf16[640,1024]{1,0:T(8,128)(2,1)}, bf16[640,1024]{1,0:T(8,128)(2,1)}, u32[]{:S(2)}, u32[]{:S(2)}) collective-permute-start(bf16[640,1024]{1,0:T(8,128)(2,1)} %pad_maximum_fusion.4.x_ref.refs_0_), channel_id=1, source_target_pairs={{0,1},{1,0},{2,3},{3,2},{4,5},{5,4},{6,7},{7,6},{8,9},{9,8},{10,11... | collective-permute-start | bytes 3932168 | tf_op jit(solution)/shard_map/ppermute | solution.py:460
  54.4 129.1 %collective-permute-start.1 = (bf16[640,1024]{1,0:T(8,128)(2,1)S(1)}, bf16[640,1024]{1,0:T(8,128)(2,1)}, u32[]{:S(2)}, u32[]{:S(2)}) collective-permute-start(bf16[640,1024]{1,0:T(8,128)(2,1)S(1)} %pad_maximum_fusion.3.dy_ref.refs_2_.refs_1_.refs_6_), channel_id=1, source_target_pairs={{0,1},{1,0},{2,3},{3,2},{4,5},{5,4},{6,7},{7,6},{8,9},{9,8},{10,11... | collective-permute-start | bytes 3932168 | tf_op jit(solution)/shard_map/ppermute | solution.py:460
  55.9 107.0 %collective-permute-start.8 = (bf16[640,1024]{1,0:T(8,128)(2,1)}, bf16[640,1024]{1,0:T(8,128)(2,1)}, u32[]{:S(2)}, u32[]{:S(2)}) collective-permute-start(bf16[640,1024]{1,0:T(8,128)(2,1)} %pad_maximum_fusion.5.dy_ref.refs_2_.refs_1_.refs_4_), channel_id=1, source_target_pairs={{0,1},{1,0},{2,3},{3,2},{4,5},{5,4},{6,7},{7,6},{8,9},{9,8},{10,11... | collective-permute-start | bytes 3932168 | tf_op jit(solution)/shard_map/ppermute | solution.py:460
  360.4 127.7 %reduce-scatter.5.cloned.1.call-start = ((), (), s32[]{:S(2)}) async-start(), calls=%async_computation.4 | async-start | bytes 3342336 | tf_op jit(solution)/shard_map/reduce_scatter | solution.py:502
  374.1 190.1 %reduce-scatter.11.cloned.1.call-start = ((), (), s32[]{:S(2)}) async-start(), calls=%async_computation.10 | async-start | bytes 4456448 | tf_op jit(solution)/shard_map/reduce_scatter | solution.py:496
  392.9 247.1 %reduce-scatter.9.cloned.1.call-start = ((), (), s32[]{:S(2)}) async-start(), calls=%async_computation.8 | async-start | bytes 4456448 | tf_op jit(solution)/shard_map/reduce_scatter | solution.py:502
  412.4 398.4 %all-gather.11.cloned.1.call-start = ((), (), s32[]{:S(2)}) async-start(), calls=%async_computation.7 | async-start | bytes 1114112 | tf_op jit(solution)/shard_map/all_gather | solution.py:497
  418.2 395.5 %all-gather.9.cloned.1.call-start = ((), (), s32[]{:S(2)}) async-start(), calls=%async_computation.5 | async-start | bytes 3342336 | tf_op jit(solution)/shard_map/all_gather | solution.py:508
  489.0 4.7 collective-permute-start.11
  494.0 153.3 %copy-start.10 = (bf16[512,1024]{1,0:T(8,128)(2,1)S(1)}, bf16[512,1024]{1,0:T(8,128)(2,1)}, u32[]{:S(2)}) copy-start(bf16[512,1024]{1,0:T(8,128)(2,1)} %copy-done.9) | copy-start | bytes 3145732
  494.0 153.3 %copy-start.12 = (bf16[512,1024]{1,0:T(8,128)(2,1)S(1)}, bf16[512,1024]{1,0:T(8,128)(2,1)}, u32[]{:S(2)}) copy-start(bf16[512,1024]{1,0:T(8,128)(2,1)} %copy-done.11) | copy-start | bytes 3145732
  494.0 153.3 %copy-start.14 = (bf16[128,1024]{1,0:T(8,128)(2,1)S(1)}, bf16[128,1024]{1,0:T(8,128)(2,1)}, u32[]{:S(2)}) copy-start(bf16[128,1024]{1,0:T(8,128)(2,1)} %copy-done.13) | copy-start | bytes 786436
  494.1 153.3 %copy-start.16 = (bf16[128,1024]{1,0:T(8,128)(2,1)S(1)}, bf16[128,1024]{1,0:T(8,128)(2,1)}, u32[]{:S(2)}) copy-start(bf16[128,1024]{1,0:T(8,128)(2,1)} %copy-done.15) | copy-start | bytes 786436
  495.1 324.0 %all-gather.15.cloned.1.call-start = ((), (), s32[]{:S(2)}) async-start(), calls=%async_computation.11 | async-start | bytes 4456448 | tf_op jit(solution)/shard_map/all_gather | solution.py:497
  564.2 267.3 %all-gather.13.cloned.1.call-start = ((), (), s32[]{:S(2)}) async-start(), calls=%async_computation.9 | async-start | bytes 4456448 | tf_op jit(solution)/shard_map/all_gather | solution.py:508
  640.9 5.0 collective-permute-start.12
  646.2 5.8 copy-start.23
  646.2 5.8 copy-start.25
  646.2 5.8 copy-start.27
  646.2 5.8 copy-start.28
  646.2 6.0 copy-start.21
  646.2 6.0 copy-start.22
  646.2 6.0 copy-start.24
  646.2 6.0 copy-start.26
  647.8 158.5 %collective-permute-start.5 = (bf16[640,1024]{1,0:T(8,128)(2,1)}, bf16[640,1024]{1,0:T(8,128)(2,1)S(1)}, u32[]{:S(2)}, u32[]{:S(2)}) collective-permute-start(bf16[640,1024]{1,0:T(8,128)(2,1)} %get-tuple-element.77), channel_id=1, source_target_pairs={{0,1},{1,0},{2,3},{3,2},{4,5},{5,4},{6,7},{7,6},{8,9},{9,8},{10,11... | collective-permute-start | bytes 3932168 | tf_op jit(solution)/shard_map/ppermute | solution.py:460
  649.5 156.8 %collective-permute-start.6 = (bf16[640,1024]{1,0:T(8,128)(2,1)}, bf16[640,1024]{1,0:T(8,128)(2,1)S(1)}, u32[]{:S(2)}, u32[]{:S(2)}) collective-permute-start(bf16[640,1024]{1,0:T(8,128)(2,1)} %get-tuple-element.79), channel_id=1, source_target_pairs={{0,1},{1,0},{2,3},{3,2},{4,5},{5,4},{6,7},{7,6},{8,9},{9,8},{10,11... | collective-permute-start | bytes 3932168 | tf_op jit(solution)/shard_map/ppermute | solution.py:460
  649.9 146.1 %collective-permute-start.9 = (bf16[640,1024]{1,0:T(8,128)(2,1)}, bf16[640,1024]{1,0:T(8,128)(2,1)}, u32[]{:S(2)}, u32[]{:S(2)}) collective-permute-start(bf16[640,1024]{1,0:T(8,128)(2,1)} %get-tuple-element.85), channel_id=1, source_target_pairs={{0,1},{1,0},{2,3},{3,2},{4,5},{5,4},{6,7},{7,6},{8,9},{9,8},{10,11... | collective-permute-start | bytes 3932168 | tf_op jit(solution)/shard_map/ppermute | solution.py:460
  651.5 144.5 %collective-permute-start.10 = (bf16[640,1024]{1,0:T(8,128)(2,1)}, bf16[640,1024]{1,0:T(8,128)(2,1)}, u32[]{:S(2)}, u32[]{:S(2)}) collective-permute-start(bf16[640,1024]{1,0:T(8,128)(2,1)} %get-tuple-element.87), channel_id=1, source_target_pairs={{0,1},{1,0},{2,3},{3,2},{4,5},{5,4},{6,7},{7,6},{8,9},{9,8},{10,11... | collective-permute-start | bytes 3932168 | tf_op jit(solution)/shard_map/ppermute | solution.py:460
  796.0 42.2 %copy-start.33 = (f32[512]{0:T(512)}, f32[512]{0:T(512)S(1)}, u32[]{:S(2)}) copy-start(f32[512]{0:T(512)S(1)} %get-tuple-element.259) | copy-start | bytes 6148
  798.6 7.6 copy-start.1
  798.6 7.7 copy-start.3
  798.6 7.7 copy-start.4
  798.6 7.7 copy-start.5
  (17 other events, 55.1 us)
Sparse Core Ops, SparseCore 0:
  25.1 41.1 all-gather.18
  69.1 40.1 all-gather.16
  360.5 57.5 reduce-scatter.6
  422.8 65.1 reduce-scatter.4
  492.8 71.3 reduce-scatter.10
  568.5 71.4 reduce-scatter.8
  642.3 37.0 all-gather.10
  682.5 44.0 all-gather.8
  729.0 49.9 all-gather.14
  781.8 49.6 all-gather.12

commit v2 on v1

--- a/solution.py
+++ b/solution.py
@@ -146,72 +146,98 @@
 def attn_kernel(S, PD, CL, QB, HG, adding, me_ref, *refs):
     it = iter(refs)
     take = lambda n: [next(it) for _ in range(n)]
-    xs = take(S)
-    dys = take(S)
-    yps = take(S * adding)
-    g2s = take(S * adding)
+    stacked = S > 2
+    per = 1 if stacked else S
+    xs = take(per)
+    dys = take(per)
+    yps = take(per * adding)
+    g2s = take(per * adding)
     wq, wk, wv = take(3)
     bq, bk, bv = take(3)
     wo, gb = take(2)
     cr, s1r, s2r = take(3)
-    ys = take(S)
-    gs = take(S)
-    dl, ctx, h1, dyc, ln, db = take(6)
+    ys = take(per)
+    gs = take(per)
+    dl, ctx, h1, ln, db = take(5)
     yacc, dacc, q_s, k_s, v_s, dc_s, kT, vT, dk_s, dv_s = take(10)
     g = pl.program_id(0)
     last = pl.num_programs(0) - 1
     me = me_ref[0]
-    N, _ = xs[0].shape
+    N = xs[0].shape[-2]
     T = N * S
     PR = PD * S
     CR = N - PD
     W = HG * HD
 
-    def each_slot(fn):
-        for s in range(S):
+    def every_slot(fn):
+        if stacked:
+
+            @pl.loop(0, S)
+            def _(j):
+                fn(j, lambda refs: refs[0].at[j])
+
+        else:
             for j in range(S):
-
-                @pl.when(lax.rem(me + j, S) == s)
-                def _():
-                    fn(s, j)
-
-    def spans(s):
-        return ((0, PD, s * PD), (PD, CR, PR + s * CR))
+                fn(j, lambda refs: refs[j])
+
+    def slot_rows(start, n):
+        if start < PR:
+            s, off = start // PD, start % PD
+        else:
+            s, off = (start - PR) // CR, PD + (start - PR) % CR
+        return pl.ds(pl.multiple_of(lax.rem(s - me + S, S) * N + off, 128), n)
+
+    def pieces(start, n):
+        step = min(n, PD if start < PR else CR)
+        return [(i, step) for i in range(0, n, step)]
 
     @pl.when(g == 0)
     def _():
-        def load(s, j):
-            for a, n, c in spans(s):
-                xh, _ = normed(xs[j][a : a + n, :])
-                h1[c : c + n, :] = (xh * gb[0:1, :] + gb[1:2, :]).astype(BF)
-                dyc[c : c + n, :] = dys[j][a : a + n, :]
-
-        each_slot(load)
-
-    RT = T // 2
-
-    def proj(i, _):
-        r = tile(i, RT)
+        def load(j, of):
+            x = of(xs)
+
+            @pl.loop(0, N // 128)
+            def _(i):
+                xh, _ = normed(x[tile(i, 128), :])
+                h1[pl.ds(pl.multiple_of(j * N + i * 128, 128), 128), :] = (xh * gb[0:1, :] + gb[1:2, :]).astype(BF)
+
+        every_slot(load)
+
+    def rot(y, r, scale):
         c = cr[r, :]
         s1 = s1r[r, :]
         s2 = s2r[r, :]
-
-        def rot(y, scale):
-            out = []
-            for p in range(W // 128):
-                z = y[:, p * 128 : (p + 1) * 128]
-                z = (z * c + roll8(z, True) * s1 + roll8(z, False) * s2).astype(BF)
-                out.append(z * jnp.asarray(scale, BF))
-            return jnp.concatenate(out, axis=1) if len(out) > 1 else out[0]
-
-        hh = h1[r, :]
-        q_s[r, :] = rot(dnn(hh, wq[...]) + bq[...], HD**-0.5)
-        k_s[r, :] = rot(dnn(hh, wk[...]) + bk[...], 1.0)
-        v_s[r, :] = (dnn(hh, wv[...]) + bv[...]).astype(BF)
-        dc_s[r, :] = dnt(dyc[r, :], wo[...]).astype(BF)
-        return 0
-
-    lax.fori_loop(0, 2, proj, 0)
+        out = []
+        for p in range(W // 128):
+            z = y[:, p * 128 : (p + 1) * 128]
+            z = (z * c + roll8(z, True) * s1 + roll8(z, False) * s2).astype(BF)
+            out.append(z * jnp.asarray(scale, BF) if scale != 1.0 else z)
+        return jnp.concatenate(out, axis=1) if len(out) > 1 else out[0]
+
+    def proj(j, of):
+        s = lax.rem(me + j, S)
+        rp = pl.ds(pl.multiple_of(s * PD, 128), PD)
+        rc = pl.ds(pl.multiple_of(PR + s * CR, 128), CR)
+        hh = h1[pl.ds(pl.multiple_of(j * N, 128), N), :]
+        y = dnn(hh, wq[...]) + bq[...]
+        q_s[rp, :] = rot(y[:PD], rp, HD**-0.5)
+        q_s[rc, :] = rot(y[PD:], rc, HD**-0.5)
+        y = dnn(hh, wk[...]) + bk[...]
+        k_s[rp, :] = rot(y[:PD], rp, 1.0)
+        k_s[rc, :] = rot(y[PD:], rc, 1.0)
+        y = (dnn(hh, wv[...]) + bv[...]).astype(BF)
+        v_s[rp, :] = y[:PD]
+        v_s[rc, :] = y[PD:]
+        y = dnt(of(dys)[...], wo[...]).astype(BF)
+        dc_s[rp, :] = y[:PD]
+        dc_s[rc, :] = y[PD:]
+        if adding:
+            nb = of(yps).shape[0]
+            r = pl.ds(pl.multiple_of(g * nb, 16), nb)
+            of(ys)[r, :] = of(yps)[...]
+            of(gs)[r, :] = of(g2s)[...]
+
+    every_slot(proj)
     lane = lax.broadcasted_iota(jnp.int32, (1, 128), 1)
     row_i = lax.broadcasted_iota(jnp.int32, (QB, QB), 0)
     col_i = lax.broadcasted_iota(jnp.int32, (QB, QB), 1)
@@ -230,28 +256,36 @@
         vT[...] = v_s[:, lanes].T
         dk_s[...] = jnp.zeros_like(dk_s)
         dv_s[...] = jnp.zeros_like(dv_s)
-        for q0, parts in blocks:
-            rq = pl.ds(q0, QB)
-            qb = q_s[rq, lanes]
-            dcb = dc_s[rq, lanes]
-            P_, DS, qh, dch, cT, dqT = [], [], [], [], [], []
+        def begin(q0, parts):
+            qb = q_s[pl.ds(q0, QB), lanes]
+            dcb = dc_s[pl.ds(q0, QB), lanes]
+            out = []
             for h in range(2):
                 sel = (lane >= HD * h) & (lane < HD * h + HD)
                 qm = jnp.where(sel, qb, jnp.zeros_like(qb))
                 dm = jnp.where(sel, dcb, jnp.zeros_like(dcb))
-                qh.append(qm)
-                dch.append(dm)
                 ss = []
                 for k0, n, mask in parts:
                     s = dnt(k_s[k0 : k0 + n, lanes], qm)
-                    if mask is not None:
-                        s = jnp.where(mask, s, -1e30)
-                    ss.append(s)
+                    ss.append(s if mask is None else jnp.where(mask, s, -1e30))
+                out.append((qm, dm, ss, [dnt(v_s[k0 : k0 + n, lanes], dm) for k0, n, _ in parts]))
+            return out
+
+        ahead = begin(*blocks[0])
+        for b, (q0, parts) in enumerate(blocks):
+            now = ahead
+            if b + 1 < len(blocks):
+                ahead = begin(*blocks[b + 1])
+            rq = pl.ds(q0, QB)
+            P_, DS, cT, dqT = [], [], [], []
+            qh = [t[0] for t in now]
+            dch = [t[1] for t in now]
+            for h in range(2):
+                _, _, ss, dps = now[h]
                 m = functools.reduce(jnp.maximum, [jnp.max(s, axis=0, keepdims=True) for s in ss])
                 es = [jnp.exp(s - m) for s in ss]
                 rl = 1.0 / sum(jnp.sum(e, axis=0, keepdims=True) for e in es)
                 ps = [e * rl for e in es]
-                dps = [dnt(v_s[k0 : k0 + n, lanes], dm) for k0, n, _ in parts]
                 delta = sum(jnp.sum(a * b, axis=0, keepdims=True) for a, b in zip(ps, dps))
                 P_.append([a.astype(BF) for a in ps])
                 DS.append([(a * (b - delta)).astype(BF) for a, b in zip(ps, dps)])
@@ -263,60 +297,67 @@
             for i, (k0, n, _) in enumerate(parts):
                 dv_s[k0 : k0 + n, :] += dnn(jnp.concatenate([P_[0][i], P_[1][i]], axis=1), dc2)
                 dk_s[k0 : k0 + n, :] += dnn(jnp.concatenate([DS[0][i], DS[1][i]], axis=1), q2)
-            ctx[rq, lanes] = jnp.concatenate(cT, axis=0).T.astype(BF)
+            co = jnp.concatenate(cT, axis=0).T.astype(BF)
             z = jnp.concatenate(dqT, axis=0).T * (HD**-0.5)
-            z = z * cr[rq, :] - roll8(z, True) * s1r[rq, :] - roll8(z, False) * s2r[rq, :]
-            dl[0, rq, lanes] = z.astype(BF)
-        z = dk_s[...]
-        z = z * cr[...] - roll8(z, True) * s1r[...] - roll8(z, False) * s2r[...]
-        dl[1, :, lanes] = z.astype(BF)
-        dl[2, :, lanes] = dv_s[...].astype(BF)
+            z = (z * cr[rq, :] - roll8(z, True) * s1r[rq, :] - roll8(z, False) * s2r[rq, :]).astype(BF)
+            for o, n in pieces(q0, QB):
+                ctx[slot_rows(q0 + o, n), lanes] = co[o : o + n]
+                dl[0, slot_rows(q0 + o, n), lanes] = z[o : o + n]
+
+        @pl.loop(0, S)
+        def _(s):
+            to = lax.rem(s - me + S, S) * N
+            for src, off, n in ((s * PD, 0, PD), (PR + s * CR, PD, CR)):
+                r = pl.ds(pl.multiple_of(src, 128), n)
+                w = pl.ds(pl.multiple_of(to + off, 128), n)
+                z = dk_s[r, :]
+                z = z * cr[r, :] - roll8(z, True) * s1r[r, :] - roll8(z, False) * s2r[r, :]
+                dl[1, w, lanes] = z.astype(BF)
+                dl[2, w, lanes] = dv_s[r, :].astype(BF)
 
     for c in range(3):
         db[c : c + 1, :] = jnp.sum(dl[c].astype(F32), axis=0, keepdims=True)
 
-    def post(i, first):
-        r = tile(i, RT)
+    @pl.loop(0, S)
+    def _(j):
+        r = pl.ds(pl.multiple_of(j * N, 128), N)
         y = dnn(ctx[r, :], wo[...])
         d = dnt(dl[0, r, :], wq[...]) + dnt(dl[1, r, :], wk[...]) + dnt(dl[2, r, :], wv[...])
-        if first:
+
+        @pl.when(g == 0)
+        def _():
             yacc[r, :] = y
             dacc[r, :] = d
-        else:
+
+        @pl.when(g > 0)
+        def _():
             yacc[r, :] += y
             dacc[r, :] += d
-
-    @pl.when(g == 0)
-    def _():
-        @pl.loop(0, 2)
-        def _(i):
-            post(i, True)
-
-    @pl.when(g > 0)
-    def _():
-        @pl.loop(0, 2)
-        def _(i):
-            post(i, False)
 
     @pl.when(g == last)
     def _():
         ln[...] = jnp.zeros_like(ln)
 
-        def store(s, j):
-            for a, n, c in spans(s):
-                xh, _ = normed(xs[j][a : a + n, :])
-                d = dacc[c : c + n, :]
-                y = yacc[c : c + n, :]
+        def store(j, of):
+            x, yo, go = of(xs), of(ys), of(gs)
+
+            @pl.loop(0, N // 128)
+            def _(i):
+                r = tile(i, 128)
+                w = pl.ds(pl.multiple_of(j * N + i * 128, 128), 128)
+                xh, _ = normed(x[r, :])
+                d = dacc[w, :]
+                y = yacc[w, :]
                 gg = d * gb[0:1, :]
                 if adding:
-                    y = y + yps[j][a : a + n, :].astype(F32)
-                    gg = gg + g2s[j][a : a + n, :].astype(F32)
-                ys[j][a : a + n, :] = y.astype(BF)
-                gs[j][a : a + n, :] = gg.astype(BF)
+                    y = y + yo[r, :].astype(F32)
+                    gg = gg + go[r, :].astype(F32)
+                yo[r, :] = y.astype(BF)
+                go[r, :] = gg.astype(BF)
                 ln[0:1, :] += jnp.sum(d * xh, axis=0, keepdims=True)
                 ln[1:2, :] += jnp.sum(d, axis=0, keepdims=True)
 
-        each_slot(store)
+        every_slot(store)
 
 
 def attn_group(S, PD, CL, me, xs, dys, yps, g2s, wqkv, bqkv, wo, gb, tabs):
@@ -329,11 +370,19 @@
     G = CW // W
     full = lambda s: pl.BlockSpec(s, lambda g, m: (0,) * len(s), pipeline_mode=pl.Buffered(1))
     keep = lambda s: pl.BlockSpec(s, lambda g, m: (0,) * len(s))
-    tok = full((N, D))
+    tok, tok_out, per = full((N, D)), keep((N, D)), S
     adding = int(T * D <= 1536 * 1024)
+    others = (yps, g2s)
     if not adding:
-        others = (yps, g2s)
         yps, g2s = [], []
+    out_tok = SD((N, D), BF)
+    if S > 2:
+        xs, dys, yps, g2s = [[jnp.stack(v, axis=0)] if v else v for v in (xs, dys, yps, g2s)]
+        tok, tok_out, per = full((S, N, D)), keep((S, N, D)), 1
+        out_tok = SD((S, N, D), BF)
+        part = pl.BlockSpec((S, N // G, D), lambda g, m: (0, g, 0))
+    else:
+        part = pl.BlockSpec((N // G, D), lambda g, m: (g, 0))
     wspec = lambda c: pl.BlockSpec((D, W), lambda g, m: (0, c * G + g))
     bspec = lambda c: pl.BlockSpec((1, W), lambda g, m: (0, c * G + g))
     outs = pl.pallas_call(
@@ -341,15 +390,15 @@
         grid_spec=pltpu.PrefetchScalarGridSpec(
             num_scalar_prefetch=1,
             grid=(G,),
-            in_specs=[tok] * ((2 + 2 * adding) * S)
+            in_specs=[tok] * (2 * per)
+            + [part] * (2 * adding * per)
             + [wspec(0), wspec(1), wspec(2), bspec(0), bspec(1), bspec(2)]
             + [pl.BlockSpec((W, D), lambda g, m: (g, 0)), full((2, D))]
             + [full((T, 128))] * 3,
-            out_specs=[keep((N, D))] * (2 * S)
+            out_specs=[tok_out] * (2 * per)
             + [
                 pl.BlockSpec((3, T, W), lambda g, m: (0, 0, g)),
                 pl.BlockSpec((T, W), lambda g, m: (0, g)),
-                keep((T, D)),
                 keep((T, D)),
                 keep((2, D)),
                 pl.BlockSpec((3, W), lambda g, m: (0, g)),
@@ -359,17 +408,21 @@
             + [pltpu.VMEM((128, T), BF)] * 2
             + [pltpu.VMEM((T, 128), F32)] * 2,
         ),
-        out_shape=[SD((N, D), BF)] * (2 * S)
-        + [SD((3, T, CW), BF), SD((T, CW), BF), SD((T, D), BF), SD((T, D), BF), SD((2, D), F32), SD((3, CW), F32)],
+        out_shape=[out_tok] * (2 * per)
+        + [SD((3, T, CW), BF), SD((T, CW), BF), SD((T, D), BF), SD((2, D), F32), SD((3, CW), F32)],
         compiler_params=pltpu.CompilerParams(vmem_limit_bytes=62 * MIB),
         cost_estimate=pl.CostEstimate(
-            flops=16 * T * D * CW + 48 * T * T * CW, bytes_accessed=16 * T * D + 12 * T * CW + 8 * D * CW, transcendentals=T * T * CW // HD
+            flops=16 * T * D * CW + 40 * T * T * CW,
+            bytes_accessed=12 * T * D + 12 * T * CW + 8 * D * CW,
+            transcendentals=T * T * CW // HD,
         ),
     )(me, *xs, *dys, *yps, *g2s, wqkv, wqkv, wqkv, bqkv, bqkv, bqkv, wo, gb, *tabs)
-    ys, gs = outs[:S], outs[S : 2 * S]
+    ys, gs = outs[:per], outs[per : 2 * per]
+    if S > 2:
+        ys, gs = [[v[0][j] for j in range(S)] for v in (ys, gs)]
     if not adding:
         ys, gs = [[a + b for a, b in zip(p, q)] for p, q in zip((ys, gs), others)]
-    return ys, gs, outs[2 * S :]
+    return ys, gs, outs[2 * per :]
 
 
 def tn_kernel(n, wide, *refs):
@@ -400,6 +453,171 @@
         compiler_params=pltpu.CompilerParams(vmem_limit_bytes=60 * MIB),
         cost_estimate=pl.CostEstimate(flops=2 * n * rows * da * db, bytes_accessed=2 * (n * rows * (da + db) + da * db), transcendentals=0),
     )(*a, *b)
+
+
+def joined(refs):
+    return jnp.concatenate([r[...] for r in refs], axis=0)
+
+
+def down_kernel(n, *refs):
+    a = refs[:n]
+    b = refs[n : 2 * n]
+    o = refs[-1]
+    o[...] = dtn(joined(a), joined(b)).astype(BF).reshape(o.shape)
+
+
+def up_kernel(n, *refs):
+    a = refs[:n]
+    b = refs[n : 2 * n]
+    o = refs[-1]
+    c, rows, w = o.shape
+    k = b[0].shape[1] // w
+    t = dtn(joined(a), joined(b)).astype(BF)
+    for i in range(k):
+        o[:, i * (rows // k) : (i + 1) * (rows // k), :] = t[:, i * w : (i + 1) * w].reshape(c, rows // k, w)
+
+
+def mlp_grads(S, R, acts, dys, hs, dpres):
+    n = len(acts)
+    rows, FL = acts[0].shape
+    D = dys[0].shape[1]
+    DR = D // S
+    blk = 256
+    rd = FL // R
+    ru = DR // R
+    k = FL // D
+    per = rd + S * ru * k
+    one = pl.Buffered(1)
+    keep = lambda s: pl.BlockSpec(s, lambda i: (0,) * len(s), pipeline_mode=one)
+    cost = pl.CostEstimate(flops=2 * n * rows * D * FL, bytes_accessed=2 * (n * rows * (D + FL) + D * FL), transcendentals=0)
+    params = pltpu.CompilerParams(vmem_limit_bytes=60 * MIB)
+    g = pl.pallas_call(
+        functools.partial(down_kernel, n),
+        grid=(FL // blk,),
+        in_specs=[pl.BlockSpec((rows, blk), lambda i: (0, i))] * n + [keep((rows, D))] * n,
+        out_specs=pl.BlockSpec((blk // rd, rd, D), lambda i: (i, 0, 0)),
+        out_shape=SD((R, per, D), BF),
+        compiler_params=params,
+        cost_estimate=cost,
+    )(*acts, *dys)
+    steps = DR // blk
+    return pl.pallas_call(
+        functools.partial(up_kernel, n),
+        grid=(D // blk,),
+        in_specs=[pl.BlockSpec((rows, blk), lambda i: (0, i))] * n + [keep((rows, FL))] * n + [pl.BlockSpec(memory_space=pl.ANY)],
+        out_specs=pl.BlockSpec((blk // ru, ru * k, D), lambda i: (i % steps, rd // (ru * k) + i // steps, 0)),
+        out_shape=SD((R, per, D), BF),
+        input_output_aliases={2 * n: 0},
+        compiler_params=params,
+        cost_estimate=cost,
+    )(*hs, *dpres, g)
+
+
+def mlp_finish_kernel(S, rd, ru, g, down, up):
+    D = g.shape[2]
+    k = (g.shape[1] - rd) // (S * ru)
+    down[...] = g[0, :rd, :].astype(F32)
+    for t in range(S):
+        for i in range(k):
+            a = rd + (t * k + i) * ru
+            up[:, (t * k + i) * D : (t * k + i + 1) * D] = g[0, a : a + ru, :].astype(F32)
+
+
+def mlp_finish(S, g, FL):
+    R, per, D = g.shape
+    rd = FL // R
+    ru = D // S // R
+    return pl.pallas_call(
+        functools.partial(mlp_finish_kernel, S, rd, ru),
+        grid=(R,),
+        in_specs=[pl.BlockSpec((1, per, D), lambda c: (c, 0, 0))],
+        out_specs=[pl.BlockSpec((rd, D), lambda c: (c, 0)), pl.BlockSpec((ru, S * FL), lambda c: (c, 0))],
+        out_shape=[SD((FL, D), F32), SD((D // S, S * FL), F32)],
+        cost_estimate=pl.CostEstimate(flops=0, bytes_accessed=6 * R * per * D, transcendentals=0),
+    )(g)
+
+
+def attn_grads_kernel(n, S, R, q_ref, *refs):
+    h = refs[:n]
+    dl = refs[n : 2 * n]
+    ctx = refs[2 * n : 3 * n]
+    dy = refs[3 * n : -1]
+    o = refs[-1]
+    i = pl.program_id(0)
+    q = q_ref[0]
+    blk = h[0].shape[1]
+    D = dy[0].shape[1]
+    DR = D // S
+    CW = dl[0].shape[2]
+    ru = DR // R
+    k = D // CW
+    steps = DR // blk
+    s = i // steps
+    base = (i % steps) * (blk // ru)
+    for p in range(3):
+        t = dtn(joined(h), jnp.concatenate([y[p] for y in dl], axis=0)).astype(BF)
+        for c in range(blk // ru):
+            o[(base + c) ^ q, pl.ds(k * ru + s * 3 * ru + p * ru, ru), :] = t[c * ru : (c + 1) * ru, :]
+    t = dtn(joined(ctx), joined(dy)).astype(BF)
+    m = ctx[0].shape[1] // ru
+    for c in range(m):
+        for j in range(k):
+            o[(i * m + c) ^ q, j * ru : (j + 1) * ru, :] = t[c * ru : (c + 1) * ru, j * CW : (j + 1) * CW]
+
+
+def attn_grads(S, R, q, hs, dls, ctxs, dys):
+    n = len(hs)
+    T, D = hs[0].shape
+    CW = ctxs[0].shape[1]
+    DR = D // S
+    ru = DR // R
+    blk = 256
+    G = D // blk
+    per = (D // CW) * ru + S * 3 * ru
+    keep = lambda s: pl.BlockSpec(s, lambda i, q: (0,) * len(s), pipeline_mode=pl.Buffered(1))
+    return pl.pallas_call(
+        functools.partial(attn_grads_kernel, n, S, R),
+        grid_spec=pltpu.PrefetchScalarGridSpec(
+            num_scalar_prefetch=1,
+            grid=(G,),
+            in_specs=[pl.BlockSpec((T, blk), lambda i, q: (0, i))] * n
+            + [keep((3, T, CW))] * n
+            + [pl.BlockSpec((T, CW // G), lambda i, q: (0, i))] * n
+            + [keep(dys[0].shape)] * len(dys),
+            out_specs=pl.BlockSpec((R, per, CW), lambda i, q: (0, 0, 0)),
+        ),
+        out_shape=SD((R, per, CW), BF),
+        compiler_params=pltpu.CompilerParams(vmem_limit_bytes=60 * MIB),
+        cost_estimate=pl.CostEstimate(flops=8 * n * T * D * CW, bytes_accessed=2 * n * T * (2 * D + 4 * CW) + 8 * D * CW, transcendentals=0),
+    )(q, *hs, *dls, *ctxs, *dys)
+
+
+def attn_finish_kernel(S, ru, k, q_ref, g, out, qkv):
+    CW = g.shape[2]
+    D = out.shape[1]
+    for j in range(k):
+        out[:, j * CW : (j + 1) * CW] = g[0, j * ru : (j + 1) * ru, :].astype(F32)
+    for t in range(S):
+        for p in range(3):
+            a = k * ru + (t * 3 + p) * ru
+            qkv[:, p * D + t * CW : p * D + (t + 1) * CW] = g[0, a : a + ru, :].astype(F32)
+
+
+def attn_finish(S, q, g):
+    R, per, CW = g.shape
+    D = CW * S
+    ru = D // S // R
+    return pl.pallas_call(
+        functools.partial(attn_finish_kernel, S, ru, S),
+        grid_spec=pltpu.PrefetchScalarGridSpec(
+            num_scalar_prefetch=1,
+            grid=(R,),
+            in_specs=[pl.BlockSpec((1, per, CW), lambda c, q: (c ^ q[0], 0, 0))],
+            out_specs=[pl.BlockSpec((ru, D), lambda c, q: (c, 0)), pl.BlockSpec((ru, 3 * D), lambda c, q: (c, 0))],
+        ),
+        out_shape=[SD((CW, D), F32), SD((D // S, 3 * D), F32)],
+        cost_estimate=pl.CostEstimate(flops=0, bytes_accessed=6 * R * per * CW, transcendentals=0),
+    )(q, g)
 
 
 def final_kernel(S, first, PT, *refs):
@@ -463,17 +681,39 @@
 def canonical(slots, me, S, back):
     if S == 1:
         return slots
+    if S == 2:
+        a, b = slots
+        return [jnp.where(me == 0, a, b), jnp.where(me == 0, b, a)]
     stacked = jnp.stack(slots, axis=0)
     return [
         lax.dynamic_index_in_dim(stacked, lax.rem((me - s if back else s - me) + S, S), 0, keepdims=False) for s in range(S)
     ]
 
 
-def columns_for(weight, me, S, j, parts):
-    rows, cols = weight.shape
-    w = weight.reshape(rows, parts, S, cols // (parts * S))
-    w = lax.dynamic_index_in_dim(w, lax.rem(me + j, S), 2, keepdims=False)
-    return w.reshape(rows, cols // S)
+def exchanged(value, R, bit):
+    return lax.ppermute(value, "rep", [(i, i ^ bit) for i in range(R)])
+
+
+def columns_for(weight, me, S, j, parts, row=0, rows=None):
+    cols = weight.shape[1] // parts
+    rows = weight.shape[0] if rows is None else rows
+    w = cols // S
+    at = lax.rem(me + j, S) * w
+    got = [lax.dynamic_slice(weight, (row, p * cols + at), (rows, w)) for p in range(parts)]
+    return got[0] if parts == 1 else jnp.concatenate(got, axis=1)
+
+
+def my_columns_halves(weight, me, S, R):
+    rows = weight.shape[0]
+    half = rows // 2
+    core = lax.rem(lax.axis_index("rep"), 2)
+    slots = [columns_for(weight, me, S, 0, 1)]
+    for j in range(1, S):
+        piece = shifted(columns_for(weight, me, S, j, 1, core * half, half), S, j)
+        other = exchanged(piece, R, 1)
+        first = core == 0
+        slots.append(jnp.concatenate([jnp.where(first, piece, other), jnp.where(first, other, piece)], axis=0))
+    return jnp.concatenate(canonical(slots, me, S, True), axis=0), piece
 
 
 def my_columns(weight, me, S, R, parts):
@@ -485,11 +725,56 @@
     chunk = rows // R
     got = []
     for j in range(1, S):
-        piece = columns_for(weight, me, S, j, parts)
-        piece = lax.dynamic_slice_in_dim(piece, rep * chunk, chunk, 0)
-        got.append(shifted(piece, S, j))
+        got.append(shifted(columns_for(weight, me, S, j, parts, rep * chunk, chunk), S, j))
     others = lax.all_gather(jnp.stack(got, axis=0), "rep", axis=1, tiled=True)
     return jnp.concatenate(canonical([own] + [others[j] for j in range(S - 1)], me, S, True), axis=0)
+
+
+def add_low(a, b):
+    return (a.astype(F32) + b.astype(F32)).astype(BF)
+
+
+def halving(g, v, R, beside):
+    bit = 1
+    while bit < R:
+        h = g.shape[0] // 2
+        got = exchanged(g[h:], R, bit)
+        v = v + exchanged(v, R, bit)
+        got, v = lax.optimization_barrier((got, v))
+        if bit in beside:
+            got, beside[bit] = lax.optimization_barrier((got, beside[bit]))
+        g = add_low(g[:h], got)
+        bit *= 2
+    return g[0], v
+
+
+def doubling(part, R, beside):
+    g = part[None]
+    bit = R // 2
+    while bit:
+        got = exchanged(g, R, bit)
+        if bit in beside:
+            got, beside[bit] = lax.optimization_barrier((got, beside[bit]))
+        g = jnp.concatenate([g, got], axis=0)
+        bit //= 2
+    return g
+
+
+def sum_all(v, S, R):
+    bit = 1
+    while bit < R:
+        v = v + exchanged(v, R, bit)
+        bit *= 2
+    return v
+
+
+def swap_shards(part, me, S, head):
+    n = (part.shape[0] - head) // S
+    slots = []
+    for j in range(S):
+        b = lax.dynamic_slice_in_dim(part, head + lax.rem(me + j, S) * n, n, 0)
+        slots.append(shifted(b, S, j) if j else b)
+    return jnp.concatenate([part[:head]] + canonical(slots, me, S, True), axis=0)
 
 
 def reduce_rows(grad):
@@ -552,71 +837,116 @@
     FL = up_weight.shape[1] // S
     me_arr = jnp.reshape(me, (1,)).astype(jnp.int32)
 
-    small = jnp.concatenate([ln1_gain, ln1_bias, ln2_gain, ln2_bias, out_bias, down_bias, qkv_bias])
+    one = lambda v: v.astype(F32).reshape(-1, CW)
+    small = jnp.concatenate([one(v) for v in (ln1_gain, ln1_bias, ln2_gain, ln2_bias, out_bias, down_bias, qkv_bias)], axis=0)
+    w_up, brought = my_columns_halves(up_weight, me, S, R)
     slots = [small] + [shifted(small, S, j) for j in range(1, S)]
-    whole = jnp.stack(canonical(slots, me, S, True), axis=0).astype(F32)
-    vec = whole[:, : 6 * CW].reshape(S, 6, CW).transpose(1, 0, 2).reshape(6, D)
+    whole = jnp.stack(canonical(slots, me, S, True), axis=0)
+    vec = whole[:, :6].transpose(1, 0, 2).reshape(6, D)
     gb1 = vec[0:2]
     gb2 = vec[2:4]
     vb = vec[4:6]
-    bqkv = whole[:, 6 * CW :].reshape(3, S, CW)
+    bqkv = whole[:, 6:].reshape(3, S, CW)
     bqkv = lax.dynamic_index_in_dim(bqkv, me, 1, keepdims=False).reshape(1, 3 * CW)
     bup = up_bias.astype(F32).reshape(1, FL)
 
-    w_up = my_columns(up_weight, me, S, R, 1)
     w_qkv = my_columns(qkv_weight, me, S, R, 3)
 
     X = [[jnp.concatenate([prompt_in[m, 0], cont_in[m, 0].reshape(CR, D)], axis=0)] for m in range(MB)]
     DY = [[jnp.concatenate([prompt_cot[m, 0], cont_cot[m, 0].reshape(CR, D)], axis=0)] for m in range(MB)]
+    tabs = rotary_tables(PD * S, CR * S, CL)
+    src = [(X[m][0], DY[m][0]) for m in range(MB)]
+    src[1:], brought = lax.optimization_barrier((src[1:], brought))
     for m in range(MB):
         for j in range(1, S):
-            X[m].append(shifted(X[m][0], S, S - j))
-            DY[m].append(shifted(DY[m][0], S, S - j))
-
-    tabs = rotary_tables(PD * S, CR * S, CL)
+            X[m].append(shifted(src[m][0], S, S - j))
+            DY[m].append(shifted(src[m][1], S, S - j))
+
     ff = [[None] * S for _ in range(MB)]
+
+    def mlp(m, j):
+        ff[m][j] = mlp_rows(X[m][j], DY[m][j], w_up, bup, down_weight, gb2)
+
     for m in range(MB):
-        ff[m][0] = mlp_rows(X[m][0], DY[m][0], w_up, bup, down_weight, gb2)
-    y_own, g_own, rest = [], [], []
+        mlp(m, 0)
+    rest = []
     y_got, g_got = [], []
-    for m in range(MB):
-        for j in range(1, S):
-            ff[m][j] = mlp_rows(X[m][j], DY[m][j], w_up, bup, down_weight, gb2)
+
+    def attend(m):
         ys, gs, more = attn_group(
             S, PD, CL, me_arr, X[m], DY[m], [f[3] for f in ff[m]], [f[4] for f in ff[m]], w_qkv, bqkv, out_weight, gb1, tabs
         )
-        rest.append(more)
+        rest.append(list(more))
         y_got.append([ys[0]] + [shifted(ys[j], S, j) for j in range(1, S)])
         g_got.append([gs[0]] + [shifted(gs[j], S, j) for j in range(1, S)])
 
+    chunked = (D // S // R) % 16 == 0 and R & (R - 1) == 0
+    for m in range(MB):
+        for j in range(1, S):
+            mlp(m, j)
+        if m + 1 < MB:
+            attend(m)
+            w_up, rest[m][3] = lax.optimization_barrier((w_up, rest[m][3]))
     every = [ff[m][j] for m in range(MB) for j in range(S)]
     dys = [DY[m][j] for m in range(MB) for j in range(S)]
-    d_down = tn_sum([f[0] for f in every], dys, 256)
-    d_up = tn_sum([f[2] for f in every], [f[1] for f in every], 256)
-    d_qkv = tn_sum([r[2] for r in rest], [r[0] for r in rest], 256)
-    d_out = tn_sum([r[1] for r in rest], [r[3] for r in rest], 256)
-
-    g_down = reduce_rows(d_down)
-    g_up = reduce_columns(d_up, me, S, 1)
-    g_out = reduce_rows(d_out)
-    g_qkv = reduce_columns(d_qkv, me, S, 3)
-
-    ln1 = sum(r[4] for r in rest).reshape(2 * D)
-    ln2 = sum(f[5] for f in every).reshape(2 * D)
-    db_out = sum(jnp.sum(DY[m][0].astype(F32), axis=0) for m in range(MB))
+    acts, dpres, hs = [[f[k] for f in every] for k in range(3)]
+    if chunked:
+        gmlp = mlp_grads(S, R, acts, dys, hs, dpres)
+        part = lax.psum_scatter(gmlp, "rep", scatter_dimension=0, tiled=True)[0]
+    else:
+        gmlp = tn_sum(acts, dys, 256)
+        g_down = reduce_rows(gmlp)
+        g_up = reduce_columns(tn_sum(hs, dpres, 256), me, S, 1)
+    w_qkv, gmlp = lax.optimization_barrier((w_qkv, gmlp))
+    attend(MB - 1)
+    ln1 = sum(r[3] for r in rest).reshape(-1, CW)
+    ln2 = sum(f[5] for f in every).reshape(-1, CW)
+    db_out = sum(jnp.sum(DY[m][0].astype(F32), axis=0) for m in range(MB)).reshape(-1, CW)
     mine = (jnp.arange(S) == me).astype(F32)
-    db_qkv = (sum(r[5] for r in rest)[:, None, :] * mine[None, :, None]).reshape(3 * D)
-    db_up = (sum(f[6] for f in every) * mine[:, None]).reshape(S * FL)
-    tot = lax.psum(jnp.concatenate([ln1, ln2, db_out, db_qkv, db_up]), ("rep", "shard"))
-    own = lambda a, n: lax.dynamic_slice_in_dim(tot, a + me * n, n, 0)
-    v_ln1g, v_ln1b, v_ln2g, v_ln2b, v_out = [own(k * D, CW) for k in range(5)]
-    v_qkv = own(5 * D, 3 * CW)
-    v_up = own(8 * D, FL)
-
-    prior = None
-    for m in range(MB):
-        prior = final_rows(m, MB, PD, X[m][0], DY[m][0], y_got[m], g_got[m], vb, prior)
-    po, co, pg, cg = prior
+    db_qkv = (sum(r[4] for r in rest)[:, None, :] * mine[None, :, None]).reshape(-1, CW)
+    db_up = (sum(f[6] for f in every) * mine[:, None]).reshape(-1, CW)
+    vecs = jnp.concatenate([ln1, ln2, db_out, db_qkv, db_up], axis=0)
+
+    finals = lambda m, prior: final_rows(m, MB, PD, X[m][0], DY[m][0], y_got[m], g_got[m], vb, prior)
+    hs, dls, ctxs = [[r[k] for r in rest] for k in (2, 0, 1)]
+    if chunked:
+        rep = lax.axis_index("rep")
+        q = jnp.zeros((), jnp.int32)
+        for b in range(R.bit_length() - 1):
+            q = 2 * q + ((rep >> b) & 1)
+        q = q.reshape(1).astype(jnp.int32)
+        hs, y_got[:-1], g_got[:-1] = lax.optimization_barrier((hs, y_got[:-1], g_got[:-1]))
+        gatt = attn_grads(S, R, q, hs, dls, ctxs, dys)
+        gatt, part = lax.optimization_barrier((gatt, part))
+        gmlp_all = lax.all_gather(swap_shards(part, me, S, FL // R), "rep", axis=0, tiled=False)
+        early = None
+        for m in range(MB - 1):
+            early = finals(m, early)
+        beside = {2: early}
+        half, vecs = halving(gatt, vecs, R, beside)
+        early = beside[2]
+        half, y_got[-1], g_got[-1] = lax.optimization_barrier((half, y_got[-1], g_got[-1]))
+        outs = finals(MB - 1, early)
+        beside = {2: outs}
+        gatt_all = doubling(swap_shards(half, me, S, D // R), R, beside)
+        outs = beside[2]
+        g_out, g_qkv = attn_finish(S, q, gatt_all)
+        g_down, g_up = mlp_finish(S, gmlp_all, FL)
+    else:
+        dycs = [jnp.concatenate(DY[m], axis=0) for m in range(MB)]
+        g_out = reduce_rows(tn_sum(ctxs, dycs, 256))
+        g_qkv = reduce_columns(tn_sum(hs, dls, 256), me, S, 3)
+        vecs = sum_all(vecs, S, R)
+        outs = None
+        for m in range(MB):
+            outs = finals(m, outs)
+    tot = vecs + sum(shifted(vecs, S, j) for j in range(1, S))
+    own = lambda a, n: lax.dynamic_slice_in_dim(tot, a + me * n, n, 0).reshape(-1)
+    v_ln1g, v_ln1b, v_ln2g, v_ln2b, v_out = [own(k * S, 1) for k in range(5)]
+    v_qkv = own(5 * S, 3)
+    v_up = own(8 * S, FL // CW)
+
+    po, co, pg, cg = outs
     return (
         po.reshape(MB, 1, PD, D),
         co.reshape(MB, 1, CD, CL, D),

time: 850 us -> 578 us (0.68)
  blocking collectives: 142 us -> 0 us
  waiting for transfers between devices: 280 us -> 162 us
  local copies, waits for them, and re-layouts: 50.6 us -> 32.4 us
  other arithmetic: 39.7 us -> 24.6 us
  Pallas kernels: 302 us -> 313 us
  starting transfers between devices: 17.3 us -> 26.6 us
    reduce_scatter x4 -> x1, waiting for transfers between devices: 220 us -> 19.6 us  [per_device(): part = lax.psum_scatter(gmlp, 'rep', scatter_dimension=0, tiled=True)[0]]
    psum x1 -> x0, blocking collectives: 142 us -> none  [per_device(): lax.psum(jnp.concatenate([ln1, ln2, db_out, db_qkv, db_up]), ('rep', 'sha...]
    ppermute x0 -> x13, waiting for transfers between devices: none -> 116 us  [exchanged(): return lax.ppermute(value, 'rep', [(i, i ^ bit) for i in range(R)])]
    all_gather x2 -> x1, waiting for transfers between devices: 27.2 us -> 0.02 us  [my_columns(): others = lax.all_gather(jnp.stack(got, axis=0), 'rep', axis=1, tiled=True)]
    pallas_call x4 -> x5, Pallas kernels: 58.7 us -> 77.9 us  [the longest x1 20 us: attn_grads(): pl.pallas_call(functools.partial(attn_grads_kernel, n, S, R), grid_spec=p...]
    convert_element_type x5 -> x3, other arithmetic: 21.6 us -> 3.63 us  [add_low(): return (a.astype(F32) + b.astype(F32)).astype(BF)]
    unnamed x100 -> x102, local copies, waits for them, and re-layouts: 23.5 us -> 8.26 us
    ppermute x0 -> x13, starting transfers between devices: none -> 10.4 us  [exchanged(): return lax.ppermute(value, 'rep', [(i, i ^ bit) for i in range(R)])]
  transfers between devices with their start and end apart: 23 -> 30, of which waited for: 12 -> 14; matrix products, arithmetic and copies ran while one was open for 9% -> 8% of each run, Pallas kernels for 15% -> 43%
where the time goes in v2:
time: 578 us; the launch traced here: 574 us
  Pallas kernels  313 us (54%)
  waiting for transfers between devices  162 us (28%)
  local copies, waits for them, and re-layouts  32.4 us (6%)
  starting transfers between devices  26.6 us (5%)
  other arithmetic  24.6 us (4%)
  between operations  14.8 us (3%)
    pallas_call x2, Pallas kernels, attn_group(): pl.pallas_call(functools.partial(attn_kernel, S, PD, CL, QB, HG, adding),...  142 us
    ppermute x13, waiting for transfers between devices, exchanged(): return lax.ppermute(value, 'rep', [(i, i ^ bit) for i in range(R)])  116 us
    pallas_call x4, Pallas kernels, mlp_rows(): pl.pallas_call(functools.partial(mlp_kernel, rows_tile(rows, 640)), grid=...  80.7 us
    ppermute x14, waiting for transfers between devices, shifted(): return lax.ppermute(value, 'shard', [(i, (i + j) % S) for i in range(S)])  26.5 us
    pallas_call x1, Pallas kernels, attn_grads(): pl.pallas_call(functools.partial(attn_grads_kernel, n, S, R), grid_spec=p...  20 us
    reduce_scatter x1, waiting for transfers between devices, per_device(): part = lax.psum_scatter(gmlp, 'rep', scatter_dimension=0, tiled=True)[0]  19.6 us
    pallas_call x1, Pallas kernels, mlp_grads(): pl.pallas_call(functools.partial(up_kernel, n), grid=(D // blk,), in_spec...  17.4 us
    pallas_call x1, Pallas kernels, mlp_grads(): pl.pallas_call(functools.partial(down_kernel, n), grid=(FL // blk,), in_s...  16.6 us
  transfers between devices with their start and end apart: 30, of which 14 were waited for; matrix products, arithmetic and copies ran while one was open for 8% of the time, Pallas kernels for 43%

profile of v2, /device:TPU:0, one launch (start us, length us, event | category | flops | bytes accessed | tf_op | source)
XLA Modules:
  0.0 574.3 jit_solution(13003728760976277125)
XLA Ops:
  12.3 3.0 collective-permute-start.4
  16.8 2.3 dynamic_slice.62
  19.1 2.0 collective-permute-start.2
  27.9 2.6 constant_dynamic-slice_fusion.11
  30.5 15.0 %collective-permute-done.2 = bf16[256,2048]{1,0:T(8,128)(2,1)} collective-permute-done((bf16[256,2048]{1,0:T(8,128)(2,1)}, bf16[256,2048]{1,0:T(8,128)(2,1)}, u32[]{:S(2)}, u32[]{:S(2)}) %collective-permute-start.2) | collective-permute-done | bytes 1048608 | tf_op jit(solution)/shard_map/ppermute | solution.py:678
  50.8 2.1 collective-permute-start.6
  53.0 1.7 broadcast_select_fusion.5
  55.8 2.6 pad_maximum_fusion.wu_ref
  58.4 20.2 %shard_map.309 = (bf16[640,2048]{1,0:T(8,128)(2,1)}, bf16[640,2048]{1,0:T(8,128)(2,1)}, bf16[640,1024]{1,0:T(8,128)(2,1)}, bf16[640,1024]{1,0:T(8,128)(2,1)}, bf...) custom-call(bf16[640,1024]{1,0:T(8,128)(2,1)} %copy-done, ...), custom_call_target="tpu_custom_call" | custom-call | flops 10737418240 | bytes 20185088 | tf_op jit(solution)/shard_map/pallas_call | solution.py:102
  78.5 20.2 %shard_map.306 = (bf16[640,2048]{1,0:T(8,128)(2,1)}, bf16[640,2048]{1,0:T(8,128)(2,1)}, bf16[640,1024]{1,0:T(8,128)(2,1)}, bf16[640,1024]{1,0:T(8,128)(2,1)}, bf...) custom-call(bf16[640,1024]{1,0:T(8,128)(2,1)} %copy-done.2, ...), custom_call_target="tpu_custom_call" | custom-call | flops 10737418240 | bytes 20185088 | tf_op jit(solution)/shard_map/pallas_call | solution.py:102
  98.8 2.9 collective-permute-done.1.dy_ref.refs_3_.refs_5_.refs_7_
  101.7 20.1 %shard_map.307 = (bf16[640,2048]{1,0:T(8,128)(2,1)}, bf16[640,2048]{1,0:T(8,128)(2,1)}, bf16[640,1024]{1,0:T(8,128)(2,1)}, bf16[640,1024]{1,0:T(8,128)(2,1)}, bf...) custom-call(bf16[640,1024]{1,0:T(8,128)(2,1)} %collective-permute-done.x_ref.refs_1_, ...), custom_call_target="tpu_custom_call" | custom-call | flops 10737418240 | bytes 20185088 | tf_op jit(solution)/shard_map/pallas_call | solution.py:102
  121.9 2.0 broadcast_select_fusion.3
  123.9 1.8 pad_maximum_fusion.1.refs_8_.refs_9_.refs_10_
  125.7 77.5 %shard_map.308 = (bf16[640,1024]{1,0:T(8,128)(2,1)}, bf16[640,1024]{1,0:T(8,128)(2,1)}, bf16[640,1024]{1,0:T(8,128)(2,1)}, bf16[640,1024]{1,0:T(8,128)(2,1)}, bf...) custom-call(s32[1]{0:T(128)} %bitcast.1.me_ref, ...), custom_call_target="tpu_custom_call" | custom-call | flops 44291850240 | bytes 27787264 | tf_op jit(solution)/shard_map/pallas_call | solution.py:388
  203.3 20.2 %shard_map.310 = (bf16[640,2048]{1,0:T(8,128)(2,1)}, bf16[640,2048]{1,0:T(8,128)(2,1)}, bf16[640,1024]{1,0:T(8,128)(2,1)}, bf16[640,1024]{1,0:T(8,128)(2,1)}, bf...) custom-call(bf16[640,1024]{1,0:T(8,128)(2,1)} %collective-permute-done.6.x_ref.refs_1_, ...), custom_call_target="tpu_custom_call" | custom-call | flops 10737418240 | bytes 20185088 | tf_op jit(solution)/shard_map/pallas_call | solution.py:102
  223.5 16.6 %shard_map.311.refs_8_ = bf16[16,256,1024]{2,1,0:T(8,128)(2,1)} custom-call(bf16[640,2048]{1,0:T(8,128)(2,1)} %get-tuple-element.131.refs_0_, bf16[640,2048]{1,0:T(8,128)(2,1)} %get-tuple-element.132.refs_1_, bf16[640,2048]{1,0:T(8,128)(2,1)} %get-tuple-element.133.refs_2_, bf16[640,2048]{1,0:T(8,128)(2,1)} %get-tuple-element.134.refs_3_, ...), custom_call_target="tpu_custom_call" | custom-call | flops 10737418240 | bytes 19922944 | tf_op jit(solution)/shard_map/pallas_call | solution.py:494
  240.1 17.4 %shard_map.312 = bf16[16,256,1024]{2,1,0:T(8,128)(2,1)} custom-call(bf16[640,1024]{1,0:T(8,128)(2,1)} %get-tuple-element.123.refs_0_, bf16[640,1024]{1,0:T(8,128)(2,1)} %get-tuple-element.124.refs_1_, bf16[640,1024]{1,0:T(8,128)(2,1)} %get-tuple-element.125.refs_2_, bf16[640,1024]{1,0:T(8,128)(2,1)} %get-tuple-element.126.refs_3_, ...), custom_call_target="tpu_custom_call", output_to_operand_aliasing={{}: (8, {})} | custom-call | flops 10737418240 | bytes 19922944 | tf_op jit(solution)/shard_map/pallas_call | solution.py:504
  257.6 2.1 collective-permute-start.8
  259.7 64.8 %shard_map.313 = (bf16[640,1024]{1,0:T(8,128)(2,1)}, bf16[640,1024]{1,0:T(8,128)(2,1)}, bf16[640,1024]{1,0:T(8,128)(2,1)}, bf16[640,1024]{1,0:T(8,128)(2,1)}, bf...) custom-call(s32[1]{0:T(128)} %bitcast.1.me_ref, ...), custom_call_target="tpu_custom_call" | custom-call | flops 44291850240 | bytes 27787264 | tf_op jit(solution)/shard_map/pallas_call | solution.py:388
  324.5 20.0 %shard_map.314 = bf16[16,256,512]{2,1,0:T(8,128)(2,1)} custom-call(s32[1]{0:T(128)} %bitcast.q_ref, bf16[1280,1024]{1,0:T(8,128)(2,1)} %get-tuple-element.141.refs_0_, bf16[1280,1024]{1,0:T(8,128)(2,1)} %get-tuple-element.142.refs_1_, bf16[3,1280,512]{2,1,0:T(8,128)(2,1)} %get-tuple-element.143.refs_2_, bf16[3,1280,512]{2,1,0:T(8,128)(2,1)} %get-tuple-element.144.refs_3_, ...), custom_call_target="tpu_custom_call" | custom-call | flops 10737418240 | bytes 25165824 | tf_op jit(solution)/shard_map/pallas_call | solution.py:578
  344.5 19.6 %reduce-scatter.2.cloned.1.call-done = bf16[1,256,1024]{2,1,0:T(8,128)(2,1)} async-done(((bf16[16,256,1024]{2,1,0:T(8,128)(2,1)}), bf16[1,256,1024]{2,1,0:T(8,128)(2,1)}) %reduce-scatter.2.cloned.1.call-update) | async-done | bytes 524304 | tf_op jit(solution)/shard_map/reduce_scatter | solution.py:895
  365.0 1.4 collective-permute-start.26
  367.4 2.8 collective-permute-done.26
  372.1 3.2 slice.93
  377.2 2.4 collective-permute-done.11
  379.9 3.2 add_convert_fusion
  383.2 1.6 collective-permute-start.12
  385.3 1.6 collective-permute-start.18
  387.4 6.4 %shard_map.315 = (bf16[2,512,1024]{2,1,0:T(8,128)(2,1)}, bf16[2,128,1024]{2,1,0:T(8,128)(2,1)}, f32[2,512,1024]{2,1,0:T(8,128)}, f32[2,128,1024]{2,1,0:T(8,128)}) custom-call(bf16[640,1024]{1,0:T(8,128)(2,1)S(1)} %copy-done.3, bf16[640,1024]{1,0:T(8,128)(2,1)} %pad_maximum_fusion.6.dy_ref.refs_2_.refs_4_.refs_6_.refs_1_, bf16[640,1024]{1,0:T(8,128)(2,1)S(1)} %copy-done.6, ...), custom_call_target="tpu_custom_call" | custom-call | flops 13107200 | bytes 11796480 | tf_op jit(solution)/shard_map/pallas_call | solution.py:665
  393.8 22.5 %collective-permute-done.13 = f32[24,512]{1,0:T(8,128)S(1)} collective-permute-done((f32[24,512]{1,0:T(8,128)S(1)}, f32[24,512]{1,0:T(8,128)S(1)}, u32[]{:S(2)}, u32[]{:S(2)}) %collective-permute-start.13) | collective-permute-done | bytes 49184 | tf_op jit(solution)/shard_map/ppermute | solution.py:694
  416.6 1.6 collective-permute-start.14
  418.7 35.2 %collective-permute-done.15 = f32[24,512]{1,0:T(8,128)S(1)} collective-permute-done((f32[24,512]{1,0:T(8,128)S(1)}, f32[24,512]{1,0:T(8,128)S(1)}, u32[]{:S(2)}, u32[]{:S(2)}) %collective-permute-start.15) | collective-permute-done | bytes 49184 | tf_op jit(solution)/shard_map/ppermute | solution.py:694
  454.6 2.5 collective-permute-start.17
  457.1 12.9 %collective-permute-done.17 = f32[24,512]{1,0:T(8,128)S(1)} collective-permute-done((f32[24,512]{1,0:T(8,128)S(1)}, f32[24,512]{1,0:T(8,128)S(1)}, u32[]{:S(2)}, u32[]{:S(2)}) %collective-permute-start.17) | collective-permute-done | bytes 49184 | tf_op jit(solution)/shard_map/ppermute | solution.py:694
  471.7 1.6 collective-permute-start.20
  473.3 3.2 collective-permute-done.20
  477.3 12.8 %collective-permute-done.21 = bf16[1,256,512]{2,1,0:T(8,128)(2,1)S(1)} collective-permute-done((bf16[1,256,512]{2,1,0:T(8,128)(2,1)S(1)}, bf16[1,256,512]{2,1,0:T(8,128)(2,1)S(1)}, u32[]{:S(2)}, u32[]{:S(2)}) %collective-permute-start.21) | collective-permute-done | bytes 262176 | tf_op jit(solution)/shard_map/ppermute | solution.py:694
  490.2 13.8 %collective-permute-done.22 = bf16[2,256,512]{2,1,0:T(8,128)(2,1)S(1)} collective-permute-done((bf16[2,256,512]{2,1,0:T(8,128)(2,1)S(1)}, bf16[2,256,512]{2,1,0:T(8,128)(2,1)S(1)}, u32[]{:S(2)}, u32[]{:S(2)}) %collective-permute-start.22) | collective-permute-done | bytes 524320 | tf_op jit(solution)/shard_map/ppermute | solution.py:694
  504.1 2.4 collective-permute-start.23
  506.6 6.1 %shard_map.316 = (bf16[2,512,1024]{2,1,0:T(8,128)(2,1)}, bf16[2,128,1024]{2,1,0:T(8,128)(2,1)}, f32[2,512,1024]{2,1,0:T(8,128)}, f32[2,128,1024]{2,1,0:T(8,128)}) custom-call(bf16[640,1024]{1,0:T(8,128)(2,1)S(1)} %copy-done.1, ...), custom_call_target="tpu_custom_call", output_to_operand_aliasing={{0}: (7, {}), {1}: (8, {}), {2}: (9, {}), {3}: (10, {})} | custom-call | flops 13107200 | bytes 11796480 | tf_op jit(solution)/shard_map/pallas_call | solution.py:665
  512.7 16.4 %collective-permute-done.23 = bf16[4,256,512]{2,1,0:T(8,128)(2,1)S(1)} collective-permute-done((bf16[4,256,512]{2,1,0:T(8,128)(2,1)S(1)}, bf16[4,256,512]{2,1,0:T(8,128)(2,1)S(1)}, u32[]{:S(2)}, u32[]{:S(2)}) %collective-permute-start.23) | collective-permute-done | bytes 1048608 | tf_op jit(solution)/shard_map/ppermute | solution.py:694
  529.1 1.5 pad_maximum_fusion.3
  530.7 1.5 collective-permute-start.24
  532.2 2.6 collective-permute-done.24
  540.0 3.0 constant_dynamic-update-slice_fusion.g
  543.1 10.7 %shard_map.317 = (f32[512,1024]{1,0:T(8,128)}, f32[512,3072]{1,0:T(8,128)}) custom-call(s32[1]{0:T(128)} %bitcast.q_ref, bf16[16,256,512]{2,1,0:T(8,128)(2,1)} %constant_dynamic-update-slice_fusion.g), custom_call_target="tpu_custom_call" | custom-call | bytes 12582912 | tf_op jit(solution)/shard_map/pallas_call | solution.py:610
  553.8 13.2 %shard_map.318 = (f32[2048,1024]{1,0:T(8,128)}, f32[512,4096]{1,0:T(8,128)}) custom-call(bf16[16,256,1024]{2,1,0:T(8,128)(2,1)} %bitcast.59), custom_call_target="tpu_custom_call" | custom-call | bytes 25165824 | tf_op jit(solution)/shard_map/pallas_call | solution.py:530
  (214 shorter events, 36.7 us)
Async XLA Ops:
  7.2 13.9 %copy-start.24 = (bf16[2,1,512,1024]{3,2,1,0:T(8,128)(2,1)S(1)}, bf16[2,1,512,1024]{3,2,1,0:T(8,128)(2,1)}, u32[]{:S(2)}) copy-start(bf16[2,1,512,1024]{3,2,1,0:T(8,128)(2,1)} %param.19) | copy-start | bytes 6291460
  7.2 114.7 %all-gather.5.cloned.1.call-start = ((), (), s32[]{:S(2)}) async-start(), calls=%async_computation.2 | async-start | bytes 1671168 | tf_op jit(solution)/shard_map/all_gather | solution.py:729
  12.3 36.5 %collective-permute-start.4 = (f32[9,512]{1,0:T(8,128)S(1)}, f32[9,512]{1,0:T(8,128)S(1)}, u32[]{:S(2)}, u32[]{:S(2)}) collective-permute-start(f32[9,512]{1,0:T(8,128)S(1)} %concatenate.62), channel_id=1, source_target_pairs={{0,1},{1,0},{2,3},{3,2},{4,5},{5,4},{6,7},{7,6},{8,9},{9,8},{10,11... | collective-permute-start | bytes 55304 | tf_op jit(solution)/shard_map/ppermute | solution.py:678
  16.8 33.3 %collective-permute-start.5 = (bf16[32,1536]{1,0:T(8,128)(2,1)}, bf16[32,1536]{1,0:T(8,128)(2,1)S(1)}, u32[]{:S(2)}, u32[]{:S(2)}) collective-permute-start(bf16[32,1536]{1,0:T(8,128)(2,1)} %pad_maximum_fusion.12), channel_id=1, source_target_pairs={{0,1},{1,0},{2,3},{3,2},{4,5},{5,4},{6,7},{7,6},{8,9},{9,8},{10,11... | collective-permute-start | bytes 294920 | tf_op jit(solution)/shard_map/ppermute | solution.py:678
  19.1 26.4 %collective-permute-start.2 = (bf16[256,2048]{1,0:T(8,128)(2,1)}, bf16[256,2048]{1,0:T(8,128)(2,1)}, u32[]{:S(2)}, u32[]{:S(2)}) collective-permute-start(bf16[256,2048]{1,0:T(8,128)(2,1)} %dynamic_slice.62), channel_id=1, source_target_pairs={{0,1},{1,0},{2,3},{3,2},{4,5},{5,4},{6,7},{7,6},{8,9},{9,8},{10,11... | collective-permute-start | bytes 3145736 | tf_op jit(solution)/shard_map/ppermute | solution.py:678
  22.4 76.3 %collective-permute-start = (bf16[640,1024]{1,0:T(8,128)(2,1)S(1)}, bf16[640,1024]{1,0:T(8,128)(2,1)}, u32[]{:S(2)}, u32[]{:S(2)}) collective-permute-start(bf16[640,1024]{1,0:T(8,128)(2,1)S(1)} %pad_maximum_fusion.5.x_ref.refs_0_), channel_id=1, source_target_pairs={{0,1},{1,0},{2,3},{3,2},{4,5},{5,4},{6,7},{7,6},{8,9},{9,8},{10,11... | collective-permute-start | bytes 3932168 | tf_op jit(solution)/shard_map/ppermute | solution.py:678
  24.5 22.4 %copy-start.17 = (bf16[128,1024]{1,0:T(8,128)(2,1)}, bf16[128,1024]{1,0:T(8,128)(2,1)S(1)}, u32[]{:S(2)}) copy-start(bf16[128,1024]{1,0:T(8,128)(2,1)S(1)} %get-tuple-element.254) | copy-start | bytes 786436
  27.8 73.8 %collective-permute-start.1 = (bf16[640,1024]{1,0:T(8,128)(2,1)}, bf16[640,1024]{1,0:T(8,128)(2,1)}, u32[]{:S(2)}, u32[]{:S(2)}) collective-permute-start(bf16[640,1024]{1,0:T(8,128)(2,1)} %pad_maximum_fusion.6.dy_ref.refs_2_.refs_4_.refs_6_.refs_1_), channel_id=1, source_target_pairs={{0,1},{1,0},{2,3},{3,2},{4,5},{5,4},{6,7},{7,6},{8,9},{9,8},{10,11... | collective-permute-start | bytes 3932168 | tf_op jit(solution)/shard_map/ppermute | solution.py:678
  30.5 16.4 %copy-start.10 = (bf16[512,1024]{1,0:T(8,128)(2,1)S(1)}, bf16[512,1024]{1,0:T(8,128)(2,1)}, u32[]{:S(2)}) copy-start(bf16[512,1024]{1,0:T(8,128)(2,1)} %get-tuple-element.246) | copy-start | bytes 3145732
  45.5 7.4 %collective-permute-start.3 = (bf16[256,2048]{1,0:T(8,128)(2,1)}, bf16[256,2048]{1,0:T(8,128)(2,1)}, u32[]{:S(2)}, u32[]{:S(2)}) collective-permute-start(bf16[256,2048]{1,0:T(8,128)(2,1)} %collective-permute-done.2), channel_id=1, source_target_pairs={{0,2},{2,0},{4,6},{6,4},{8,10},{10,8},{12,14},{14,12},{16,18},{18,... | collective-permute-start | bytes 3145736 | tf_op jit(solution)/shard_map/ppermute | solution.py:694
  46.9 7.8 %copy-start = (bf16[640,1024]{1,0:T(8,128)(2,1)}, bf16[640,1024]{1,0:T(8,128)(2,1)S(1)}, u32[]{:S(2)}) copy-start(bf16[640,1024]{1,0:T(8,128)(2,1)S(1)} %pad_maximum_fusion.7.x_ref.refs_0_) | copy-start | bytes 3932164
  50.7 313.3 %reduce-scatter.2.cloned.1.call-start = ((), (), s32[]{:S(2)}) async-start(), calls=%async_computation.1 | async-start | bytes 8912896 | tf_op jit(solution)/shard_map/reduce_scatter | solution.py:895
  50.8 152.4 %collective-permute-start.6 = (bf16[640,1024]{1,0:T(8,128)(2,1)S(1)}, bf16[640,1024]{1,0:T(8,128)(2,1)}, u32[]{:S(2)}, u32[]{:S(2)}) collective-permute-start(bf16[640,1024]{1,0:T(8,128)(2,1)S(1)} %pad_maximum_fusion.7.x_ref.refs_0_), channel_id=1, source_target_pairs={{0,1},{1,0},{2,3},{3,2},{4,5},{5,4},{6,7},{7,6},{8,9},{9,8},{10,11... | collective-permute-start | bytes 3932168 | tf_op jit(solution)/shard_map/ppermute | solution.py:678
  52.9 150.4 %collective-permute-start.7 = (bf16[640,1024]{1,0:T(8,128)(2,1)}, bf16[640,1024]{1,0:T(8,128)(2,1)}, u32[]{:S(2)}, u32[]{:S(2)}) collective-permute-start(bf16[640,1024]{1,0:T(8,128)(2,1)} %pad_maximum_fusion.8.dy_ref.refs_6_.refs_2_.refs_8_.refs_1_), channel_id=1, source_target_pairs={{0,1},{1,0},{2,3},{3,2},{4,5},{5,4},{6,7},{7,6},{8,9},{9,8},{10,11... | collective-permute-start | bytes 3932168 | tf_op jit(solution)/shard_map/ppermute | solution.py:678
  98.7 23.2 %copy-start.21 = (bf16[512,512]{1,0:T(8,128)(2,1)S(1)}, bf16[512,512]{1,0:T(8,128)(2,1)}, u32[]{:S(2)}) copy-start(bf16[512,512]{1,0:T(8,128)(2,1)} %get-tuple-element.240) | copy-start | bytes 1572868
  98.7 23.1 %copy-start.22 = (bf16[512,512]{1,0:T(8,128)(2,1)S(1)}, bf16[512,512]{1,0:T(8,128)(2,1)}, u32[]{:S(2)}) copy-start(bf16[512,512]{1,0:T(8,128)(2,1)} %get-tuple-element.241) | copy-start | bytes 1572868
  98.8 23.1 %copy-start.23 = (bf16[512,512]{1,0:T(8,128)(2,1)S(1)}, bf16[512,512]{1,0:T(8,128)(2,1)}, u32[]{:S(2)}) copy-start(bf16[512,512]{1,0:T(8,128)(2,1)} %get-tuple-element.242) | copy-start | bytes 1572868
  257.5 296.3 %all-gather.7.cloned.1.call-start = ((), (), s32[]{:S(2)}) async-start(), calls=%async_computation.3 | async-start | bytes 8912896 | tf_op jit(solution)/shard_map/all_gather | solution.py:921
  257.6 66.9 %collective-permute-start.8 = (bf16[640,1024]{1,0:T(8,128)(2,1)}, bf16[640,1024]{1,0:T(8,128)(2,1)S(1)}, u32[]{:S(2)}, u32[]{:S(2)}) collective-permute-start(bf16[640,1024]{1,0:T(8,128)(2,1)} %get-tuple-element.138), channel_id=1, source_target_pairs={{0,1},{1,0},{2,3},{3,2},{4,5},{5,4},{6,7},{7,6},{8,9},{9,8},{10,11... | collective-permute-start | bytes 3932168 | tf_op jit(solution)/shard_map/ppermute | solution.py:678
  259.6 64.9 %collective-permute-start.9 = (bf16[640,1024]{1,0:T(8,128)(2,1)}, bf16[640,1024]{1,0:T(8,128)(2,1)}, u32[]{:S(2)}, u32[]{:S(2)}) collective-permute-start(bf16[640,1024]{1,0:T(8,128)(2,1)} %get-tuple-element.140), channel_id=1, source_target_pairs={{0,1},{1,0},{2,3},{3,2},{4,5},{5,4},{6,7},{7,6},{8,9},{9,8},{10,11... | collective-permute-start | bytes 3932168 | tf_op jit(solution)/shard_map/ppermute | solution.py:678
  324.5 20.0 %copy-start.8 = (bf16[640,1024]{1,0:T(8,128)(2,1)}, bf16[640,1024]{1,0:T(8,128)(2,1)S(1)}, u32[]{:S(2)}) copy-start(bf16[640,1024]{1,0:T(8,128)(2,1)S(1)} %collective-permute-done.8.refs_3_) | copy-start | bytes 3932164
  365.0 5.2 collective-permute-start.26
  375.4 4.6 collective-permute-start.10
  376.7 3.0 collective-permute-start.11
  379.9 7.4 %copy-start.6 = (bf16[640,1024]{1,0:T(8,128)(2,1)S(1)}, bf16[640,1024]{1,0:T(8,128)(2,1)}, u32[]{:S(2)}) copy-start(bf16[640,1024]{1,0:T(8,128)(2,1)} %get-tuple-element.163.refs_2_) | copy-start | bytes 3932164
  379.9 7.4 %copy-start.7 = (bf16[640,1024]{1,0:T(8,128)(2,1)S(1)}, bf16[640,1024]{1,0:T(8,128)(2,1)}, u32[]{:S(2)}) copy-start(bf16[640,1024]{1,0:T(8,128)(2,1)} %get-tuple-element.165.refs_4_) | copy-start | bytes 3932164
  379.9 7.4 %copy-start.9 = (bf16[640,1024]{1,0:T(8,128)(2,1)S(1)}, bf16[640,1024]{1,0:T(8,128)(2,1)}, u32[]{:S(2)}) copy-start(bf16[640,1024]{1,0:T(8,128)(2,1)} %copy-done.8) | copy-start | bytes 3932164
  383.2 33.1 %collective-permute-start.12 = (bf16[4,256,512]{2,1,0:T(8,128)(2,1)S(1)}, bf16[4,256,512]{2,1,0:T(8,128)(2,1)S(1)}, u32[]{:S(2)}, u32[]{:S(2)}) collective-permute-start(bf16[4,256,512]{2,1,0:T(8,128)(2,1)S(1)} %slice.109), channel_id=1, source_target_pairs={{0,4},{2,6},{4,0},{6,2},{8,12},{10,14},{12,8},{14,10},{16,20},{18,... | collective-permute-start | bytes 3145736 | tf_op jit(solution)/shard_map/ppermute | solution.py:694
  384.9 31.4 %collective-permute-start.13 = (f32[24,512]{1,0:T(8,128)S(1)}, f32[24,512]{1,0:T(8,128)S(1)}, u32[]{:S(2)}, u32[]{:S(2)}) collective-permute-start(f32[24,512]{1,0:T(8,128)S(1)} %add.229), channel_id=1, source_target_pairs={{0,4},{2,6},{4,0},{6,2},{8,12},{10,14},{12,8},{14,10},{16,20},{18,... | collective-permute-start | bytes 147464 | tf_op jit(solution)/shard_map/ppermute | solution.py:694
  385.3 86.3 %collective-permute-start.18 = (bf16[640,1024]{1,0:T(8,128)(2,1)}, bf16[640,1024]{1,0:T(8,128)(2,1)S(1)}, u32[]{:S(2)}, u32[]{:S(2)}) collective-permute-start(bf16[640,1024]{1,0:T(8,128)(2,1)} %get-tuple-element.177), channel_id=1, source_target_pairs={{0,1},{1,0},{2,3},{3,2},{4,5},{5,4},{6,7},{7,6},{8,9},{9,8},{10,11... | collective-permute-start | bytes 3932168 | tf_op jit(solution)/shard_map/ppermute | solution.py:678
  386.9 84.8 %collective-permute-start.19 = (bf16[640,1024]{1,0:T(8,128)(2,1)}, bf16[640,1024]{1,0:T(8,128)(2,1)S(1)}, u32[]{:S(2)}, u32[]{:S(2)}) collective-permute-start(bf16[640,1024]{1,0:T(8,128)(2,1)} %get-tuple-element.179), channel_id=1, source_target_pairs={{0,1},{1,0},{2,3},{3,2},{4,5},{5,4},{6,7},{7,6},{8,9},{9,8},{10,11... | collective-permute-start | bytes 3932168 | tf_op jit(solution)/shard_map/ppermute | solution.py:678
  416.6 37.3 %collective-permute-start.14 = (bf16[2,256,512]{2,1,0:T(8,128)(2,1)S(1)}, bf16[2,256,512]{2,1,0:T(8,128)(2,1)S(1)}, u32[]{:S(2)}, u32[]{:S(2)}) collective-permute-start(bf16[2,256,512]{2,1,0:T(8,128)(2,1)S(1)} %slice.112), channel_id=1, source_target_pairs={{0,8},{2,10},{4,12},{6,14},{8,0},{10,2},{12,4},{14,6},{16,24},{18,... | collective-permute-start | bytes 1572872 | tf_op jit(solution)/shard_map/ppermute | solution.py:694
  418.2 35.8 %collective-permute-start.15 = (f32[24,512]{1,0:T(8,128)S(1)}, f32[24,512]{1,0:T(8,128)S(1)}, u32[]{:S(2)}, u32[]{:S(2)}) collective-permute-start(f32[24,512]{1,0:T(8,128)S(1)} %add.231), channel_id=1, source_target_pairs={{0,8},{2,10},{4,12},{6,14},{8,0},{10,2},{12,4},{14,6},{16,24},{18,... | collective-permute-start | bytes 147464 | tf_op jit(solution)/shard_map/ppermute | solution.py:694
  454.2 16.5 %collective-permute-start.16 = (bf16[1,256,512]{2,1,0:T(8,128)(2,1)S(1)}, bf16[1,256,512]{2,1,0:T(8,128)(2,1)}, u32[]{:S(2)}, u32[]{:S(2)}) collective-permute-start(bf16[1,256,512]{2,1,0:T(8,128)(2,1)S(1)} %slice.114), channel_id=1, source_target_pairs={{0,16},{2,18},{4,20},{6,22},{8,24},{10,26},{12,28},{14,30},{16,0},... | collective-permute-start | bytes 786440 | tf_op jit(solution)/shard_map/ppermute | solution.py:694
  454.6 15.4 %collective-permute-start.17 = (f32[24,512]{1,0:T(8,128)S(1)}, f32[24,512]{1,0:T(8,128)S(1)}, u32[]{:S(2)}, u32[]{:S(2)}) collective-permute-start(f32[24,512]{1,0:T(8,128)S(1)} %add.233), channel_id=1, source_target_pairs={{0,16},{2,18},{4,20},{6,22},{8,24},{10,26},{12,28},{14,30},{16,0},... | collective-permute-start | bytes 147464 | tf_op jit(solution)/shard_map/ppermute | solution.py:694
  471.7 4.8 collective-permute-start.20
  473.3 33.2 %copy-start.1 = (bf16[640,1024]{1,0:T(8,128)(2,1)S(1)}, bf16[640,1024]{1,0:T(8,128)(2,1)}, u32[]{:S(2)}) copy-start(bf16[640,1024]{1,0:T(8,128)(2,1)} %copy-done) | copy-start | bytes 3932164
  473.3 33.2 %copy-start.4 = (bf16[640,1024]{1,0:T(8,128)(2,1)S(1)}, bf16[640,1024]{1,0:T(8,128)(2,1)}, u32[]{:S(2)}) copy-start(bf16[640,1024]{1,0:T(8,128)(2,1)} %get-tuple-element.181.refs_2_) | copy-start | bytes 3932164
  473.3 33.2 %copy-start.5 = (bf16[640,1024]{1,0:T(8,128)(2,1)S(1)}, bf16[640,1024]{1,0:T(8,128)(2,1)}, u32[]{:S(2)}) copy-start(bf16[640,1024]{1,0:T(8,128)(2,1)} %get-tuple-element.183.refs_4_) | copy-start | bytes 3932164
  477.2 12.8 %collective-permute-start.21 = (bf16[1,256,512]{2,1,0:T(8,128)(2,1)S(1)}, bf16[1,256,512]{2,1,0:T(8,128)(2,1)S(1)}, u32[]{:S(2)}, u32[]{:S(2)}) collective-permute-start(bf16[1,256,512]{2,1,0:T(8,128)(2,1)S(1)} %maximum_bitcast_fusion), channel_id=1, source_target_pairs={{0,16},{2,18},{4,20},{6,22},{8,24},{10,26},{12,28},{14,30},{16,0},... | collective-permute-start | bytes 786440 | tf_op jit(solution)/shard_map/ppermute | solution.py:694
  490.1 13.9 %collective-permute-start.22 = (bf16[2,256,512]{2,1,0:T(8,128)(2,1)S(1)}, bf16[2,256,512]{2,1,0:T(8,128)(2,1)S(1)}, u32[]{:S(2)}, u32[]{:S(2)}) collective-permute-start(bf16[2,256,512]{2,1,0:T(8,128)(2,1)S(1)} %pad_maximum_fusion.10), channel_id=1, source_target_pairs={{0,8},{2,10},{4,12},{6,14},{8,0},{10,2},{12,4},{14,6},{16,24},{18,... | collective-permute-start | bytes 1572872 | tf_op jit(solution)/shard_map/ppermute | solution.py:694
  504.1 24.9 %collective-permute-start.23 = (bf16[4,256,512]{2,1,0:T(8,128)(2,1)S(1)}, bf16[4,256,512]{2,1,0:T(8,128)(2,1)S(1)}, u32[]{:S(2)}, u32[]{:S(2)}) collective-permute-start(bf16[4,256,512]{2,1,0:T(8,128)(2,1)S(1)} %pad_maximum_fusion.9), channel_id=1, source_target_pairs={{0,4},{2,6},{4,0},{6,2},{8,12},{10,14},{12,8},{14,10},{16,20},{18,... | collective-permute-start | bytes 3145736 | tf_op jit(solution)/shard_map/ppermute | solution.py:694
  529.0 7.7 %copy-start.27 = (bf16[96,512]{1,0:T(8,128)(2,1)S(1)}, bf16[96,512]{1,0:T(8,128)(2,1)}, u32[]{:S(2)}) copy-start(bf16[96,512]{1,0:T(8,128)(2,1)} %copy-done.26) | copy-start | bytes 294916
  529.0 7.7 %copy-start.29 = (bf16[64,512]{1,0:T(8,128)(2,1)S(1)}, bf16[64,512]{1,0:T(8,128)(2,1)}, u32[]{:S(2)}) copy-start(bf16[64,512]{1,0:T(8,128)(2,1)} %copy-done.28) | copy-start | bytes 196612
  530.7 9.3 %collective-permute-start.25 = (bf16[8,256,512]{2,1,0:T(8,128)(2,1)}, bf16[8,256,512]{2,1,0:T(8,128)(2,1)}, u32[]{:S(2)}, u32[]{:S(2)}) collective-permute-start(bf16[8,256,512]{2,1,0:T(8,128)(2,1)} %pad_maximum_fusion.3), channel_id=1, source_target_pairs={{0,2},{2,0},{4,6},{6,4},{8,10},{10,8},{12,14},{14,12},{16,18},{18,... | collective-permute-start | bytes 6291464 | tf_op jit(solution)/shard_map/ppermute | solution.py:694
  530.7 8.3 %copy-start.15 = (bf16[4,256,512]{2,1,0:T(8,128)(2,1)S(1)}, bf16[4,256,512]{2,1,0:T(8,128)(2,1)}, u32[]{:S(2)}) copy-start(bf16[4,256,512]{2,1,0:T(8,128)(2,1)} %copy-done.14) | copy-start | bytes 3145732
  530.7 4.2 collective-permute-start.24
  536.7 30.2 %copy-start.46 = (f32[1,512]{1,0:T(1,128)}, f32[1,512]{1,0:T(1,128)S(1)}, u32[]{:S(2)}) copy-start(f32[1,512]{1,0:T(1,128)S(1)} %get-tuple-element.260) | copy-start | bytes 6148
  (30 other events, 56.9 us)
Sparse Core Ops, SparseCore 0:
  50.9 41.5 all-gather.4
  257.6 106.4 reduce-scatter.1
  372.2 83.8 all-gather.6

commit v3 on v2

--- a/solution.py
+++ b/solution.py
@@ -459,25 +459,24 @@
     return jnp.concatenate([r[...] for r in refs], axis=0)
 
 
-def down_kernel(n, *refs):
-    a = refs[:n]
-    b = refs[n : 2 * n]
+def down_kernel(n, more, *refs):
     o = refs[-1]
-    o[...] = dtn(joined(a), joined(b)).astype(BF).reshape(o.shape)
-
-
-def up_kernel(n, *refs):
-    a = refs[:n]
-    b = refs[n : 2 * n]
+    t = dtn(joined(refs[:n]), joined(refs[n : 2 * n])).reshape(o.shape)
+    o[...] = (t + refs[2 * n][...].astype(F32) if more else t).astype(BF)
+
+
+def up_kernel(n, more, *refs):
     o = refs[-1]
     c, rows, w = o.shape
-    k = b[0].shape[1] // w
-    t = dtn(joined(a), joined(b)).astype(BF)
+    t = dtn(joined(refs[:n]), joined(refs[n : 2 * n]))
+    k = t.shape[1] // w
     for i in range(k):
-        o[:, i * (rows // k) : (i + 1) * (rows // k), :] = t[:, i * w : (i + 1) * w].reshape(c, rows // k, w)
-
-
-def mlp_grads(S, R, acts, dys, hs, dpres):
+        r = slice(i * (rows // k), (i + 1) * (rows // k))
+        p = t[:, i * w : (i + 1) * w].reshape(c, rows // k, w)
+        o[:, r, :] = (p + refs[2 * n][:, r, :].astype(F32) if more else p).astype(BF)
+
+
+def mlp_grads(S, R, acts, dys, hs, dpres, g=None):
     n = len(acts)
     rows, FL = acts[0].shape
     D = dys[0].shape[1]
@@ -487,52 +486,56 @@
     ru = DR // R
     k = FL // D
     per = rd + S * ru * k
-    one = pl.Buffered(1)
-    keep = lambda s: pl.BlockSpec(s, lambda i: (0,) * len(s), pipeline_mode=one)
-    cost = pl.CostEstimate(flops=2 * n * rows * D * FL, bytes_accessed=2 * (n * rows * (D + FL) + D * FL), transcendentals=0)
-    params = pltpu.CompilerParams(vmem_limit_bytes=60 * MIB)
-    g = pl.pallas_call(
-        functools.partial(down_kernel, n),
-        grid=(FL // blk,),
-        in_specs=[pl.BlockSpec((rows, blk), lambda i: (0, i))] * n + [keep((rows, D))] * n,
-        out_specs=pl.BlockSpec((blk // rd, rd, D), lambda i: (i, 0, 0)),
-        out_shape=SD((R, per, D), BF),
-        compiler_params=params,
-        cost_estimate=cost,
-    )(*acts, *dys)
+    keep = lambda s: pl.BlockSpec(s, lambda i: (0,) * len(s), pipeline_mode=pl.Buffered(1))
     steps = DR // blk
-    return pl.pallas_call(
-        functools.partial(up_kernel, n),
-        grid=(D // blk,),
-        in_specs=[pl.BlockSpec((rows, blk), lambda i: (0, i))] * n + [keep((rows, FL))] * n + [pl.BlockSpec(memory_space=pl.ANY)],
-        out_specs=pl.BlockSpec((blk // ru, ru * k, D), lambda i: (i % steps, rd // (ru * k) + i // steps, 0)),
-        out_shape=SD((R, per, D), BF),
-        input_output_aliases={2 * n: 0},
-        compiler_params=params,
-        cost_estimate=cost,
-    )(*hs, *dpres, g)
+    more = g is not None
+    hbm = pl.BlockSpec(memory_space=pl.ANY)
+
+    def call(kernel, a, b, spec, g):
+        width = b[0].shape[1]
+        prior = [] if g is None else [g]
+        return pl.pallas_call(
+            functools.partial(kernel, n, more),
+            grid=(a[0].shape[1] // blk,),
+            in_specs=[pl.BlockSpec((rows, blk), lambda i: (0, i))] * n
+            + [keep((rows, width))] * n
+            + ([spec if more else hbm] if prior else []),
+            out_specs=spec,
+            out_shape=SD((R, per, D), BF),
+            input_output_aliases={2 * n: 0} if prior else {},
+            compiler_params=pltpu.CompilerParams(vmem_limit_bytes=60 * MIB),
+            cost_estimate=pl.CostEstimate(
+                flops=2 * n * rows * D * FL, bytes_accessed=2 * (n * rows * (D + FL) + (1 + more) * D * FL), transcendentals=0
+            ),
+        )(*a, *b, *prior)
+
+    g = call(down_kernel, acts, dys, pl.BlockSpec((blk // rd, rd, D), lambda i: (i, 0, 0)), g)
+    spec = pl.BlockSpec((blk // ru, ru * k, D), lambda i: (i % steps, rd // (ru * k) + i // steps, 0))
+    return call(up_kernel, hs, dpres, spec, g)
 
 
 def mlp_finish_kernel(S, rd, ru, g, down, up):
-    D = g.shape[2]
-    k = (g.shape[1] - rd) // (S * ru)
-    down[...] = g[0, :rd, :].astype(F32)
-    for t in range(S):
-        for i in range(k):
-            a = rd + (t * k + i) * ru
-            up[:, (t * k + i) * D : (t * k + i + 1) * D] = g[0, a : a + ru, :].astype(F32)
+    n, per, D = g.shape
+    k = (per - rd) // (S * ru)
+    for c in range(n):
+        down[c * rd : (c + 1) * rd, :] = g[c, :rd, :].astype(F32)
+        for t in range(S * k):
+            a = rd + t * ru
+            up[c * ru : (c + 1) * ru, t * D : (t + 1) * D] = g[c, a : a + ru, :].astype(F32)
 
 
 def mlp_finish(S, g, FL):
     R, per, D = g.shape
     rd = FL // R
     ru = D // S // R
+    n = 4
     return pl.pallas_call(
         functools.partial(mlp_finish_kernel, S, rd, ru),
-        grid=(R,),
-        in_specs=[pl.BlockSpec((1, per, D), lambda c: (c, 0, 0))],
-        out_specs=[pl.BlockSpec((rd, D), lambda c: (c, 0)), pl.BlockSpec((ru, S * FL), lambda c: (c, 0))],
+        grid=(R // n,),
+        in_specs=[pl.BlockSpec((n, per, D), lambda c: (c, 0, 0))],
+        out_specs=[pl.BlockSpec((n * rd, D), lambda c: (c, 0)), pl.BlockSpec((n * ru, S * FL), lambda c: (c, 0))],
         out_shape=[SD((FL, D), F32), SD((D // S, S * FL), F32)],
+        compiler_params=pltpu.CompilerParams(vmem_limit_bytes=40 * MIB),
         cost_estimate=pl.CostEstimate(flops=0, bytes_accessed=6 * R * per * D, transcendentals=0),
     )(g)
 
@@ -541,10 +544,11 @@
     h = refs[:n]
     dl = refs[n : 2 * n]
     ctx = refs[2 * n : 3 * n]
-    dy = refs[3 * n : -1]
-    o = refs[-1]
+    dy = refs[3 * n : -2]
+    first, second = refs[-2:]
     i = pl.program_id(0)
-    q = q_ref[0]
+    q1 = q_ref[0]
+    q2 = q_ref[1]
     blk = h[0].shape[1]
     D = dy[0].shape[1]
     DR = D // S
@@ -557,12 +561,16 @@
     for p in range(3):
         t = dtn(joined(h), jnp.concatenate([y[p] for y in dl], axis=0)).astype(BF)
         for c in range(blk // ru):
-            o[(base + c) ^ q, pl.ds(k * ru + s * 3 * ru + p * ru, ru), :] = t[c * ru : (c + 1) * ru, :]
+            v = t[c * ru : (c + 1) * ru, :]
+            if p < 2:
+                first[(base + c) ^ q1, pl.ds(s * 2 * ru + p * ru, ru), :] = v
+            else:
+                second[(base + c) ^ q2, pl.ds(k * ru + s * ru, ru), :] = v
     t = dtn(joined(ctx), joined(dy)).astype(BF)
     m = ctx[0].shape[1] // ru
     for c in range(m):
         for j in range(k):
-            o[(i * m + c) ^ q, j * ru : (j + 1) * ru, :] = t[c * ru : (c + 1) * ru, j * CW : (j + 1) * CW]
+            second[(i * m + c) ^ q2, j * ru : (j + 1) * ru, :] = t[c * ru : (c + 1) * ru, j * CW : (j + 1) * CW]
 
 
 def attn_grads(S, R, q, hs, dls, ctxs, dys):
@@ -573,8 +581,8 @@
     ru = DR // R
     blk = 256
     G = D // blk
-    per = (D // CW) * ru + S * 3 * ru
     keep = lambda s: pl.BlockSpec(s, lambda i, q: (0,) * len(s), pipeline_mode=pl.Buffered(1))
+    shapes = [(R, S * 2 * ru, CW), (R, (D // CW + S) * ru, CW)]
     return pl.pallas_call(
         functools.partial(attn_grads_kernel, n, S, R),
         grid_spec=pltpu.PrefetchScalarGridSpec(
@@ -584,40 +592,49 @@
             + [keep((3, T, CW))] * n
             + [pl.BlockSpec((T, CW // G), lambda i, q: (0, i))] * n
             + [keep(dys[0].shape)] * len(dys),
-            out_specs=pl.BlockSpec((R, per, CW), lambda i, q: (0, 0, 0)),
+            out_specs=[pl.BlockSpec(s, lambda i, q: (0, 0, 0)) for s in shapes],
         ),
-        out_shape=SD((R, per, CW), BF),
+        out_shape=[SD(s, BF) for s in shapes],
         compiler_params=pltpu.CompilerParams(vmem_limit_bytes=60 * MIB),
         cost_estimate=pl.CostEstimate(flops=8 * n * T * D * CW, bytes_accessed=2 * n * T * (2 * D + 4 * CW) + 8 * D * CW, transcendentals=0),
     )(q, *hs, *dls, *ctxs, *dys)
 
 
-def attn_finish_kernel(S, ru, k, q_ref, g, out, qkv):
-    CW = g.shape[2]
+def attn_finish_kernel(S, ru, k, n, q_ref, *refs):
+    firsts, seconds = refs[:n], refs[n : 2 * n]
+    out, qkv = refs[2 * n :]
+    CW = seconds[0].shape[2]
     D = out.shape[1]
-    for j in range(k):
-        out[:, j * CW : (j + 1) * CW] = g[0, j * ru : (j + 1) * ru, :].astype(F32)
-    for t in range(S):
-        for p in range(3):
-            a = k * ru + (t * 3 + p) * ru
-            qkv[:, p * D + t * CW : p * D + (t + 1) * CW] = g[0, a : a + ru, :].astype(F32)
-
-
-def attn_finish(S, q, g):
-    R, per, CW = g.shape
+    for c in range(n):
+        r = slice(c * ru, (c + 1) * ru)
+        for j in range(k):
+            out[r, j * CW : (j + 1) * CW] = seconds[c][0, j * ru : (j + 1) * ru, :].astype(F32)
+        for t in range(S):
+            for p in range(3):
+                a = (t * 2 + p) * ru if p < 2 else (k + t) * ru
+                v = (firsts if p < 2 else seconds)[c][0, a : a + ru, :]
+                qkv[r, p * D + t * CW : p * D + (t + 1) * CW] = v.astype(F32)
+
+
+def attn_finish(S, q, g1, g2):
+    R, per1, CW = g1.shape
+    per2 = g2.shape[1]
     D = CW * S
     ru = D // S // R
+    n = 4
+    block = lambda per, k, c: pl.BlockSpec((1, per, CW), lambda i, q: ((i * n + c) ^ q[k], 0, 0))
     return pl.pallas_call(
-        functools.partial(attn_finish_kernel, S, ru, S),
+        functools.partial(attn_finish_kernel, S, ru, S, n),
         grid_spec=pltpu.PrefetchScalarGridSpec(
             num_scalar_prefetch=1,
-            grid=(R,),
-            in_specs=[pl.BlockSpec((1, per, CW), lambda c, q: (c ^ q[0], 0, 0))],
-            out_specs=[pl.BlockSpec((ru, D), lambda c, q: (c, 0)), pl.BlockSpec((ru, 3 * D), lambda c, q: (c, 0))],
+            grid=(R // n,),
+            in_specs=[block(per1, 0, c) for c in range(n)] + [block(per2, 1, c) for c in range(n)],
+            out_specs=[pl.BlockSpec((n * ru, D), lambda c, q: (c, 0)), pl.BlockSpec((n * ru, 3 * D), lambda c, q: (c, 0))],
         ),
         out_shape=[SD((CW, D), F32), SD((D // S, 3 * D), F32)],
-        cost_estimate=pl.CostEstimate(flops=0, bytes_accessed=6 * R * per * CW, transcendentals=0),
-    )(q, g)
+        compiler_params=pltpu.CompilerParams(vmem_limit_bytes=40 * MIB),
+        cost_estimate=pl.CostEstimate(flops=0, bytes_accessed=6 * R * (per1 + per2) * CW, transcendentals=0),
+    )(q, *[g1] * n, *[g2] * n)
 
 
 def final_kernel(S, first, PT, *refs):
@@ -705,15 +722,21 @@
 
 def my_columns_halves(weight, me, S, R):
     rows = weight.shape[0]
-    half = rows // 2
-    core = lax.rem(lax.axis_index("rep"), 2)
+    rep = lax.axis_index("rep")
+    core = rep % 2
+    y = (rep // 2) % 2
+    n = rows // 4
+    cut = [columns_for(weight, me, S, j, 1, (2 * core + y) * n, n) for j in range(1, S)]
     slots = [columns_for(weight, me, S, 0, 1)]
+
+    def both(piece, other, first):
+        return jnp.concatenate([jnp.where(first, piece, other), jnp.where(first, other, piece)], axis=0)
+
     for j in range(1, S):
-        piece = shifted(columns_for(weight, me, S, j, 1, core * half, half), S, j)
-        other = exchanged(piece, R, 1)
-        first = core == 0
-        slots.append(jnp.concatenate([jnp.where(first, piece, other), jnp.where(first, other, piece)], axis=0))
-    return jnp.concatenate(canonical(slots, me, S, True), axis=0), piece
+        piece = shifted(cut[j - 1], S, j)
+        pair = both(piece, exchanged(piece, R, 2), y == 0)
+        slots.append(both(pair, exchanged(pair, R, 1), core == 0))
+    return jnp.concatenate(canonical(slots, me, S, True), axis=0), piece, cut[0]
 
 
 def my_columns(weight, me, S, R, parts):
@@ -734,30 +757,43 @@
     return (a.astype(F32) + b.astype(F32)).astype(BF)
 
 
-def halving(g, v, R, beside):
-    bit = 1
-    while bit < R:
-        h = g.shape[0] // 2
-        got = exchanged(g[h:], R, bit)
-        v = v + exchanged(v, R, bit)
+def orders(R):
+    bits = [1 << i for i in range(R.bit_length() - 1)]
+    return bits, bits[:1] + bits[2:] + bits[1:2]
+
+
+def place(rep, order):
+    q = jnp.zeros((), jnp.int32)
+    for bit in order:
+        q = 2 * q + (rep & bit) // bit
+    return q
+
+
+def beside_it(got, key, beside):
+    if key in beside:
+        got, beside[key] = lax.optimization_barrier((got, beside[key]))
+    return got
+
+
+def halving(pair, v, R, beside):
+    pair = list(pair)
+    for i, bits in enumerate(zip(*orders(R))):
+        h = pair[0].shape[0] // 2
+        got = [exchanged(g[h:], R, bit) for g, bit in zip(pair, bits)]
+        v = v + exchanged(v, R, bits[0])
         got, v = lax.optimization_barrier((got, v))
-        if bit in beside:
-            got, beside[bit] = lax.optimization_barrier((got, beside[bit]))
-        g = add_low(g[:h], got)
-        bit *= 2
-    return g[0], v
-
-
-def doubling(part, R, beside):
-    g = part[None]
-    bit = R // 2
-    while bit:
-        got = exchanged(g, R, bit)
-        if bit in beside:
-            got, beside[bit] = lax.optimization_barrier((got, beside[bit]))
-        g = jnp.concatenate([g, got], axis=0)
-        bit //= 2
-    return g
+        got = beside_it(got, i, beside)
+        pair = [add_low(g[:h], t) for g, t in zip(pair, got)]
+    return [g[0] for g in pair], v
+
+
+def doubling(parts, R, beside):
+    pair = [p[None] for p in parts]
+    for i, bits in reversed(list(enumerate(zip(*orders(R))))):
+        got = [exchanged(g, R, bit) for g, bit in zip(pair, bits)]
+        got = beside_it(got, i, beside)
+        pair = [jnp.concatenate([g, t], axis=0) for g, t in zip(pair, got)]
+    return pair
 
 
 def sum_all(v, S, R):
@@ -774,7 +810,7 @@
     for j in range(S):
         b = lax.dynamic_slice_in_dim(part, head + lax.rem(me + j, S) * n, n, 0)
         slots.append(shifted(b, S, j) if j else b)
-    return jnp.concatenate([part[:head]] + canonical(slots, me, S, True), axis=0)
+    return jnp.concatenate(([part[:head]] if head else []) + canonical(slots, me, S, True), axis=0)
 
 
 def reduce_rows(grad):
@@ -839,7 +875,8 @@
 
     one = lambda v: v.astype(F32).reshape(-1, CW)
     small = jnp.concatenate([one(v) for v in (ln1_gain, ln1_bias, ln2_gain, ln2_bias, out_bias, down_bias, qkv_bias)], axis=0)
-    w_up, brought = my_columns_halves(up_weight, me, S, R)
+    w_up, brought, cut = my_columns_halves(up_weight, me, S, R)
+    (small, qkv_weight), cut = lax.optimization_barrier(((small, qkv_weight), cut))
     slots = [small] + [shifted(small, S, j) for j in range(1, S)]
     whole = jnp.stack(canonical(slots, me, S, True), axis=0)
     vec = whole[:, :6].transpose(1, 0, 2).reshape(6, D)
@@ -881,58 +918,61 @@
         g_got.append([gs[0]] + [shifted(gs[j], S, j) for j in range(1, S)])
 
     chunked = (D // S // R) % 16 == 0 and R & (R - 1) == 0
+    rep = lax.axis_index("rep")
+    late = [(MB - 1, j) for j in range(1, S)]
+    early = [(m, j) for m in range(MB) for j in range(S) if (m, j) not in late]
+    of = lambda set_, k: [ff[m][j][k] for m, j in set_]
+    for m, j in early:
+        if j:
+            mlp(m, j)
+    if chunked:
+        gmlp = mlp_grads(S, R, of(early, 0), [DY[m][j] for m, j in early], of(early, 2), of(early, 1))
+        w_up, gmlp = lax.optimization_barrier((w_up, gmlp))
+    for m, j in late:
+        mlp(m, j)
+    if chunked:
+        if late:
+            gmlp = mlp_grads(S, R, of(late, 0), [DY[m][j] for m, j in late], of(late, 2), of(late, 1), gmlp)
+        part = lax.psum_scatter(gmlp, "rep", scatter_dimension=0, tiled=True)[0]
+        w_qkv, gmlp = lax.optimization_barrier((w_qkv, gmlp))
     for m in range(MB):
-        for j in range(1, S):
-            mlp(m, j)
+        attend(m)
         if m + 1 < MB:
-            attend(m)
-            w_up, rest[m][3] = lax.optimization_barrier((w_up, rest[m][3]))
-    every = [ff[m][j] for m in range(MB) for j in range(S)]
-    dys = [DY[m][j] for m in range(MB) for j in range(S)]
-    acts, dpres, hs = [[f[k] for f in every] for k in range(3)]
-    if chunked:
-        gmlp = mlp_grads(S, R, acts, dys, hs, dpres)
-        part = lax.psum_scatter(gmlp, "rep", scatter_dimension=0, tiled=True)[0]
-    else:
-        gmlp = tn_sum(acts, dys, 256)
-        g_down = reduce_rows(gmlp)
-        g_up = reduce_columns(tn_sum(hs, dpres, 256), me, S, 1)
-    w_qkv, gmlp = lax.optimization_barrier((w_qkv, gmlp))
-    attend(MB - 1)
+            w_qkv, rest[m][3] = lax.optimization_barrier((w_qkv, rest[m][3]))
+    every = early + late
     ln1 = sum(r[3] for r in rest).reshape(-1, CW)
-    ln2 = sum(f[5] for f in every).reshape(-1, CW)
+    ln2 = sum(of(every, 5)).reshape(-1, CW)
     db_out = sum(jnp.sum(DY[m][0].astype(F32), axis=0) for m in range(MB)).reshape(-1, CW)
     mine = (jnp.arange(S) == me).astype(F32)
     db_qkv = (sum(r[4] for r in rest)[:, None, :] * mine[None, :, None]).reshape(-1, CW)
-    db_up = (sum(f[6] for f in every) * mine[:, None]).reshape(-1, CW)
+    db_up = (sum(of(every, 6)) * mine[:, None]).reshape(-1, CW)
     vecs = jnp.concatenate([ln1, ln2, db_out, db_qkv, db_up], axis=0)
 
     finals = lambda m, prior: final_rows(m, MB, PD, X[m][0], DY[m][0], y_got[m], g_got[m], vb, prior)
     hs, dls, ctxs = [[r[k] for r in rest] for k in (2, 0, 1)]
     if chunked:
-        rep = lax.axis_index("rep")
-        q = jnp.zeros((), jnp.int32)
-        for b in range(R.bit_length() - 1):
-            q = 2 * q + ((rep >> b) & 1)
-        q = q.reshape(1).astype(jnp.int32)
+        q = jnp.stack([place(rep, order) for order in orders(R)]).astype(jnp.int32)
         hs, y_got[:-1], g_got[:-1] = lax.optimization_barrier((hs, y_got[:-1], g_got[:-1]))
-        gatt = attn_grads(S, R, q, hs, dls, ctxs, dys)
-        gatt, part = lax.optimization_barrier((gatt, part))
-        gmlp_all = lax.all_gather(swap_shards(part, me, S, FL // R), "rep", axis=0, tiled=False)
-        early = None
+        gatt = attn_grads(S, R, q, hs, dls, ctxs, [DY[m][j] for m in range(MB) for j in range(S)])
+        outs = None
         for m in range(MB - 1):
-            early = finals(m, early)
-        beside = {2: early}
+            outs = finals(m, outs)
+        part = swap_shards(part, me, S, FL // R)
+        beside = {0: part, 1: outs, 2: (y_got[-1], g_got[-1])}
         half, vecs = halving(gatt, vecs, R, beside)
-        early = beside[2]
-        half, y_got[-1], g_got[-1] = lax.optimization_barrier((half, y_got[-1], g_got[-1]))
-        outs = finals(MB - 1, early)
-        beside = {2: outs}
-        gatt_all = doubling(swap_shards(half, me, S, D // R), R, beside)
+        part, outs, (y_got[-1], g_got[-1]) = beside[0], beside[1], beside[2]
+        gmlp_all = lax.all_gather(part, "rep", axis=0, tiled=False)
+        outs = finals(MB - 1, outs)
+        k = D // CW * (D // S // R)
+        beside = {2: outs, 1: mlp_finish(S, gmlp_all, FL)}
+        g1, g2 = doubling([swap_shards(half[0], me, S, 0), swap_shards(half[1], me, S, k)], R, beside)
         outs = beside[2]
-        g_out, g_qkv = attn_finish(S, q, gatt_all)
-        g_down, g_up = mlp_finish(S, gmlp_all, FL)
+        g_down, g_up = beside[1]
+        g_out, g_qkv = attn_finish(S, q, g1, g2)
     else:
+        dls, ctxs, hs = [[r[k] for r in rest] for k in (0, 1, 2)]
+        g_down = reduce_rows(tn_sum(of(every, 0), [DY[m][j] for m, j in every], 256))
+        g_up = reduce_columns(tn_sum(of(every, 2), of(every, 1), 256), me, S, 1)
         dycs = [jnp.concatenate(DY[m], axis=0) for m in range(MB)]
         g_out = reduce_rows(tn_sum(ctxs, dycs, 256))
         g_qkv = reduce_columns(tn_sum(hs, dls, 256), me, S, 3)

time: 578 us -> 514 us (0.89)
  waiting for transfers between devices: 162 us -> 87.1 us
  Pallas kernels: 313 us -> 298 us
  starting transfers between devices: 26.6 us -> 39.6 us
  local copies, waits for them, and re-layouts: 32.4 us -> 39.5 us
    ppermute x13 -> x22, waiting for transfers between devices: 116 us -> 66.1 us  [exchanged(): return lax.ppermute(value, 'rep', [(i, i ^ bit) for i in range(R)])]
    reduce_scatter x1, waiting for transfers between devices: 19.6 us -> 0.01 us  [per_device(): part = lax.psum_scatter(gmlp, 'rep', scatter_dimension=0, tiled=True)[0]]
    pallas_call x2, Pallas kernels: 142 us -> 130 us  [attn_group(): pl.pallas_call(functools.partial(attn_kernel, S, PD, CL, QB, HG, adding),...]
    ppermute x13 -> x22, starting transfers between devices: 10.4 us -> 20.7 us  [exchanged(): return lax.ppermute(value, 'rep', [(i, i ^ bit) for i in range(R)])]
    unnamed x102 -> x117, local copies, waits for them, and re-layouts: 8.26 us -> 17 us
    ppermute x14 -> x15, waiting for transfers between devices: 26.5 us -> 20.9 us  [shifted(): return lax.ppermute(value, 'shard', [(i, (i + j) % S) for i in range(S)])]
    ppermute x14 -> x15, starting transfers between devices: 16.1 us -> 18.8 us  [shifted(): return lax.ppermute(value, 'shard', [(i, (i + j) % S) for i in range(S)])]
    pallas_call x4 -> x6, Pallas kernels: 57.8 us -> 56.3 us  [the longest x4 46.1 us: call(): pl.pallas_call(functools.partial(kernel, n, more), grid=(a[0].shape[1] //...]
  transfers between devices with their start and end apart: 30 -> 40, of which waited for: 14 -> 15; matrix products, arithmetic and copies ran while one was open for 8% -> 10% of each run, Pallas kernels for 43% -> 58%
where the time goes in v3:
time: 514 us; the launch traced here: 509 us
  Pallas kernels  298 us (58%)
  waiting for transfers between devices  87.1 us (17%)
  starting transfers between devices  39.6 us (8%)
  local copies, waits for them, and re-layouts  39.5 us (8%)
  other arithmetic  29.4 us (6%)
  between operations  15.2 us (3%)
    pallas_call x2, Pallas kernels, attn_group(): pl.pallas_call(functools.partial(attn_kernel, S, PD, CL, QB, HG, adding),...  130 us
    pallas_call x4, Pallas kernels, mlp_rows(): pl.pallas_call(functools.partial(mlp_kernel, rows_tile(rows, 640)), grid=...  81.3 us
    ppermute x22, waiting for transfers between devices, exchanged(): return lax.ppermute(value, 'rep', [(i, i ^ bit) for i in range(R)])  66.1 us
    pallas_call x4, Pallas kernels, call(): pl.pallas_call(functools.partial(kernel, n, more), grid=(a[0].shape[1] //...  46.1 us
    ppermute x15, waiting for transfers between devices, shifted(): return lax.ppermute(value, 'shard', [(i, (i + j) % S) for i in range(S)])  20.9 us
    ppermute x22, starting transfers between devices, exchanged(): return lax.ppermute(value, 'rep', [(i, i ^ bit) for i in range(R)])  20.7 us
    pallas_call x1, Pallas kernels, attn_grads(): pl.pallas_call(functools.partial(attn_grads_kernel, n, S, R), grid_spec=p...  19.4 us
    ppermute x15, starting transfers between devices, shifted(): return lax.ppermute(value, 'shard', [(i, (i + j) % S) for i in range(S)])  18.8 us
  transfers between devices with their start and end apart: 40, of which 15 were waited for; matrix products, arithmetic and copies ran while one was open for 10% of the time, Pallas kernels for 58%

profile of v3, /device:TPU:0, one launch (start us, length us, event | category | flops | bytes accessed | tf_op | source)
XLA Modules:
  0.0 508.6 jit_solution(7296098757524981580)
XLA Ops:
  8.4 3.0 collective-permute-start.2
  17.9 2.0 collective-permute-start.6
  19.9 1.7 slice_bitcast_fusion.1
  21.6 2.5 collective-permute-done.2
  24.1 2.1 collective-permute-start.3
  28.9 1.7 slice_bitcast_fusion
  30.6 5.8 %collective-permute-done.3 = bf16[128,2048]{1,0:T(8,128)(2,1)S(1)} collective-permute-done((bf16[128,2048]{1,0:T(8,128)(2,1)S(1)}, bf16[128,2048]{1,0:T(8,128)(2,1)S(1)}, u32[]{:S(2)}, u32[]{:S(2)}) %collective-permute-start.3) | collective-permute-done | bytes 524320 | tf_op jit(solution)/shard_map/ppermute | solution.py:711
  46.9 1.8 broadcast_select_fusion.5
  49.8 2.6 pad_maximum_fusion.wu_ref
  52.4 20.4 %shard_map.308 = (bf16[640,2048]{1,0:T(8,128)(2,1)}, bf16[640,2048]{1,0:T(8,128)(2,1)}, bf16[640,1024]{1,0:T(8,128)(2,1)}, bf16[640,1024]{1,0:T(8,128)(2,1)}, bf...) custom-call(bf16[640,1024]{1,0:T(8,128)(2,1)} %copy-done.1, bf16[640,1024]{1,0:T(8,128)(2,1)} %copy-done.3, ...), custom_call_target="tpu_custom_call" | custom-call | flops 10737418240 | bytes 20185088 | tf_op jit(solution)/shard_map/pallas_call | solution.py:102
  72.9 20.2 %shard_map.306 = (bf16[640,2048]{1,0:T(8,128)(2,1)}, bf16[640,2048]{1,0:T(8,128)(2,1)}, bf16[640,1024]{1,0:T(8,128)(2,1)}, bf16[640,1024]{1,0:T(8,128)(2,1)}, bf...) custom-call(bf16[640,1024]{1,0:T(8,128)(2,1)} %pad_maximum_fusion.4.x_ref.refs_0_, ...), custom_call_target="tpu_custom_call" | custom-call | flops 10737418240 | bytes 20185088 | tf_op jit(solution)/shard_map/pallas_call | solution.py:102
  93.1 20.1 %shard_map.307 = (bf16[640,2048]{1,0:T(8,128)(2,1)}, bf16[640,2048]{1,0:T(8,128)(2,1)}, bf16[640,1024]{1,0:T(8,128)(2,1)}, bf16[640,1024]{1,0:T(8,128)(2,1)}, bf...) custom-call(bf16[640,1024]{1,0:T(8,128)(2,1)} %collective-permute-done.x_ref.refs_1_, ...), custom_call_target="tpu_custom_call" | custom-call | flops 10737418240 | bytes 20185088 | tf_op jit(solution)/shard_map/pallas_call | solution.py:102
  113.1 14.0 %shard_map.309.refs_6_ = bf16[16,256,1024]{2,1,0:T(8,128)(2,1)} custom-call(bf16[640,2048]{1,0:T(8,128)(2,1)} %get-tuple-element.142.refs_0_, bf16[640,2048]{1,0:T(8,128)(2,1)} %get-tuple-element.143.refs_1_, bf16[640,2048]{1,0:T(8,128)(2,1)} %get-tuple-element.144.refs_2_, bf16[640,1024]{1,0:T(8,128)(2,1)} %pad_maximum_fusion.5.dy_ref.refs_3_.refs_2_.refs_6_.refs_1_, ...), custom_call_target="tpu_custom_call" | custom-call | flops 8053063680 | bytes 15990784 | tf_op jit(solution)/shard_map/pallas_call | solution.py:497
  127.1 14.4 %shard_map.310.refs_2_ = bf16[16,256,1024]{2,1,0:T(8,128)(2,1)} custom-call(bf16[640,1024]{1,0:T(8,128)(2,1)} %get-tuple-element.136.refs_0_, bf16[640,1024]{1,0:T(8,128)(2,1)} %get-tuple-element.137.refs_1_, bf16[640,1024]{1,0:T(8,128)(2,1)} %get-tuple-element.138.refs_2_, ...), custom_call_target="tpu_custom_call", output_to_operand_aliasing={{}: (6, {})} | custom-call | flops 8053063680 | bytes 15990784 | tf_op jit(solution)/shard_map/pallas_call | solution.py:497
  141.5 20.6 %shard_map.311 = (bf16[640,2048]{1,0:T(8,128)(2,1)}, bf16[640,2048]{1,0:T(8,128)(2,1)}, bf16[640,1024]{1,0:T(8,128)(2,1)}, bf16[640,1024]{1,0:T(8,128)(2,1)}, bf...) custom-call(bf16[640,1024]{1,0:T(8,128)(2,1)} %collective-permute-done.7.x_ref.refs_1_, ...), custom_call_target="tpu_custom_call" | custom-call | flops 10737418240 | bytes 20185088 | tf_op jit(solution)/shard_map/pallas_call | solution.py:102
  162.2 9.6 %shard_map.312.refs_2_ = bf16[16,256,1024]{2,1,0:T(8,128)(2,1)} custom-call(bf16[640,2048]{1,0:T(8,128)(2,1)} %get-tuple-element.148.refs_0_, bf16[640,1024]{1,0:T(8,128)(2,1)} %collective-permute-done.8.dy_ref.refs_1_.refs_3_.refs_9_, bf16[16,256,1024]{2,1,0:T(8,128)(2,1)} %shard_map.310.refs_2_), custom_call_target="tpu_custom_call", output_to_operand_aliasing={{}: (2, {})} | custom-call | flops 2684354560 | bytes 12320768 | tf_op jit(solution)/shard_map/pallas_call | solution.py:497
  171.8 8.1 %shard_map.313 = bf16[16,256,1024]{2,1,0:T(8,128)(2,1)} custom-call(bf16[640,1024]{1,0:T(8,128)(2,1)} %get-tuple-element.146.refs_0_, bf16[640,2048]{1,0:T(8,128)(2,1)} %get-tuple-element.147.refs_1_, bf16[16,256,1024]{2,1,0:T(8,128)(2,1)} %shard_map.312.refs_2_), custom_call_target="tpu_custom_call", output_to_operand_aliasing={{}: (2, {})} | custom-call | flops 2684354560 | bytes 12320768 | tf_op jit(solution)/shard_map/pallas_call | solution.py:497
  182.8 2.0 broadcast_select_fusion.3
  184.8 1.9 pad_maximum_fusion.1.refs_8_.refs_9_.refs_10_
  186.6 65.2 %shard_map.314 = (bf16[640,1024]{1,0:T(8,128)(2,1)}, bf16[640,1024]{1,0:T(8,128)(2,1)}, bf16[640,1024]{1,0:T(8,128)(2,1)}, bf16[640,1024]{1,0:T(8,128)(2,1)}, bf...) custom-call(s32[1]{0:T(128)} %bitcast.2.me_ref, ...), custom_call_target="tpu_custom_call" | custom-call | flops 44291850240 | bytes 27787264 | tf_op jit(solution)/shard_map/pallas_call | solution.py:388
  252.3 1.7 collective-permute-start.10
  254.0 64.4 %shard_map.315 = (bf16[640,1024]{1,0:T(8,128)(2,1)}, bf16[640,1024]{1,0:T(8,128)(2,1)}, bf16[640,1024]{1,0:T(8,128)(2,1)}, bf16[640,1024]{1,0:T(8,128)(2,1)}, bf...) custom-call(s32[1]{0:T(128)} %bitcast.2.me_ref, ...), custom_call_target="tpu_custom_call" | custom-call | flops 44291850240 | bytes 27787264 | tf_op jit(solution)/shard_map/pallas_call | solution.py:388
  318.4 19.4 %shard_map.316 = (bf16[16,128,512]{2,1,0:T(8,128)(2,1)}, bf16[16,128,512]{2,1,0:T(8,128)(2,1)}) custom-call(s32[2]{0:T(128)} %pad_add_fusion.q_ref, bf16[1280,1024]{1,0:T(8,128)(2,1)} %get-tuple-element.163.refs_0_, bf16[1280,1024]{1,0:T(8,128)(2,1)} %get-tuple-element.164.refs_1_, bf16[3,1280,512]{2,1,0:T(8,128)(2,1)} %get-tuple-element.165.refs_2_, ...), custom_call_target="tpu_custom_call" | custom-call | flops 10737418240 | bytes 25165824 | tf_op jit(solution)/shard_map/pallas_call | solution.py:586
  337.9 2.4 slice.123
  342.2 1.8 convert_reduce_fusion
  348.2 4.3 collective-permute-done.14
  354.3 2.0 add_convert_fusion.1
  356.5 1.7 add_convert_fusion
  358.3 1.6 collective-permute-start.16
  361.7 1.7 collective-permute-start.22
  363.9 6.7 %shard_map.317 = (bf16[2,512,1024]{2,1,0:T(8,128)(2,1)}, bf16[2,128,1024]{2,1,0:T(8,128)(2,1)}, f32[2,512,1024]{2,1,0:T(8,128)}, f32[2,128,1024]{2,1,0:T(8,128)}) custom-call(bf16[640,1024]{1,0:T(8,128)(2,1)} %pad_maximum_fusion.4.x_ref.refs_0_, bf16[640,1024]{1,0:T(8,128)(2,1)} %pad_maximum_fusion.5.dy_ref.refs_3_.refs_2_.refs_6_.refs_1_, ...), custom_call_target="tpu_custom_call" | custom-call | flops 13107200 | bytes 11796480 | tf_op jit(solution)/shard_map/pallas_call | solution.py:682
  370.6 8.8 %collective-permute-done.17 = f32[24,512]{1,0:T(8,128)S(1)} collective-permute-done((f32[24,512]{1,0:T(8,128)S(1)}, f32[24,512]{1,0:T(8,128)S(1)}, u32[]{:S(2)}, u32[]{:S(2)}) %collective-permute-start.17) | collective-permute-done | bytes 49184 | tf_op jit(solution)/shard_map/ppermute | solution.py:711
  379.4 7.3 %collective-permute-done.16 = bf16[4,128,512]{2,1,0:T(8,128)(2,1)S(1)} collective-permute-done((bf16[4,128,512]{2,1,0:T(8,128)(2,1)S(1)}, bf16[4,128,512]{2,1,0:T(8,128)(2,1)S(1)}, u32[]{:S(2)}, u32[]{:S(2)}) %collective-permute-start.16) | collective-permute-done | bytes 524320 | tf_op jit(solution)/shard_map/ppermute | solution.py:711
  387.1 4.8 collective-permute-start.19
  391.9 2.7 collective-permute-start.18
  394.6 12.2 %collective-permute-done.20 = f32[24,512]{1,0:T(8,128)S(1)} collective-permute-done((f32[24,512]{1,0:T(8,128)S(1)}, f32[24,512]{1,0:T(8,128)S(1)}, u32[]{:S(2)}, u32[]{:S(2)}) %collective-permute-start.20) | collective-permute-done | bytes 49184 | tf_op jit(solution)/shard_map/ppermute | solution.py:711
  407.9 11.0 %collective-permute-done.22.refs_5_ = bf16[640,1024]{1,0:T(8,128)(2,1)S(1)} collective-permute-done((bf16[640,1024]{1,0:T(8,128)(2,1)S(1)}, bf16[640,1024]{1,0:T(8,128)(2,1)S(1)}, u32[]{:S(2)}, u32[]{:S(2)}) %collective-permute-start.22) | collective-permute-done | bytes 1310752 | tf_op jit(solution)/shard_map/ppermute | solution.py:695
  421.4 2.5 collective-permute-start.23
  424.9 16.4 %collective-permute-done.25 = f32[24,512]{1,0:T(8,128)S(1)} collective-permute-done((f32[24,512]{1,0:T(8,128)S(1)}, f32[24,512]{1,0:T(8,128)S(1)}, u32[]{:S(2)}, u32[]{:S(2)}) %collective-permute-start.25) | collective-permute-done | bytes 49184 | tf_op jit(solution)/shard_map/ppermute | solution.py:711
  442.3 1.9 collective-permute-start.26
  444.2 1.8 collective-permute-done.29
  447.7 3.3 collective-permute-done.30
  451.1 10.2 %collective-permute-done.27 = bf16[1,128,512]{2,1,0:T(8,128)(2,1)S(1)} collective-permute-done((bf16[1,128,512]{2,1,0:T(8,128)(2,1)S(1)}, bf16[1,128,512]{2,1,0:T(8,128)(2,1)S(1)}, u32[]{:S(2)}, u32[]{:S(2)}) %collective-permute-start.27) | collective-permute-done | bytes 131104 | tf_op jit(solution)/shard_map/ppermute | solution.py:711
  465.4 4.5 shard_map.318
  474.5 2.0 collective-permute-start.32
  482.1 3.4 copy-done
  485.5 6.1 %shard_map.319 = (f32[2048,1024]{1,0:T(8,128)}, f32[512,4096]{1,0:T(8,128)}) custom-call(bf16[16,256,1024]{2,1,0:T(8,128)(2,1)S(1)} %bitcast.78), custom_call_target="tpu_custom_call" | custom-call | bytes 25165824 | tf_op jit(solution)/shard_map/pallas_call | solution.py:532
  497.1 4.1 shard_map.320
  (270 shorter events, 63.2 us)
Async XLA Ops:
  7.2 175.6 %all-gather.5.cloned.1.call-start = ((), (), s32[]{:S(2)}) async-start(), calls=%async_computation.2 | async-start | bytes 1671168 | tf_op jit(solution)/shard_map/all_gather | solution.py:752
  8.4 15.8 %collective-permute-start.2 = (bf16[128,2048]{1,0:T(8,128)(2,1)S(1)}, bf16[128,2048]{1,0:T(8,128)(2,1)S(1)}, u32[]{:S(2)}, u32[]{:S(2)}) collective-permute-start(bf16[128,2048]{1,0:T(8,128)(2,1)S(1)} %dynamic_slice.80), channel_id=1, source_target_pairs={{0,1},{1,0},{2,3},{3,2},{4,5},{5,4},{6,7},{7,6},{8,9},{9,8},{10,11... | collective-permute-start | bytes 1572872 | tf_op jit(solution)/shard_map/ppermute | solution.py:695
  16.3 26.4 %collective-permute-start.5 = (f32[9,512]{1,0:T(8,128)S(1)}, f32[9,512]{1,0:T(8,128)}, u32[]{:S(2)}, u32[]{:S(2)}) collective-permute-start(f32[9,512]{1,0:T(8,128)S(1)} %concatenate.84), channel_id=1, source_target_pairs={{0,1},{1,0},{2,3},{3,2},{4,5},{5,4},{6,7},{7,6},{8,9},{9,8},{10,11... | collective-permute-start | bytes 55304 | tf_op jit(solution)/shard_map/ppermute | solution.py:695
  17.9 26.2 %collective-permute-start.6 = (bf16[32,1536]{1,0:T(8,128)(2,1)}, bf16[32,1536]{1,0:T(8,128)(2,1)S(1)}, u32[]{:S(2)}, u32[]{:S(2)}) collective-permute-start(bf16[32,1536]{1,0:T(8,128)(2,1)} %pad_maximum_fusion.16), channel_id=1, source_target_pairs={{0,1},{1,0},{2,3},{3,2},{4,5},{5,4},{6,7},{7,6},{8,9},{9,8},{10,11... | collective-permute-start | bytes 294920 | tf_op jit(solution)/shard_map/ppermute | solution.py:695
  24.1 12.3 %collective-permute-start.3 = (bf16[128,2048]{1,0:T(8,128)(2,1)S(1)}, bf16[128,2048]{1,0:T(8,128)(2,1)S(1)}, u32[]{:S(2)}, u32[]{:S(2)}) collective-permute-start(bf16[128,2048]{1,0:T(8,128)(2,1)S(1)} %collective-permute-done.2), channel_id=1, source_target_pairs={{0,4},{2,6},{4,0},{6,2},{8,12},{10,14},{12,8},{14,10},{16,20},{18,... | collective-permute-start | bytes 1572872 | tf_op jit(solution)/shard_map/ppermute | solution.py:711
  27.4 65.7 %collective-permute-start = (bf16[640,1024]{1,0:T(8,128)(2,1)}, bf16[640,1024]{1,0:T(8,128)(2,1)}, u32[]{:S(2)}, u32[]{:S(2)}) collective-permute-start(bf16[640,1024]{1,0:T(8,128)(2,1)} %pad_maximum_fusion.4.x_ref.refs_0_), channel_id=1, source_target_pairs={{0,1},{1,0},{2,3},{3,2},{4,5},{5,4},{6,7},{7,6},{8,9},{9,8},{10,11... | collective-permute-start | bytes 3932168 | tf_op jit(solution)/shard_map/ppermute | solution.py:695
  30.6 10.6 %copy-start.14 = (bf16[512,1024]{1,0:T(8,128)(2,1)}, bf16[512,1024]{1,0:T(8,128)(2,1)S(1)}, u32[]{:S(2)}) copy-start(bf16[512,1024]{1,0:T(8,128)(2,1)S(1)} %get-tuple-element.282) | copy-start | bytes 3145732
  38.3 8.5 %collective-permute-start.4 = (bf16[256,2048]{1,0:T(8,128)(2,1)}, bf16[256,2048]{1,0:T(8,128)(2,1)}, u32[]{:S(2)}, u32[]{:S(2)}) collective-permute-start(bf16[256,2048]{1,0:T(8,128)(2,1)} %pad_maximum_fusion.8), channel_id=1, source_target_pairs={{0,2},{2,0},{4,6},{6,4},{8,10},{10,8},{12,14},{14,12},{16,18},{18,... | collective-permute-start | bytes 3145736 | tf_op jit(solution)/shard_map/ppermute | solution.py:711
  39.7 53.4 %collective-permute-start.1 = (bf16[640,1024]{1,0:T(8,128)(2,1)}, bf16[640,1024]{1,0:T(8,128)(2,1)}, u32[]{:S(2)}, u32[]{:S(2)}) collective-permute-start(bf16[640,1024]{1,0:T(8,128)(2,1)} %pad_maximum_fusion.5.dy_ref.refs_3_.refs_2_.refs_6_.refs_1_), channel_id=1, source_target_pairs={{0,1},{1,0},{2,3},{3,2},{4,5},{5,4},{6,7},{7,6},{8,9},{9,8},{10,11... | collective-permute-start | bytes 3932168 | tf_op jit(solution)/shard_map/ppermute | solution.py:695
  44.7 301.3 %reduce-scatter.2.cloned.1.call-start = ((), (), s32[]{:S(2)}) async-start(), calls=%async_computation.1 | async-start | bytes 8912896 | tf_op jit(solution)/shard_map/reduce_scatter | solution.py:936
  44.8 96.8 %collective-permute-start.7 = (bf16[640,1024]{1,0:T(8,128)(2,1)S(1)}, bf16[640,1024]{1,0:T(8,128)(2,1)}, u32[]{:S(2)}, u32[]{:S(2)}) collective-permute-start(bf16[640,1024]{1,0:T(8,128)(2,1)S(1)} %pad_maximum_fusion.6.x_ref.refs_0_), channel_id=1, source_target_pairs={{0,1},{1,0},{2,3},{3,2},{4,5},{5,4},{6,7},{7,6},{8,9},{9,8},{10,11... | collective-permute-start | bytes 3932168 | tf_op jit(solution)/shard_map/ppermute | solution.py:695
  45.4 96.1 %collective-permute-start.8 = (bf16[640,1024]{1,0:T(8,128)(2,1)S(1)}, bf16[640,1024]{1,0:T(8,128)(2,1)}, u32[]{:S(2)}, u32[]{:S(2)}) collective-permute-start(bf16[640,1024]{1,0:T(8,128)(2,1)S(1)} %pad_maximum_fusion.7.dy_ref.refs_5_.refs_2_.refs_8_.refs_1_), channel_id=1, source_target_pairs={{0,1},{1,0},{2,3},{3,2},{4,5},{5,4},{6,7},{7,6},{8,9},{9,8},{10,11... | collective-permute-start | bytes 3932168 | tf_op jit(solution)/shard_map/ppermute | solution.py:695
  179.9 302.2 %all-gather.7.cloned.1.call-start = ((), (), s32[]{:S(2)}) async-start(), calls=%async_computation.3 | async-start | bytes 8912896 | tf_op jit(solution)/shard_map/all_gather | solution.py:964
  251.9 66.5 %collective-permute-start.9 = (bf16[640,1024]{1,0:T(8,128)(2,1)}, bf16[640,1024]{1,0:T(8,128)(2,1)S(1)}, u32[]{:S(2)}, u32[]{:S(2)}) collective-permute-start(bf16[640,1024]{1,0:T(8,128)(2,1)} %get-tuple-element.160), channel_id=1, source_target_pairs={{0,1},{1,0},{2,3},{3,2},{4,5},{5,4},{6,7},{7,6},{8,9},{9,8},{10,11... | collective-permute-start | bytes 3932168 | tf_op jit(solution)/shard_map/ppermute | solution.py:695
  252.3 66.1 %collective-permute-start.10 = (bf16[640,1024]{1,0:T(8,128)(2,1)}, bf16[640,1024]{1,0:T(8,128)(2,1)}, u32[]{:S(2)}, u32[]{:S(2)}) collective-permute-start(bf16[640,1024]{1,0:T(8,128)(2,1)} %get-tuple-element.162), channel_id=1, source_target_pairs={{0,1},{1,0},{2,3},{3,2},{4,5},{5,4},{6,7},{7,6},{8,9},{9,8},{10,11... | collective-permute-start | bytes 3932168 | tf_op jit(solution)/shard_map/ppermute | solution.py:695
  341.5 4.4 collective-permute-start.12
  341.5 4.5 collective-permute-start.11
  344.5 1.3 collective-permute-start.13
  346.9 5.6 %collective-permute-start.14 = (bf16[64,1024]{1,0:T(8,128)(2,1)S(1)}, bf16[64,1024]{1,0:T(8,128)(2,1)S(1)}, u32[]{:S(2)}, u32[]{:S(2)}) collective-permute-start(bf16[64,1024]{1,0:T(8,128)(2,1)S(1)} %dynamic-slice_bitcast_fusion), channel_id=1, source_target_pairs={{0,1},{1,0},{2,3},{3,2},{4,5},{5,4},{6,7},{7,6},{8,9},{9,8},{10,11... | collective-permute-start | bytes 393224 | tf_op jit(solution)/shard_map/ppermute | solution.py:695
  358.3 28.4 %collective-permute-start.16 = (bf16[4,128,512]{2,1,0:T(8,128)(2,1)S(1)}, bf16[4,128,512]{2,1,0:T(8,128)(2,1)S(1)}, u32[]{:S(2)}, u32[]{:S(2)}) collective-permute-start(bf16[4,128,512]{2,1,0:T(8,128)(2,1)S(1)} %slice.151), channel_id=1, source_target_pairs={{0,8},{2,10},{4,12},{6,14},{8,0},{10,2},{12,4},{14,6},{16,24},{18,... | collective-permute-start | bytes 1572872 | tf_op jit(solution)/shard_map/ppermute | solution.py:711
  359.9 26.8 %collective-permute-start.15 = (bf16[4,128,512]{2,1,0:T(8,128)(2,1)S(1)}, bf16[4,128,512]{2,1,0:T(8,128)(2,1)S(1)}, u32[]{:S(2)}, u32[]{:S(2)}) collective-permute-start(bf16[4,128,512]{2,1,0:T(8,128)(2,1)S(1)} %slice.150), channel_id=1, source_target_pairs={{0,4},{2,6},{4,0},{6,2},{8,12},{10,14},{12,8},{14,10},{16,20},{18,... | collective-permute-start | bytes 1572872 | tf_op jit(solution)/shard_map/ppermute | solution.py:711
  361.3 45.5 %collective-permute-start.21 = (bf16[640,1024]{1,0:T(8,128)(2,1)S(1)}, bf16[640,1024]{1,0:T(8,128)(2,1)S(1)}, u32[]{:S(2)}, u32[]{:S(2)}) collective-permute-start(bf16[640,1024]{1,0:T(8,128)(2,1)S(1)} %copy-done.53), channel_id=1, source_target_pairs={{0,1},{1,0},{2,3},{3,2},{4,5},{5,4},{6,7},{7,6},{8,9},{9,8},{10,11... | collective-permute-start | bytes 3932168 | tf_op jit(solution)/shard_map/ppermute | solution.py:695
  361.7 57.1 %collective-permute-start.22 = (bf16[640,1024]{1,0:T(8,128)(2,1)S(1)}, bf16[640,1024]{1,0:T(8,128)(2,1)S(1)}, u32[]{:S(2)}, u32[]{:S(2)}) collective-permute-start(bf16[640,1024]{1,0:T(8,128)(2,1)S(1)} %copy-done.52), channel_id=1, source_target_pairs={{0,1},{1,0},{2,3},{3,2},{4,5},{5,4},{6,7},{7,6},{8,9},{9,8},{10,11... | collective-permute-start | bytes 3932168 | tf_op jit(solution)/shard_map/ppermute | solution.py:695
  363.4 16.1 %collective-permute-start.17 = (f32[24,512]{1,0:T(8,128)S(1)}, f32[24,512]{1,0:T(8,128)S(1)}, u32[]{:S(2)}, u32[]{:S(2)}) collective-permute-start(f32[24,512]{1,0:T(8,128)S(1)} %add.277), channel_id=1, source_target_pairs={{0,4},{2,6},{4,0},{6,2},{8,12},{10,14},{12,8},{14,10},{16,20},{18,... | collective-permute-start | bytes 147464 | tf_op jit(solution)/shard_map/ppermute | solution.py:711
  387.1 19.7 %collective-permute-start.19 = (bf16[2,128,512]{2,1,0:T(8,128)(2,1)S(1)}, bf16[2,128,512]{2,1,0:T(8,128)(2,1)S(1)}, u32[]{:S(2)}, u32[]{:S(2)}) collective-permute-start(bf16[2,128,512]{2,1,0:T(8,128)(2,1)S(1)} %slice.156), channel_id=1, source_target_pairs={{0,16},{2,18},{4,20},{6,22},{8,24},{10,26},{12,28},{14,30},{16,0},... | collective-permute-start | bytes 786440 | tf_op jit(solution)/shard_map/ppermute | solution.py:711
  391.9 14.9 %collective-permute-start.18 = (bf16[2,128,512]{2,1,0:T(8,128)(2,1)S(1)}, bf16[2,128,512]{2,1,0:T(8,128)(2,1)S(1)}, u32[]{:S(2)}, u32[]{:S(2)}) collective-permute-start(bf16[2,128,512]{2,1,0:T(8,128)(2,1)S(1)} %slice.154), channel_id=1, source_target_pairs={{0,8},{2,10},{4,12},{6,14},{8,0},{10,2},{12,4},{14,6},{16,24},{18,... | collective-permute-start | bytes 786440 | tf_op jit(solution)/shard_map/ppermute | solution.py:711
  394.6 12.2 %collective-permute-start.20 = (f32[24,512]{1,0:T(8,128)S(1)}, f32[24,512]{1,0:T(8,128)S(1)}, u32[]{:S(2)}, u32[]{:S(2)}) collective-permute-start(f32[24,512]{1,0:T(8,128)S(1)} %add.284), channel_id=1, source_target_pairs={{0,8},{2,10},{4,12},{6,14},{8,0},{10,2},{12,4},{14,6},{16,24},{18,... | collective-permute-start | bytes 147464 | tf_op jit(solution)/shard_map/ppermute | solution.py:711
  420.6 40.8 %copy-start.2 = (bf16[640,1024]{1,0:T(8,128)(2,1)S(1)}, bf16[640,1024]{1,0:T(8,128)(2,1)}, u32[]{:S(2)}) copy-start(bf16[640,1024]{1,0:T(8,128)(2,1)} %copy-done.1) | copy-start | bytes 3932164
  420.6 40.8 %copy-start.4 = (bf16[640,1024]{1,0:T(8,128)(2,1)S(1)}, bf16[640,1024]{1,0:T(8,128)(2,1)}, u32[]{:S(2)}) copy-start(bf16[640,1024]{1,0:T(8,128)(2,1)} %copy-done.3) | copy-start | bytes 3932164
  421.4 20.5 %collective-permute-start.23 = (bf16[1,128,512]{2,1,0:T(8,128)(2,1)}, bf16[1,128,512]{2,1,0:T(8,128)(2,1)S(1)}, u32[]{:S(2)}, u32[]{:S(2)}) collective-permute-start(bf16[1,128,512]{2,1,0:T(8,128)(2,1)} %slice.158), channel_id=1, source_target_pairs={{0,16},{2,18},{4,20},{6,22},{8,24},{10,26},{12,28},{14,30},{16,0},... | collective-permute-start | bytes 393224 | tf_op jit(solution)/shard_map/ppermute | solution.py:711
  423.9 18.0 %collective-permute-start.24 = (bf16[1,128,512]{2,1,0:T(8,128)(2,1)}, bf16[1,128,512]{2,1,0:T(8,128)(2,1)S(1)}, u32[]{:S(2)}, u32[]{:S(2)}) collective-permute-start(bf16[1,128,512]{2,1,0:T(8,128)(2,1)} %slice.160), channel_id=1, source_target_pairs={{0,4},{2,6},{4,0},{6,2},{8,12},{10,14},{12,8},{14,10},{16,20},{18,... | collective-permute-start | bytes 393224 | tf_op jit(solution)/shard_map/ppermute | solution.py:711
  424.6 16.7 %collective-permute-start.25 = (f32[24,512]{1,0:T(8,128)S(1)}, f32[24,512]{1,0:T(8,128)S(1)}, u32[]{:S(2)}, u32[]{:S(2)}) collective-permute-start(f32[24,512]{1,0:T(8,128)S(1)} %add.287), channel_id=1, source_target_pairs={{0,16},{2,18},{4,20},{6,22},{8,24},{10,26},{12,28},{14,30},{16,0},... | collective-permute-start | bytes 147464 | tf_op jit(solution)/shard_map/ppermute | solution.py:711
  424.9 36.6 %copy-start.5 = (bf16[640,1024]{1,0:T(8,128)(2,1)S(1)}, bf16[640,1024]{1,0:T(8,128)(2,1)}, u32[]{:S(2)}) copy-start(bf16[640,1024]{1,0:T(8,128)(2,1)} %get-tuple-element.212.refs_2_) | copy-start | bytes 3932164
  442.0 4.0 collective-permute-start.29
  442.2 19.1 %copy-start.27 = (bf16[64,512]{1,0:T(8,128)(2,1)}, bf16[64,512]{1,0:T(8,128)(2,1)S(1)}, u32[]{:S(2)}) copy-start(bf16[64,512]{1,0:T(8,128)(2,1)S(1)} %slice_bitcast_fusion.9) | copy-start | bytes 196612
  442.3 4.7 collective-permute-start.26
  446.0 15.4 %copy-start.34 = (bf16[32,512]{1,0:T(8,128)(2,1)}, bf16[32,512]{1,0:T(8,128)(2,1)S(1)}, u32[]{:S(2)}) copy-start(bf16[32,512]{1,0:T(8,128)(2,1)S(1)} %get-tuple-element.298) | copy-start | bytes 98308
  446.0 15.4 %copy-start.35 = (bf16[32,512]{1,0:T(8,128)(2,1)}, bf16[32,512]{1,0:T(8,128)(2,1)S(1)}, u32[]{:S(2)}) copy-start(bf16[32,512]{1,0:T(8,128)(2,1)S(1)} %get-tuple-element.299) | copy-start | bytes 98308
  446.0 5.0 collective-permute-start.30
  447.7 25.1 %copy-start.24 = (bf16[1,128,512]{2,1,0:T(8,128)(2,1)}, bf16[1,128,512]{2,1,0:T(8,128)(2,1)S(1)}, u32[]{:S(2)}) copy-start(bf16[1,128,512]{2,1,0:T(8,128)(2,1)S(1)} %maximum_bitcast_fusion) | copy-start | bytes 393220
  447.7 13.6 %collective-permute-start.27 = (bf16[1,128,512]{2,1,0:T(8,128)(2,1)S(1)}, bf16[1,128,512]{2,1,0:T(8,128)(2,1)S(1)}, u32[]{:S(2)}, u32[]{:S(2)}) collective-permute-start(bf16[1,128,512]{2,1,0:T(8,128)(2,1)S(1)} %maximum_bitcast_fusion), channel_id=1, source_target_pairs={{0,16},{2,18},{4,20},{6,22},{8,24},{10,26},{12,28},{14,30},{16,0},... | collective-permute-start | bytes 393224 | tf_op jit(solution)/shard_map/ppermute | solution.py:711
  451.1 18.8 %collective-permute-start.31 = (bf16[2,128,512]{2,1,0:T(8,128)(2,1)S(1)}, bf16[2,128,512]{2,1,0:T(8,128)(2,1)S(1)}, u32[]{:S(2)}, u32[]{:S(2)}) collective-permute-start(bf16[2,128,512]{2,1,0:T(8,128)(2,1)S(1)} %pad_maximum_fusion.15), channel_id=1, source_target_pairs={{0,16},{2,18},{4,20},{6,22},{8,24},{10,26},{12,28},{14,30},{16,0},... | collective-permute-start | bytes 786440 | tf_op jit(solution)/shard_map/ppermute | solution.py:711
  461.4 9.4 %collective-permute-start.28 = (bf16[2,128,512]{2,1,0:T(8,128)(2,1)S(1)}, bf16[2,128,512]{2,1,0:T(8,128)(2,1)S(1)}, u32[]{:S(2)}, u32[]{:S(2)}) collective-permute-start(bf16[2,128,512]{2,1,0:T(8,128)(2,1)S(1)} %pad_maximum_fusion.14), channel_id=1, source_target_pairs={{0,8},{2,10},{4,12},{6,14},{8,0},{10,2},{12,4},{14,6},{16,24},{18,... | collective-permute-start | bytes 786440 | tf_op jit(solution)/shard_map/ppermute | solution.py:711
  471.6 20.0 %collective-permute-start.34 = (bf16[4,128,512]{2,1,0:T(8,128)(2,1)}, bf16[4,128,512]{2,1,0:T(8,128)(2,1)S(1)}, u32[]{:S(2)}, u32[]{:S(2)}) collective-permute-start(bf16[4,128,512]{2,1,0:T(8,128)(2,1)} %pad_maximum_fusion.13), channel_id=1, source_target_pairs={{0,8},{2,10},{4,12},{6,14},{8,0},{10,2},{12,4},{14,6},{16,24},{18,... | collective-permute-start | bytes 1572872 | tf_op jit(solution)/shard_map/ppermute | solution.py:711
  473.6 18.0 %collective-permute-start.33 = (bf16[4,128,512]{2,1,0:T(8,128)(2,1)}, bf16[4,128,512]{2,1,0:T(8,128)(2,1)}, u32[]{:S(2)}, u32[]{:S(2)}) collective-permute-start(bf16[4,128,512]{2,1,0:T(8,128)(2,1)} %pad_maximum_fusion.12), channel_id=1, source_target_pairs={{0,4},{2,6},{4,0},{6,2},{8,12},{10,14},{12,8},{14,10},{16,20},{18,... | collective-permute-start | bytes 1572872 | tf_op jit(solution)/shard_map/ppermute | solution.py:711
  474.5 4.3 collective-permute-start.32
  491.8 4.7 collective-permute-start.36
  493.7 2.9 collective-permute-start.35
  (46 other events, 165.8 us)
Sparse Core Ops, SparseCore 0:
  44.8 39.9 all-gather.4
  180.0 104.9 reduce-scatter.1
  354.4 90.4 all-gather.6

commit v4 on v3

--- a/solution.py
+++ b/solution.py
@@ -49,8 +49,10 @@
     return t
 
 
-def mlp_kernel(rt, x_ref, dy_ref, wu_ref, bu_ref, wd_ref, gb_ref, act_ref, dpre_ref, h_ref, yp_ref, g2_ref, ln_ref, bu_out, yacc, dacc):
+def mlp_kernel(rt, x_ref, dy_ref, wu_ref, bu_ref, wd_ref, gb_ref, act_ref, dpre_ref, h_ref, bu_out, *back):
     f = pl.program_id(0)
+    if back:
+        yp_ref, g2_ref, ln_ref, yacc, dacc = back
     last = pl.num_programs(0) - 1
     rows = x_ref.shape[0]
 
@@ -61,8 +63,9 @@
             r = tile(i, 128)
             xh, _ = normed(x_ref[r, :])
             h_ref[r, :] = (xh * gb_ref[0:1, :] + gb_ref[1:2, :]).astype(BF)
-            yacc[r, :] = jnp.zeros((128, yacc.shape[1]), F32)
-            dacc[r, :] = jnp.zeros((128, dacc.shape[1]), F32)
+            if back:
+                yacc[r, :] = jnp.zeros((128, yacc.shape[1]), F32)
+                dacc[r, :] = jnp.zeros((128, dacc.shape[1]), F32)
 
     def step(i, bsum):
         r = tile(i, rt)
@@ -73,11 +76,14 @@
         dpre = (da * (cdf + pre * jnp.exp(-0.5 * pre * pre) * 0.3989422804014327)).astype(BF)
         act_ref[r, :] = act
         dpre_ref[r, :] = dpre
-        yacc[r, :] += dnn(act, wd_ref[...])
-        dacc[r, :] += dnt(dpre, wu_ref[...])
+        if back:
+            yacc[r, :] += dnn(act, wd_ref[...])
+            dacc[r, :] += dnt(dpre, wu_ref[...])
         return bsum + jnp.sum(dpre.astype(F32), axis=0, keepdims=True)
 
     bu_out[...] = lax.fori_loop(0, rows // rt, step, jnp.zeros(bu_out.shape, F32))
+    if not back:
+        return
 
     @pl.when(f == last)
     def _():
@@ -94,7 +100,7 @@
             ln_ref[1:2, :] += jnp.sum(dh, axis=0, keepdims=True)
 
 
-def mlp_rows(x, dy, wu, bu, wd, gb):
+def mlp_rows(x, dy, wu, bu, wd, gb, back):
     rows, width = x.shape
     hidden = wu.shape[1]
     fb = min(512, hidden)
@@ -114,25 +120,16 @@
             pl.BlockSpec((rows, fb), lambda f: (0, f)),
             pl.BlockSpec((rows, fb), lambda f: (0, f)),
             full((rows, width)),
-            full((rows, width)),
-            full((rows, width)),
-            full((2, width)),
             pl.BlockSpec((1, fb), lambda f: (0, f)),
-        ],
-        out_shape=[
-            SD((rows, hidden), BF),
-            SD((rows, hidden), BF),
-            SD((rows, width), BF),
-            SD((rows, width), BF),
-            SD((rows, width), BF),
-            SD((2, width), F32),
-            SD((1, hidden), F32),
-        ],
-        scratch_shapes=[pltpu.VMEM((rows, width), F32)] * 2,
+        ]
+        + [full((rows, width)), full((rows, width)), full((2, width))] * back,
+        out_shape=[SD((rows, hidden), BF), SD((rows, hidden), BF), SD((rows, width), BF), SD((1, hidden), F32)]
+        + [SD((rows, width), BF), SD((rows, width), BF), SD((2, width), F32)] * back,
+        scratch_shapes=[pltpu.VMEM((rows, width), F32)] * (2 * back),
         compiler_params=pltpu.CompilerParams(vmem_limit_bytes=60 * MIB),
         cost_estimate=pl.CostEstimate(
-            flops=8 * rows * width * hidden,
-            bytes_accessed=4 * (width * hidden + rows * hidden) + 10 * rows * width,
+            flops=4 * (1 + back) * rows * width * hidden,
+            bytes_accessed=4 * (width * hidden + rows * hidden) + (6 + 4 * back) * rows * width,
             transcendentals=2 * rows * hidden,
         ),
     )(x, dy, wu, bu, wd, gb)
@@ -150,14 +147,15 @@
     per = 1 if stacked else S
     xs = take(per)
     dys = take(per)
-    yps = take(per * adding)
-    g2s = take(per * adding)
+    far = 1 if stacked else S - 1
+    yps = take(far * adding)
+    g2s = take(far * adding)
     wq, wk, wv = take(3)
     bq, bk, bv = take(3)
     wo, gb = take(2)
     cr, s1r, s2r = take(3)
-    ys = take(per)
-    gs = take(per)
+    ys = take(far)
+    gs = take(far)
     dl, ctx, h1, ln, db = take(5)
     yacc, dacc, q_s, k_s, v_s, dc_s, kT, vT, dk_s, dv_s = take(10)
     g = pl.program_id(0)
@@ -169,16 +167,16 @@
     CR = N - PD
     W = HG * HD
 
-    def every_slot(fn):
+    def every_slot(fn, start=0):
         if stacked:
 
-            @pl.loop(0, S)
+            @pl.loop(start, S)
             def _(j):
-                fn(j, lambda refs: refs[0].at[j])
+                fn(j, lambda refs: refs[0].at[j], lambda refs: refs[0].at[j - 1])
 
         else:
-            for j in range(S):
-                fn(j, lambda refs: refs[j])
+            for j in range(start, S):
+                fn(j, lambda refs: refs[j], lambda refs: refs[j - 1])
 
     def slot_rows(start, n):
         if start < PR:
@@ -193,7 +191,7 @@
 
     @pl.when(g == 0)
     def _():
-        def load(j, of):
+        def load(j, of, away):
             x = of(xs)
 
             @pl.loop(0, N // 128)
@@ -214,7 +212,7 @@
             out.append(z * jnp.asarray(scale, BF) if scale != 1.0 else z)
         return jnp.concatenate(out, axis=1) if len(out) > 1 else out[0]
 
-    def proj(j, of):
+    def proj(j, of, away):
         s = lax.rem(me + j, S)
         rp = pl.ds(pl.multiple_of(s * PD, 128), PD)
         rc = pl.ds(pl.multiple_of(PR + s * CR, 128), CR)
@@ -231,13 +229,16 @@
         y = dnt(of(dys)[...], wo[...]).astype(BF)
         dc_s[rp, :] = y[:PD]
         dc_s[rc, :] = y[PD:]
-        if adding:
-            nb = of(yps).shape[0]
-            r = pl.ds(pl.multiple_of(g * nb, 16), nb)
-            of(ys)[r, :] = of(yps)[...]
-            of(gs)[r, :] = of(g2s)[...]
+
+    def bring(j, of, away):
+        nb = away(yps).shape[0]
+        r = pl.ds(pl.multiple_of(g * nb, 16), nb)
+        away(ys)[r, :] = away(yps)[...]
+        away(gs)[r, :] = away(g2s)[...]
 
     every_slot(proj)
+    if adding:
+        every_slot(bring, 1)
     lane = lax.broadcasted_iota(jnp.int32, (1, 128), 1)
     row_i = lax.broadcasted_iota(jnp.int32, (QB, QB), 0)
     col_i = lax.broadcasted_iota(jnp.int32, (QB, QB), 1)
@@ -318,33 +319,34 @@
     for c in range(3):
         db[c : c + 1, :] = jnp.sum(dl[c].astype(F32), axis=0, keepdims=True)
 
-    @pl.loop(0, S)
+    @pl.loop(1, S)
     def _(j):
         r = pl.ds(pl.multiple_of(j * N, 128), N)
+        w = pl.ds(pl.multiple_of((j - 1) * N, 128), N)
         y = dnn(ctx[r, :], wo[...])
         d = dnt(dl[0, r, :], wq[...]) + dnt(dl[1, r, :], wk[...]) + dnt(dl[2, r, :], wv[...])
 
         @pl.when(g == 0)
         def _():
-            yacc[r, :] = y
-            dacc[r, :] = d
+            yacc[w, :] = y
+            dacc[w, :] = d
 
         @pl.when(g > 0)
         def _():
-            yacc[r, :] += y
-            dacc[r, :] += d
+            yacc[w, :] += y
+            dacc[w, :] += d
 
     @pl.when(g == last)
     def _():
         ln[...] = jnp.zeros_like(ln)
 
-        def store(j, of):
-            x, yo, go = of(xs), of(ys), of(gs)
+        def store(j, of, away):
+            x, yo, go = of(xs), away(ys), away(gs)
 
             @pl.loop(0, N // 128)
             def _(i):
                 r = tile(i, 128)
-                w = pl.ds(pl.multiple_of(j * N + i * 128, 128), 128)
+                w = pl.ds(pl.multiple_of((j - 1) * N + i * 128, 128), 128)
                 xh, _ = normed(x[r, :])
                 d = dacc[w, :]
                 y = yacc[w, :]
@@ -357,7 +359,7 @@
                 ln[0:1, :] += jnp.sum(d * xh, axis=0, keepdims=True)
                 ln[1:2, :] += jnp.sum(d, axis=0, keepdims=True)
 
-        every_slot(store)
+        every_slot(store, 1)
 
 
 def attn_group(S, PD, CL, me, xs, dys, yps, g2s, wqkv, bqkv, wo, gb, tabs):
@@ -370,19 +372,18 @@
     G = CW // W
     full = lambda s: pl.BlockSpec(s, lambda g, m: (0,) * len(s), pipeline_mode=pl.Buffered(1))
     keep = lambda s: pl.BlockSpec(s, lambda g, m: (0,) * len(s))
-    tok, tok_out, per = full((N, D)), keep((N, D)), S
+    tok, tok_out, per, far = full((N, D)), keep((N, D)), S, S - 1
     adding = int(T * D <= 1536 * 1024)
     others = (yps, g2s)
     if not adding:
         yps, g2s = [], []
     out_tok = SD((N, D), BF)
+    part = pl.BlockSpec((N // G, D), lambda g, m: (g, 0))
     if S > 2:
         xs, dys, yps, g2s = [[jnp.stack(v, axis=0)] if v else v for v in (xs, dys, yps, g2s)]
-        tok, tok_out, per = full((S, N, D)), keep((S, N, D)), 1
-        out_tok = SD((S, N, D), BF)
-        part = pl.BlockSpec((S, N // G, D), lambda g, m: (0, g, 0))
-    else:
-        part = pl.BlockSpec((N // G, D), lambda g, m: (g, 0))
+        tok, tok_out, per, far = full((S, N, D)), keep((S - 1, N, D)), 1, 1
+        out_tok = SD((S - 1, N, D), BF)
+        part = pl.BlockSpec((S - 1, N // G, D), lambda g, m: (0, g, 0))
     wspec = lambda c: pl.BlockSpec((D, W), lambda g, m: (0, c * G + g))
     bspec = lambda c: pl.BlockSpec((1, W), lambda g, m: (0, c * G + g))
     outs = pl.pallas_call(
@@ -391,11 +392,11 @@
             num_scalar_prefetch=1,
             grid=(G,),
             in_specs=[tok] * (2 * per)
-            + [part] * (2 * adding * per)
+            + [part] * (2 * adding * far)
             + [wspec(0), wspec(1), wspec(2), bspec(0), bspec(1), bspec(2)]
             + [pl.BlockSpec((W, D), lambda g, m: (g, 0)), full((2, D))]
             + [full((T, 128))] * 3,
-            out_specs=[tok_out] * (2 * per)
+            out_specs=[tok_out] * (2 * far)
             + [
                 pl.BlockSpec((3, T, W), lambda g, m: (0, 0, g)),
                 pl.BlockSpec((T, W), lambda g, m: (0, g)),
@@ -403,12 +404,12 @@
                 keep((2, D)),
                 pl.BlockSpec((3, W), lambda g, m: (0, g)),
             ],
-            scratch_shapes=[pltpu.VMEM((T, D), F32)] * 2
+            scratch_shapes=[pltpu.VMEM((T - N, D), F32)] * 2
             + [pltpu.VMEM((T, W), BF)] * 4
             + [pltpu.VMEM((128, T), BF)] * 2
             + [pltpu.VMEM((T, 128), F32)] * 2,
         ),
-        out_shape=[out_tok] * (2 * per)
+        out_shape=[out_tok] * (2 * far)
         + [SD((3, T, CW), BF), SD((T, CW), BF), SD((T, D), BF), SD((2, D), F32), SD((3, CW), F32)],
         compiler_params=pltpu.CompilerParams(vmem_limit_bytes=62 * MIB),
         cost_estimate=pl.CostEstimate(
@@ -417,12 +418,12 @@
             transcendentals=T * T * CW // HD,
         ),
     )(me, *xs, *dys, *yps, *g2s, wqkv, wqkv, wqkv, bqkv, bqkv, bqkv, wo, gb, *tabs)
-    ys, gs = outs[:per], outs[per : 2 * per]
+    ys, gs = outs[:far], outs[far : 2 * far]
     if S > 2:
-        ys, gs = [[v[0][j] for j in range(S)] for v in (ys, gs)]
+        ys, gs = [[v[0][j] for j in range(S - 1)] for v in (ys, gs)]
     if not adding:
         ys, gs = [[a + b for a, b in zip(p, q)] for p, q in zip((ys, gs), others)]
-    return ys, gs, outs[2 * per :]
+    return ys, gs, outs[2 * far :]
 
 
 def tn_kernel(n, wide, *refs):
@@ -637,6 +638,62 @@
     )(q, *[g1] * n, *[g2] * n)
 
 
+def own_kernel(act, dpre, wu, wd, dl, ctx, wqkv, wo, x, gb, y, g, ln, yacc, d1, d2):
+    f = pl.program_id(0)
+    last = pl.num_programs(0) - 1
+    N = x.shape[0]
+    CW = ctx.shape[1]
+
+    @pl.when(f == 0)
+    def _():
+        yacc[...] = dnn(ctx[...], wo[...])
+        d1[...] = sum(dnt(dl[p], wqkv[:, p * CW : (p + 1) * CW]) for p in range(3))
+        d2[...] = jnp.zeros_like(d2)
+
+    yacc[...] += dnn(act[...], wd[...])
+    d2[...] += dnt(dpre[...], wu[...])
+
+    @pl.when(f == last)
+    def _():
+        ln[...] = jnp.zeros_like(ln)
+
+        @pl.loop(0, N // 128)
+        def _(i):
+            r = tile(i, 128)
+            xh, _ = normed(x[r, :])
+            a = d1[r, :]
+            b = d2[r, :]
+            y[r, :] = yacc[r, :].astype(BF)
+            g[r, :] = (a * gb[0:1, :] + b * gb[2:3, :]).astype(BF)
+            ln[0:1, :] += jnp.sum(a * xh, axis=0, keepdims=True)
+            ln[1:2, :] += jnp.sum(a, axis=0, keepdims=True)
+            ln[2:3, :] += jnp.sum(b * xh, axis=0, keepdims=True)
+            ln[3:4, :] += jnp.sum(b, axis=0, keepdims=True)
+
+
+def own_rows(x, act, dpre, wu, wd, dl, ctx, wqkv, wo, gb):
+    N, D = x.shape
+    FL = wu.shape[1]
+    CW = wo.shape[0]
+    fb = min(512, FL)
+    full = lambda s: pl.BlockSpec(s, lambda f: (0,) * len(s), pipeline_mode=pl.Buffered(1))
+    keep = lambda s: pl.BlockSpec(s, lambda f: (0,) * len(s))
+    rows = pl.BlockSpec((N, fb), lambda f: (0, f))
+    return pl.pallas_call(
+        own_kernel,
+        grid=(FL // fb,),
+        in_specs=[rows, rows, pl.BlockSpec((D, fb), lambda f: (0, f)), pl.BlockSpec((fb, D), lambda f: (f, 0))]
+        + [full((3, N, CW)), full((N, CW)), full((D, 3 * CW)), full((CW, D)), full((N, D)), full((4, D))],
+        out_specs=[keep((N, D)), keep((N, D)), keep((4, D))],
+        out_shape=[SD((N, D), BF), SD((N, D), BF), SD((4, D), F32)],
+        scratch_shapes=[pltpu.VMEM((N, D), F32)] * 3,
+        compiler_params=pltpu.CompilerParams(vmem_limit_bytes=60 * MIB),
+        cost_estimate=pl.CostEstimate(
+            flops=4 * N * D * FL + 8 * N * D * CW, bytes_accessed=4 * (N + D) * FL + 8 * (N + D) * CW + 6 * N * D, transcendentals=0
+        ),
+    )(act, dpre, wu, wd, dl, ctx, wqkv, wo, x, gb)
+
+
 def final_kernel(S, first, PT, *refs):
     it = iter(refs)
     take = lambda n: [next(it) for _ in range(n)]
@@ -775,16 +832,13 @@
     return got
 
 
-def halving(pair, v, R, beside):
+def halving(pair, R, beside):
     pair = list(pair)
     for i, bits in enumerate(zip(*orders(R))):
         h = pair[0].shape[0] // 2
-        got = [exchanged(g[h:], R, bit) for g, bit in zip(pair, bits)]
-        v = v + exchanged(v, R, bits[0])
-        got, v = lax.optimization_barrier((got, v))
-        got = beside_it(got, i, beside)
+        got = beside_it([exchanged(g[h:], R, bit) for g, bit in zip(pair, bits)], i, beside)
         pair = [add_low(g[:h], t) for g, t in zip(pair, got)]
-    return [g[0] for g in pair], v
+    return [g[0] for g in pair]
 
 
 def doubling(parts, R, beside):
@@ -880,6 +934,7 @@
     slots = [small] + [shifted(small, S, j) for j in range(1, S)]
     whole = jnp.stack(canonical(slots, me, S, True), axis=0)
     vec = whole[:, :6].transpose(1, 0, 2).reshape(6, D)
+    gb = vec[0:4]
     gb1 = vec[0:2]
     gb2 = vec[2:4]
     vb = vec[4:6]
@@ -902,7 +957,7 @@
     ff = [[None] * S for _ in range(MB)]
 
     def mlp(m, j):
-        ff[m][j] = mlp_rows(X[m][j], DY[m][j], w_up, bup, down_weight, gb2)
+        ff[m][j] = mlp_rows(X[m][j], DY[m][j], w_up, bup, down_weight, gb2, int(j > 0))
 
     for m in range(MB):
         mlp(m, 0)
@@ -911,11 +966,15 @@
 
     def attend(m):
         ys, gs, more = attn_group(
-            S, PD, CL, me_arr, X[m], DY[m], [f[3] for f in ff[m]], [f[4] for f in ff[m]], w_qkv, bqkv, out_weight, gb1, tabs
+            S, PD, CL, me_arr, X[m], DY[m], [f[4] for f in ff[m][1:]], [f[5] for f in ff[m][1:]], w_qkv, bqkv, out_weight, gb1, tabs
         )
         rest.append(list(more))
-        y_got.append([ys[0]] + [shifted(ys[j], S, j) for j in range(1, S)])
-        g_got.append([gs[0]] + [shifted(gs[j], S, j) for j in range(1, S)])
+        y_got.append([shifted(ys[j - 1], S, j) for j in range(1, S)])
+        g_got.append([shifted(gs[j - 1], S, j) for j in range(1, S)])
+
+    def own(m):
+        f = ff[m][0]
+        return own_rows(X[m][0], f[0], f[1], w_up, down_weight, rest[m][0], rest[m][1], w_qkv, out_weight, gb)
 
     chunked = (D // S // R) % 16 == 0 and R & (R - 1) == 0
     rep = lax.axis_index("rep")
@@ -940,51 +999,60 @@
         if m + 1 < MB:
             w_qkv, rest[m][3] = lax.optimization_barrier((w_qkv, rest[m][3]))
     every = early + late
-    ln1 = sum(r[3] for r in rest).reshape(-1, CW)
-    ln2 = sum(of(every, 5)).reshape(-1, CW)
-    db_out = sum(jnp.sum(DY[m][0].astype(F32), axis=0) for m in range(MB)).reshape(-1, CW)
-    mine = (jnp.arange(S) == me).astype(F32)
-    db_qkv = (sum(r[4] for r in rest)[:, None, :] * mine[None, :, None]).reshape(-1, CW)
-    db_up = (sum(of(every, 6)) * mine[:, None]).reshape(-1, CW)
-    vecs = jnp.concatenate([ln1, ln2, db_out, db_qkv, db_up], axis=0)
-
-    finals = lambda m, prior: final_rows(m, MB, PD, X[m][0], DY[m][0], y_got[m], g_got[m], vb, prior)
+    def vectors(mine_):
+        ln1 = sum(r[3] for r in rest) + sum(o[2][0:2] for o in mine_)
+        ln2 = sum(f[6] for f in (ff[m][j] for m, j in every if j)) + sum(o[2][2:4] for o in mine_)
+        db_out = sum(jnp.sum(DY[m][0].astype(F32), axis=0) for m in range(MB)).reshape(-1, CW)
+        mine = (jnp.arange(S) == me).astype(F32)
+        db_qkv = (sum(r[4] for r in rest)[:, None, :] * mine[None, :, None]).reshape(-1, CW)
+        db_up = (sum(of(every, 3)) * mine[:, None]).reshape(-1, CW)
+        return jnp.concatenate([ln1.reshape(-1, CW), ln2.reshape(-1, CW), db_out, db_qkv, db_up], axis=0)
+
+    finals = lambda m, o, prior: final_rows(m, MB, PD, X[m][0], DY[m][0], [o[0]] + y_got[m], [o[1]] + g_got[m], vb, prior)
     hs, dls, ctxs = [[r[k] for r in rest] for k in (2, 0, 1)]
     if chunked:
         q = jnp.stack([place(rep, order) for order in orders(R)]).astype(jnp.int32)
-        hs, y_got[:-1], g_got[:-1] = lax.optimization_barrier((hs, y_got[:-1], g_got[:-1]))
+        part = swap_shards(part, me, S, FL // R)
+        hs, y_got[:-1], g_got[:-1], part = lax.optimization_barrier((hs, y_got[:-1], g_got[:-1], part))
+        gmlp_all = lax.all_gather(part, "rep", axis=0, tiled=False)
         gatt = attn_grads(S, R, q, hs, dls, ctxs, [DY[m][j] for m in range(MB) for j in range(S)])
+        dls_own, _ = lax.optimization_barrier(([r[0] for r in rest], gatt))
+        for m in range(MB):
+            rest[m][0] = dls_own[m]
+        mine = [own(m) for m in range(MB)]
+        beside = {1: mine[:1], 2: (mine[1:], y_got[-1], g_got[-1])}
+        half = halving(gatt, R, beside)
+        mine[:1] = beside[1]
+        mine[1:], y_got[-1], g_got[-1] = beside[2]
         outs = None
         for m in range(MB - 1):
-            outs = finals(m, outs)
-        part = swap_shards(part, me, S, FL // R)
-        beside = {0: part, 1: outs, 2: (y_got[-1], g_got[-1])}
-        half, vecs = halving(gatt, vecs, R, beside)
-        part, outs, (y_got[-1], g_got[-1]) = beside[0], beside[1], beside[2]
-        gmlp_all = lax.all_gather(part, "rep", axis=0, tiled=False)
-        outs = finals(MB - 1, outs)
+            outs = finals(m, mine[m], outs)
+        vecs = sum_all(vectors(mine), S, R)
         k = D // CW * (D // S // R)
-        beside = {2: outs, 1: mlp_finish(S, gmlp_all, FL)}
+        outs = finals(MB - 1, mine[-1], outs)
+        beside = {3: outs, 2: vecs, 1: mlp_finish(S, gmlp_all, FL)}
         g1, g2 = doubling([swap_shards(half[0], me, S, 0), swap_shards(half[1], me, S, k)], R, beside)
-        outs = beside[2]
+        outs = beside[3]
+        vecs = beside[2]
         g_down, g_up = beside[1]
         g_out, g_qkv = attn_finish(S, q, g1, g2)
     else:
         dls, ctxs, hs = [[r[k] for r in rest] for k in (0, 1, 2)]
+        mine = [own(m) for m in range(MB)]
         g_down = reduce_rows(tn_sum(of(every, 0), [DY[m][j] for m, j in every], 256))
         g_up = reduce_columns(tn_sum(of(every, 2), of(every, 1), 256), me, S, 1)
         dycs = [jnp.concatenate(DY[m], axis=0) for m in range(MB)]
         g_out = reduce_rows(tn_sum(ctxs, dycs, 256))
         g_qkv = reduce_columns(tn_sum(hs, dls, 256), me, S, 3)
-        vecs = sum_all(vecs, S, R)
+        vecs = sum_all(vectors(mine), S, R)
         outs = None
         for m in range(MB):
-            outs = finals(m, outs)
+            outs = finals(m, mine[m], outs)
     tot = vecs + sum(shifted(vecs, S, j) for j in range(1, S))
-    own = lambda a, n: lax.dynamic_slice_in_dim(tot, a + me * n, n, 0).reshape(-1)
-    v_ln1g, v_ln1b, v_ln2g, v_ln2b, v_out = [own(k * S, 1) for k in range(5)]
-    v_qkv = own(5 * S, 3)
-    v_up = own(8 * S, FL // CW)
+    held = lambda a, n: lax.dynamic_slice_in_dim(tot, a + me * n, n, 0).reshape(-1)
+    v_ln1g, v_ln1b, v_ln2g, v_ln2b, v_out = [held(k * S, 1) for k in range(5)]
+    v_qkv = held(5 * S, 3)
+    v_up = held(8 * S, FL // CW)
 
     po, co, pg, cg = outs
     return (

time: 514 us -> 503 us (0.979)
  waiting for transfers between devices: 87.1 us -> 56.5 us
  other arithmetic: 29.4 us -> 40.3 us
  starting transfers between devices: 39.6 us -> 48.6 us
    pallas_call x0 -> x2, Pallas kernels: none -> 36.1 us  [own_rows(): pl.pallas_call(own_kernel, grid=(FL // fb,), in_specs=[rows, rows, pl.Blo...]
    ppermute x22, waiting for transfers between devices: 66.1 us -> 33.4 us  [exchanged(): return lax.ppermute(value, 'rep', [(i, i ^ bit) for i in range(R)])]
    pallas_call x4, Pallas kernels: 81.3 us -> 63.2 us  [mlp_rows(): pl.pallas_call(functools.partial(mlp_kernel, rows_tile(rows, 640)), grid=...]
    pallas_call x2, Pallas kernels: 130 us -> 112 us  [attn_group(): pl.pallas_call(functools.partial(attn_kernel, S, PD, CL, QB, HG, adding),...]
    ppermute x22, starting transfers between devices: 20.7 us -> 27.7 us  [exchanged(): return lax.ppermute(value, 'rep', [(i, i ^ bit) for i in range(R)])]
    unnamed x117 -> x128, local copies, waits for them, and re-layouts: 17 us -> 10.4 us
  transfers between devices with their start and end apart: 40 -> 40, of which waited for: 15 -> 15; matrix products, arithmetic and copies ran while one was open for 10% -> 14% of each run, Pallas kernels for 58% -> 59%
where the time goes in v4:
time: 503 us; the launch traced here: 497 us
  Pallas kernels  299 us (59%)
  waiting for transfers between devices  56.5 us (11%)
  starting transfers between devices  48.6 us (10%)
  other arithmetic  40.3 us (8%)
  local copies, waits for them, and re-layouts  37.8 us (8%)
  between operations  15.2 us (3%)
    pallas_call x2, Pallas kernels, attn_group(): pl.pallas_call(functools.partial(attn_kernel, S, PD, CL, QB, HG, adding),...  112 us
    pallas_call x4, Pallas kernels, mlp_rows(): pl.pallas_call(functools.partial(mlp_kernel, rows_tile(rows, 640)), grid=...  63.2 us
    pallas_call x4, Pallas kernels, call(): pl.pallas_call(functools.partial(kernel, n, more), grid=(a[0].shape[1] //...  46.1 us
    pallas_call x2, Pallas kernels, own_rows(): pl.pallas_call(own_kernel, grid=(FL // fb,), in_specs=[rows, rows, pl.Blo...  36.1 us
    ppermute x22, waiting for transfers between devices, exchanged(): return lax.ppermute(value, 'rep', [(i, i ^ bit) for i in range(R)])  33.4 us
    ppermute x22, starting transfers between devices, exchanged(): return lax.ppermute(value, 'rep', [(i, i ^ bit) for i in range(R)])  27.7 us
    ppermute x15, waiting for transfers between devices, shifted(): return lax.ppermute(value, 'shard', [(i, (i + j) % S) for i in range(S)])  23 us
    ppermute x15, starting transfers between devices, shifted(): return lax.ppermute(value, 'shard', [(i, (i + j) % S) for i in range(S)])  20.7 us
  transfers between devices with their start and end apart: 40, of which 15 were waited for; matrix products, arithmetic and copies ran while one was open for 14% of the time, Pallas kernels for 59%

profile of v4, /device:TPU:0, one launch (start us, length us, event | category | flops | bytes accessed | tf_op | source)
XLA Modules:
  0.0 497.4 jit_solution(13321861801816119450)
XLA Ops:
  7.3 1.9 dynamic_slice.80
  9.2 2.9 collective-permute-start.2
  18.6 2.0 collective-permute-start.6
  22.3 2.9 collective-permute-done.2
  25.2 2.1 collective-permute-start.3
  30.9 6.8 %collective-permute-done.3 = bf16[128,2048]{1,0:T(8,128)(2,1)} collective-permute-done((bf16[128,2048]{1,0:T(8,128)(2,1)}, bf16[128,2048]{1,0:T(8,128)(2,1)}, u32[]{:S(2)}, u32[]{:S(2)}) %collective-permute-start.3) | collective-permute-done | bytes 524320 | tf_op jit(solution)/shard_map/ppermute | solution.py:768
  37.8 2.1 broadcast_select_fusion.7
  39.8 2.1 pad_maximum_fusion.8
  49.1 1.8 broadcast_select_fusion.5
  52.1 2.6 pad_maximum_fusion.wu_ref.wu
  54.7 11.6 %shard_map.308 = (bf16[640,2048]{1,0:T(8,128)(2,1)}, bf16[640,2048]{1,0:T(8,128)(2,1)}, bf16[640,1024]{1,0:T(8,128)(2,1)}, f32[1,2048]{1,0:T(1,128)}) custom-call(bf16[640,1024]{1,0:T(8,128)(2,1)} %copy-done.2, bf16[640,1024]{1,0:T(8,128)(2,1)} %copy-done.4, bf16[1024,2048]{1,0:T(8,128)(2,1)} %pad_maximum_fusion.wu_ref.wu, f32[1,2048]{1,0:T(1,128)} %bitcast.90, ...), custom_call_target="tpu_custom_call" | custom-call | flops 5368709120 | bytes 17563648 | tf_op jit(solution)/shard_map/pallas_call | solution.py:108
  66.4 11.4 %shard_map.307 = (bf16[640,2048]{1,0:T(8,128)(2,1)}, bf16[640,2048]{1,0:T(8,128)(2,1)}, bf16[640,1024]{1,0:T(8,128)(2,1)}, f32[1,2048]{1,0:T(1,128)}) custom-call(bf16[640,1024]{1,0:T(8,128)(2,1)} %pad_maximum_fusion.4.x_ref.refs_0_.x, bf16[640,1024]{1,0:T(8,128)(2,1)} %pad_maximum_fusion.5.dy_ref.refs_3_.refs_2_.refs_6_.refs_1_, ...), custom_call_target="tpu_custom_call" | custom-call | flops 5368709120 | bytes 17563648 | tf_op jit(solution)/shard_map/pallas_call | solution.py:108
  77.8 11.6 %collective-permute-done.1.dy_ref.refs_4_.refs_3_.refs_7_ = bf16[640,1024]{1,0:T(8,128)(2,1)} collective-permute-done((bf16[640,1024]{1,0:T(8,128)(2,1)}, bf16[640,1024]{1,0:T(8,128)(2,1)}, u32[]{:S(2)}, u32[]{:S(2)}) %collective-permute-start.1) | collective-permute-done | bytes 1310752 | tf_op jit(solution)/shard_map/ppermute | solution.py:752
  89.4 20.1 %shard_map.306 = (bf16[640,2048]{1,0:T(8,128)(2,1)}, bf16[640,2048]{1,0:T(8,128)(2,1)}, bf16[640,1024]{1,0:T(8,128)(2,1)}, f32[1,2048]{1,0:T(1,128)}, bf16[640,1...) custom-call(bf16[640,1024]{1,0:T(8,128)(2,1)} %collective-permute-done.x_ref.refs_1_, ...), custom_call_target="tpu_custom_call" | custom-call | flops 10737418240 | bytes 20185088 | tf_op jit(solution)/shard_map/pallas_call | solution.py:108
  109.4 14.0 %shard_map.309.refs_6_ = bf16[16,256,1024]{2,1,0:T(8,128)(2,1)} custom-call(bf16[640,2048]{1,0:T(8,128)(2,1)} %get-tuple-element.125.refs_0_.act, bf16[640,2048]{1,0:T(8,128)(2,1)} %get-tuple-element.126.refs_1_, bf16[640,2048]{1,0:T(8,128)(2,1)} %get-tuple-element.127.refs_2_.act, ...), custom_call_target="tpu_custom_call" | custom-call | flops 8053063680 | bytes 15990784 | tf_op jit(solution)/shard_map/pallas_call | solution.py:498
  123.4 14.4 %shard_map.310.refs_2_ = bf16[16,256,1024]{2,1,0:T(8,128)(2,1)} custom-call(bf16[640,1024]{1,0:T(8,128)(2,1)} %get-tuple-element.119.refs_0_, bf16[640,1024]{1,0:T(8,128)(2,1)} %get-tuple-element.120.refs_1_, bf16[640,1024]{1,0:T(8,128)(2,1)} %get-tuple-element.121.refs_2_, ...), custom_call_target="tpu_custom_call", output_to_operand_aliasing={{}: (6, {})} | custom-call | flops 8053063680 | bytes 15990784 | tf_op jit(solution)/shard_map/pallas_call | solution.py:498
  137.8 4.2 collective-permute-done.8.dy_ref.refs_1_.refs_3_.refs_9_
  142.0 20.1 %shard_map.311 = (bf16[640,2048]{1,0:T(8,128)(2,1)}, bf16[640,2048]{1,0:T(8,128)(2,1)}, bf16[640,1024]{1,0:T(8,128)(2,1)}, f32[1,2048]{1,0:T(1,128)}, bf16[640,1...) custom-call(bf16[640,1024]{1,0:T(8,128)(2,1)} %collective-permute-done.7.x_ref.refs_1_, ...), custom_call_target="tpu_custom_call" | custom-call | flops 10737418240 | bytes 20185088 | tf_op jit(solution)/shard_map/pallas_call | solution.py:108
  162.1 9.6 %shard_map.312.refs_2_ = bf16[16,256,1024]{2,1,0:T(8,128)(2,1)} custom-call(bf16[640,2048]{1,0:T(8,128)(2,1)} %get-tuple-element.131.refs_0_, bf16[640,1024]{1,0:T(8,128)(2,1)} %collective-permute-done.8.dy_ref.refs_1_.refs_3_.refs_9_, bf16[16,256,1024]{2,1,0:T(8,128)(2,1)} %shard_map.310.refs_2_), custom_call_target="tpu_custom_call", output_to_operand_aliasing={{}: (2, {})} | custom-call | flops 2684354560 | bytes 12320768 | tf_op jit(solution)/shard_map/pallas_call | solution.py:498
  171.8 8.1 %shard_map.313 = bf16[16,256,1024]{2,1,0:T(8,128)(2,1)} custom-call(bf16[640,1024]{1,0:T(8,128)(2,1)} %get-tuple-element.129.refs_0_, bf16[640,2048]{1,0:T(8,128)(2,1)} %get-tuple-element.130.refs_1_, bf16[16,256,1024]{2,1,0:T(8,128)(2,1)} %shard_map.312.refs_2_), custom_call_target="tpu_custom_call", output_to_operand_aliasing={{}: (2, {})} | custom-call | flops 2684354560 | bytes 12320768 | tf_op jit(solution)/shard_map/pallas_call | solution.py:498
  182.1 2.0 broadcast_select_fusion.3
  184.0 1.9 pad_maximum_fusion.1.refs_6_.refs_7_.refs_8_.wqkv
  186.0 56.7 %shard_map.314 = (bf16[640,1024]{1,0:T(8,128)(2,1)}, bf16[640,1024]{1,0:T(8,128)(2,1)}, bf16[3,1280,512]{2,1,0:T(8,128)(2,1)}, bf16[1280,512]{1,0:T(8,128)(2,1)}...) custom-call(s32[1]{0:T(128)} %bitcast.2.me_ref, ...), custom_call_target="tpu_custom_call" | custom-call | flops 44291850240 | bytes 27787264 | tf_op jit(solution)/shard_map/pallas_call | solution.py:389
  244.8 55.5 %shard_map.315 = (bf16[640,1024]{1,0:T(8,128)(2,1)}, bf16[640,1024]{1,0:T(8,128)(2,1)}, bf16[3,1280,512]{2,1,0:T(8,128)(2,1)}, bf16[1280,512]{1,0:T(8,128)(2,1)}...) custom-call(s32[1]{0:T(128)} %bitcast.2.me_ref, bf16[640,1024]{1,0:T(8,128)(2,1)} %copy-done.2, ...), custom_call_target="tpu_custom_call" | custom-call | flops 44291850240 | bytes 27787264 | tf_op jit(solution)/shard_map/pallas_call | solution.py:389
  303.7 2.6 collective-permute-done.11
  308.8 19.3 %shard_map.316 = (bf16[16,128,512]{2,1,0:T(8,128)(2,1)}, bf16[16,128,512]{2,1,0:T(8,128)(2,1)}) custom-call(s32[2]{0:T(128)} %pad_add_fusion.q_ref, bf16[1280,1024]{1,0:T(8,128)(2,1)} %get-tuple-element.142.refs_0_, bf16[1280,1024]{1,0:T(8,128)(2,1)} %get-tuple-element.143.refs_1_, bf16[3,1280,512]{2,1,0:T(8,128)(2,1)} %get-tuple-element.150.refs_2_.dl, ...), custom_call_target="tpu_custom_call" | custom-call | flops 10737418240 | bytes 25165824 | tf_op jit(solution)/shard_map/pallas_call | solution.py:587
  328.2 2.4 slice.147
  337.7 1.9 add_convert_fusion
  342.1 1.8 add_convert_fusion.1
  345.1 18.0 %shard_map.317 = (bf16[640,1024]{1,0:T(8,128)(2,1)}, bf16[640,1024]{1,0:T(8,128)(2,1)}, f32[4,1024]{1,0:T(4,128)}) custom-call(bf16[640,2048]{1,0:T(8,128)(2,1)} %get-tuple-element.125.refs_0_.act, bf16[640,2048]{1,0:T(8,128)(2,1)} %get-tuple-element.122.refs_3_.dpre, bf16[1024,2048]{1,0:T(8,128)(2,1)} %pad_maximum_fusion.wu_ref.wu, bf16[2048,1024]{1,0:T(8,128)(2,1)} %wd.3, ...), custom_call_target="tpu_custom_call" | custom-call | flops 8053063680 | bytes 24379392 | tf_op jit(solution)/shard_map/pallas_call | solution.py:682
  363.1 10.7 %collective-permute-done.15 = bf16[4,128,512]{2,1,0:T(8,128)(2,1)} collective-permute-done((bf16[4,128,512]{2,1,0:T(8,128)(2,1)}, bf16[4,128,512]{2,1,0:T(8,128)(2,1)}, u32[]{:S(2)}, u32[]{:S(2)}) %collective-permute-start.15) | collective-permute-done | bytes 524320 | tf_op jit(solution)/shard_map/ppermute | solution.py:768
  379.8 2.4 collective-permute-start.16
  382.2 18.2 %shard_map.318 = (bf16[640,1024]{1,0:T(8,128)(2,1)}, bf16[640,1024]{1,0:T(8,128)(2,1)}, f32[4,1024]{1,0:T(4,128)}) custom-call(bf16[640,2048]{1,0:T(8,128)(2,1)} %get-tuple-element.127.refs_2_.act, bf16[640,2048]{1,0:T(8,128)(2,1)} %get-tuple-element.124.refs_5_.dpre, bf16[1024,2048]{1,0:T(8,128)(2,1)} %pad_maximum_fusion.wu_ref.wu, bf16[2048,1024]{1,0:T(8,128)(2,1)} %wd.3, ...), custom_call_target="tpu_custom_call" | custom-call | flops 8053063680 | bytes 24379392 | tf_op jit(solution)/shard_map/pallas_call | solution.py:682
  400.4 2.7 collective-permute-done.17
  405.4 2.5 collective-permute-start.20
  410.9 2.4 collective-permute-done.20
  419.8 7.3 %shard_map.319 = (bf16[2,512,1024]{2,1,0:T(8,128)(2,1)}, bf16[2,128,1024]{2,1,0:T(8,128)(2,1)}, f32[2,512,1024]{2,1,0:T(8,128)}, f32[2,128,1024]{2,1,0:T(8,128)}) custom-call(bf16[640,1024]{1,0:T(8,128)(2,1)} %pad_maximum_fusion.4.x_ref.refs_0_.x, bf16[640,1024]{1,0:T(8,128)(2,1)} %pad_maximum_fusion.5.dy_ref.refs_3_.refs_2_.refs_6_.refs_1_, ...), custom_call_target="tpu_custom_call" | custom-call | flops 13107200 | bytes 11796480 | tf_op jit(solution)/shard_map/pallas_call | solution.py:739
  427.1 4.5 shard_map.320
  431.8 2.4 collective-permute-start.27
  439.2 2.4 collective-permute-done.29
  442.0 3.8 collective-permute-done.30
  445.8 4.5 collective-permute-start.31
  450.3 2.1 collective-permute-done.31
  461.0 3.4 copy-done.1
  464.3 6.1 %shard_map.321 = (f32[2048,1024]{1,0:T(8,128)}, f32[512,4096]{1,0:T(8,128)}) custom-call(bf16[16,256,1024]{2,1,0:T(8,128)(2,1)S(1)} %bitcast.79), custom_call_target="tpu_custom_call" | custom-call | bytes 25165824 | tf_op jit(solution)/shard_map/pallas_call | solution.py:533
  471.6 2.1 pad_maximum_fusion.9
  480.8 1.9 constant_dynamic-update-slice_fusion.1
  485.9 4.1 shard_map.322
  (283 shorter events, 84.3 us)
Async XLA Ops:
  7.2 174.9 %all-gather.5.cloned.1.call-start = ((), (), s32[]{:S(2)}) async-start(), calls=%async_computation.2 | async-start | bytes 1671168 | tf_op jit(solution)/shard_map/all_gather | solution.py:809
  9.2 16.0 %collective-permute-start.2 = (bf16[128,2048]{1,0:T(8,128)(2,1)}, bf16[128,2048]{1,0:T(8,128)(2,1)}, u32[]{:S(2)}, u32[]{:S(2)}) collective-permute-start(bf16[128,2048]{1,0:T(8,128)(2,1)} %dynamic_slice.80), channel_id=1, source_target_pairs={{0,1},{1,0},{2,3},{3,2},{4,5},{5,4},{6,7},{7,6},{8,9},{9,8},{10,11... | collective-permute-start | bytes 1572872 | tf_op jit(solution)/shard_map/ppermute | solution.py:752
  17.0 29.2 %collective-permute-start.5 = (f32[9,512]{1,0:T(8,128)S(1)}, f32[9,512]{1,0:T(8,128)S(1)}, u32[]{:S(2)}, u32[]{:S(2)}) collective-permute-start(f32[9,512]{1,0:T(8,128)S(1)} %concatenate.84), channel_id=1, source_target_pairs={{0,1},{1,0},{2,3},{3,2},{4,5},{5,4},{6,7},{7,6},{8,9},{9,8},{10,11... | collective-permute-start | bytes 55304 | tf_op jit(solution)/shard_map/ppermute | solution.py:752
  18.6 28.3 %collective-permute-start.6 = (bf16[32,1536]{1,0:T(8,128)(2,1)}, bf16[32,1536]{1,0:T(8,128)(2,1)}, u32[]{:S(2)}, u32[]{:S(2)}) collective-permute-start(bf16[32,1536]{1,0:T(8,128)(2,1)} %pad_maximum_fusion.16), channel_id=1, source_target_pairs={{0,1},{1,0},{2,3},{3,2},{4,5},{5,4},{6,7},{7,6},{8,9},{9,8},{10,11... | collective-permute-start | bytes 294920 | tf_op jit(solution)/shard_map/ppermute | solution.py:752
  25.2 12.6 %collective-permute-start.3 = (bf16[128,2048]{1,0:T(8,128)(2,1)}, bf16[128,2048]{1,0:T(8,128)(2,1)}, u32[]{:S(2)}, u32[]{:S(2)}) collective-permute-start(bf16[128,2048]{1,0:T(8,128)(2,1)} %collective-permute-done.2), channel_id=1, source_target_pairs={{0,4},{2,6},{4,0},{6,2},{8,12},{10,14},{12,8},{14,10},{16,20},{18,... | collective-permute-start | bytes 1572872 | tf_op jit(solution)/shard_map/ppermute | solution.py:768
  29.2 48.6 %collective-permute-start = (bf16[640,1024]{1,0:T(8,128)(2,1)}, bf16[640,1024]{1,0:T(8,128)(2,1)}, u32[]{:S(2)}, u32[]{:S(2)}) collective-permute-start(bf16[640,1024]{1,0:T(8,128)(2,1)} %pad_maximum_fusion.4.x_ref.refs_0_.x), channel_id=1, source_target_pairs={{0,1},{1,0},{2,3},{3,2},{4,5},{5,4},{6,7},{7,6},{8,9},{9,8},{10,11... | collective-permute-start | bytes 3932168 | tf_op jit(solution)/shard_map/ppermute | solution.py:752
  30.9 13.9 %copy-start.13 = (bf16[512,1024]{1,0:T(8,128)(2,1)}, bf16[512,1024]{1,0:T(8,128)(2,1)S(1)}, u32[]{:S(2)}) copy-start(bf16[512,1024]{1,0:T(8,128)(2,1)S(1)} %get-tuple-element.253) | copy-start | bytes 3145732
  42.0 7.1 %collective-permute-start.4 = (bf16[256,2048]{1,0:T(8,128)(2,1)}, bf16[256,2048]{1,0:T(8,128)(2,1)}, u32[]{:S(2)}, u32[]{:S(2)}) collective-permute-start(bf16[256,2048]{1,0:T(8,128)(2,1)} %pad_maximum_fusion.8), channel_id=1, source_target_pairs={{0,2},{2,0},{4,6},{6,4},{8,10},{10,8},{12,14},{14,12},{16,18},{18,... | collective-permute-start | bytes 3145736 | tf_op jit(solution)/shard_map/ppermute | solution.py:768
  43.3 46.1 %collective-permute-start.1 = (bf16[640,1024]{1,0:T(8,128)(2,1)}, bf16[640,1024]{1,0:T(8,128)(2,1)}, u32[]{:S(2)}, u32[]{:S(2)}) collective-permute-start(bf16[640,1024]{1,0:T(8,128)(2,1)} %pad_maximum_fusion.5.dy_ref.refs_3_.refs_2_.refs_6_.refs_1_), channel_id=1, source_target_pairs={{0,1},{1,0},{2,3},{3,2},{4,5},{5,4},{6,7},{7,6},{8,9},{9,8},{10,11... | collective-permute-start | bytes 3932168 | tf_op jit(solution)/shard_map/ppermute | solution.py:752
  46.9 253.4 %reduce-scatter.2.cloned.1.call-start = ((), (), s32[]{:S(2)}) async-start(), calls=%async_computation.1 | async-start | bytes 8912896 | tf_op jit(solution)/shard_map/reduce_scatter | solution.py:995
  47.0 90.8 %collective-permute-start.7 = (bf16[640,1024]{1,0:T(8,128)(2,1)S(1)}, bf16[640,1024]{1,0:T(8,128)(2,1)}, u32[]{:S(2)}, u32[]{:S(2)}) collective-permute-start(bf16[640,1024]{1,0:T(8,128)(2,1)S(1)} %pad_maximum_fusion.6.x_ref.refs_0_.x), channel_id=1, source_target_pairs={{0,1},{1,0},{2,3},{3,2},{4,5},{5,4},{6,7},{7,6},{8,9},{9,8},{10,11... | collective-permute-start | bytes 3932168 | tf_op jit(solution)/shard_map/ppermute | solution.py:752
  47.7 94.4 %collective-permute-start.8 = (bf16[640,1024]{1,0:T(8,128)(2,1)S(1)}, bf16[640,1024]{1,0:T(8,128)(2,1)}, u32[]{:S(2)}, u32[]{:S(2)}) collective-permute-start(bf16[640,1024]{1,0:T(8,128)(2,1)S(1)} %pad_maximum_fusion.7.dy_ref.refs_5_.refs_2_.refs_8_.refs_1_), channel_id=1, source_target_pairs={{0,1},{1,0},{2,3},{3,2},{4,5},{5,4},{6,7},{7,6},{8,9},{9,8},{10,11... | collective-permute-start | bytes 3932168 | tf_op jit(solution)/shard_map/ppermute | solution.py:752
  179.9 281.1 %all-gather.7.cloned.1.call-start = ((), (), s32[]{:S(2)}) async-start(), calls=%async_computation.3 | async-start | bytes 8912896 | tf_op jit(solution)/shard_map/all_gather | solution.py:1017
  242.7 65.4 %collective-permute-start.9 = (bf16[640,1024]{1,0:T(8,128)(2,1)}, bf16[640,1024]{1,0:T(8,128)(2,1)S(1)}, u32[]{:S(2)}, u32[]{:S(2)}) collective-permute-start(bf16[640,1024]{1,0:T(8,128)(2,1)} %get-tuple-element.140), channel_id=1, source_target_pairs={{0,1},{1,0},{2,3},{3,2},{4,5},{5,4},{6,7},{7,6},{8,9},{9,8},{10,11... | collective-permute-start | bytes 3932168 | tf_op jit(solution)/shard_map/ppermute | solution.py:752
  244.1 63.9 %collective-permute-start.10 = (bf16[640,1024]{1,0:T(8,128)(2,1)}, bf16[640,1024]{1,0:T(8,128)(2,1)}, u32[]{:S(2)}, u32[]{:S(2)}) collective-permute-start(bf16[640,1024]{1,0:T(8,128)(2,1)} %get-tuple-element.141), channel_id=1, source_target_pairs={{0,1},{1,0},{2,3},{3,2},{4,5},{5,4},{6,7},{7,6},{8,9},{9,8},{10,11... | collective-permute-start | bytes 3932168 | tf_op jit(solution)/shard_map/ppermute | solution.py:752
  301.2 5.0 %collective-permute-start.11 = (bf16[64,1024]{1,0:T(8,128)(2,1)S(1)}, bf16[64,1024]{1,0:T(8,128)(2,1)S(1)}, u32[]{:S(2)}, u32[]{:S(2)}) collective-permute-start(bf16[64,1024]{1,0:T(8,128)(2,1)S(1)} %dynamic-slice_bitcast_fusion), channel_id=1, source_target_pairs={{0,1},{1,0},{2,3},{3,2},{4,5},{5,4},{6,7},{7,6},{8,9},{9,8},{10,11... | collective-permute-start | bytes 393224 | tf_op jit(solution)/shard_map/ppermute | solution.py:752
  330.6 7.1 %collective-permute-start.14 = (bf16[8,128,512]{2,1,0:T(8,128)(2,1)}, bf16[8,128,512]{2,1,0:T(8,128)(2,1)}, u32[]{:S(2)}, u32[]{:S(2)}) collective-permute-start(bf16[8,128,512]{2,1,0:T(8,128)(2,1)} %slice.147), channel_id=1, source_target_pairs={{0,2},{2,0},{4,6},{6,4},{8,10},{10,8},{12,14},{14,12},{16,18},{18,... | collective-permute-start | bytes 3145736 | tf_op jit(solution)/shard_map/ppermute | solution.py:768
  331.7 10.4 %collective-permute-start.12 = (bf16[8,128,512]{2,1,0:T(8,128)(2,1)}, bf16[8,128,512]{2,1,0:T(8,128)(2,1)}, u32[]{:S(2)}, u32[]{:S(2)}) collective-permute-start(bf16[8,128,512]{2,1,0:T(8,128)(2,1)} %slice.143), channel_id=1, source_target_pairs={{0,2},{2,0},{4,6},{6,4},{8,10},{10,8},{12,14},{14,12},{16,18},{18,... | collective-permute-start | bytes 3145736 | tf_op jit(solution)/shard_map/ppermute | solution.py:768
  335.6 64.8 %collective-permute-start.18 = (bf16[640,1024]{1,0:T(8,128)(2,1)}, bf16[640,1024]{1,0:T(8,128)(2,1)S(1)}, u32[]{:S(2)}, u32[]{:S(2)}) collective-permute-start(bf16[640,1024]{1,0:T(8,128)(2,1)} %get-tuple-element.160), channel_id=1, source_target_pairs={{0,1},{1,0},{2,3},{3,2},{4,5},{5,4},{6,7},{7,6},{8,9},{9,8},{10,11... | collective-permute-start | bytes 3932168 | tf_op jit(solution)/shard_map/ppermute | solution.py:752
  337.1 63.4 %collective-permute-start.19 = (bf16[640,1024]{1,0:T(8,128)(2,1)}, bf16[640,1024]{1,0:T(8,128)(2,1)S(1)}, u32[]{:S(2)}, u32[]{:S(2)}) collective-permute-start(bf16[640,1024]{1,0:T(8,128)(2,1)} %get-tuple-element.161), channel_id=1, source_target_pairs={{0,1},{1,0},{2,3},{3,2},{4,5},{5,4},{6,7},{7,6},{8,9},{9,8},{10,11... | collective-permute-start | bytes 3932168 | tf_op jit(solution)/shard_map/ppermute | solution.py:752
  340.5 33.4 %collective-permute-start.15 = (bf16[4,128,512]{2,1,0:T(8,128)(2,1)}, bf16[4,128,512]{2,1,0:T(8,128)(2,1)}, u32[]{:S(2)}, u32[]{:S(2)}) collective-permute-start(bf16[4,128,512]{2,1,0:T(8,128)(2,1)} %slice.175), channel_id=1, source_target_pairs={{0,8},{2,10},{4,12},{6,14},{8,0},{10,2},{12,4},{14,6},{16,24},{18,... | collective-permute-start | bytes 1572872 | tf_op jit(solution)/shard_map/ppermute | solution.py:768
  345.1 28.7 %collective-permute-start.13 = (bf16[4,128,512]{2,1,0:T(8,128)(2,1)}, bf16[4,128,512]{2,1,0:T(8,128)(2,1)}, u32[]{:S(2)}, u32[]{:S(2)}) collective-permute-start(bf16[4,128,512]{2,1,0:T(8,128)(2,1)} %slice.174), channel_id=1, source_target_pairs={{0,4},{2,6},{4,0},{6,2},{8,12},{10,14},{12,8},{14,10},{16,20},{18,... | collective-permute-start | bytes 1572872 | tf_op jit(solution)/shard_map/ppermute | solution.py:768
  378.1 25.0 %collective-permute-start.17 = (bf16[2,128,512]{2,1,0:T(8,128)(2,1)}, bf16[2,128,512]{2,1,0:T(8,128)(2,1)}, u32[]{:S(2)}, u32[]{:S(2)}) collective-permute-start(bf16[2,128,512]{2,1,0:T(8,128)(2,1)} %slice.180), channel_id=1, source_target_pairs={{0,16},{2,18},{4,20},{6,22},{8,24},{10,26},{12,28},{14,30},{16,0},... | collective-permute-start | bytes 786440 | tf_op jit(solution)/shard_map/ppermute | solution.py:768
  379.8 23.3 %collective-permute-start.16 = (bf16[2,128,512]{2,1,0:T(8,128)(2,1)}, bf16[2,128,512]{2,1,0:T(8,128)(2,1)}, u32[]{:S(2)}, u32[]{:S(2)}) collective-permute-start(bf16[2,128,512]{2,1,0:T(8,128)(2,1)} %slice.178), channel_id=1, source_target_pairs={{0,8},{2,10},{4,12},{6,14},{8,0},{10,2},{12,4},{14,6},{16,24},{18,... | collective-permute-start | bytes 786440 | tf_op jit(solution)/shard_map/ppermute | solution.py:768
  400.4 18.7 %copy-start.45 = (f32[6,512]{1,0:T(8,128)S(1)}, f32[6,512]{1,0:T(8,128)}, u32[]{:S(2)}) copy-start(f32[6,512]{1,0:T(8,128)} %mul.116) | copy-start | bytes 36868
  400.4 19.4 %copy-start.8 = (bf16[640,1024]{1,0:T(8,128)(2,1)S(1)}, bf16[640,1024]{1,0:T(8,128)(2,1)}, u32[]{:S(2)}) copy-start(bf16[640,1024]{1,0:T(8,128)(2,1)} %get-tuple-element.168.refs_2_) | copy-start | bytes 3932164
  400.4 19.4 %copy-start.9 = (bf16[640,1024]{1,0:T(8,128)(2,1)S(1)}, bf16[640,1024]{1,0:T(8,128)(2,1)}, u32[]{:S(2)}) copy-start(bf16[640,1024]{1,0:T(8,128)(2,1)} %get-tuple-element.170.refs_4_) | copy-start | bytes 3932164
  404.2 5.0 %collective-permute-start.23 = (bf16[1,128,512]{2,1,0:T(8,128)(2,1)S(1)}, bf16[1,128,512]{2,1,0:T(8,128)(2,1)S(1)}, u32[]{:S(2)}, u32[]{:S(2)}) collective-permute-start(bf16[1,128,512]{2,1,0:T(8,128)(2,1)S(1)} %slice.185), channel_id=1, source_target_pairs={{0,4},{2,6},{4,0},{6,2},{8,12},{10,14},{12,8},{14,10},{16,20},{18,... | collective-permute-start | bytes 393224 | tf_op jit(solution)/shard_map/ppermute | solution.py:768
  405.4 7.9 %collective-permute-start.20 = (bf16[1,128,512]{2,1,0:T(8,128)(2,1)S(1)}, bf16[1,128,512]{2,1,0:T(8,128)(2,1)S(1)}, u32[]{:S(2)}, u32[]{:S(2)}) collective-permute-start(bf16[1,128,512]{2,1,0:T(8,128)(2,1)S(1)} %slice.182), channel_id=1, source_target_pairs={{0,16},{2,18},{4,20},{6,22},{8,24},{10,26},{12,28},{14,30},{16,0},... | collective-permute-start | bytes 393224 | tf_op jit(solution)/shard_map/ppermute | solution.py:768
  409.3 5.9 %collective-permute-start.24 = (bf16[32,512]{1,0:T(8,128)(2,1)S(1)}, bf16[32,512]{1,0:T(8,128)(2,1)S(1)}, u32[]{:S(2)}, u32[]{:S(2)}) collective-permute-start(bf16[32,512]{1,0:T(8,128)(2,1)S(1)} %dynamic-slice_bitcast_fusion.2), channel_id=1, source_target_pairs={{0,1},{1,0},{2,3},{3,2},{4,5},{5,4},{6,7},{7,6},{8,9},{9,8},{10,11... | collective-permute-start | bytes 98312 | tf_op jit(solution)/shard_map/ppermute | solution.py:752
  413.4 4.3 collective-permute-start.21
  415.8 15.9 %copy-start.26 = (bf16[1,128,512]{2,1,0:T(8,128)(2,1)}, bf16[1,128,512]{2,1,0:T(8,128)(2,1)S(1)}, u32[]{:S(2)}) copy-start(bf16[1,128,512]{2,1,0:T(8,128)(2,1)S(1)} %maximum_bitcast_fusion.1) | copy-start | bytes 393220
  415.8 15.9 %collective-permute-start.25 = (bf16[1,128,512]{2,1,0:T(8,128)(2,1)S(1)}, bf16[1,128,512]{2,1,0:T(8,128)(2,1)S(1)}, u32[]{:S(2)}, u32[]{:S(2)}) collective-permute-start(bf16[1,128,512]{2,1,0:T(8,128)(2,1)S(1)} %maximum_bitcast_fusion.1), channel_id=1, source_target_pairs={{0,4},{2,6},{4,0},{6,2},{8,12},{10,14},{12,8},{14,10},{16,20},{18,... | collective-permute-start | bytes 393224 | tf_op jit(solution)/shard_map/ppermute | solution.py:768
  418.4 15.8 %copy-start.30 = (bf16[1,128,512]{2,1,0:T(8,128)(2,1)}, bf16[1,128,512]{2,1,0:T(8,128)(2,1)S(1)}, u32[]{:S(2)}) copy-start(bf16[1,128,512]{2,1,0:T(8,128)(2,1)S(1)} %maximum_bitcast_fusion) | copy-start | bytes 393220
  418.4 13.3 %collective-permute-start.22 = (bf16[1,128,512]{2,1,0:T(8,128)(2,1)S(1)}, bf16[1,128,512]{2,1,0:T(8,128)(2,1)S(1)}, u32[]{:S(2)}, u32[]{:S(2)}) collective-permute-start(bf16[1,128,512]{2,1,0:T(8,128)(2,1)S(1)} %maximum_bitcast_fusion), channel_id=1, source_target_pairs={{0,16},{2,18},{4,20},{6,22},{8,24},{10,26},{12,28},{14,30},{16,0},... | collective-permute-start | bytes 393224 | tf_op jit(solution)/shard_map/ppermute | solution.py:768
  431.7 27.0 %copy-start.35 = (bf16[64,512]{1,0:T(8,128)(2,1)S(1)}, bf16[64,512]{1,0:T(8,128)(2,1)}, u32[]{:S(2)}) copy-start(bf16[64,512]{1,0:T(8,128)(2,1)} %copy-done.34) | copy-start | bytes 196612
  431.8 23.1 %copy-start.27 = (bf16[1,128,512]{2,1,0:T(8,128)(2,1)S(1)}, bf16[1,128,512]{2,1,0:T(8,128)(2,1)}, u32[]{:S(2)}) copy-start(bf16[1,128,512]{2,1,0:T(8,128)(2,1)} %copy-done.26) | copy-start | bytes 393220
  431.8 21.3 %collective-permute-start.27 = (bf16[2,128,512]{2,1,0:T(8,128)(2,1)S(1)}, bf16[2,128,512]{2,1,0:T(8,128)(2,1)S(1)}, u32[]{:S(2)}, u32[]{:S(2)}) collective-permute-start(bf16[2,128,512]{2,1,0:T(8,128)(2,1)S(1)} %pad_maximum_fusion.15), channel_id=1, source_target_pairs={{0,16},{2,18},{4,20},{6,22},{8,24},{10,26},{12,28},{14,30},{16,0},... | collective-permute-start | bytes 786440 | tf_op jit(solution)/shard_map/ppermute | solution.py:768
  434.2 18.8 %collective-permute-start.26 = (bf16[2,128,512]{2,1,0:T(8,128)(2,1)S(1)}, bf16[2,128,512]{2,1,0:T(8,128)(2,1)S(1)}, u32[]{:S(2)}, u32[]{:S(2)}) collective-permute-start(bf16[2,128,512]{2,1,0:T(8,128)(2,1)S(1)} %pad_maximum_fusion.14), channel_id=1, source_target_pairs={{0,8},{2,10},{4,12},{6,14},{8,0},{10,2},{12,4},{14,6},{16,24},{18,... | collective-permute-start | bytes 786440 | tf_op jit(solution)/shard_map/ppermute | solution.py:768
  436.2 1.3 collective-permute-start.28
  437.5 4.2 collective-permute-start.29
  441.6 4.2 collective-permute-start.30
  445.8 6.6 %collective-permute-start.31 = (f32[24,512]{1,0:T(8,128)S(1)}, f32[24,512]{1,0:T(8,128)S(1)}, u32[]{:S(2)}, u32[]{:S(2)}) collective-permute-start(f32[24,512]{1,0:T(8,128)S(1)} %add.303), channel_id=1, source_target_pairs={{0,16},{2,18},{4,20},{6,22},{8,24},{10,26},{12,28},{14,30},{16,0},... | collective-permute-start | bytes 147464 | tf_op jit(solution)/shard_map/ppermute | solution.py:768
  455.7 14.7 %collective-permute-start.34 = (bf16[4,128,512]{2,1,0:T(8,128)(2,1)}, bf16[4,128,512]{2,1,0:T(8,128)(2,1)S(1)}, u32[]{:S(2)}, u32[]{:S(2)}) collective-permute-start(bf16[4,128,512]{2,1,0:T(8,128)(2,1)} %pad_maximum_fusion.13), channel_id=1, source_target_pairs={{0,8},{2,10},{4,12},{6,14},{8,0},{10,2},{12,4},{14,6},{16,24},{18,... | collective-permute-start | bytes 1572872 | tf_op jit(solution)/shard_map/ppermute | solution.py:768
  457.4 13.0 %collective-permute-start.33 = (bf16[4,128,512]{2,1,0:T(8,128)(2,1)}, bf16[4,128,512]{2,1,0:T(8,128)(2,1)}, u32[]{:S(2)}, u32[]{:S(2)}) collective-permute-start(bf16[4,128,512]{2,1,0:T(8,128)(2,1)} %pad_maximum_fusion.12), channel_id=1, source_target_pairs={{0,4},{2,6},{4,0},{6,2},{8,12},{10,14},{12,8},{14,10},{16,20},{18,... | collective-permute-start | bytes 1572872 | tf_op jit(solution)/shard_map/ppermute | solution.py:768
  471.6 11.2 %collective-permute-start.36 = (bf16[8,128,512]{2,1,0:T(8,128)(2,1)}, bf16[8,128,512]{2,1,0:T(8,128)(2,1)}, u32[]{:S(2)}, u32[]{:S(2)}) collective-permute-start(bf16[8,128,512]{2,1,0:T(8,128)(2,1)} %pad_maximum_fusion.10), channel_id=1, source_target_pairs={{0,2},{2,0},{4,6},{6,4},{8,10},{10,8},{12,14},{14,12},{16,18},{18,... | collective-permute-start | bytes 3145736 | tf_op jit(solution)/shard_map/ppermute | solution.py:768
  473.7 10.5 %collective-permute-start.35 = (bf16[8,128,512]{2,1,0:T(8,128)(2,1)}, bf16[8,128,512]{2,1,0:T(8,128)(2,1)}, u32[]{:S(2)}, u32[]{:S(2)}) collective-permute-start(bf16[8,128,512]{2,1,0:T(8,128)(2,1)} %pad_maximum_fusion.9), channel_id=1, source_target_pairs={{0,2},{2,0},{4,6},{6,4},{8,10},{10,8},{12,14},{14,12},{16,18},{18,... | collective-permute-start | bytes 3145736 | tf_op jit(solution)/shard_map/ppermute | solution.py:768
  474.9 4.1 collective-permute-start.32
  (52 other events, 272.2 us)
Sparse Core Ops, SparseCore 0:
  47.1 39.9 all-gather.4
  180.0 104.8 reduce-scatter.1
  308.2 96.7 all-gather.6

commit v5 on v4

--- a/solution.py
+++ b/solution.py
@@ -49,58 +49,31 @@
     return t
 
 
-def mlp_kernel(rt, x_ref, dy_ref, wu_ref, bu_ref, wd_ref, gb_ref, act_ref, dpre_ref, h_ref, bu_out, *back):
-    f = pl.program_id(0)
-    if back:
-        yp_ref, g2_ref, ln_ref, yacc, dacc = back
-    last = pl.num_programs(0) - 1
+def mlp_kernel(rt, x_ref, dy_ref, wu_ref, bu_ref, wd_ref, gb_ref, act_ref, dpre_ref, h_ref, bu_out):
     rows = x_ref.shape[0]
 
-    @pl.when(f == 0)
+    @pl.when(pl.program_id(0) == 0)
     def _():
         @pl.loop(0, rows // 128)
         def _(i):
             r = tile(i, 128)
             xh, _ = normed(x_ref[r, :])
             h_ref[r, :] = (xh * gb_ref[0:1, :] + gb_ref[1:2, :]).astype(BF)
-            if back:
-                yacc[r, :] = jnp.zeros((128, yacc.shape[1]), F32)
-                dacc[r, :] = jnp.zeros((128, dacc.shape[1]), F32)
 
     def step(i, bsum):
         r = tile(i, rt)
         pre = dnn(h_ref[r, :], wu_ref[...]) + bu_ref[...]
         da = dnt(dy_ref[r, :], wd_ref[...])
         cdf = 0.5 * (1.0 + lax.erf(pre * 0.7071067811865476))
-        act = (pre * cdf).astype(BF)
+        act_ref[r, :] = (pre * cdf).astype(BF)
         dpre = (da * (cdf + pre * jnp.exp(-0.5 * pre * pre) * 0.3989422804014327)).astype(BF)
-        act_ref[r, :] = act
         dpre_ref[r, :] = dpre
-        if back:
-            yacc[r, :] += dnn(act, wd_ref[...])
-            dacc[r, :] += dnt(dpre, wu_ref[...])
         return bsum + jnp.sum(dpre.astype(F32), axis=0, keepdims=True)
 
     bu_out[...] = lax.fori_loop(0, rows // rt, step, jnp.zeros(bu_out.shape, F32))
-    if not back:
-        return
-
-    @pl.when(f == last)
-    def _():
-        ln_ref[...] = jnp.zeros_like(ln_ref)
-
-        @pl.loop(0, rows // 128)
-        def _(i):
-            r = tile(i, 128)
-            xh, _ = normed(x_ref[r, :])
-            dh = dacc[r, :]
-            yp_ref[r, :] = yacc[r, :].astype(BF)
-            g2_ref[r, :] = (dh * gb_ref[0:1, :]).astype(BF)
-            ln_ref[0:1, :] += jnp.sum(dh * xh, axis=0, keepdims=True)
-            ln_ref[1:2, :] += jnp.sum(dh, axis=0, keepdims=True)
-
-
-def mlp_rows(x, dy, wu, bu, wd, gb, back):
+
+
+def mlp_rows(x, dy, wu, bu, wd, gb):
     rows, width = x.shape
     hidden = wu.shape[1]
     fb = min(512, hidden)
@@ -121,16 +94,11 @@
             pl.BlockSpec((rows, fb), lambda f: (0, f)),
             full((rows, width)),
             pl.BlockSpec((1, fb), lambda f: (0, f)),
-        ]
-        + [full((rows, width)), full((rows, width)), full((2, width))] * back,
-        out_shape=[SD((rows, hidden), BF), SD((rows, hidden), BF), SD((rows, width), BF), SD((1, hidden), F32)]
-        + [SD((rows, width), BF), SD((rows, width), BF), SD((2, width), F32)] * back,
-        scratch_shapes=[pltpu.VMEM((rows, width), F32)] * (2 * back),
+        ],
+        out_shape=[SD((rows, hidden), BF), SD((rows, hidden), BF), SD((rows, width), BF), SD((1, hidden), F32)],
         compiler_params=pltpu.CompilerParams(vmem_limit_bytes=60 * MIB),
         cost_estimate=pl.CostEstimate(
-            flops=4 * (1 + back) * rows * width * hidden,
-            bytes_accessed=4 * (width * hidden + rows * hidden) + (6 + 4 * back) * rows * width,
-            transcendentals=2 * rows * hidden,
+            flops=4 * rows * width * hidden, bytes_accessed=4 * (width * hidden + rows * hidden) + 6 * rows * width, transcendentals=2 * rows * hidden
         ),
     )(x, dy, wu, bu, wd, gb)
 
@@ -140,26 +108,20 @@
     return pltpu.roll(x, (w - 8) if left else 8, 1)
 
 
-def attn_kernel(S, PD, CL, QB, HG, adding, me_ref, *refs):
+def attn_kernel(S, PD, CL, QB, HG, me_ref, *refs):
     it = iter(refs)
     take = lambda n: [next(it) for _ in range(n)]
     stacked = S > 2
     per = 1 if stacked else S
     xs = take(per)
     dys = take(per)
-    far = 1 if stacked else S - 1
-    yps = take(far * adding)
-    g2s = take(far * adding)
     wq, wk, wv = take(3)
     bq, bk, bv = take(3)
     wo, gb = take(2)
     cr, s1r, s2r = take(3)
-    ys = take(far)
-    gs = take(far)
-    dl, ctx, h1, ln, db = take(5)
-    yacc, dacc, q_s, k_s, v_s, dc_s, kT, vT, dk_s, dv_s = take(10)
+    dl, ctx, h1, db = take(4)
+    q_s, k_s, v_s, dc_s, kT, vT, dk_s, dv_s = take(8)
     g = pl.program_id(0)
-    last = pl.num_programs(0) - 1
     me = me_ref[0]
     N = xs[0].shape[-2]
     T = N * S
@@ -167,16 +129,16 @@
     CR = N - PD
     W = HG * HD
 
-    def every_slot(fn, start=0):
+    def every_slot(fn):
         if stacked:
 
-            @pl.loop(start, S)
+            @pl.loop(0, S)
             def _(j):
-                fn(j, lambda refs: refs[0].at[j], lambda refs: refs[0].at[j - 1])
+                fn(j, lambda refs: refs[0].at[j])
 
         else:
-            for j in range(start, S):
-                fn(j, lambda refs: refs[j], lambda refs: refs[j - 1])
+            for j in range(S):
+                fn(j, lambda refs: refs[j])
 
     def slot_rows(start, n):
         if start < PR:
@@ -191,7 +153,7 @@
 
     @pl.when(g == 0)
     def _():
-        def load(j, of, away):
+        def load(j, of):
             x = of(xs)
 
             @pl.loop(0, N // 128)
@@ -212,7 +174,7 @@
             out.append(z * jnp.asarray(scale, BF) if scale != 1.0 else z)
         return jnp.concatenate(out, axis=1) if len(out) > 1 else out[0]
 
-    def proj(j, of, away):
+    def proj(j, of):
         s = lax.rem(me + j, S)
         rp = pl.ds(pl.multiple_of(s * PD, 128), PD)
         rc = pl.ds(pl.multiple_of(PR + s * CR, 128), CR)
@@ -230,15 +192,7 @@
         dc_s[rp, :] = y[:PD]
         dc_s[rc, :] = y[PD:]
 
-    def bring(j, of, away):
-        nb = away(yps).shape[0]
-        r = pl.ds(pl.multiple_of(g * nb, 16), nb)
-        away(ys)[r, :] = away(yps)[...]
-        away(gs)[r, :] = away(g2s)[...]
-
     every_slot(proj)
-    if adding:
-        every_slot(bring, 1)
     lane = lax.broadcasted_iota(jnp.int32, (1, 128), 1)
     row_i = lax.broadcasted_iota(jnp.int32, (QB, QB), 0)
     col_i = lax.broadcasted_iota(jnp.int32, (QB, QB), 1)
@@ -319,50 +273,8 @@
     for c in range(3):
         db[c : c + 1, :] = jnp.sum(dl[c].astype(F32), axis=0, keepdims=True)
 
-    @pl.loop(1, S)
-    def _(j):
-        r = pl.ds(pl.multiple_of(j * N, 128), N)
-        w = pl.ds(pl.multiple_of((j - 1) * N, 128), N)
-        y = dnn(ctx[r, :], wo[...])
-        d = dnt(dl[0, r, :], wq[...]) + dnt(dl[1, r, :], wk[...]) + dnt(dl[2, r, :], wv[...])
-
-        @pl.when(g == 0)
-        def _():
-            yacc[w, :] = y
-            dacc[w, :] = d
-
-        @pl.when(g > 0)
-        def _():
-            yacc[w, :] += y
-            dacc[w, :] += d
-
-    @pl.when(g == last)
-    def _():
-        ln[...] = jnp.zeros_like(ln)
-
-        def store(j, of, away):
-            x, yo, go = of(xs), away(ys), away(gs)
-
-            @pl.loop(0, N // 128)
-            def _(i):
-                r = tile(i, 128)
-                w = pl.ds(pl.multiple_of((j - 1) * N + i * 128, 128), 128)
-                xh, _ = normed(x[r, :])
-                d = dacc[w, :]
-                y = yacc[w, :]
-                gg = d * gb[0:1, :]
-                if adding:
-                    y = y + yo[r, :].astype(F32)
-                    gg = gg + go[r, :].astype(F32)
-                yo[r, :] = y.astype(BF)
-                go[r, :] = gg.astype(BF)
-                ln[0:1, :] += jnp.sum(d * xh, axis=0, keepdims=True)
-                ln[1:2, :] += jnp.sum(d, axis=0, keepdims=True)
-
-        every_slot(store, 1)
-
-
-def attn_group(S, PD, CL, me, xs, dys, yps, g2s, wqkv, bqkv, wo, gb, tabs):
+
+def attn_group(S, PD, CL, me, xs, dys, wqkv, bqkv, wo, gb, tabs):
     N, D = xs[0].shape
     CW = wo.shape[0]
     T = N * S
@@ -371,59 +283,35 @@
     W = HG * HD
     G = CW // W
     full = lambda s: pl.BlockSpec(s, lambda g, m: (0,) * len(s), pipeline_mode=pl.Buffered(1))
-    keep = lambda s: pl.BlockSpec(s, lambda g, m: (0,) * len(s))
-    tok, tok_out, per, far = full((N, D)), keep((N, D)), S, S - 1
-    adding = int(T * D <= 1536 * 1024)
-    others = (yps, g2s)
-    if not adding:
-        yps, g2s = [], []
-    out_tok = SD((N, D), BF)
-    part = pl.BlockSpec((N // G, D), lambda g, m: (g, 0))
+    tok = full((N, D))
     if S > 2:
-        xs, dys, yps, g2s = [[jnp.stack(v, axis=0)] if v else v for v in (xs, dys, yps, g2s)]
-        tok, tok_out, per, far = full((S, N, D)), keep((S - 1, N, D)), 1, 1
-        out_tok = SD((S - 1, N, D), BF)
-        part = pl.BlockSpec((S - 1, N // G, D), lambda g, m: (0, g, 0))
+        xs, dys = [[jnp.stack(v, axis=0)] for v in (xs, dys)]
+        tok = full((S, N, D))
     wspec = lambda c: pl.BlockSpec((D, W), lambda g, m: (0, c * G + g))
     bspec = lambda c: pl.BlockSpec((1, W), lambda g, m: (0, c * G + g))
-    outs = pl.pallas_call(
-        functools.partial(attn_kernel, S, PD, CL, QB, HG, adding),
+    return pl.pallas_call(
+        functools.partial(attn_kernel, S, PD, CL, QB, HG),
         grid_spec=pltpu.PrefetchScalarGridSpec(
             num_scalar_prefetch=1,
             grid=(G,),
-            in_specs=[tok] * (2 * per)
-            + [part] * (2 * adding * far)
+            in_specs=[tok] * (len(xs) + len(dys))
             + [wspec(0), wspec(1), wspec(2), bspec(0), bspec(1), bspec(2)]
             + [pl.BlockSpec((W, D), lambda g, m: (g, 0)), full((2, D))]
             + [full((T, 128))] * 3,
-            out_specs=[tok_out] * (2 * far)
-            + [
+            out_specs=[
                 pl.BlockSpec((3, T, W), lambda g, m: (0, 0, g)),
                 pl.BlockSpec((T, W), lambda g, m: (0, g)),
-                keep((T, D)),
-                keep((2, D)),
+                pl.BlockSpec((T, D), lambda g, m: (0, 0)),
                 pl.BlockSpec((3, W), lambda g, m: (0, g)),
             ],
-            scratch_shapes=[pltpu.VMEM((T - N, D), F32)] * 2
-            + [pltpu.VMEM((T, W), BF)] * 4
-            + [pltpu.VMEM((128, T), BF)] * 2
-            + [pltpu.VMEM((T, 128), F32)] * 2,
+            scratch_shapes=[pltpu.VMEM((T, W), BF)] * 4 + [pltpu.VMEM((128, T), BF)] * 2 + [pltpu.VMEM((T, 128), F32)] * 2,
         ),
-        out_shape=[out_tok] * (2 * far)
-        + [SD((3, T, CW), BF), SD((T, CW), BF), SD((T, D), BF), SD((2, D), F32), SD((3, CW), F32)],
+        out_shape=[SD((3, T, CW), BF), SD((T, CW), BF), SD((T, D), BF), SD((3, CW), F32)],
         compiler_params=pltpu.CompilerParams(vmem_limit_bytes=62 * MIB),
         cost_estimate=pl.CostEstimate(
-            flops=16 * T * D * CW + 40 * T * T * CW,
-            bytes_accessed=12 * T * D + 12 * T * CW + 8 * D * CW,
-            transcendentals=T * T * CW // HD,
+            flops=8 * T * D * CW + 40 * T * T * CW, bytes_accessed=6 * T * D + 8 * T * CW + 8 * D * CW, transcendentals=T * T * CW // HD
         ),
-    )(me, *xs, *dys, *yps, *g2s, wqkv, wqkv, wqkv, bqkv, bqkv, bqkv, wo, gb, *tabs)
-    ys, gs = outs[:far], outs[far : 2 * far]
-    if S > 2:
-        ys, gs = [[v[0][j] for j in range(S - 1)] for v in (ys, gs)]
-    if not adding:
-        ys, gs = [[a + b for a, b in zip(p, q)] for p, q in zip((ys, gs), others)]
-    return ys, gs, outs[2 * far :]
+    )(me, *xs, *dys, wqkv, wqkv, wqkv, bqkv, bqkv, bqkv, wo, gb, *tabs)
 
 
 def tn_kernel(n, wide, *refs):
@@ -638,7 +526,7 @@
     )(q, *[g1] * n, *[g2] * n)
 
 
-def own_kernel(act, dpre, wu, wd, dl, ctx, wqkv, wo, x, gb, y, g, ln, yacc, d1, d2):
+def rows_kernel(act, dpre, wu, wd, dl, ctx, wqkv, wo, x, gb, y, g, ln, yacc, d1, d2):
     f = pl.program_id(0)
     last = pl.num_programs(0) - 1
     N = x.shape[0]
@@ -671,7 +559,7 @@
             ln[3:4, :] += jnp.sum(b, axis=0, keepdims=True)
 
 
-def own_rows(x, act, dpre, wu, wd, dl, ctx, wqkv, wo, gb):
+def branch_rows(j, x, act, dpre, wu, wd, dl, ctx, wqkv, wo, gb):
     N, D = x.shape
     FL = wu.shape[1]
     CW = wo.shape[0]
@@ -680,10 +568,14 @@
     keep = lambda s: pl.BlockSpec(s, lambda f: (0,) * len(s))
     rows = pl.BlockSpec((N, fb), lambda f: (0, f))
     return pl.pallas_call(
-        own_kernel,
+        rows_kernel,
         grid=(FL // fb,),
         in_specs=[rows, rows, pl.BlockSpec((D, fb), lambda f: (0, f)), pl.BlockSpec((fb, D), lambda f: (f, 0))]
-        + [full((3, N, CW)), full((N, CW)), full((D, 3 * CW)), full((CW, D)), full((N, D)), full((4, D))],
+        + [
+            pl.BlockSpec((3, N, CW), lambda f: (0, j, 0), pipeline_mode=pl.Buffered(1)),
+            pl.BlockSpec((N, CW), lambda f: (j, 0), pipeline_mode=pl.Buffered(1)),
+        ]
+        + [full((D, 3 * CW)), full((CW, D)), full((N, D)), full((4, D))],
         out_specs=[keep((N, D)), keep((N, D)), keep((4, D))],
         out_shape=[SD((N, D), BF), SD((N, D), BF), SD((4, D), F32)],
         scratch_shapes=[pltpu.VMEM((N, D), F32)] * 3,
@@ -777,7 +669,7 @@
     return got[0] if parts == 1 else jnp.concatenate(got, axis=1)
 
 
-def my_columns_halves(weight, me, S, R):
+def my_columns_halves(weight, me, S, R, ahead):
     rows = weight.shape[0]
     rep = lax.axis_index("rep")
     core = rep % 2
@@ -791,9 +683,10 @@
 
     for j in range(1, S):
         piece = shifted(cut[j - 1], S, j)
+        piece, _ = lax.optimization_barrier((piece, ahead))
         pair = both(piece, exchanged(piece, R, 2), y == 0)
         slots.append(both(pair, exchanged(pair, R, 1), core == 0))
-    return jnp.concatenate(canonical(slots, me, S, True), axis=0), piece, cut[0]
+    return jnp.concatenate(canonical(slots, me, S, True), axis=0), piece
 
 
 def my_columns(weight, me, S, R, parts):
@@ -927,10 +820,15 @@
     FL = up_weight.shape[1] // S
     me_arr = jnp.reshape(me, (1,)).astype(jnp.int32)
 
+    X = [[jnp.concatenate([prompt_in[m, 0], cont_in[m, 0].reshape(CR, D)], axis=0)] for m in range(MB)]
+    DY = [[jnp.concatenate([prompt_cot[m, 0], cont_cot[m, 0].reshape(CR, D)], axis=0)] for m in range(MB)]
+
+    w_up, brought = my_columns_halves(up_weight, me, S, R, (X[0], DY[0]))
+    vecs_in = (ln1_gain, ln1_bias, ln2_gain, ln2_bias, out_bias, down_bias, qkv_bias)
+    (vecs_in, qkv_weight), brought = lax.optimization_barrier(((vecs_in, qkv_weight), brought))
+
     one = lambda v: v.astype(F32).reshape(-1, CW)
-    small = jnp.concatenate([one(v) for v in (ln1_gain, ln1_bias, ln2_gain, ln2_bias, out_bias, down_bias, qkv_bias)], axis=0)
-    w_up, brought, cut = my_columns_halves(up_weight, me, S, R)
-    (small, qkv_weight), cut = lax.optimization_barrier(((small, qkv_weight), cut))
+    small = jnp.concatenate([one(v) for v in vecs_in], axis=0)
     slots = [small] + [shifted(small, S, j) for j in range(1, S)]
     whole = jnp.stack(canonical(slots, me, S, True), axis=0)
     vec = whole[:, :6].transpose(1, 0, 2).reshape(6, D)
@@ -944,11 +842,9 @@
 
     w_qkv = my_columns(qkv_weight, me, S, R, 3)
 
-    X = [[jnp.concatenate([prompt_in[m, 0], cont_in[m, 0].reshape(CR, D)], axis=0)] for m in range(MB)]
-    DY = [[jnp.concatenate([prompt_cot[m, 0], cont_cot[m, 0].reshape(CR, D)], axis=0)] for m in range(MB)]
     tabs = rotary_tables(PD * S, CR * S, CL)
     src = [(X[m][0], DY[m][0]) for m in range(MB)]
-    src[1:], brought = lax.optimization_barrier((src[1:], brought))
+    src[1:], w_up = lax.optimization_barrier((src[1:], w_up))
     for m in range(MB):
         for j in range(1, S):
             X[m].append(shifted(src[m][0], S, S - j))
@@ -957,24 +853,23 @@
     ff = [[None] * S for _ in range(MB)]
 
     def mlp(m, j):
-        ff[m][j] = mlp_rows(X[m][j], DY[m][j], w_up, bup, down_weight, gb2, int(j > 0))
+        ff[m][j] = mlp_rows(X[m][j], DY[m][j], w_up, bup, down_weight, gb2)
 
     for m in range(MB):
         mlp(m, 0)
     rest = []
-    y_got, g_got = [], []
 
     def attend(m):
-        ys, gs, more = attn_group(
-            S, PD, CL, me_arr, X[m], DY[m], [f[4] for f in ff[m][1:]], [f[5] for f in ff[m][1:]], w_qkv, bqkv, out_weight, gb1, tabs
-        )
-        rest.append(list(more))
-        y_got.append([shifted(ys[j - 1], S, j) for j in range(1, S)])
-        g_got.append([shifted(gs[j - 1], S, j) for j in range(1, S)])
-
-    def own(m):
-        f = ff[m][0]
-        return own_rows(X[m][0], f[0], f[1], w_up, down_weight, rest[m][0], rest[m][1], w_qkv, out_weight, gb)
+        rest.append(list(attn_group(S, PD, CL, me_arr, X[m], DY[m], w_qkv, bqkv, out_weight, gb1, tabs)))
+
+    def rows(m, j):
+        f = ff[m][j]
+        return branch_rows(j, X[m][j], f[0], f[1], w_up, down_weight, rest[m][0], rest[m][1], w_qkv, out_weight, gb)
+
+    def far_rows(m):
+        r = [rows(m, j) for j in range(1, S)]
+        got = [[shifted(r[j - 1][i], S, j) for j in range(1, S)] for i in range(2)]
+        return got, [v[2] for v in r]
 
     chunked = (D // S // R) % 16 == 0 and R & (R - 1) == 0
     rep = lax.axis_index("rep")
@@ -999,55 +894,69 @@
         if m + 1 < MB:
             w_qkv, rest[m][3] = lax.optimization_barrier((w_qkv, rest[m][3]))
     every = early + late
-    def vectors(mine_):
-        ln1 = sum(r[3] for r in rest) + sum(o[2][0:2] for o in mine_)
-        ln2 = sum(f[6] for f in (ff[m][j] for m, j in every if j)) + sum(o[2][2:4] for o in mine_)
+    def vectors(sums):
+        ln1 = sum(o[0:2] for o in sums)
+        ln2 = sum(o[2:4] for o in sums)
         db_out = sum(jnp.sum(DY[m][0].astype(F32), axis=0) for m in range(MB)).reshape(-1, CW)
         mine = (jnp.arange(S) == me).astype(F32)
-        db_qkv = (sum(r[4] for r in rest)[:, None, :] * mine[None, :, None]).reshape(-1, CW)
+        db_qkv = (sum(r[3] for r in rest)[:, None, :] * mine[None, :, None]).reshape(-1, CW)
         db_up = (sum(of(every, 3)) * mine[:, None]).reshape(-1, CW)
         return jnp.concatenate([ln1.reshape(-1, CW), ln2.reshape(-1, CW), db_out, db_qkv, db_up], axis=0)
 
-    finals = lambda m, o, prior: final_rows(m, MB, PD, X[m][0], DY[m][0], [o[0]] + y_got[m], [o[1]] + g_got[m], vb, prior)
+    def finals(m, o, got, prior):
+        return final_rows(m, MB, PD, X[m][0], DY[m][0], [o[0]] + got[0], [o[1]] + got[1], vb, prior)
+
     hs, dls, ctxs = [[r[k] for r in rest] for k in (2, 0, 1)]
     if chunked:
         q = jnp.stack([place(rep, order) for order in orders(R)]).astype(jnp.int32)
+        gatt = attn_grads(S, R, q, hs, dls, ctxs, [DY[m][j] for m in range(MB) for j in range(S)])
+        part, gatt = lax.optimization_barrier((part, gatt))
         part = swap_shards(part, me, S, FL // R)
-        hs, y_got[:-1], g_got[:-1], part = lax.optimization_barrier((hs, y_got[:-1], g_got[:-1], part))
         gmlp_all = lax.all_gather(part, "rep", axis=0, tiled=False)
-        gatt = attn_grads(S, R, q, hs, dls, ctxs, [DY[m][j] for m in range(MB) for j in range(S)])
-        dls_own, _ = lax.optimization_barrier(([r[0] for r in rest], gatt))
+        dls, _ = lax.optimization_barrier(([r[0] for r in rest], part))
         for m in range(MB):
-            rest[m][0] = dls_own[m]
-        mine = [own(m) for m in range(MB)]
-        beside = {1: mine[:1], 2: (mine[1:], y_got[-1], g_got[-1])}
+            rest[m][0] = dls[m]
+        levels = R.bit_length() - 1
+        beside = {}
+        far, mine = [], []
+        for m in range(MB):
+            far.append(far_rows(m))
+            beside.setdefault(min(m, levels - 1), {})["far", m] = far[m][1]
+            dls, beside[min(m, levels - 1)] = lax.optimization_barrier(([r[0] for r in rest], beside[min(m, levels - 1)]))
+            for k in range(MB):
+                rest[k][0] = dls[k]
+        for m in range(MB):
+            mine.append(rows(m, 0))
+            beside.setdefault(min(MB + m, levels - 1), {})["own", m] = mine[m]
+        beside.setdefault(levels - 1, {})["got", 0] = far[0][0]
         half = halving(gatt, R, beside)
-        mine[:1] = beside[1]
-        mine[1:], y_got[-1], g_got[-1] = beside[2]
+        done = {k: v for d in beside.values() for k, v in d.items()}
+        sums = [v for m in range(MB) for v in done["far", m]]
+        mine = [done["own", m] for m in range(MB)]
+        vecs = sum_all(vectors(sums + [o[2] for o in mine]), S, R)
+        got = [f[0] for f in far]
+        got[0] = done["got", 0]
+        beside = {1: (got[1:], mlp_finish(S, gmlp_all, FL), vecs)}
+        k = D // CW * (D // S // R)
+        g1, g2 = doubling([swap_shards(half[0], me, S, 0), swap_shards(half[1], me, S, k)], R, beside)
+        got[1:], (g_down, g_up), vecs = beside[1]
         outs = None
-        for m in range(MB - 1):
-            outs = finals(m, mine[m], outs)
-        vecs = sum_all(vectors(mine), S, R)
-        k = D // CW * (D // S // R)
-        outs = finals(MB - 1, mine[-1], outs)
-        beside = {3: outs, 2: vecs, 1: mlp_finish(S, gmlp_all, FL)}
-        g1, g2 = doubling([swap_shards(half[0], me, S, 0), swap_shards(half[1], me, S, k)], R, beside)
-        outs = beside[3]
-        vecs = beside[2]
-        g_down, g_up = beside[1]
+        for m in range(MB):
+            outs = finals(m, mine[m], got[m], outs)
         g_out, g_qkv = attn_finish(S, q, g1, g2)
     else:
         dls, ctxs, hs = [[r[k] for r in rest] for k in (0, 1, 2)]
-        mine = [own(m) for m in range(MB)]
+        far = [far_rows(m) for m in range(MB)]
+        mine = [rows(m, 0) for m in range(MB)]
         g_down = reduce_rows(tn_sum(of(every, 0), [DY[m][j] for m, j in every], 256))
         g_up = reduce_columns(tn_sum(of(every, 2), of(every, 1), 256), me, S, 1)
         dycs = [jnp.concatenate(DY[m], axis=0) for m in range(MB)]
         g_out = reduce_rows(tn_sum(ctxs, dycs, 256))
         g_qkv = reduce_columns(tn_sum(hs, dls, 256), me, S, 3)
-        vecs = sum_all(vectors(mine), S, R)
+        vecs = sum_all(vectors([v for f in far for v in f[1]] + [o[2] for o in mine]), S, R)
         outs = None
         for m in range(MB):
-            outs = finals(m, mine[m], outs)
+            outs = finals(m, mine[m], far[m][0], outs)
     tot = vecs + sum(shifted(vecs, S, j) for j in range(1, S))
     held = lambda a, n: lax.dynamic_slice_in_dim(tot, a + me * n, n, 0).reshape(-1)
     v_ln1g, v_ln1b, v_ln2g, v_ln2b, v_out = [held(k * S, 1) for k in range(5)]

time: 503 us -> 549 us (1.091)
  waiting for transfers between devices: 56.5 us -> 100 us
  starting transfers between devices: 48.6 us -> 33.6 us
  local copies, waits for them, and re-layouts: 37.8 us -> 47.8 us
  Pallas kernels: 299 us -> 305 us
    ppermute x15, waiting for transfers between devices: 23 us -> 52.9 us  [shifted(): return lax.ppermute(value, 'shard', [(i, (i + j) % S) for i in range(S)])]
    pallas_call x4 -> x6, Pallas kernels: 148 us -> 169 us  [the longest x2 97.2 us: attn_group(): pl.pallas_call(functools.partial(attn_kernel, S, PD, CL, QB, HG), grid_sp...]
    pallas_call x4, Pallas kernels: 63.2 us -> 45.9 us  [mlp_rows(): pl.pallas_call(functools.partial(mlp_kernel, rows_tile(rows, 640)), grid=...]
    ppermute x22, waiting for transfers between devices: 33.4 us -> 47 us  [exchanged(): return lax.ppermute(value, 'rep', [(i, i ^ bit) for i in range(R)])]
    ppermute x22, starting transfers between devices: 27.7 us -> 16.3 us  [exchanged(): return lax.ppermute(value, 'rep', [(i, i ^ bit) for i in range(R)])]
    unnamed x128 -> x145, local copies, waits for them, and re-layouts: 10.4 us -> 21.7 us
  transfers between devices with their start and end apart: 40 -> 40, of which waited for: 15 -> 15; matrix products, arithmetic and copies ran while one was open for 14% -> 12% of each run, Pallas kernels for 59% -> 55%
where the time goes in v5:
time: 549 us; the launch traced here: 543 us
  Pallas kernels  305 us (56%)
  waiting for transfers between devices  100 us (18%)
  local copies, waits for them, and re-layouts  47.8 us (9%)
  other arithmetic  40.7 us (7%)
  starting transfers between devices  33.6 us (6%)
  between operations  15.4 us (3%)
    pallas_call x2, Pallas kernels, attn_group(): pl.pallas_call(functools.partial(attn_kernel, S, PD, CL, QB, HG), grid_sp...  97.2 us
    pallas_call x4, Pallas kernels, branch_rows(): pl.pallas_call(rows_kernel, grid=(FL // fb,), in_specs=[rows, rows, pl.Bl...  71.9 us
    ppermute x15, waiting for transfers between devices, shifted(): return lax.ppermute(value, 'shard', [(i, (i + j) % S) for i in range(S)])  52.9 us
    ppermute x22, waiting for transfers between devices, exchanged(): return lax.ppermute(value, 'rep', [(i, i ^ bit) for i in range(R)])  47 us
    pallas_call x4, Pallas kernels, call(): pl.pallas_call(functools.partial(kernel, n, more), grid=(a[0].shape[1] //...  46.1 us
    pallas_call x4, Pallas kernels, mlp_rows(): pl.pallas_call(functools.partial(mlp_kernel, rows_tile(rows, 640)), grid=...  45.9 us
    unnamed x145, local copies, waits for them, and re-layouts  21.7 us
    pallas_call x1, Pallas kernels, attn_grads(): pl.pallas_call(functools.partial(attn_grads_kernel, n, S, R), grid_spec=p...  19.5 us
  transfers between devices with their start and end apart: 40, of which 15 were waited for; matrix products, arithmetic and copies ran while one was open for 12% of the time, Pallas kernels for 55%

profile of v5, /device:TPU:0, one launch (start us, length us, event | category | flops | bytes accessed | tf_op | source)
XLA Modules:
  0.0 542.7 jit_solution(15218402735554017514)
XLA Ops:
  8.5 3.0 collective-permute-start
  18.2 5.4 collective-permute-done
  28.1 8.9 %collective-permute-done.1 = bf16[128,2048]{1,0:T(8,128)(2,1)} collective-permute-done((bf16[128,2048]{1,0:T(8,128)(2,1)}, bf16[128,2048]{1,0:T(8,128)(2,1)}, u32[]{:S(2)}, u32[]{:S(2)}) %collective-permute-start.1) | collective-permute-done | bytes 524320 | tf_op jit(solution)/shard_map/ppermute | solution.py:660
  42.8 41.9 %collective-permute-done.5 = f32[9,512]{1,0:T(8,128)S(1)} collective-permute-done((f32[9,512]{1,0:T(8,128)S(1)}, f32[9,512]{1,0:T(8,128)S(1)}, u32[]{:S(2)}, u32[]{:S(2)}) %collective-permute-start.5) | collective-permute-done | bytes 18464 | tf_op jit(solution)/shard_map/ppermute | solution.py:644
  86.5 2.0 broadcast_select_fusion.5
  90.3 2.6 pad_maximum_fusion.wu_ref.wu
  95.0 11.6 %shard_map.308 = (bf16[640,2048]{1,0:T(8,128)(2,1)}, bf16[640,2048]{1,0:T(8,128)(2,1)}, bf16[640,1024]{1,0:T(8,128)(2,1)}, f32[1,2048]{1,0:T(1,128)}) custom-call(bf16[640,1024]{1,0:T(8,128)(2,1)} %copy-done.1, bf16[640,1024]{1,0:T(8,128)(2,1)} %copy-done.3, bf16[1024,2048]{1,0:T(8,128)(2,1)} %pad_maximum_fusion.wu_ref.wu, f32[1,2048]{1,0:T(1,128)} %bitcast.89, ...), custom_call_target="tpu_custom_call" | custom-call | flops 5368709120 | bytes 17563648 | tf_op jit(solution)/shard_map/pallas_call | solution.py:81
  106.6 11.4 %shard_map.306 = (bf16[640,2048]{1,0:T(8,128)(2,1)}, bf16[640,2048]{1,0:T(8,128)(2,1)}, bf16[640,1024]{1,0:T(8,128)(2,1)}, f32[1,2048]{1,0:T(1,128)}) custom-call(bf16[640,1024]{1,0:T(8,128)(2,1)} %pad_maximum_fusion.6.x_ref.refs_0_.x, bf16[640,1024]{1,0:T(8,128)(2,1)} %pad_maximum_fusion.7.dy_ref.refs_3_.refs_2_.refs_6_.refs_1_, ...), custom_call_target="tpu_custom_call" | custom-call | flops 5368709120 | bytes 17563648 | tf_op jit(solution)/shard_map/pallas_call | solution.py:81
  118.0 11.5 %shard_map.307 = (bf16[640,2048]{1,0:T(8,128)(2,1)}, bf16[640,2048]{1,0:T(8,128)(2,1)}, bf16[640,1024]{1,0:T(8,128)(2,1)}, f32[1,2048]{1,0:T(1,128)}) custom-call(bf16[640,1024]{1,0:T(8,128)(2,1)} %collective-permute-done.6.x_ref.refs_1_.x, bf16[640,1024]{1,0:T(8,128)(2,1)} %collective-permute-done.7.dy_ref.refs_4_.refs_3_.refs_7_, ...), custom_call_target="tpu_custom_call" | custom-call | flops 5368709120 | bytes 17563648 | tf_op jit(solution)/shard_map/pallas_call | solution.py:81
  129.5 14.0 %shard_map.309.refs_6_ = bf16[16,256,1024]{2,1,0:T(8,128)(2,1)} custom-call(bf16[640,2048]{1,0:T(8,128)(2,1)} %get-tuple-element.136.refs_0_.act, bf16[640,2048]{1,0:T(8,128)(2,1)} %get-tuple-element.137.refs_1_.act, bf16[640,2048]{1,0:T(8,128)(2,1)} %get-tuple-element.138.refs_2_.act, ...), custom_call_target="tpu_custom_call" | custom-call | flops 8053063680 | bytes 15990784 | tf_op jit(solution)/shard_map/pallas_call | solution.py:386
  143.5 14.4 %shard_map.310.refs_2_ = bf16[16,256,1024]{2,1,0:T(8,128)(2,1)} custom-call(bf16[640,1024]{1,0:T(8,128)(2,1)} %get-tuple-element.130.refs_0_, bf16[640,1024]{1,0:T(8,128)(2,1)} %get-tuple-element.131.refs_1_, bf16[640,1024]{1,0:T(8,128)(2,1)} %get-tuple-element.132.refs_2_, ...), custom_call_target="tpu_custom_call", output_to_operand_aliasing={{}: (6, {})} | custom-call | flops 8053063680 | bytes 15990784 | tf_op jit(solution)/shard_map/pallas_call | solution.py:386
  157.8 11.4 %shard_map.311 = (bf16[640,2048]{1,0:T(8,128)(2,1)}, bf16[640,2048]{1,0:T(8,128)(2,1)}, bf16[640,1024]{1,0:T(8,128)(2,1)}, f32[1,2048]{1,0:T(1,128)}) custom-call(bf16[640,1024]{1,0:T(8,128)(2,1)} %collective-permute-done.3.x_ref.refs_1_.x, bf16[640,1024]{1,0:T(8,128)(2,1)} %collective-permute-done.4.dy_ref.refs_1_.refs_3_.refs_9_, ...), custom_call_target="tpu_custom_call" | custom-call | flops 5368709120 | bytes 17563648 | tf_op jit(solution)/shard_map/pallas_call | solution.py:81
  169.3 9.6 %shard_map.312.refs_2_ = bf16[16,256,1024]{2,1,0:T(8,128)(2,1)} custom-call(bf16[640,2048]{1,0:T(8,128)(2,1)} %get-tuple-element.142.refs_0_.act, bf16[640,1024]{1,0:T(8,128)(2,1)} %collective-permute-done.4.dy_ref.refs_1_.refs_3_.refs_9_, bf16[16,256,1024]{2,1,0:T(8,128)(2,1)} %shard_map.310.refs_2_), custom_call_target="tpu_custom_call", output_to_operand_aliasing={{}: (2, {})} | custom-call | flops 2684354560 | bytes 12320768 | tf_op jit(solution)/shard_map/pallas_call | solution.py:386
  178.9 8.1 %shard_map.313 = bf16[16,256,1024]{2,1,0:T(8,128)(2,1)} custom-call(bf16[640,1024]{1,0:T(8,128)(2,1)} %get-tuple-element.140.refs_0_, bf16[640,2048]{1,0:T(8,128)(2,1)} %get-tuple-element.141.refs_1_.dpre, bf16[16,256,1024]{2,1,0:T(8,128)(2,1)} %shard_map.312.refs_2_), custom_call_target="tpu_custom_call", output_to_operand_aliasing={{}: (2, {})} | custom-call | flops 2684354560 | bytes 12320768 | tf_op jit(solution)/shard_map/pallas_call | solution.py:386
  189.8 2.0 broadcast_select_fusion.3
  191.8 2.0 pad_maximum_fusion.1.refs_4_.refs_5_.refs_6_.wqkv
  193.8 49.2 %shard_map.314 = (bf16[3,1280,512]{2,1,0:T(8,128)(2,1)}, bf16[1280,512]{1,0:T(8,128)(2,1)}, bf16[1280,1024]{1,0:T(8,128)(2,1)}, f32[3,512]{1,0:T(4,128)}) custom-call(s32[1]{0:T(128)} %bitcast.16.me_ref, bf16[640,1024]{1,0:T(8,128)(2,1)} %pad_maximum_fusion.6.x_ref.refs_0_.x, bf16[640,1024]{1,0:T(8,128)(2,1)} %collective-permute-done.6.x_ref.refs_1_.x, ...), custom_call_target="tpu_custom_call" | custom-call | flops 38923141120 | bytes 17301504 | tf_op jit(solution)/shard_map/pallas_call | solution.py:292
  243.0 48.0 %shard_map.315 = (bf16[3,1280,512]{2,1,0:T(8,128)(2,1)}, bf16[1280,512]{1,0:T(8,128)(2,1)}, bf16[1280,1024]{1,0:T(8,128)(2,1)}, f32[3,512]{1,0:T(4,128)}) custom-call(s32[1]{0:T(128)} %bitcast.16.me_ref, bf16[640,1024]{1,0:T(8,128)(2,1)} %copy-done.1, bf16[640,1024]{1,0:T(8,128)(2,1)} %collective-permute-done.3.x_ref.refs_1_.x, bf16[640,1024]{1,0:T(8,128)(2,1)} %copy-done.3, ...), custom_call_target="tpu_custom_call" | custom-call | flops 38923141120 | bytes 17301504 | tf_op jit(solution)/shard_map/pallas_call | solution.py:292
  291.0 19.5 %shard_map.316 = (bf16[16,128,512]{2,1,0:T(8,128)(2,1)}, bf16[16,128,512]{2,1,0:T(8,128)(2,1)}) custom-call(s32[2]{0:T(128)} %pad_add_fusion.q_ref, bf16[1280,1024]{1,0:T(8,128)(2,1)} %get-tuple-element.146.refs_0_, bf16[1280,1024]{1,0:T(8,128)(2,1)} %get-tuple-element.149.refs_1_, bf16[3,1280,512]{2,1,0:T(8,128)(2,1)} %get-tuple-element.171.refs_2_.dl, ...), custom_call_target="tpu_custom_call" | custom-call | flops 10737418240 | bytes 25165824 | tf_op jit(solution)/shard_map/pallas_call | solution.py:475
  313.9 2.5 collective-permute-done.11
  318.3 2.4 slice.150
  320.8 2.3 slice.151
  326.1 18.2 %shard_map.317 = (bf16[640,1024]{1,0:T(8,128)(2,1)}, bf16[640,1024]{1,0:T(8,128)(2,1)}, f32[4,1024]{1,0:T(4,128)}) custom-call(bf16[640,2048]{1,0:T(8,128)(2,1)} %get-tuple-element.137.refs_1_.act, bf16[640,2048]{1,0:T(8,128)(2,1)} %get-tuple-element.134.refs_4_.dpre, bf16[1024,2048]{1,0:T(8,128)(2,1)} %pad_maximum_fusion.wu_ref.wu, bf16[2048,1024]{1,0:T(8,128)(2,1)} %wd.7, ...), custom_call_target="tpu_custom_call" | custom-call | flops 8053063680 | bytes 24379392 | tf_op jit(solution)/shard_map/pallas_call | solution.py:570
  353.4 17.8 %shard_map.318 = (bf16[640,1024]{1,0:T(8,128)(2,1)}, bf16[640,1024]{1,0:T(8,128)(2,1)}, f32[4,1024]{1,0:T(4,128)}) custom-call(bf16[640,2048]{1,0:T(8,128)(2,1)} %get-tuple-element.142.refs_0_.act, bf16[640,2048]{1,0:T(8,128)(2,1)} %get-tuple-element.141.refs_1_.dpre, bf16[1024,2048]{1,0:T(8,128)(2,1)} %pad_maximum_fusion.wu_ref.wu, bf16[2048,1024]{1,0:T(8,128)(2,1)} %wd.7, ...), custom_call_target="tpu_custom_call" | custom-call | flops 8053063680 | bytes 24379392 | tf_op jit(solution)/shard_map/pallas_call | solution.py:570
  373.3 11.7 %collective-permute-done.13 = bf16[4,128,512]{2,1,0:T(8,128)(2,1)S(1)} collective-permute-done((bf16[4,128,512]{2,1,0:T(8,128)(2,1)}, bf16[4,128,512]{2,1,0:T(8,128)(2,1)S(1)}, u32[]{:S(2)}, u32[]{:S(2)}) %collective-permute-start.13) | collective-permute-done | bytes 524320 | tf_op jit(solution)/shard_map/ppermute | solution.py:660
  389.7 2.2 collective-permute-start.14
  392.0 18.2 %shard_map.319 = (bf16[640,1024]{1,0:T(8,128)(2,1)}, bf16[640,1024]{1,0:T(8,128)(2,1)}, f32[4,1024]{1,0:T(4,128)}) custom-call(bf16[640,2048]{1,0:T(8,128)(2,1)} %get-tuple-element.136.refs_0_.act, bf16[640,2048]{1,0:T(8,128)(2,1)} %get-tuple-element.133.refs_3_.dpre, bf16[1024,2048]{1,0:T(8,128)(2,1)} %pad_maximum_fusion.wu_ref.wu, bf16[2048,1024]{1,0:T(8,128)(2,1)} %wd.7, ...), custom_call_target="tpu_custom_call" | custom-call | flops 8053063680 | bytes 24379392 | tf_op jit(solution)/shard_map/pallas_call | solution.py:570
  410.1 4.0 collective-permute-done.15
  418.7 17.8 %shard_map.320 = (bf16[640,1024]{1,0:T(8,128)(2,1)}, bf16[640,1024]{1,0:T(8,128)(2,1)}, f32[4,1024]{1,0:T(4,128)}) custom-call(bf16[640,2048]{1,0:T(8,128)(2,1)} %get-tuple-element.138.refs_2_.act, bf16[640,2048]{1,0:T(8,128)(2,1)} %get-tuple-element.135.refs_5_.dpre, bf16[1024,2048]{1,0:T(8,128)(2,1)} %pad_maximum_fusion.wu_ref.wu, bf16[2048,1024]{1,0:T(8,128)(2,1)} %wd.7, ...), custom_call_target="tpu_custom_call" | custom-call | flops 8053063680 | bytes 24379392 | tf_op jit(solution)/shard_map/pallas_call | solution.py:570
  438.8 2.1 collective-permute-done.24
  443.3 1.9 collective-permute-start.21
  450.6 7.2 %collective-permute-done.21 = bf16[1,128,512]{2,1,0:T(8,128)(2,1)} collective-permute-done((bf16[1,128,512]{2,1,0:T(8,128)(2,1)}, bf16[1,128,512]{2,1,0:T(8,128)(2,1)}, u32[]{:S(2)}, u32[]{:S(2)}) %collective-permute-start.21) | collective-permute-done | bytes 131104 | tf_op jit(solution)/shard_map/ppermute | solution.py:660
  460.3 2.2 collective-permute-done.26
  462.4 1.9 pad_maximum_fusion.13
  464.3 3.8 collective-permute-done.22
  468.1 1.9 pad_maximum_fusion.12
  476.4 6.5 %shard_map.322 = (bf16[2,512,1024]{2,1,0:T(8,128)(2,1)}, bf16[2,128,1024]{2,1,0:T(8,128)(2,1)}, f32[2,512,1024]{2,1,0:T(8,128)}, f32[2,128,1024]{2,1,0:T(8,128)}) custom-call(bf16[640,1024]{1,0:T(8,128)(2,1)} %pad_maximum_fusion.6.x_ref.refs_0_.x, bf16[640,1024]{1,0:T(8,128)(2,1)} %pad_maximum_fusion.7.dy_ref.refs_3_.refs_2_.refs_6_.refs_1_, ...), custom_call_target="tpu_custom_call" | custom-call | flops 13107200 | bytes 11796480 | tf_op jit(solution)/shard_map/pallas_call | solution.py:631
  483.7 2.0 collective-permute-start.31
  488.3 4.0 collective-permute-done.32
  494.0 3.4 collective-permute-done.33
  498.0 3.4 copy-done
  501.4 6.1 %shard_map.321 = (f32[2048,1024]{1,0:T(8,128)}, f32[512,4096]{1,0:T(8,128)}) custom-call(bf16[16,256,1024]{2,1,0:T(8,128)(2,1)S(1)} %bitcast.73), custom_call_target="tpu_custom_call" | custom-call | bytes 25165824 | tf_op jit(solution)/shard_map/pallas_call | solution.py:421
  507.5 2.2 pad_maximum_fusion.10
  509.7 2.4 pad_maximum_fusion.9
  515.6 1.9 constant_dynamic-update-slice_fusion.6
  517.5 6.1 %shard_map.323 = (bf16[2,512,1024]{2,1,0:T(8,128)(2,1)}, bf16[2,128,1024]{2,1,0:T(8,128)(2,1)}, f32[2,512,1024]{2,1,0:T(8,128)}, f32[2,128,1024]{2,1,0:T(8,128)}) custom-call(bf16[640,1024]{1,0:T(8,128)(2,1)S(1)} %copy-done.2, bf16[640,1024]{1,0:T(8,128)(2,1)S(1)} %copy-done.4, ...), custom_call_target="tpu_custom_call", output_to_operand_aliasing={{0}: (7, {}), {1}: (8, {}), {2}: (9, {}), {3}: (10, {})} | custom-call | flops 13107200 | bytes 11796480 | tf_op jit(solution)/shard_map/pallas_call | solution.py:631
  525.5 2.3 constant_dynamic-update-slice_fusion.5.refs_4_.refs_5_.refs_6_.refs_7_
  529.1 6.0 %shard_map.324 = (f32[512,1024]{1,0:T(8,128)}, f32[512,3072]{1,0:T(8,128)}) custom-call(s32[2]{0:T(128)S(1)} %copy-done.11, bf16[16,128,512]{2,1,0:T(8,128)(2,1)S(1)} %constant_dynamic-update-slice_fusion.refs_0_.refs_1_.refs_2_.refs_3_, bf16[16,128,512]{2,1,0:T(8,128)(2,1)S(1)} %constant_dynamic-update-slice_fusion.refs_0_.refs_1_.refs_2_.refs_3_, ...), custom_call_target="tpu_custom_call" | custom-call | bytes 12582912 | tf_op jit(solution)/shard_map/pallas_call | solution.py:515
  (302 shorter events, 86.6 us)
Async XLA Ops:
  7.2 182.6 %all-gather.5.cloned.1.call-start = ((), (), s32[]{:S(2)}) async-start(), calls=%async_computation.2 | async-start | bytes 1671168 | tf_op jit(solution)/shard_map/all_gather | solution.py:702
  8.5 15.0 %collective-permute-start = (bf16[128,2048]{1,0:T(8,128)(2,1)S(1)}, bf16[128,2048]{1,0:T(8,128)(2,1)}, u32[]{:S(2)}, u32[]{:S(2)}) collective-permute-start(bf16[128,2048]{1,0:T(8,128)(2,1)S(1)} %dynamic_slice.76), channel_id=1, source_target_pairs={{0,1},{1,0},{2,3},{3,2},{4,5},{5,4},{6,7},{7,6},{8,9},{9,8},{10,11... | collective-permute-start | bytes 1572872 | tf_op jit(solution)/shard_map/ppermute | solution.py:644
  12.7 26.8 %copy-start.22 = (bf16[128,1024]{1,0:T(8,128)(2,1)}, bf16[128,1024]{1,0:T(8,128)(2,1)S(1)}, u32[]{:S(2)}) copy-start(bf16[128,1024]{1,0:T(8,128)(2,1)S(1)} %get-tuple-element.275) | copy-start | bytes 786436
  23.6 13.4 %collective-permute-start.1 = (bf16[128,2048]{1,0:T(8,128)(2,1)}, bf16[128,2048]{1,0:T(8,128)(2,1)}, u32[]{:S(2)}, u32[]{:S(2)}) collective-permute-start(bf16[128,2048]{1,0:T(8,128)(2,1)} %collective-permute-done), channel_id=1, source_target_pairs={{0,4},{2,6},{4,0},{6,2},{8,12},{10,14},{12,8},{14,10},{16,20},{18,... | collective-permute-start | bytes 1572872 | tf_op jit(solution)/shard_map/ppermute | solution.py:660
  25.3 92.7 %collective-permute-start.6 = (bf16[640,1024]{1,0:T(8,128)(2,1)}, bf16[640,1024]{1,0:T(8,128)(2,1)}, u32[]{:S(2)}, u32[]{:S(2)}) collective-permute-start(bf16[640,1024]{1,0:T(8,128)(2,1)} %pad_maximum_fusion.6.x_ref.refs_0_.x), channel_id=1, source_target_pairs={{0,1},{1,0},{2,3},{3,2},{4,5},{5,4},{6,7},{7,6},{8,9},{9,8},{10,11... | collective-permute-start | bytes 3932168 | tf_op jit(solution)/shard_map/ppermute | solution.py:644
  26.8 91.2 %collective-permute-start.7 = (bf16[640,1024]{1,0:T(8,128)(2,1)}, bf16[640,1024]{1,0:T(8,128)(2,1)}, u32[]{:S(2)}, u32[]{:S(2)}) collective-permute-start(bf16[640,1024]{1,0:T(8,128)(2,1)} %pad_maximum_fusion.7.dy_ref.refs_3_.refs_2_.refs_6_.refs_1_), channel_id=1, source_target_pairs={{0,1},{1,0},{2,3},{3,2},{4,5},{5,4},{6,7},{7,6},{8,9},{9,8},{10,11... | collective-permute-start | bytes 3932168 | tf_op jit(solution)/shard_map/ppermute | solution.py:644
  28.1 64.9 %copy-start.1 = (bf16[640,1024]{1,0:T(8,128)(2,1)}, bf16[640,1024]{1,0:T(8,128)(2,1)S(1)}, u32[]{:S(2)}) copy-start(bf16[640,1024]{1,0:T(8,128)(2,1)S(1)} %pad_maximum_fusion.4.x_ref.refs_0_.x) | copy-start | bytes 3932164
  39.4 47.1 %collective-permute-start.2 = (bf16[256,2048]{1,0:T(8,128)(2,1)}, bf16[256,2048]{1,0:T(8,128)(2,1)}, u32[]{:S(2)}, u32[]{:S(2)}) collective-permute-start(bf16[256,2048]{1,0:T(8,128)(2,1)} %pad_maximum_fusion.8), channel_id=1, source_target_pairs={{0,2},{2,0},{4,6},{6,4},{8,10},{10,8},{12,14},{14,12},{16,18},{18,... | collective-permute-start | bytes 3145736 | tf_op jit(solution)/shard_map/ppermute | solution.py:660
  39.6 54.9 %copy-start.3 = (bf16[640,1024]{1,0:T(8,128)(2,1)}, bf16[640,1024]{1,0:T(8,128)(2,1)S(1)}, u32[]{:S(2)}) copy-start(bf16[640,1024]{1,0:T(8,128)(2,1)S(1)} %pad_maximum_fusion.5.dy_ref.refs_5_.refs_2_.refs_8_.refs_1_) | copy-start | bytes 3932164
  39.9 44.9 %collective-permute-start.5 = (f32[9,512]{1,0:T(8,128)S(1)}, f32[9,512]{1,0:T(8,128)S(1)}, u32[]{:S(2)}, u32[]{:S(2)}) collective-permute-start(f32[9,512]{1,0:T(8,128)S(1)} %concatenate.86), channel_id=1, source_target_pairs={{0,1},{1,0},{2,3},{3,2},{4,5},{5,4},{6,7},{7,6},{8,9},{9,8},{10,11... | collective-permute-start | bytes 55304 | tf_op jit(solution)/shard_map/ppermute | solution.py:644
  42.2 43.6 %collective-permute-start.8 = (bf16[32,1536]{1,0:T(8,128)(2,1)S(1)}, bf16[32,1536]{1,0:T(8,128)(2,1)S(1)}, u32[]{:S(2)}, u32[]{:S(2)}) collective-permute-start(bf16[32,1536]{1,0:T(8,128)(2,1)S(1)} %pad_maximum_fusion.16), channel_id=1, source_target_pairs={{0,1},{1,0},{2,3},{3,2},{4,5},{5,4},{6,7},{7,6},{8,9},{9,8},{10,11... | collective-permute-start | bytes 294920 | tf_op jit(solution)/shard_map/ppermute | solution.py:644
  86.5 224.0 %reduce-scatter.2.cloned.1.call-start = ((), (), s32[]{:S(2)}) async-start(), calls=%async_computation.1 | async-start | bytes 8912896 | tf_op jit(solution)/shard_map/reduce_scatter | solution.py:890
  93.0 64.9 %collective-permute-start.3 = (bf16[640,1024]{1,0:T(8,128)(2,1)S(1)}, bf16[640,1024]{1,0:T(8,128)(2,1)}, u32[]{:S(2)}, u32[]{:S(2)}) collective-permute-start(bf16[640,1024]{1,0:T(8,128)(2,1)S(1)} %pad_maximum_fusion.4.x_ref.refs_0_.x), channel_id=1, source_target_pairs={{0,1},{1,0},{2,3},{3,2},{4,5},{5,4},{6,7},{7,6},{8,9},{9,8},{10,11... | collective-permute-start | bytes 3932168 | tf_op jit(solution)/shard_map/ppermute | solution.py:644
  94.4 63.4 %collective-permute-start.4 = (bf16[640,1024]{1,0:T(8,128)(2,1)S(1)}, bf16[640,1024]{1,0:T(8,128)(2,1)}, u32[]{:S(2)}, u32[]{:S(2)}) collective-permute-start(bf16[640,1024]{1,0:T(8,128)(2,1)S(1)} %pad_maximum_fusion.5.dy_ref.refs_5_.refs_2_.refs_8_.refs_1_), channel_id=1, source_target_pairs={{0,1},{1,0},{2,3},{3,2},{4,5},{5,4},{6,7},{7,6},{8,9},{9,8},{10,11... | collective-permute-start | bytes 3932168 | tf_op jit(solution)/shard_map/ppermute | solution.py:644
  187.0 311.0 %all-gather.7.cloned.1.call-start = ((), (), s32[]{:S(2)}) async-start(), calls=%async_computation.3 | async-start | bytes 8912896 | tf_op jit(solution)/shard_map/all_gather | solution.py:915
  311.4 5.0 collective-permute-start.11
  323.1 21.3 %collective-permute-start.10 = (bf16[8,128,512]{2,1,0:T(8,128)(2,1)}, bf16[8,128,512]{2,1,0:T(8,128)(2,1)}, u32[]{:S(2)}, u32[]{:S(2)}) collective-permute-start(bf16[8,128,512]{2,1,0:T(8,128)(2,1)} %slice.151), channel_id=1, source_target_pairs={{0,2},{2,0},{4,6},{6,4},{8,10},{10,8},{12,14},{14,12},{16,18},{18,... | collective-permute-start | bytes 3145736 | tf_op jit(solution)/shard_map/ppermute | solution.py:660
  323.1 21.3 %collective-permute-start.9 = (bf16[8,128,512]{2,1,0:T(8,128)(2,1)}, bf16[8,128,512]{2,1,0:T(8,128)(2,1)}, u32[]{:S(2)}, u32[]{:S(2)}) collective-permute-start(bf16[8,128,512]{2,1,0:T(8,128)(2,1)} %slice.150), channel_id=1, source_target_pairs={{0,2},{2,0},{4,6},{6,4},{8,10},{10,8},{12,14},{14,12},{16,18},{18,... | collective-permute-start | bytes 3145736 | tf_op jit(solution)/shard_map/ppermute | solution.py:660
  351.2 33.8 %collective-permute-start.13 = (bf16[4,128,512]{2,1,0:T(8,128)(2,1)}, bf16[4,128,512]{2,1,0:T(8,128)(2,1)S(1)}, u32[]{:S(2)}, u32[]{:S(2)}) collective-permute-start(bf16[4,128,512]{2,1,0:T(8,128)(2,1)} %slice.187), channel_id=1, source_target_pairs={{0,8},{2,10},{4,12},{6,14},{8,0},{10,2},{12,4},{14,6},{16,24},{18,... | collective-permute-start | bytes 1572872 | tf_op jit(solution)/shard_map/ppermute | solution.py:660
  352.8 33.0 %collective-permute-start.12 = (bf16[4,128,512]{2,1,0:T(8,128)(2,1)}, bf16[4,128,512]{2,1,0:T(8,128)(2,1)S(1)}, u32[]{:S(2)}, u32[]{:S(2)}) collective-permute-start(bf16[4,128,512]{2,1,0:T(8,128)(2,1)} %slice.186), channel_id=1, source_target_pairs={{0,4},{2,6},{4,0},{6,2},{8,12},{10,14},{12,8},{14,10},{16,20},{18,... | collective-permute-start | bytes 1572872 | tf_op jit(solution)/shard_map/ppermute | solution.py:660
  371.2 65.3 %collective-permute-start.18 = (bf16[640,1024]{1,0:T(8,128)(2,1)}, bf16[640,1024]{1,0:T(8,128)(2,1)S(1)}, u32[]{:S(2)}, u32[]{:S(2)}) collective-permute-start(bf16[640,1024]{1,0:T(8,128)(2,1)} %get-tuple-element.177), channel_id=1, source_target_pairs={{0,1},{1,0},{2,3},{3,2},{4,5},{5,4},{6,7},{7,6},{8,9},{9,8},{10,11... | collective-permute-start | bytes 3932168 | tf_op jit(solution)/shard_map/ppermute | solution.py:644
  372.7 63.8 %collective-permute-start.19 = (bf16[640,1024]{1,0:T(8,128)(2,1)}, bf16[640,1024]{1,0:T(8,128)(2,1)S(1)}, u32[]{:S(2)}, u32[]{:S(2)}) collective-permute-start(bf16[640,1024]{1,0:T(8,128)(2,1)} %get-tuple-element.178), channel_id=1, source_target_pairs={{0,1},{1,0},{2,3},{3,2},{4,5},{5,4},{6,7},{7,6},{8,9},{9,8},{10,11... | collective-permute-start | bytes 3932168 | tf_op jit(solution)/shard_map/ppermute | solution.py:644
  388.6 25.6 %collective-permute-start.15 = (bf16[2,128,512]{2,1,0:T(8,128)(2,1)}, bf16[2,128,512]{2,1,0:T(8,128)(2,1)S(1)}, u32[]{:S(2)}, u32[]{:S(2)}) collective-permute-start(bf16[2,128,512]{2,1,0:T(8,128)(2,1)} %slice.191), channel_id=1, source_target_pairs={{0,16},{2,18},{4,20},{6,22},{8,24},{10,26},{12,28},{14,30},{16,0},... | collective-permute-start | bytes 786440 | tf_op jit(solution)/shard_map/ppermute | solution.py:660
  389.7 24.4 %collective-permute-start.14 = (bf16[2,128,512]{2,1,0:T(8,128)(2,1)}, bf16[2,128,512]{2,1,0:T(8,128)(2,1)}, u32[]{:S(2)}, u32[]{:S(2)}) collective-permute-start(bf16[2,128,512]{2,1,0:T(8,128)(2,1)} %slice.189), channel_id=1, source_target_pairs={{0,8},{2,10},{4,12},{6,14},{8,0},{10,2},{12,4},{14,6},{16,24},{18,... | collective-permute-start | bytes 786440 | tf_op jit(solution)/shard_map/ppermute | solution.py:660
  416.9 28.2 %copy-start.51 = (f32[8,512]{1,0:T(8,128)S(1)}, f32[8,512]{1,0:T(8,128)}, u32[]{:S(2)}) copy-start(f32[8,512]{1,0:T(8,128)} %mul.123) | copy-start | bytes 49156
  416.9 28.2 %copy-start.67 = (f32[8]{0:T(128)S(1)}, f32[8]{0:T(128)}, u32[]{:S(2)}) copy-start(f32[8]{0:T(128)} %mul.125) | copy-start | bytes 100
  417.0 28.8 %copy-start.56 = (f32[3,512]{1,0:T(4,128)S(1)}, f32[3,512]{1,0:T(4,128)}, u32[]{:S(2)}) copy-start(f32[3,512]{1,0:T(4,128)} %get-tuple-element.194) | copy-start | bytes 18436
  417.0 28.8 %copy-start.57 = (f32[3,512]{1,0:T(4,128)S(1)}, f32[3,512]{1,0:T(4,128)}, u32[]{:S(2)}) copy-start(f32[3,512]{1,0:T(4,128)} %get-tuple-element.195) | copy-start | bytes 18436
  417.0 19.5 %collective-permute-start.17 = (bf16[1,128,512]{2,1,0:T(8,128)(2,1)S(1)}, bf16[1,128,512]{2,1,0:T(8,128)(2,1)S(1)}, u32[]{:S(2)}, u32[]{:S(2)}) collective-permute-start(bf16[1,128,512]{2,1,0:T(8,128)(2,1)S(1)} %slice.194), channel_id=1, source_target_pairs={{0,4},{2,6},{4,0},{6,2},{8,12},{10,14},{12,8},{14,10},{16,20},{18,... | collective-permute-start | bytes 393224 | tf_op jit(solution)/shard_map/ppermute | solution.py:660
  417.6 18.9 %collective-permute-start.16 = (bf16[1,128,512]{2,1,0:T(8,128)(2,1)S(1)}, bf16[1,128,512]{2,1,0:T(8,128)(2,1)S(1)}, u32[]{:S(2)}, u32[]{:S(2)}) collective-permute-start(bf16[1,128,512]{2,1,0:T(8,128)(2,1)S(1)} %slice.192), channel_id=1, source_target_pairs={{0,16},{2,18},{4,20},{6,22},{8,24},{10,26},{12,28},{14,30},{16,0},... | collective-permute-start | bytes 393224 | tf_op jit(solution)/shard_map/ppermute | solution.py:660
  436.6 4.3 collective-permute-start.24
  438.2 4.3 collective-permute-start.20
  441.0 7.6 %collective-permute-start.25 = (bf16[1,128,512]{2,1,0:T(8,128)(2,1)S(1)}, bf16[1,128,512]{2,1,0:T(8,128)(2,1)}, u32[]{:S(2)}, u32[]{:S(2)}) collective-permute-start(bf16[1,128,512]{2,1,0:T(8,128)(2,1)S(1)} %maximum_bitcast_fusion.1), channel_id=1, source_target_pairs={{0,4},{2,6},{4,0},{6,2},{8,12},{10,14},{12,8},{14,10},{16,20},{18,... | collective-permute-start | bytes 393224 | tf_op jit(solution)/shard_map/ppermute | solution.py:660
  443.3 14.5 %collective-permute-start.21 = (bf16[1,128,512]{2,1,0:T(8,128)(2,1)}, bf16[1,128,512]{2,1,0:T(8,128)(2,1)}, u32[]{:S(2)}, u32[]{:S(2)}) collective-permute-start(bf16[1,128,512]{2,1,0:T(8,128)(2,1)} %maximum_bitcast_fusion), channel_id=1, source_target_pairs={{0,16},{2,18},{4,20},{6,22},{8,24},{10,26},{12,28},{14,30},{16,0},... | collective-permute-start | bytes 393224 | tf_op jit(solution)/shard_map/ppermute | solution.py:660
  446.4 61.0 %collective-permute-start.28 = (bf16[640,1024]{1,0:T(8,128)(2,1)}, bf16[640,1024]{1,0:T(8,128)(2,1)S(1)}, u32[]{:S(2)}, u32[]{:S(2)}) collective-permute-start(bf16[640,1024]{1,0:T(8,128)(2,1)} %get-tuple-element.186), channel_id=1, source_target_pairs={{0,1},{1,0},{2,3},{3,2},{4,5},{5,4},{6,7},{7,6},{8,9},{9,8},{10,11... | collective-permute-start | bytes 3932168 | tf_op jit(solution)/shard_map/ppermute | solution.py:644
  447.6 59.9 %collective-permute-start.29 = (bf16[640,1024]{1,0:T(8,128)(2,1)}, bf16[640,1024]{1,0:T(8,128)(2,1)}, u32[]{:S(2)}, u32[]{:S(2)}) collective-permute-start(bf16[640,1024]{1,0:T(8,128)(2,1)} %get-tuple-element.187), channel_id=1, source_target_pairs={{0,1},{1,0},{2,3},{3,2},{4,5},{5,4},{6,7},{7,6},{8,9},{9,8},{10,11... | collective-permute-start | bytes 3932168 | tf_op jit(solution)/shard_map/ppermute | solution.py:644
  449.5 13.0 %collective-permute-start.26 = (bf16[2,128,512]{2,1,0:T(8,128)(2,1)S(1)}, bf16[2,128,512]{2,1,0:T(8,128)(2,1)S(1)}, u32[]{:S(2)}, u32[]{:S(2)}) collective-permute-start(bf16[2,128,512]{2,1,0:T(8,128)(2,1)S(1)} %pad_maximum_fusion.15), channel_id=1, source_target_pairs={{0,16},{2,18},{4,20},{6,22},{8,24},{10,26},{12,28},{14,30},{16,0},... | collective-permute-start | bytes 786440 | tf_op jit(solution)/shard_map/ppermute | solution.py:660
  458.8 9.3 %collective-permute-start.22 = (bf16[2,128,512]{2,1,0:T(8,128)(2,1)S(1)}, bf16[2,128,512]{2,1,0:T(8,128)(2,1)S(1)}, u32[]{:S(2)}, u32[]{:S(2)}) collective-permute-start(bf16[2,128,512]{2,1,0:T(8,128)(2,1)S(1)} %pad_maximum_fusion.14), channel_id=1, source_target_pairs={{0,8},{2,10},{4,12},{6,14},{8,0},{10,2},{12,4},{14,6},{16,24},{18,... | collective-permute-start | bytes 786440 | tf_op jit(solution)/shard_map/ppermute | solution.py:660
  462.4 20.4 %copy-start.24 = (bf16[2,128,512]{2,1,0:T(8,128)(2,1)}, bf16[2,128,512]{2,1,0:T(8,128)(2,1)S(1)}, u32[]{:S(2)}) copy-start(bf16[2,128,512]{2,1,0:T(8,128)(2,1)S(1)} %collective-permute-done.26) | copy-start | bytes 786436
  464.3 43.2 %collective-permute-start.27 = (bf16[4,128,512]{2,1,0:T(8,128)(2,1)}, bf16[4,128,512]{2,1,0:T(8,128)(2,1)}, u32[]{:S(2)}, u32[]{:S(2)}) collective-permute-start(bf16[4,128,512]{2,1,0:T(8,128)(2,1)} %pad_maximum_fusion.13), channel_id=1, source_target_pairs={{0,8},{2,10},{4,12},{6,14},{8,0},{10,2},{12,4},{14,6},{16,24},{18,... | collective-permute-start | bytes 1572872 | tf_op jit(solution)/shard_map/ppermute | solution.py:660
  470.0 37.5 %collective-permute-start.23 = (bf16[4,128,512]{2,1,0:T(8,128)(2,1)}, bf16[4,128,512]{2,1,0:T(8,128)(2,1)}, u32[]{:S(2)}, u32[]{:S(2)}) collective-permute-start(bf16[4,128,512]{2,1,0:T(8,128)(2,1)} %pad_maximum_fusion.12), channel_id=1, source_target_pairs={{0,4},{2,6},{4,0},{6,2},{8,12},{10,14},{12,8},{14,10},{16,20},{18,... | collective-permute-start | bytes 1572872 | tf_op jit(solution)/shard_map/ppermute | solution.py:660
  472.4 10.5 %collective-permute-start.30 = (f32[24,512]{1,0:T(8,128)S(1)}, f32[24,512]{1,0:T(8,128)}, u32[]{:S(2)}, u32[]{:S(2)}) collective-permute-start(f32[24,512]{1,0:T(8,128)S(1)} %concatenate.97), channel_id=1, source_target_pairs={{0,2},{2,0},{4,6},{6,4},{8,10},{10,8},{12,14},{14,12},{16,18},{18,... | collective-permute-start | bytes 147464 | tf_op jit(solution)/shard_map/ppermute | solution.py:660
  483.7 4.4 collective-permute-start.31
  488.1 4.2 collective-permute-start.32
  492.3 5.1 collective-permute-start.33
  509.7 15.8 %collective-permute-start.36 = (bf16[8,128,512]{2,1,0:T(8,128)(2,1)}, bf16[8,128,512]{2,1,0:T(8,128)(2,1)}, u32[]{:S(2)}, u32[]{:S(2)}) collective-permute-start(bf16[8,128,512]{2,1,0:T(8,128)(2,1)} %pad_maximum_fusion.10), channel_id=1, source_target_pairs={{0,2},{2,0},{4,6},{6,4},{8,10},{10,8},{12,14},{14,12},{16,18},{18,... | collective-permute-start | bytes 3145736 | tf_op jit(solution)/shard_map/ppermute | solution.py:660
  512.1 15.7 %collective-permute-start.35 = (bf16[8,128,512]{2,1,0:T(8,128)(2,1)}, bf16[8,128,512]{2,1,0:T(8,128)(2,1)}, u32[]{:S(2)}, u32[]{:S(2)}) collective-permute-start(bf16[8,128,512]{2,1,0:T(8,128)(2,1)} %pad_maximum_fusion.9), channel_id=1, source_target_pairs={{0,2},{2,0},{4,6},{6,4},{8,10},{10,8},{12,14},{14,12},{16,18},{18,... | collective-permute-start | bytes 3145736 | tf_op jit(solution)/shard_map/ppermute | solution.py:660
  514.5 9.2 %collective-permute-start.34 = (f32[24,512]{1,0:T(8,128)S(1)}, f32[24,512]{1,0:T(8,128)S(1)}, u32[]{:S(2)}, u32[]{:S(2)}) collective-permute-start(f32[24,512]{1,0:T(8,128)S(1)} %copy-done.47), channel_id=1, source_target_pairs={{0,1},{1,0},{2,3},{3,2},{4,5},{5,4},{6,7},{7,6},{8,9},{9,8},{10,11... | collective-permute-start | bytes 147464 | tf_op jit(solution)/shard_map/ppermute | solution.py:644
  (60 other events, 303.6 us)
Sparse Core Ops, SparseCore 0:
  86.6 39.9 all-gather.4
  187.1 104.9 reduce-scatter.1
  318.4 97.6 all-gather.6

commit v6 on v5

--- a/solution.py
+++ b/solution.py
@@ -581,7 +581,7 @@
         scratch_shapes=[pltpu.VMEM((N, D), F32)] * 3,
         compiler_params=pltpu.CompilerParams(vmem_limit_bytes=60 * MIB),
         cost_estimate=pl.CostEstimate(
-            flops=4 * N * D * FL + 8 * N * D * CW, bytes_accessed=4 * (N + D) * FL + 8 * (N + D) * CW + 6 * N * D, transcendentals=0
+            flops=N * D * FL // 8, bytes_accessed=N * D, transcendentals=0
         ),
     )(act, dpre, wu, wd, dl, ctx, wqkv, wo, x, gb)
 
@@ -686,7 +686,7 @@
         piece, _ = lax.optimization_barrier((piece, ahead))
         pair = both(piece, exchanged(piece, R, 2), y == 0)
         slots.append(both(pair, exchanged(pair, R, 1), core == 0))
-    return jnp.concatenate(canonical(slots, me, S, True), axis=0), piece
+    return jnp.concatenate(canonical(slots, me, S, True), axis=0), cut[0]
 
 
 def my_columns(weight, me, S, R, parts):
@@ -844,6 +844,7 @@
 
     tabs = rotary_tables(PD * S, CR * S, CL)
     src = [(X[m][0], DY[m][0]) for m in range(MB)]
+    src[0], small = lax.optimization_barrier((src[0], small))
     src[1:], w_up = lax.optimization_barrier((src[1:], w_up))
     for m in range(MB):
         for j in range(1, S):
@@ -909,37 +910,51 @@
     hs, dls, ctxs = [[r[k] for r in rest] for k in (2, 0, 1)]
     if chunked:
         q = jnp.stack([place(rep, order) for order in orders(R)]).astype(jnp.int32)
+        part = swap_shards(part, me, S, FL // R)
+        hs, part = lax.optimization_barrier((hs, part))
+        gmlp_all = lax.all_gather(part, "rep", axis=0, tiled=False)
         gatt = attn_grads(S, R, q, hs, dls, ctxs, [DY[m][j] for m in range(MB) for j in range(S)])
-        part, gatt = lax.optimization_barrier((part, gatt))
-        part = swap_shards(part, me, S, FL // R)
-        gmlp_all = lax.all_gather(part, "rep", axis=0, tiled=False)
-        dls, _ = lax.optimization_barrier(([r[0] for r in rest], part))
-        for m in range(MB):
-            rest[m][0] = dls[m]
         levels = R.bit_length() - 1
-        beside = {}
+        beside, after = {}, {}
         far, mine = [], []
+
+        def behind(value):
+            dls, value = lax.optimization_barrier(([r[0] for r in rest], value))
+            for k in range(MB):
+                rest[k][0] = dls[k]
+            return value
+
+        behind(gatt)
         for m in range(MB):
             far.append(far_rows(m))
-            beside.setdefault(min(m, levels - 1), {})["far", m] = far[m][1]
-            dls, beside[min(m, levels - 1)] = lax.optimization_barrier(([r[0] for r in rest], beside[min(m, levels - 1)]))
-            for k in range(MB):
-                rest[k][0] = dls[k]
+            at = min(m + 1, levels - 1)
+            beside.setdefault(at, {})["far", m] = behind(far[m][1])
         for m in range(MB):
             mine.append(rows(m, 0))
-            beside.setdefault(min(MB + m, levels - 1), {})["own", m] = mine[m]
+            if m == 0:
+                beside.setdefault(levels - 1, {})["own", m] = behind(mine[m])
+            else:
+                after.setdefault(levels - 2, {})["own", m] = mine[m]
         beside.setdefault(levels - 1, {})["got", 0] = far[0][0]
         half = halving(gatt, R, beside)
-        done = {k: v for d in beside.values() for k, v in d.items()}
-        sums = [v for m in range(MB) for v in done["far", m]]
-        mine = [done["own", m] for m in range(MB)]
-        vecs = sum_all(vectors(sums + [o[2] for o in mine]), S, R)
-        got = [f[0] for f in far]
-        got[0] = done["got", 0]
-        beside = {1: (got[1:], mlp_finish(S, gmlp_all, FL), vecs)}
+        for d in beside.values():
+            for (kind, m), v in d.items():
+                if kind == "far":
+                    far[m] = (far[m][0], v)
+                elif kind == "got":
+                    far[m] = (v, far[m][1])
+                else:
+                    mine[m] = v
+        sums = [v for f in far for v in f[1]] + [o[2] for o in mine]
+        after[1] = {("vec", 0): sum_all(vectors(sums), S, R), ("mlp", 0): mlp_finish(S, gmlp_all, FL)}
+        after[1].update({("got", m): far[m][0] for m in range(1, MB)})
         k = D // CW * (D // S // R)
-        g1, g2 = doubling([swap_shards(half[0], me, S, 0), swap_shards(half[1], me, S, k)], R, beside)
-        got[1:], (g_down, g_up), vecs = beside[1]
+        g1, g2 = doubling([swap_shards(half[0], me, S, 0), swap_shards(half[1], me, S, k)], R, after)
+        done = {k_: v for d in after.values() for k_, v in d.items()}
+        got = [done.get(("got", m), far[m][0]) for m in range(MB)]
+        mine = [done.get(("own", m), mine[m]) for m in range(MB)]
+        vecs = done["vec", 0]
+        g_down, g_up = done["mlp", 0]
         outs = None
         for m in range(MB):
             outs = finals(m, mine[m], got[m], outs)

time: 549 us -> 532 us (0.969)
  waiting for transfers between devices: 100 us -> 82.9 us
    ppermute x22, waiting for transfers between devices: 47 us -> 28.1 us  [exchanged(): return lax.ppermute(value, 'rep', [(i, i ^ bit) for i in range(R)])]
    unnamed x145 -> x171, local copies, waits for them, and re-layouts: 21.7 us -> 19.9 us
  transfers between devices with their start and end apart: 40 -> 40, of which waited for: 15 -> 15; matrix products, arithmetic and copies ran while one was open for 12% -> 12% of each run, Pallas kernels for 55% -> 57%
where the time goes in v6:
time: 532 us; the launch traced here: 526 us
  Pallas kernels  307 us (58%)
  waiting for transfers between devices  82.9 us (16%)
  local copies, waits for them, and re-layouts  46.2 us (9%)
  starting transfers between devices  37.9 us (7%)
  other arithmetic  36.9 us (7%)
  between operations  15.3 us (3%)
    pallas_call x2, Pallas kernels, attn_group(): pl.pallas_call(functools.partial(attn_kernel, S, PD, CL, QB, HG), grid_sp...  98.5 us
    pallas_call x4, Pallas kernels, branch_rows(): pl.pallas_call(rows_kernel, grid=(FL // fb,), in_specs=[rows, rows, pl.Bl...  72.1 us
    ppermute x15, waiting for transfers between devices, shifted(): return lax.ppermute(value, 'shard', [(i, (i + j) % S) for i in range(S)])  53.4 us
    pallas_call x4, Pallas kernels, call(): pl.pallas_call(functools.partial(kernel, n, more), grid=(a[0].shape[1] //...  46.1 us
    pallas_call x4, Pallas kernels, mlp_rows(): pl.pallas_call(functools.partial(mlp_kernel, rows_tile(rows, 640)), grid=...  45.8 us
    ppermute x22, waiting for transfers between devices, exchanged(): return lax.ppermute(value, 'rep', [(i, i ^ bit) for i in range(R)])  28.1 us
    unnamed x171, local copies, waits for them, and re-layouts  19.9 us
    pallas_call x1, Pallas kernels, attn_grads(): pl.pallas_call(functools.partial(attn_grads_kernel, n, S, R), grid_spec=p...  19.5 us
  transfers between devices with their start and end apart: 40, of which 15 were waited for; matrix products, arithmetic and copies ran while one was open for 12% of the time, Pallas kernels for 57%

profile of v6, /device:TPU:0, one launch (start us, length us, event | category | flops | bytes accessed | tf_op | source)
XLA Modules:
  0.0 526.0 jit_solution(8421598704136049002)
XLA Ops:
  8.5 3.0 collective-permute-start.3
  11.5 1.8 slice_bitcast_fusion.6
  18.0 5.4 %collective-permute-done.3 = bf16[128,2048]{1,0:T(8,128)(2,1)S(1)} collective-permute-done((bf16[128,2048]{1,0:T(8,128)(2,1)S(1)}, bf16[128,2048]{1,0:T(8,128)(2,1)S(1)}, u32[]{:S(2)}, u32[]{:S(2)}) %collective-permute-start.3) | collective-permute-done | bytes 524320 | tf_op jit(solution)/shard_map/ppermute | solution.py:644
  23.4 1.8 collective-permute-start.4
  28.4 8.1 %collective-permute-done.4 = bf16[128,2048]{1,0:T(8,128)(2,1)S(1)} collective-permute-done((bf16[128,2048]{1,0:T(8,128)(2,1)S(1)}, bf16[128,2048]{1,0:T(8,128)(2,1)S(1)}, u32[]{:S(2)}, u32[]{:S(2)}) %collective-permute-start.4) | collective-permute-done | bytes 524320 | tf_op jit(solution)/shard_map/ppermute | solution.py:660
  47.0 2.0 broadcast_select_fusion.5
  50.8 2.6 pad_maximum_fusion.wu_ref.wu
  55.4 11.6 %shard_map.308 = (bf16[640,2048]{1,0:T(8,128)(2,1)}, bf16[640,2048]{1,0:T(8,128)(2,1)}, bf16[640,1024]{1,0:T(8,128)(2,1)}, f32[1,2048]{1,0:T(1,128)}) custom-call(bf16[640,1024]{1,0:T(8,128)(2,1)} %copy-done, bf16[640,1024]{1,0:T(8,128)(2,1)} %pad_maximum_fusion.5.dy_ref.refs_5_.refs_2_.refs_8_.refs_1_, bf16[1024,2048]{1,0:T(8,128)(2,1)} %pad_maximum_fusion.wu_ref.wu, ...), custom_call_target="tpu_custom_call" | custom-call | flops 5368709120 | bytes 17563648 | tf_op jit(solution)/shard_map/pallas_call | solution.py:81
  67.0 11.4 %shard_map.306 = (bf16[640,2048]{1,0:T(8,128)(2,1)}, bf16[640,2048]{1,0:T(8,128)(2,1)}, bf16[640,1024]{1,0:T(8,128)(2,1)}, f32[1,2048]{1,0:T(1,128)}) custom-call(bf16[640,1024]{1,0:T(8,128)(2,1)} %copy-done.2, bf16[640,1024]{1,0:T(8,128)(2,1)} %get-tuple-element.132.dy_ref.refs_3_.refs_2_.refs_6_.refs_1_, bf16[1024,2048]{1,0:T(8,128)(2,1)} %pad_maximum_fusion.wu_ref.wu, ...), custom_call_target="tpu_custom_call" | custom-call | flops 5368709120 | bytes 17563648 | tf_op jit(solution)/shard_map/pallas_call | solution.py:81
  78.4 23.1 %collective-permute-done.1.dy_ref.refs_4_.refs_3_.refs_7_ = bf16[640,1024]{1,0:T(8,128)(2,1)} collective-permute-done((bf16[640,1024]{1,0:T(8,128)(2,1)}, bf16[640,1024]{1,0:T(8,128)(2,1)}, u32[]{:S(2)}, u32[]{:S(2)}) %collective-permute-start.1) | collective-permute-done | bytes 1310752 | tf_op jit(solution)/shard_map/ppermute | solution.py:644
  101.5 11.4 %shard_map.307 = (bf16[640,2048]{1,0:T(8,128)(2,1)}, bf16[640,2048]{1,0:T(8,128)(2,1)}, bf16[640,1024]{1,0:T(8,128)(2,1)}, f32[1,2048]{1,0:T(1,128)}) custom-call(bf16[640,1024]{1,0:T(8,128)(2,1)} %collective-permute-done.x_ref.refs_1_.x, bf16[640,1024]{1,0:T(8,128)(2,1)} %collective-permute-done.1.dy_ref.refs_4_.refs_3_.refs_7_, ...), custom_call_target="tpu_custom_call" | custom-call | flops 5368709120 | bytes 17563648 | tf_op jit(solution)/shard_map/pallas_call | solution.py:81
  112.8 14.0 %shard_map.309.refs_6_ = bf16[16,256,1024]{2,1,0:T(8,128)(2,1)} custom-call(bf16[640,2048]{1,0:T(8,128)(2,1)} %get-tuple-element.144.refs_0_.act, bf16[640,2048]{1,0:T(8,128)(2,1)} %get-tuple-element.145.refs_1_.act, bf16[640,2048]{1,0:T(8,128)(2,1)} %get-tuple-element.146.refs_2_.act, ...), custom_call_target="tpu_custom_call" | custom-call | flops 8053063680 | bytes 15990784 | tf_op jit(solution)/shard_map/pallas_call | solution.py:386
  126.8 14.4 %shard_map.310.refs_2_ = bf16[16,256,1024]{2,1,0:T(8,128)(2,1)} custom-call(bf16[640,1024]{1,0:T(8,128)(2,1)} %get-tuple-element.138.refs_0_, bf16[640,1024]{1,0:T(8,128)(2,1)} %get-tuple-element.139.refs_1_, bf16[640,1024]{1,0:T(8,128)(2,1)} %get-tuple-element.140.refs_2_, ...), custom_call_target="tpu_custom_call", output_to_operand_aliasing={{}: (6, {})} | custom-call | flops 8053063680 | bytes 15990784 | tf_op jit(solution)/shard_map/pallas_call | solution.py:386
  141.2 16.1 %collective-permute-done.7.dy_ref.refs_1_.refs_3_.refs_9_ = bf16[640,1024]{1,0:T(8,128)(2,1)} collective-permute-done((bf16[640,1024]{1,0:T(8,128)(2,1)}, bf16[640,1024]{1,0:T(8,128)(2,1)}, u32[]{:S(2)}, u32[]{:S(2)}) %collective-permute-start.7) | collective-permute-done | bytes 1310752 | tf_op jit(solution)/shard_map/ppermute | solution.py:644
  157.3 11.4 %shard_map.311 = (bf16[640,2048]{1,0:T(8,128)(2,1)}, bf16[640,2048]{1,0:T(8,128)(2,1)}, bf16[640,1024]{1,0:T(8,128)(2,1)}, f32[1,2048]{1,0:T(1,128)}) custom-call(bf16[640,1024]{1,0:T(8,128)(2,1)} %collective-permute-done.6.x_ref.refs_1_.x, bf16[640,1024]{1,0:T(8,128)(2,1)} %collective-permute-done.7.dy_ref.refs_1_.refs_3_.refs_9_, ...), custom_call_target="tpu_custom_call" | custom-call | flops 5368709120 | bytes 17563648 | tf_op jit(solution)/shard_map/pallas_call | solution.py:81
  168.7 9.6 %shard_map.312.refs_2_ = bf16[16,256,1024]{2,1,0:T(8,128)(2,1)} custom-call(bf16[640,2048]{1,0:T(8,128)(2,1)} %get-tuple-element.150.refs_0_.act, bf16[640,1024]{1,0:T(8,128)(2,1)} %collective-permute-done.7.dy_ref.refs_1_.refs_3_.refs_9_, bf16[16,256,1024]{2,1,0:T(8,128)(2,1)} %shard_map.310.refs_2_), custom_call_target="tpu_custom_call", output_to_operand_aliasing={{}: (2, {})} | custom-call | flops 2684354560 | bytes 12320768 | tf_op jit(solution)/shard_map/pallas_call | solution.py:386
  178.3 8.1 %shard_map.313 = bf16[16,256,1024]{2,1,0:T(8,128)(2,1)} custom-call(bf16[640,1024]{1,0:T(8,128)(2,1)} %get-tuple-element.148.refs_0_, bf16[640,2048]{1,0:T(8,128)(2,1)} %get-tuple-element.149.refs_1_.dpre, bf16[16,256,1024]{2,1,0:T(8,128)(2,1)} %shard_map.312.refs_2_), custom_call_target="tpu_custom_call", output_to_operand_aliasing={{}: (2, {})} | custom-call | flops 2684354560 | bytes 12320768 | tf_op jit(solution)/shard_map/pallas_call | solution.py:386
  188.6 2.0 broadcast_select_fusion.3
  190.6 2.0 pad_maximum_fusion.1.refs_4_.refs_5_.refs_6_.wqkv
  192.6 49.7 %shard_map.314 = (bf16[3,1280,512]{2,1,0:T(8,128)(2,1)}, bf16[1280,512]{1,0:T(8,128)(2,1)}, bf16[1280,1024]{1,0:T(8,128)(2,1)}, f32[3,512]{1,0:T(4,128)}) custom-call(s32[1]{0:T(128)} %bitcast.6.me_ref, bf16[640,1024]{1,0:T(8,128)(2,1)} %copy-done.2, bf16[640,1024]{1,0:T(8,128)(2,1)} %collective-permute-done.x_ref.refs_1_.x, ...), custom_call_target="tpu_custom_call" | custom-call | flops 38923141120 | bytes 17301504 | tf_op jit(solution)/shard_map/pallas_call | solution.py:292
  242.3 48.8 %shard_map.315 = (bf16[3,1280,512]{2,1,0:T(8,128)(2,1)}, bf16[1280,512]{1,0:T(8,128)(2,1)}, bf16[1280,1024]{1,0:T(8,128)(2,1)}, f32[3,512]{1,0:T(4,128)}) custom-call(s32[1]{0:T(128)} %bitcast.6.me_ref, bf16[640,1024]{1,0:T(8,128)(2,1)} %copy-done, bf16[640,1024]{1,0:T(8,128)(2,1)} %collective-permute-done.6.x_ref.refs_1_.x, ...), custom_call_target="tpu_custom_call" | custom-call | flops 38923141120 | bytes 17301504 | tf_op jit(solution)/shard_map/pallas_call | solution.py:292
  295.9 2.8 collective-permute-done.9
  301.2 19.5 %shard_map.316 = (bf16[16,128,512]{2,1,0:T(8,128)(2,1)}, bf16[16,128,512]{2,1,0:T(8,128)(2,1)}) custom-call(s32[2]{0:T(128)} %pad_add_fusion.q_ref, bf16[1280,1024]{1,0:T(8,128)(2,1)} %get-tuple-element.157.refs_0_, bf16[1280,1024]{1,0:T(8,128)(2,1)} %get-tuple-element.158.refs_1_, bf16[3,1280,512]{2,1,0:T(8,128)(2,1)} %get-tuple-element.179.refs_2_.dl, ...), custom_call_target="tpu_custom_call" | custom-call | flops 10737418240 | bytes 25165824 | tf_op jit(solution)/shard_map/pallas_call | solution.py:475
  322.9 2.0 collective-permute-done.12
  325.3 1.5 collective-permute-start.13
  330.4 18.0 %shard_map.317 = (bf16[640,1024]{1,0:T(8,128)(2,1)}, bf16[640,1024]{1,0:T(8,128)(2,1)}, f32[4,1024]{1,0:T(4,128)}) custom-call(bf16[640,2048]{1,0:T(8,128)(2,1)} %get-tuple-element.145.refs_1_.act, bf16[640,2048]{1,0:T(8,128)(2,1)} %get-tuple-element.142.refs_4_.dpre, bf16[1024,2048]{1,0:T(8,128)(2,1)} %pad_maximum_fusion.wu_ref.wu, bf16[2048,1024]{1,0:T(8,128)(2,1)} %wd.7, ...), custom_call_target="tpu_custom_call" | custom-call | flops 167772160 | bytes 655360 | tf_op jit(solution)/shard_map/pallas_call | solution.py:570
  354.2 1.7 collective-permute-start.15
  358.2 18.1 %shard_map.318 = (bf16[640,1024]{1,0:T(8,128)(2,1)}, bf16[640,1024]{1,0:T(8,128)(2,1)}, f32[4,1024]{1,0:T(4,128)}) custom-call(bf16[640,2048]{1,0:T(8,128)(2,1)} %get-tuple-element.150.refs_0_.act, bf16[640,2048]{1,0:T(8,128)(2,1)} %get-tuple-element.149.refs_1_.dpre, bf16[1024,2048]{1,0:T(8,128)(2,1)} %pad_maximum_fusion.wu_ref.wu, bf16[2048,1024]{1,0:T(8,128)(2,1)} %wd.7, ...), custom_call_target="tpu_custom_call" | custom-call | flops 167772160 | bytes 655360 | tf_op jit(solution)/shard_map/pallas_call | solution.py:570
  376.3 4.2 collective-permute-done.15
  385.9 18.2 %shard_map.319 = (bf16[640,1024]{1,0:T(8,128)(2,1)}, bf16[640,1024]{1,0:T(8,128)(2,1)}, f32[4,1024]{1,0:T(4,128)}) custom-call(bf16[640,2048]{1,0:T(8,128)(2,1)} %get-tuple-element.144.refs_0_.act, bf16[640,2048]{1,0:T(8,128)(2,1)} %get-tuple-element.141.refs_3_.dpre, bf16[1024,2048]{1,0:T(8,128)(2,1)} %pad_maximum_fusion.wu_ref.wu, bf16[2048,1024]{1,0:T(8,128)(2,1)} %wd.7, ...), custom_call_target="tpu_custom_call" | custom-call | flops 167772160 | bytes 655360 | tf_op jit(solution)/shard_map/pallas_call | solution.py:570
  404.1 3.0 collective-permute-done.19.refs_5_
  410.4 1.8 collective-permute-done.23
  414.2 2.1 collective-permute-start.21
  420.6 4.3 collective-permute-done.21
  431.1 17.9 %shard_map.320 = (bf16[640,1024]{1,0:T(8,128)(2,1)}, bf16[640,1024]{1,0:T(8,128)(2,1)}, f32[4,1024]{1,0:T(4,128)}) custom-call(bf16[640,2048]{1,0:T(8,128)(2,1)} %get-tuple-element.146.refs_2_.act, bf16[640,2048]{1,0:T(8,128)(2,1)} %get-tuple-element.143.refs_5_.dpre, bf16[1024,2048]{1,0:T(8,128)(2,1)} %pad_maximum_fusion.wu_ref.wu, bf16[2048,1024]{1,0:T(8,128)(2,1)} %wd.7, ...), custom_call_target="tpu_custom_call" | custom-call | flops 167772160 | bytes 655360 | tf_op jit(solution)/shard_map/pallas_call | solution.py:570
  449.9 2.0 collective-permute-start.27
  460.3 6.2 %shard_map.322 = (bf16[2,512,1024]{2,1,0:T(8,128)(2,1)}, bf16[2,128,1024]{2,1,0:T(8,128)(2,1)}, f32[2,512,1024]{2,1,0:T(8,128)}, f32[2,128,1024]{2,1,0:T(8,128)}) custom-call(bf16[640,1024]{1,0:T(8,128)(2,1)S(1)} %copy-done.3, bf16[640,1024]{1,0:T(8,128)(2,1)} %get-tuple-element.132.dy_ref.refs_3_.refs_2_.refs_6_.refs_1_, bf16[640,1024]{1,0:T(8,128)(2,1)S(1)} %copy-done.11, ...), custom_call_target="tpu_custom_call" | custom-call | flops 13107200 | bytes 11796480 | tf_op jit(solution)/shard_map/pallas_call | solution.py:631
  468.7 2.1 collective-permute-done.31
  470.9 4.0 collective-permute-done.32
  476.8 3.4 collective-permute-done.33
  480.8 3.4 copy-done.4
  484.3 6.1 %shard_map.321 = (f32[2048,1024]{1,0:T(8,128)}, f32[512,4096]{1,0:T(8,128)}) custom-call(bf16[16,256,1024]{2,1,0:T(8,128)(2,1)S(1)} %bitcast.79), custom_call_target="tpu_custom_call" | custom-call | bytes 25165824 | tf_op jit(solution)/shard_map/pallas_call | solution.py:421
  490.4 2.2 pad_maximum_fusion.10
  492.6 2.2 pad_maximum_fusion.9
  498.6 1.9 constant_dynamic-update-slice_fusion.6
  500.4 6.4 %shard_map.323 = (bf16[2,512,1024]{2,1,0:T(8,128)(2,1)}, bf16[2,128,1024]{2,1,0:T(8,128)(2,1)}, f32[2,512,1024]{2,1,0:T(8,128)}, f32[2,128,1024]{2,1,0:T(8,128)}) custom-call(bf16[640,1024]{1,0:T(8,128)(2,1)S(1)} %copy-done.1, ...), custom_call_target="tpu_custom_call", output_to_operand_aliasing={{0}: (7, {}), {1}: (8, {}), {2}: (9, {}), {3}: (10, {})} | custom-call | flops 13107200 | bytes 11796480 | tf_op jit(solution)/shard_map/pallas_call | solution.py:631
  508.7 2.3 constant_dynamic-update-slice_fusion.5.refs_4_.refs_5_.refs_6_.refs_7_
  512.4 6.0 %shard_map.324 = (f32[512,1024]{1,0:T(8,128)}, f32[512,3072]{1,0:T(8,128)}) custom-call(s32[2]{0:T(128)S(1)} %copy-done.13, bf16[16,128,512]{2,1,0:T(8,128)(2,1)S(1)} %constant_dynamic-update-slice_fusion.refs_0_.refs_1_.refs_2_.refs_3_, bf16[16,128,512]{2,1,0:T(8,128)(2,1)S(1)} %constant_dynamic-update-slice_fusion.refs_0_.refs_1_.refs_2_.refs_3_, ...), custom_call_target="tpu_custom_call" | custom-call | bytes 12582912 | tf_op jit(solution)/shard_map/pallas_call | solution.py:515
  (327 shorter events, 89.3 us)
Async XLA Ops:
  7.2 181.4 %all-gather.5.cloned.1.call-start = ((), (), s32[]{:S(2)}) async-start(), calls=%async_computation.2 | async-start | bytes 1671168 | tf_op jit(solution)/shard_map/all_gather | solution.py:702
  8.5 14.9 %collective-permute-start.3 = (bf16[128,2048]{1,0:T(8,128)(2,1)S(1)}, bf16[128,2048]{1,0:T(8,128)(2,1)S(1)}, u32[]{:S(2)}, u32[]{:S(2)}) collective-permute-start(bf16[128,2048]{1,0:T(8,128)(2,1)S(1)} %dynamic_slice.79), channel_id=1, source_target_pairs={{0,1},{1,0},{2,3},{3,2},{4,5},{5,4},{6,7},{7,6},{8,9},{9,8},{10,11... | collective-permute-start | bytes 1572872 | tf_op jit(solution)/shard_map/ppermute | solution.py:644
  15.4 27.5 %copy-start.25 = (bf16[128,1024]{1,0:T(8,128)(2,1)}, bf16[128,1024]{1,0:T(8,128)(2,1)S(1)}, u32[]{:S(2)}) copy-start(bf16[128,1024]{1,0:T(8,128)(2,1)S(1)} %get-tuple-element.285) | copy-start | bytes 786436
  23.4 13.1 %collective-permute-start.4 = (bf16[128,2048]{1,0:T(8,128)(2,1)S(1)}, bf16[128,2048]{1,0:T(8,128)(2,1)S(1)}, u32[]{:S(2)}, u32[]{:S(2)}) collective-permute-start(bf16[128,2048]{1,0:T(8,128)(2,1)S(1)} %collective-permute-done.3), channel_id=1, source_target_pairs={{0,4},{2,6},{4,0},{6,2},{8,12},{10,14},{12,8},{14,10},{16,20},{18,... | collective-permute-start | bytes 1572872 | tf_op jit(solution)/shard_map/ppermute | solution.py:660
  26.1 18.8 %collective-permute-start.8 = (f32[9,512]{1,0:T(8,128)}, f32[9,512]{1,0:T(8,128)}, u32[]{:S(2)}, u32[]{:S(2)}) collective-permute-start(f32[9,512]{1,0:T(8,128)} %concatenate.83), channel_id=1, source_target_pairs={{0,1},{1,0},{2,3},{3,2},{4,5},{5,4},{6,7},{7,6},{8,9},{9,8},{10,11... | collective-permute-start | bytes 55304 | tf_op jit(solution)/shard_map/ppermute | solution.py:644
  38.7 8.3 %collective-permute-start.5 = (bf16[256,2048]{1,0:T(8,128)(2,1)}, bf16[256,2048]{1,0:T(8,128)(2,1)}, u32[]{:S(2)}, u32[]{:S(2)}) collective-permute-start(bf16[256,2048]{1,0:T(8,128)(2,1)} %pad_maximum_fusion.8), channel_id=1, source_target_pairs={{0,2},{2,0},{4,6},{6,4},{8,10},{10,8},{12,14},{14,12},{16,18},{18,... | collective-permute-start | bytes 3145736 | tf_op jit(solution)/shard_map/ppermute | solution.py:660
  39.4 6.9 %collective-permute-start.2 = (bf16[32,1536]{1,0:T(8,128)(2,1)}, bf16[32,1536]{1,0:T(8,128)(2,1)S(1)}, u32[]{:S(2)}, u32[]{:S(2)}) collective-permute-start(bf16[32,1536]{1,0:T(8,128)(2,1)} %pad_maximum_fusion.16), channel_id=1, source_target_pairs={{0,1},{1,0},{2,3},{3,2},{4,5},{5,4},{6,7},{7,6},{8,9},{9,8},{10,11... | collective-permute-start | bytes 294920 | tf_op jit(solution)/shard_map/ppermute | solution.py:644
  40.8 37.6 %collective-permute-start = (bf16[640,1024]{1,0:T(8,128)(2,1)S(1)}, bf16[640,1024]{1,0:T(8,128)(2,1)}, u32[]{:S(2)}, u32[]{:S(2)}) collective-permute-start(bf16[640,1024]{1,0:T(8,128)(2,1)S(1)} %get-tuple-element.131.x_ref.refs_0_.x), channel_id=1, source_target_pairs={{0,1},{1,0},{2,3},{3,2},{4,5},{5,4},{6,7},{7,6},{8,9},{9,8},{10,11... | collective-permute-start | bytes 3932168 | tf_op jit(solution)/shard_map/ppermute | solution.py:644
  41.4 60.1 %collective-permute-start.1 = (bf16[640,1024]{1,0:T(8,128)(2,1)}, bf16[640,1024]{1,0:T(8,128)(2,1)}, u32[]{:S(2)}, u32[]{:S(2)}) collective-permute-start(bf16[640,1024]{1,0:T(8,128)(2,1)} %get-tuple-element.132.dy_ref.refs_3_.refs_2_.refs_6_.refs_1_), channel_id=1, source_target_pairs={{0,1},{1,0},{2,3},{3,2},{4,5},{5,4},{6,7},{7,6},{8,9},{9,8},{10,11... | collective-permute-start | bytes 3932168 | tf_op jit(solution)/shard_map/ppermute | solution.py:644
  46.9 245.5 %reduce-scatter.2.cloned.1.call-start = ((), (), s32[]{:S(2)}) async-start(), calls=%async_computation.1 | async-start | bytes 8912896 | tf_op jit(solution)/shard_map/reduce_scatter | solution.py:891
  53.4 87.8 %collective-permute-start.6 = (bf16[640,1024]{1,0:T(8,128)(2,1)S(1)}, bf16[640,1024]{1,0:T(8,128)(2,1)}, u32[]{:S(2)}, u32[]{:S(2)}) collective-permute-start(bf16[640,1024]{1,0:T(8,128)(2,1)S(1)} %pad_maximum_fusion.4.x_ref.refs_0_.x), channel_id=1, source_target_pairs={{0,1},{1,0},{2,3},{3,2},{4,5},{5,4},{6,7},{7,6},{8,9},{9,8},{10,11... | collective-permute-start | bytes 3932168 | tf_op jit(solution)/shard_map/ppermute | solution.py:644
  54.0 103.3 %collective-permute-start.7 = (bf16[640,1024]{1,0:T(8,128)(2,1)}, bf16[640,1024]{1,0:T(8,128)(2,1)}, u32[]{:S(2)}, u32[]{:S(2)}) collective-permute-start(bf16[640,1024]{1,0:T(8,128)(2,1)} %pad_maximum_fusion.5.dy_ref.refs_5_.refs_2_.refs_8_.refs_1_), channel_id=1, source_target_pairs={{0,1},{1,0},{2,3},{3,2},{4,5},{5,4},{6,7},{7,6},{8,9},{9,8},{10,11... | collective-permute-start | bytes 3932168 | tf_op jit(solution)/shard_map/ppermute | solution.py:644
  186.4 294.4 %all-gather.7.cloned.1.call-start = ((), (), s32[]{:S(2)}) async-start(), calls=%async_computation.3 | async-start | bytes 8912896 | tf_op jit(solution)/shard_map/all_gather | solution.py:915
  293.3 5.4 %collective-permute-start.9 = (bf16[64,1024]{1,0:T(8,128)(2,1)S(1)}, bf16[64,1024]{1,0:T(8,128)(2,1)S(1)}, u32[]{:S(2)}, u32[]{:S(2)}) collective-permute-start(bf16[64,1024]{1,0:T(8,128)(2,1)S(1)} %dynamic-slice_bitcast_fusion), channel_id=1, source_target_pairs={{0,1},{1,0},{2,3},{3,2},{4,5},{5,4},{6,7},{7,6},{8,9},{9,8},{10,11... | collective-permute-start | bytes 393224 | tf_op jit(solution)/shard_map/ppermute | solution.py:644
  322.1 2.7 collective-permute-start.12
  322.7 4.2 collective-permute-start.10
  325.3 25.2 %collective-permute-start.13 = (bf16[4,128,512]{2,1,0:T(8,128)(2,1)S(1)}, bf16[4,128,512]{2,1,0:T(8,128)(2,1)S(1)}, u32[]{:S(2)}, u32[]{:S(2)}) collective-permute-start(bf16[4,128,512]{2,1,0:T(8,128)(2,1)S(1)} %slice.191), channel_id=1, source_target_pairs={{0,8},{2,10},{4,12},{6,14},{8,0},{10,2},{12,4},{14,6},{16,24},{18,... | collective-permute-start | bytes 1572872 | tf_op jit(solution)/shard_map/ppermute | solution.py:660
  328.3 22.2 %collective-permute-start.11 = (bf16[4,128,512]{2,1,0:T(8,128)(2,1)}, bf16[4,128,512]{2,1,0:T(8,128)(2,1)}, u32[]{:S(2)}, u32[]{:S(2)}) collective-permute-start(bf16[4,128,512]{2,1,0:T(8,128)(2,1)} %slice.190), channel_id=1, source_target_pairs={{0,4},{2,6},{4,0},{6,2},{8,12},{10,14},{12,8},{14,10},{16,20},{18,... | collective-permute-start | bytes 1572872 | tf_op jit(solution)/shard_map/ppermute | solution.py:660
  348.4 55.6 %collective-permute-start.18 = (bf16[640,1024]{1,0:T(8,128)(2,1)}, bf16[640,1024]{1,0:T(8,128)(2,1)S(1)}, u32[]{:S(2)}, u32[]{:S(2)}) collective-permute-start(bf16[640,1024]{1,0:T(8,128)(2,1)} %get-tuple-element.177), channel_id=1, source_target_pairs={{0,1},{1,0},{2,3},{3,2},{4,5},{5,4},{6,7},{7,6},{8,9},{9,8},{10,11... | collective-permute-start | bytes 3932168 | tf_op jit(solution)/shard_map/ppermute | solution.py:644
  349.9 57.1 %collective-permute-start.19 = (bf16[640,1024]{1,0:T(8,128)(2,1)}, bf16[640,1024]{1,0:T(8,128)(2,1)S(1)}, u32[]{:S(2)}, u32[]{:S(2)}) collective-permute-start(bf16[640,1024]{1,0:T(8,128)(2,1)} %get-tuple-element.178), channel_id=1, source_target_pairs={{0,1},{1,0},{2,3},{3,2},{4,5},{5,4},{6,7},{7,6},{8,9},{9,8},{10,11... | collective-permute-start | bytes 3932168 | tf_op jit(solution)/shard_map/ppermute | solution.py:644
  354.2 26.3 %collective-permute-start.15 = (bf16[2,128,512]{2,1,0:T(8,128)(2,1)}, bf16[2,128,512]{2,1,0:T(8,128)(2,1)S(1)}, u32[]{:S(2)}, u32[]{:S(2)}) collective-permute-start(bf16[2,128,512]{2,1,0:T(8,128)(2,1)} %slice.196), channel_id=1, source_target_pairs={{0,16},{2,18},{4,20},{6,22},{8,24},{10,26},{12,28},{14,30},{16,0},... | collective-permute-start | bytes 786440 | tf_op jit(solution)/shard_map/ppermute | solution.py:660
  355.9 25.3 %collective-permute-start.14 = (bf16[2,128,512]{2,1,0:T(8,128)(2,1)}, bf16[2,128,512]{2,1,0:T(8,128)(2,1)}, u32[]{:S(2)}, u32[]{:S(2)}) collective-permute-start(bf16[2,128,512]{2,1,0:T(8,128)(2,1)} %slice.194), channel_id=1, source_target_pairs={{0,8},{2,10},{4,12},{6,14},{8,0},{10,2},{12,4},{14,6},{16,24},{18,... | collective-permute-start | bytes 786440 | tf_op jit(solution)/shard_map/ppermute | solution.py:660
  358.2 27.1 %copy-start.24 = (bf16[128,1024]{1,0:T(8,128)(2,1)S(1)}, bf16[128,1024]{1,0:T(8,128)(2,1)}, u32[]{:S(2)}) copy-start(bf16[128,1024]{1,0:T(8,128)(2,1)} %copy-done.23) | copy-start | bytes 786436
  358.2 27.1 %copy-start.26 = (bf16[128,1024]{1,0:T(8,128)(2,1)S(1)}, bf16[128,1024]{1,0:T(8,128)(2,1)}, u32[]{:S(2)}) copy-start(bf16[128,1024]{1,0:T(8,128)(2,1)} %copy-done.25) | copy-start | bytes 786436
  384.0 24.0 %collective-permute-start.17 = (bf16[1,128,512]{2,1,0:T(8,128)(2,1)}, bf16[1,128,512]{2,1,0:T(8,128)(2,1)S(1)}, u32[]{:S(2)}, u32[]{:S(2)}) collective-permute-start(bf16[1,128,512]{2,1,0:T(8,128)(2,1)} %slice.200), channel_id=1, source_target_pairs={{0,4},{2,6},{4,0},{6,2},{8,12},{10,14},{12,8},{14,10},{16,20},{18,... | collective-permute-start | bytes 393224 | tf_op jit(solution)/shard_map/ppermute | solution.py:660
  384.9 23.1 %collective-permute-start.16 = (bf16[1,128,512]{2,1,0:T(8,128)(2,1)S(1)}, bf16[1,128,512]{2,1,0:T(8,128)(2,1)S(1)}, u32[]{:S(2)}, u32[]{:S(2)}) collective-permute-start(bf16[1,128,512]{2,1,0:T(8,128)(2,1)S(1)} %slice.198), channel_id=1, source_target_pairs={{0,16},{2,18},{4,20},{6,22},{8,24},{10,26},{12,28},{14,30},{16,0},... | collective-permute-start | bytes 393224 | tf_op jit(solution)/shard_map/ppermute | solution.py:660
  385.8 30.4 %copy-start.67 = (f32[1,2048]{1,0:T(1,128)S(1)}, f32[1,2048]{1,0:T(1,128)}, u32[]{:S(2)}) copy-start(f32[1,2048]{1,0:T(1,128)} %get-tuple-element.208) | copy-start | bytes 24580
  385.8 30.4 %copy-start.68 = (f32[1,2048]{1,0:T(1,128)S(1)}, f32[1,2048]{1,0:T(1,128)}, u32[]{:S(2)}) copy-start(f32[1,2048]{1,0:T(1,128)} %get-tuple-element.206) | copy-start | bytes 24580
  385.9 30.4 %copy-start.69 = (f32[1,2048]{1,0:T(1,128)S(1)}, f32[1,2048]{1,0:T(1,128)}, u32[]{:S(2)}) copy-start(f32[1,2048]{1,0:T(1,128)} %get-tuple-element.207) | copy-start | bytes 24580
  385.9 30.4 %copy-start.70 = (f32[1,2048]{1,0:T(1,128)S(1)}, f32[1,2048]{1,0:T(1,128)}, u32[]{:S(2)}) copy-start(f32[1,2048]{1,0:T(1,128)} %get-tuple-element.209) | copy-start | bytes 24580
  408.1 4.0 collective-permute-start.23
  409.7 4.3 collective-permute-start.20
  412.2 6.8 %collective-permute-start.24 = (bf16[1,128,512]{2,1,0:T(8,128)(2,1)S(1)}, bf16[1,128,512]{2,1,0:T(8,128)(2,1)S(1)}, u32[]{:S(2)}, u32[]{:S(2)}) collective-permute-start(bf16[1,128,512]{2,1,0:T(8,128)(2,1)S(1)} %maximum_bitcast_fusion.1), channel_id=1, source_target_pairs={{0,4},{2,6},{4,0},{6,2},{8,12},{10,14},{12,8},{14,10},{16,20},{18,... | collective-permute-start | bytes 393224 | tf_op jit(solution)/shard_map/ppermute | solution.py:660
  414.2 10.7 %collective-permute-start.21 = (bf16[1,128,512]{2,1,0:T(8,128)(2,1)S(1)}, bf16[1,128,512]{2,1,0:T(8,128)(2,1)S(1)}, u32[]{:S(2)}, u32[]{:S(2)}) collective-permute-start(bf16[1,128,512]{2,1,0:T(8,128)(2,1)S(1)} %maximum_bitcast_fusion), channel_id=1, source_target_pairs={{0,16},{2,18},{4,20},{6,22},{8,24},{10,26},{12,28},{14,30},{16,0},... | collective-permute-start | bytes 393224 | tf_op jit(solution)/shard_map/ppermute | solution.py:660
  416.9 73.4 %collective-permute-start.28 = (bf16[640,1024]{1,0:T(8,128)(2,1)}, bf16[640,1024]{1,0:T(8,128)(2,1)S(1)}, u32[]{:S(2)}, u32[]{:S(2)}) collective-permute-start(bf16[640,1024]{1,0:T(8,128)(2,1)} %get-tuple-element.196), channel_id=1, source_target_pairs={{0,1},{1,0},{2,3},{3,2},{4,5},{5,4},{6,7},{7,6},{8,9},{9,8},{10,11... | collective-permute-start | bytes 3932168 | tf_op jit(solution)/shard_map/ppermute | solution.py:644
  417.5 72.9 %collective-permute-start.29 = (bf16[640,1024]{1,0:T(8,128)(2,1)}, bf16[640,1024]{1,0:T(8,128)(2,1)}, u32[]{:S(2)}, u32[]{:S(2)}) collective-permute-start(bf16[640,1024]{1,0:T(8,128)(2,1)} %get-tuple-element.197), channel_id=1, source_target_pairs={{0,1},{1,0},{2,3},{3,2},{4,5},{5,4},{6,7},{7,6},{8,9},{9,8},{10,11... | collective-permute-start | bytes 3932168 | tf_op jit(solution)/shard_map/ppermute | solution.py:644
  419.0 30.1 %copy-start.36 = (bf16[1,128,512]{2,1,0:T(8,128)(2,1)}, bf16[1,128,512]{2,1,0:T(8,128)(2,1)S(1)}, u32[]{:S(2)}) copy-start(bf16[1,128,512]{2,1,0:T(8,128)(2,1)S(1)} %collective-permute-done.24) | copy-start | bytes 393220
  419.7 29.3 %collective-permute-start.25 = (bf16[2,128,512]{2,1,0:T(8,128)(2,1)}, bf16[2,128,512]{2,1,0:T(8,128)(2,1)S(1)}, u32[]{:S(2)}, u32[]{:S(2)}) collective-permute-start(bf16[2,128,512]{2,1,0:T(8,128)(2,1)} %pad_maximum_fusion.15), channel_id=1, source_target_pairs={{0,16},{2,18},{4,20},{6,22},{8,24},{10,26},{12,28},{14,30},{16,0},... | collective-permute-start | bytes 786440 | tf_op jit(solution)/shard_map/ppermute | solution.py:660
  425.7 23.4 %collective-permute-start.22 = (bf16[2,128,512]{2,1,0:T(8,128)(2,1)}, bf16[2,128,512]{2,1,0:T(8,128)(2,1)S(1)}, u32[]{:S(2)}, u32[]{:S(2)}) collective-permute-start(bf16[2,128,512]{2,1,0:T(8,128)(2,1)} %pad_maximum_fusion.14), channel_id=1, source_target_pairs={{0,8},{2,10},{4,12},{6,14},{8,0},{10,2},{12,4},{14,6},{16,24},{18,... | collective-permute-start | bytes 786440 | tf_op jit(solution)/shard_map/ppermute | solution.py:660
  449.9 40.4 %collective-permute-start.27 = (bf16[4,128,512]{2,1,0:T(8,128)(2,1)}, bf16[4,128,512]{2,1,0:T(8,128)(2,1)}, u32[]{:S(2)}, u32[]{:S(2)}) collective-permute-start(bf16[4,128,512]{2,1,0:T(8,128)(2,1)} %pad_maximum_fusion.13), channel_id=1, source_target_pairs={{0,8},{2,10},{4,12},{6,14},{8,0},{10,2},{12,4},{14,6},{16,24},{18,... | collective-permute-start | bytes 1572872 | tf_op jit(solution)/shard_map/ppermute | solution.py:660
  452.8 37.6 %collective-permute-start.26 = (bf16[4,128,512]{2,1,0:T(8,128)(2,1)}, bf16[4,128,512]{2,1,0:T(8,128)(2,1)}, u32[]{:S(2)}, u32[]{:S(2)}) collective-permute-start(bf16[4,128,512]{2,1,0:T(8,128)(2,1)} %pad_maximum_fusion.12), channel_id=1, source_target_pairs={{0,4},{2,6},{4,0},{6,2},{8,12},{10,14},{12,8},{14,10},{16,20},{18,... | collective-permute-start | bytes 1572872 | tf_op jit(solution)/shard_map/ppermute | solution.py:660
  455.0 11.5 %collective-permute-start.30 = (f32[24,512]{1,0:T(8,128)S(1)}, f32[24,512]{1,0:T(8,128)S(1)}, u32[]{:S(2)}, u32[]{:S(2)}) collective-permute-start(f32[24,512]{1,0:T(8,128)S(1)} %concatenate.97), channel_id=1, source_target_pairs={{0,2},{2,0},{4,6},{6,4},{8,10},{10,8},{12,14},{14,12},{16,18},{18,... | collective-permute-start | bytes 147464 | tf_op jit(solution)/shard_map/ppermute | solution.py:660
  466.5 4.2 collective-permute-start.31
  470.7 4.2 collective-permute-start.32
  474.9 5.3 %collective-permute-start.33 = (f32[24,512]{1,0:T(8,128)S(1)}, f32[24,512]{1,0:T(8,128)S(1)}, u32[]{:S(2)}, u32[]{:S(2)}) collective-permute-start(f32[24,512]{1,0:T(8,128)S(1)} %add.303), channel_id=1, source_target_pairs={{0,16},{2,18},{4,20},{6,22},{8,24},{10,26},{12,28},{14,30},{16,0},... | collective-permute-start | bytes 147464 | tf_op jit(solution)/shard_map/ppermute | solution.py:660
  492.6 16.1 %collective-permute-start.36 = (bf16[8,128,512]{2,1,0:T(8,128)(2,1)}, bf16[8,128,512]{2,1,0:T(8,128)(2,1)}, u32[]{:S(2)}, u32[]{:S(2)}) collective-permute-start(bf16[8,128,512]{2,1,0:T(8,128)(2,1)} %pad_maximum_fusion.10), channel_id=1, source_target_pairs={{0,2},{2,0},{4,6},{6,4},{8,10},{10,8},{12,14},{14,12},{16,18},{18,... | collective-permute-start | bytes 3145736 | tf_op jit(solution)/shard_map/ppermute | solution.py:660
  494.9 16.2 %collective-permute-start.35 = (bf16[8,128,512]{2,1,0:T(8,128)(2,1)}, bf16[8,128,512]{2,1,0:T(8,128)(2,1)}, u32[]{:S(2)}, u32[]{:S(2)}) collective-permute-start(bf16[8,128,512]{2,1,0:T(8,128)(2,1)} %pad_maximum_fusion.9), channel_id=1, source_target_pairs={{0,2},{2,0},{4,6},{6,4},{8,10},{10,8},{12,14},{14,12},{16,18},{18,... | collective-permute-start | bytes 3145736 | tf_op jit(solution)/shard_map/ppermute | solution.py:660
  496.1 10.8 %collective-permute-start.34 = (f32[24,512]{1,0:T(8,128)S(1)}, f32[24,512]{1,0:T(8,128)S(1)}, u32[]{:S(2)}, u32[]{:S(2)}) collective-permute-start(f32[24,512]{1,0:T(8,128)S(1)} %copy-done.59), channel_id=1, source_target_pairs={{0,1},{1,0},{2,3},{3,2},{4,5},{5,4},{6,7},{7,6},{8,9},{9,8},{10,11... | collective-permute-start | bytes 147464 | tf_op jit(solution)/shard_map/ppermute | solution.py:644
  (73 other events, 534.7 us)
Sparse Core Ops, SparseCore 0:
  47.1 39.9 all-gather.4
  186.5 105.8 reduce-scatter.1
  300.7 86.2 all-gather.6

commit v7 on v4

--- a/solution.py
+++ b/solution.py
@@ -545,8 +545,8 @@
     h = refs[:n]
     dl = refs[n : 2 * n]
     ctx = refs[2 * n : 3 * n]
-    dy = refs[3 * n : -2]
-    first, second = refs[-2:]
+    dy = refs[3 * n : -4]
+    first, second = refs[-4:-2], refs[-2:]
     i = pl.program_id(0)
     q1 = q_ref[0]
     q2 = q_ref[1]
@@ -559,19 +559,27 @@
     steps = DR // blk
     s = i // steps
     base = (i % steps) * (blk // ru)
+
+    def put(pair, pos, rows, v):
+        for half in range(2):
+
+            @pl.when(pos // (R // 2) == half)
+            def _():
+                pair[half][pos % (R // 2), rows, :] = v
+
     for p in range(3):
         t = dtn(joined(h), jnp.concatenate([y[p] for y in dl], axis=0)).astype(BF)
         for c in range(blk // ru):
             v = t[c * ru : (c + 1) * ru, :]
             if p < 2:
-                first[(base + c) ^ q1, pl.ds(s * 2 * ru + p * ru, ru), :] = v
+                put(first, (base + c) ^ q1, pl.ds(s * 2 * ru + p * ru, ru), v)
             else:
-                second[(base + c) ^ q2, pl.ds(k * ru + s * ru, ru), :] = v
+                put(second, (base + c) ^ q2, pl.ds(k * ru + s * ru, ru), v)
     t = dtn(joined(ctx), joined(dy)).astype(BF)
     m = ctx[0].shape[1] // ru
     for c in range(m):
         for j in range(k):
-            second[(i * m + c) ^ q2, j * ru : (j + 1) * ru, :] = t[c * ru : (c + 1) * ru, j * CW : (j + 1) * CW]
+            put(second, (i * m + c) ^ q2, pl.ds(j * ru, ru), t[c * ru : (c + 1) * ru, j * CW : (j + 1) * CW])
 
 
 def attn_grads(S, R, q, hs, dls, ctxs, dys):
@@ -583,7 +591,7 @@
     blk = 256
     G = D // blk
     keep = lambda s: pl.BlockSpec(s, lambda i, q: (0,) * len(s), pipeline_mode=pl.Buffered(1))
-    shapes = [(R, S * 2 * ru, CW), (R, (D // CW + S) * ru, CW)]
+    shapes = [(R // 2, S * 2 * ru, CW)] * 2 + [(R // 2, (D // CW + S) * ru, CW)] * 2
     return pl.pallas_call(
         functools.partial(attn_grads_kernel, n, S, R),
         grid_spec=pltpu.PrefetchScalarGridSpec(
@@ -601,97 +609,84 @@
     )(q, *hs, *dls, *ctxs, *dys)
 
 
-def attn_finish_kernel(S, ru, k, n, q_ref, *refs):
-    firsts, seconds = refs[:n], refs[n : 2 * n]
-    out, qkv = refs[2 * n :]
-    CW = seconds[0].shape[2]
+def attn_finish_kernel(S, ru, k, n, half, q_ref, *refs):
+    out, qkv = refs[4 * n :]
+    CW = refs[0].shape[2]
     D = out.shape[1]
+    i = pl.program_id(0)
+
+    def piece(which, c, a):
+        low, high = refs[2 * which * n + c], refs[(2 * which + 1) * n + c]
+        here = ((i * n + c) ^ q_ref[which]) < half
+        rows = pl.ds(a, ru)
+        return jnp.where(here, low[0, rows, :].astype(F32), high[0, rows, :].astype(F32))
+
     for c in range(n):
         r = slice(c * ru, (c + 1) * ru)
         for j in range(k):
-            out[r, j * CW : (j + 1) * CW] = seconds[c][0, j * ru : (j + 1) * ru, :].astype(F32)
+            out[r, j * CW : (j + 1) * CW] = piece(1, c, j * ru)
         for t in range(S):
             for p in range(3):
-                a = (t * 2 + p) * ru if p < 2 else (k + t) * ru
-                v = (firsts if p < 2 else seconds)[c][0, a : a + ru, :]
-                qkv[r, p * D + t * CW : p * D + (t + 1) * CW] = v.astype(F32)
-
-
-def attn_finish(S, q, g1, g2):
-    R, per1, CW = g1.shape
-    per2 = g2.shape[1]
+                v = piece(0, c, (t * 2 + p) * ru) if p < 2 else piece(1, c, (k + t) * ru)
+                qkv[r, p * D + t * CW : p * D + (t + 1) * CW] = v
+
+
+def attn_finish(S, q, one, two):
+    half, per1, CW = one[0].shape
+    per2 = two[0].shape[1]
+    R = 2 * half
     D = CW * S
     ru = D // S // R
     n = 4
-    block = lambda per, k, c: pl.BlockSpec((1, per, CW), lambda i, q: ((i * n + c) ^ q[k], 0, 0))
+    place_of = lambda i, q, k, c: (i * n + c) ^ q[k]
+    low = lambda per, k, c: pl.BlockSpec((1, per, CW), lambda i, q: (jnp.minimum(place_of(i, q, k, c), half - 1), 0, 0))
+    high = lambda per, k, c: pl.BlockSpec((1, per, CW), lambda i, q: (jnp.maximum(place_of(i, q, k, c) - half, 0), 0, 0))
+    specs = [f(per, k, c) for k, per in ((0, per1), (1, per2)) for f in (low, high) for c in range(n)]
     return pl.pallas_call(
-        functools.partial(attn_finish_kernel, S, ru, S, n),
+        functools.partial(attn_finish_kernel, S, ru, S, n, half),
         grid_spec=pltpu.PrefetchScalarGridSpec(
             num_scalar_prefetch=1,
             grid=(R // n,),
-            in_specs=[block(per1, 0, c) for c in range(n)] + [block(per2, 1, c) for c in range(n)],
+            in_specs=specs,
             out_specs=[pl.BlockSpec((n * ru, D), lambda c, q: (c, 0)), pl.BlockSpec((n * ru, 3 * D), lambda c, q: (c, 0))],
         ),
         out_shape=[SD((CW, D), F32), SD((D // S, 3 * D), F32)],
         compiler_params=pltpu.CompilerParams(vmem_limit_bytes=40 * MIB),
         cost_estimate=pl.CostEstimate(flops=0, bytes_accessed=6 * R * (per1 + per2) * CW, transcendentals=0),
-    )(q, *[g1] * n, *[g2] * n)
-
-
-def own_kernel(act, dpre, wu, wd, dl, ctx, wqkv, wo, x, gb, y, g, ln, yacc, d1, d2):
-    f = pl.program_id(0)
-    last = pl.num_programs(0) - 1
+    )(q, *[a for pair in (one, two) for arr in pair for a in [arr] * n])
+
+
+def own_kernel(dl, ctx, wqkv, wo, x, yp, g2, gb, y, g, ln, d1):
     N = x.shape[0]
     CW = ctx.shape[1]
-
-    @pl.when(f == 0)
-    def _():
-        yacc[...] = dnn(ctx[...], wo[...])
-        d1[...] = sum(dnt(dl[p], wqkv[:, p * CW : (p + 1) * CW]) for p in range(3))
-        d2[...] = jnp.zeros_like(d2)
-
-    yacc[...] += dnn(act[...], wd[...])
-    d2[...] += dnt(dpre[...], wu[...])
-
-    @pl.when(f == last)
-    def _():
-        ln[...] = jnp.zeros_like(ln)
-
-        @pl.loop(0, N // 128)
-        def _(i):
-            r = tile(i, 128)
-            xh, _ = normed(x[r, :])
-            a = d1[r, :]
-            b = d2[r, :]
-            y[r, :] = yacc[r, :].astype(BF)
-            g[r, :] = (a * gb[0:1, :] + b * gb[2:3, :]).astype(BF)
-            ln[0:1, :] += jnp.sum(a * xh, axis=0, keepdims=True)
-            ln[1:2, :] += jnp.sum(a, axis=0, keepdims=True)
-            ln[2:3, :] += jnp.sum(b * xh, axis=0, keepdims=True)
-            ln[3:4, :] += jnp.sum(b, axis=0, keepdims=True)
-
-
-def own_rows(x, act, dpre, wu, wd, dl, ctx, wqkv, wo, gb):
+    d1[...] = sum(dnt(dl[p], wqkv[:, p * CW : (p + 1) * CW]) for p in range(3))
+    y[...] = (yp[...].astype(F32) + dnn(ctx[...], wo[...])).astype(BF)
+    ln[...] = jnp.zeros_like(ln)
+
+    @pl.loop(0, N // 128)
+    def _(i):
+        r = tile(i, 128)
+        xh, _ = normed(x[r, :])
+        a = d1[r, :]
+        g[r, :] = (a * gb[0:1, :] + g2[r, :].astype(F32)).astype(BF)
+        ln[0:1, :] += jnp.sum(a * xh, axis=0, keepdims=True)
+        ln[1:2, :] += jnp.sum(a, axis=0, keepdims=True)
+
+
+def own_rows(x, yp, g2, dl, ctx, wqkv, wo, gb):
     N, D = x.shape
-    FL = wu.shape[1]
     CW = wo.shape[0]
-    fb = min(512, FL)
-    full = lambda s: pl.BlockSpec(s, lambda f: (0,) * len(s), pipeline_mode=pl.Buffered(1))
-    keep = lambda s: pl.BlockSpec(s, lambda f: (0,) * len(s))
-    rows = pl.BlockSpec((N, fb), lambda f: (0, f))
+    full = lambda s: pl.BlockSpec(s, lambda f: (0,) * len(s))
     return pl.pallas_call(
         own_kernel,
-        grid=(FL // fb,),
-        in_specs=[rows, rows, pl.BlockSpec((D, fb), lambda f: (0, f)), pl.BlockSpec((fb, D), lambda f: (f, 0))]
-        + [full((3, N, CW)), full((N, CW)), full((D, 3 * CW)), full((CW, D)), full((N, D)), full((4, D))],
-        out_specs=[keep((N, D)), keep((N, D)), keep((4, D))],
-        out_shape=[SD((N, D), BF), SD((N, D), BF), SD((4, D), F32)],
-        scratch_shapes=[pltpu.VMEM((N, D), F32)] * 3,
+        grid=(1,),
+        in_specs=[full((3, N, CW)), full((N, CW)), full((D, 3 * CW)), full((CW, D))] + [full((N, D))] * 3 + [full((2, D))],
+        out_specs=[full((N, D)), full((N, D)), full((2, D))],
+        out_shape=[SD((N, D), BF), SD((N, D), BF), SD((2, D), F32)],
+        scratch_shapes=[pltpu.VMEM((N, D), F32)],
         compiler_params=pltpu.CompilerParams(vmem_limit_bytes=60 * MIB),
-        cost_estimate=pl.CostEstimate(
-            flops=4 * N * D * FL + 8 * N * D * CW, bytes_accessed=4 * (N + D) * FL + 8 * (N + D) * CW + 6 * N * D, transcendentals=0
-        ),
-    )(act, dpre, wu, wd, dl, ctx, wqkv, wo, x, gb)
+        cost_estimate=pl.CostEstimate(flops=8 * N * D * CW, bytes_accessed=8 * (N + D) * CW + 10 * N * D, transcendentals=0),
+    )(dl, ctx, wqkv, wo, x, yp, g2, gb)
 
 
 def final_kernel(S, first, PT, *refs):
@@ -832,22 +827,24 @@
     return got
 
 
-def halving(pair, R, beside):
-    pair = list(pair)
+def halving(pairs, R, beside):
     for i, bits in enumerate(zip(*orders(R))):
-        h = pair[0].shape[0] // 2
-        got = beside_it([exchanged(g[h:], R, bit) for g, bit in zip(pair, bits)], i, beside)
-        pair = [add_low(g[:h], t) for g, t in zip(pair, got)]
-    return [g[0] for g in pair]
+        got = beside_it([exchanged(p[1], R, bit) for p, bit in zip(pairs, bits)], i, beside)
+        h = got[0].shape[0] // 2
+        if h:
+            pairs = [(add_low(p[0][:h], t[:h]), add_low(p[0][h:], t[h:])) for p, t in zip(pairs, got)]
+        else:
+            pairs = [add_low(p[0], t) for p, t in zip(pairs, got)]
+    return [p[0] for p in pairs]
 
 
 def doubling(parts, R, beside):
     pair = [p[None] for p in parts]
     for i, bits in reversed(list(enumerate(zip(*orders(R))))):
-        got = [exchanged(g, R, bit) for g, bit in zip(pair, bits)]
-        got = beside_it(got, i, beside)
-        pair = [jnp.concatenate([g, t], axis=0) for g, t in zip(pair, got)]
-    return pair
+        got = beside_it([exchanged(g, R, bit) for g, bit in zip(pair, bits)], i, beside)
+        if i:
+            pair = [jnp.concatenate([g, t], axis=0) for g, t in zip(pair, got)]
+    return list(zip(pair, got))
 
 
 def sum_all(v, S, R):
@@ -934,7 +931,6 @@
     slots = [small] + [shifted(small, S, j) for j in range(1, S)]
     whole = jnp.stack(canonical(slots, me, S, True), axis=0)
     vec = whole[:, :6].transpose(1, 0, 2).reshape(6, D)
-    gb = vec[0:4]
     gb1 = vec[0:2]
     gb2 = vec[2:4]
     vb = vec[4:6]
@@ -957,7 +953,7 @@
     ff = [[None] * S for _ in range(MB)]
 
     def mlp(m, j):
-        ff[m][j] = mlp_rows(X[m][j], DY[m][j], w_up, bup, down_weight, gb2, int(j > 0))
+        ff[m][j] = mlp_rows(X[m][j], DY[m][j], w_up, bup, down_weight, gb2, 1)
 
     for m in range(MB):
         mlp(m, 0)
@@ -974,7 +970,7 @@
 
     def own(m):
         f = ff[m][0]
-        return own_rows(X[m][0], f[0], f[1], w_up, down_weight, rest[m][0], rest[m][1], w_qkv, out_weight, gb)
+        return own_rows(X[m][0], f[4], f[5], rest[m][0], rest[m][1], w_qkv, out_weight, gb1)
 
     chunked = (D // S // R) % 16 == 0 and R & (R - 1) == 0
     rep = lax.axis_index("rep")
@@ -1000,8 +996,8 @@
             w_qkv, rest[m][3] = lax.optimization_barrier((w_qkv, rest[m][3]))
     every = early + late
     def vectors(mine_):
-        ln1 = sum(r[3] for r in rest) + sum(o[2][0:2] for o in mine_)
-        ln2 = sum(f[6] for f in (ff[m][j] for m, j in every if j)) + sum(o[2][2:4] for o in mine_)
+        ln1 = sum(r[3] for r in rest) + sum(o[2] for o in mine_)
+        ln2 = sum(of(every, 6))
         db_out = sum(jnp.sum(DY[m][0].astype(F32), axis=0) for m in range(MB)).reshape(-1, CW)
         mine = (jnp.arange(S) == me).astype(F32)
         db_qkv = (sum(r[4] for r in rest)[:, None, :] * mine[None, :, None]).reshape(-1, CW)
@@ -1020,21 +1016,18 @@
         for m in range(MB):
             rest[m][0] = dls_own[m]
         mine = [own(m) for m in range(MB)]
-        beside = {1: mine[:1], 2: (mine[1:], y_got[-1], g_got[-1])}
-        half = halving(gatt, R, beside)
-        mine[:1] = beside[1]
-        mine[1:], y_got[-1], g_got[-1] = beside[2]
+        beside = {1: mine, 2: (y_got[-1], g_got[-1])}
+        half = halving([gatt[:2], gatt[2:]], R, beside)
+        mine = beside[1]
+        y_got[-1], g_got[-1] = beside[2]
         outs = None
         for m in range(MB - 1):
             outs = finals(m, mine[m], outs)
         vecs = sum_all(vectors(mine), S, R)
         k = D // CW * (D // S // R)
-        outs = finals(MB - 1, mine[-1], outs)
-        beside = {3: outs, 2: vecs, 1: mlp_finish(S, gmlp_all, FL)}
+        beside = {3: outs, 1: (finals(MB - 1, mine[-1], outs), vecs, mlp_finish(S, gmlp_all, FL))}
         g1, g2 = doubling([swap_shards(half[0], me, S, 0), swap_shards(half[1], me, S, k)], R, beside)
-        outs = beside[3]
-        vecs = beside[2]
-        g_down, g_up = beside[1]
+        outs, vecs, (g_down, g_up) = beside[1]
         g_out, g_qkv = attn_finish(S, q, g1, g2)
     else:
         dls, ctxs, hs = [[r[k] for r in rest] for k in (0, 1, 2)]

time: 503 us -> 555 us (1.10)
  waiting for transfers between devices: 56.5 us -> 107 us
  Pallas kernels: 299 us -> 310 us
  local copies, waits for them, and re-layouts: 37.8 us -> 30.5 us
    ppermute x15, waiting for transfers between devices: 23 us -> 64.1 us  [shifted(): return lax.ppermute(value, 'shard', [(i, (i + j) % S) for i in range(S)])]
    pallas_call x4, Pallas kernels: 63.2 us -> 81.4 us  [mlp_rows(): pl.pallas_call(functools.partial(mlp_kernel, rows_tile(rows, 640)), grid=...]
    pallas_call x3, Pallas kernels: 40.2 us -> 26 us  [the longest x2 19.6 us: own_rows(): pl.pallas_call(own_kernel, grid=(1,), in_specs=[full((3, N, CW)), full((N...]
    ppermute x22, waiting for transfers between devices: 33.4 us -> 42.5 us  [exchanged(): return lax.ppermute(value, 'rep', [(i, i ^ bit) for i in range(R)])]
    slice x9 -> x0, local copies, waits for them, and re-layouts: 7.54 us -> none  [the longest x8 6.94 us: halving(): g[h:]]
    unnamed x128 -> x95, local copies, waits for them, and re-layouts: 10.4 us -> 13.3 us
  transfers between devices with their start and end apart: 40 -> 40, of which waited for: 15 -> 16; matrix products, arithmetic and copies ran while one was open for 14% -> 10% of each run, Pallas kernels for 59% -> 55%
where the time goes in v7:
time: 555 us; the launch traced here: 549 us
  Pallas kernels  310 us (56%)
  waiting for transfers between devices  107 us (19%)
  starting transfers between devices  47.5 us (9%)
  other arithmetic  39.1 us (7%)
  local copies, waits for them, and re-layouts  30.5 us (5%)
  between operations  15 us (3%)
    pallas_call x2, Pallas kernels, attn_group(): pl.pallas_call(functools.partial(attn_kernel, S, PD, CL, QB, HG, adding),...  114 us
    pallas_call x4, Pallas kernels, mlp_rows(): pl.pallas_call(functools.partial(mlp_kernel, rows_tile(rows, 640)), grid=...  81.4 us
    ppermute x15, waiting for transfers between devices, shifted(): return lax.ppermute(value, 'shard', [(i, (i + j) % S) for i in range(S)])  64.1 us
    pallas_call x4, Pallas kernels, call(): pl.pallas_call(functools.partial(kernel, n, more), grid=(a[0].shape[1] //...  46.1 us
    ppermute x22, waiting for transfers between devices, exchanged(): return lax.ppermute(value, 'rep', [(i, i ^ bit) for i in range(R)])  42.5 us
    ppermute x22, starting transfers between devices, exchanged(): return lax.ppermute(value, 'rep', [(i, i ^ bit) for i in range(R)])  26.8 us
    pallas_call x1, Pallas kernels, attn_grads(): pl.pallas_call(functools.partial(attn_grads_kernel, n, S, R), grid_spec=p...  24.5 us
    ppermute x15, starting transfers between devices, shifted(): return lax.ppermute(value, 'shard', [(i, (i + j) % S) for i in range(S)])  20.5 us
  transfers between devices with their start and end apart: 40, of which 16 were waited for; matrix products, arithmetic and copies ran while one was open for 10% of the time, Pallas kernels for 55%

profile of v7, /device:TPU:0, one launch (start us, length us, event | category | flops | bytes accessed | tf_op | source)
XLA Modules:
  0.0 549.1 jit_solution(602644694590880800)
XLA Ops:
  8.4 3.0 collective-permute-start.2
  17.5 1.9 slice_bitcast_fusion
  20.6 2.0 collective-permute-start.1
  24.2 1.9 collective-permute-start.3
  29.8 7.0 %collective-permute-done.3 = bf16[128,2048]{1,0:T(8,128)(2,1)} collective-permute-done((bf16[128,2048]{1,0:T(8,128)(2,1)}, bf16[128,2048]{1,0:T(8,128)(2,1)}, u32[]{:S(2)}, u32[]{:S(2)}) %collective-permute-start.3) | collective-permute-done | bytes 524320 | tf_op jit(solution)/shard_map/ppermute | solution.py:763
  44.7 37.6 %collective-permute-done.6 = bf16[32,1536]{1,0:T(8,128)(2,1)S(1)} collective-permute-done((bf16[32,1536]{1,0:T(8,128)(2,1)}, bf16[32,1536]{1,0:T(8,128)(2,1)S(1)}, u32[]{:S(2)}, u32[]{:S(2)}) %collective-permute-start.6) | collective-permute-done | bytes 98336 | tf_op jit(solution)/shard_map/ppermute | solution.py:747
  83.0 1.8 collective-permute-start.7
  85.1 1.8 broadcast_select_fusion.5
  88.1 2.6 pad_maximum_fusion.wu_ref
  90.7 20.4 %shard_map.308 = (bf16[640,2048]{1,0:T(8,128)(2,1)}, bf16[640,2048]{1,0:T(8,128)(2,1)}, bf16[640,1024]{1,0:T(8,128)(2,1)}, f32[1,2048]{1,0:T(1,128)}, bf16[640,1...) custom-call(bf16[640,1024]{1,0:T(8,128)(2,1)} %copy-done, ...), custom_call_target="tpu_custom_call" | custom-call | flops 10737418240 | bytes 20185088 | tf_op jit(solution)/shard_map/pallas_call | solution.py:108
  111.1 20.2 %shard_map.307 = (bf16[640,2048]{1,0:T(8,128)(2,1)}, bf16[640,2048]{1,0:T(8,128)(2,1)}, bf16[640,1024]{1,0:T(8,128)(2,1)}, f32[1,2048]{1,0:T(1,128)}, bf16[640,1...) custom-call(bf16[640,1024]{1,0:T(8,128)(2,1)} %copy-done.2, ...), custom_call_target="tpu_custom_call" | custom-call | flops 10737418240 | bytes 20185088 | tf_op jit(solution)/shard_map/pallas_call | solution.py:108
  131.3 20.2 %shard_map.306 = (bf16[640,2048]{1,0:T(8,128)(2,1)}, bf16[640,2048]{1,0:T(8,128)(2,1)}, bf16[640,1024]{1,0:T(8,128)(2,1)}, f32[1,2048]{1,0:T(1,128)}, bf16[640,1...) custom-call(bf16[640,1024]{1,0:T(8,128)(2,1)} %collective-permute-done.x_ref.refs_1_, ...), custom_call_target="tpu_custom_call" | custom-call | flops 10737418240 | bytes 20185088 | tf_op jit(solution)/shard_map/pallas_call | solution.py:108
  151.5 14.0 %shard_map.309.refs_6_ = bf16[16,256,1024]{2,1,0:T(8,128)(2,1)} custom-call(bf16[640,2048]{1,0:T(8,128)(2,1)} %get-tuple-element.131.refs_0_, bf16[640,2048]{1,0:T(8,128)(2,1)} %get-tuple-element.132.refs_1_, bf16[640,2048]{1,0:T(8,128)(2,1)} %get-tuple-element.133.refs_2_, bf16[640,1024]{1,0:T(8,128)(2,1)} %pad_maximum_fusion.5.dy_ref.refs_3_.refs_2_.refs_6_.refs_1_, ...), custom_call_target="tpu_custom_call" | custom-call | flops 8053063680 | bytes 15990784 | tf_op jit(solution)/shard_map/pallas_call | solution.py:498
  165.5 14.4 %shard_map.310.refs_2_ = bf16[16,256,1024]{2,1,0:T(8,128)(2,1)} custom-call(bf16[640,1024]{1,0:T(8,128)(2,1)} %get-tuple-element.125.refs_0_, bf16[640,1024]{1,0:T(8,128)(2,1)} %get-tuple-element.126.refs_1_, bf16[640,1024]{1,0:T(8,128)(2,1)} %get-tuple-element.127.refs_2_, ...), custom_call_target="tpu_custom_call", output_to_operand_aliasing={{}: (6, {})} | custom-call | flops 8053063680 | bytes 15990784 | tf_op jit(solution)/shard_map/pallas_call | solution.py:498
  179.9 20.6 %shard_map.311 = (bf16[640,2048]{1,0:T(8,128)(2,1)}, bf16[640,2048]{1,0:T(8,128)(2,1)}, bf16[640,1024]{1,0:T(8,128)(2,1)}, f32[1,2048]{1,0:T(1,128)}, bf16[640,1...) custom-call(bf16[640,1024]{1,0:T(8,128)(2,1)} %collective-permute-done.7.x_ref.refs_1_, ...), custom_call_target="tpu_custom_call" | custom-call | flops 10737418240 | bytes 20185088 | tf_op jit(solution)/shard_map/pallas_call | solution.py:108
  200.5 9.6 %shard_map.312.refs_2_ = bf16[16,256,1024]{2,1,0:T(8,128)(2,1)} custom-call(bf16[640,2048]{1,0:T(8,128)(2,1)} %get-tuple-element.137.refs_0_, bf16[640,1024]{1,0:T(8,128)(2,1)} %collective-permute-done.8.dy_ref.refs_1_.refs_3_.refs_9_, bf16[16,256,1024]{2,1,0:T(8,128)(2,1)} %shard_map.310.refs_2_), custom_call_target="tpu_custom_call", output_to_operand_aliasing={{}: (2, {})} | custom-call | flops 2684354560 | bytes 12320768 | tf_op jit(solution)/shard_map/pallas_call | solution.py:498
  210.1 8.1 %shard_map.313 = bf16[16,256,1024]{2,1,0:T(8,128)(2,1)} custom-call(bf16[640,1024]{1,0:T(8,128)(2,1)} %get-tuple-element.135.refs_0_, bf16[640,2048]{1,0:T(8,128)(2,1)} %get-tuple-element.136.refs_1_, bf16[16,256,1024]{2,1,0:T(8,128)(2,1)} %shard_map.312.refs_2_), custom_call_target="tpu_custom_call", output_to_operand_aliasing={{}: (2, {})} | custom-call | flops 2684354560 | bytes 12320768 | tf_op jit(solution)/shard_map/pallas_call | solution.py:498
  220.4 2.0 broadcast_select_fusion.3
  222.4 1.9 pad_maximum_fusion.1.refs_6_.refs_7_.refs_8_.wqkv
  224.3 57.0 %shard_map.314 = (bf16[640,1024]{1,0:T(8,128)(2,1)}, bf16[640,1024]{1,0:T(8,128)(2,1)}, bf16[3,1280,512]{2,1,0:T(8,128)(2,1)}, bf16[1280,512]{1,0:T(8,128)(2,1)}...) custom-call(s32[1]{0:T(128)} %bitcast.2.me_ref, bf16[640,1024]{1,0:T(8,128)(2,1)} %copy-done.2, ...), custom_call_target="tpu_custom_call" | custom-call | flops 44291850240 | bytes 27787264 | tf_op jit(solution)/shard_map/pallas_call | solution.py:389
  281.3 1.8 collective-permute-start.10
  283.4 56.6 %shard_map.315 = (bf16[640,1024]{1,0:T(8,128)(2,1)}, bf16[640,1024]{1,0:T(8,128)(2,1)}, bf16[3,1280,512]{2,1,0:T(8,128)(2,1)}, bf16[1280,512]{1,0:T(8,128)(2,1)}...) custom-call(s32[1]{0:T(128)} %bitcast.2.me_ref, bf16[640,1024]{1,0:T(8,128)(2,1)} %copy-done, ...), custom_call_target="tpu_custom_call" | custom-call | flops 44291850240 | bytes 27787264 | tf_op jit(solution)/shard_map/pallas_call | solution.py:389
  343.6 2.3 collective-permute-done.11
  348.5 24.5 %shard_map.316 = (bf16[8,128,512]{2,1,0:T(8,128)(2,1)}, bf16[8,128,512]{2,1,0:T(8,128)(2,1)}, bf16[8,128,512]{2,1,0:T(8,128)(2,1)}, bf16[8,128,512]{2,1,0:T(8,128)(2,1)}) custom-call(s32[2]{0:T(128)} %pad_add_fusion.q_ref, bf16[1280,1024]{1,0:T(8,128)(2,1)} %get-tuple-element.148.refs_0_, bf16[1280,1024]{1,0:T(8,128)(2,1)} %get-tuple-element.149.refs_1_, ...), custom_call_target="tpu_custom_call" | custom-call | flops 10737418240 | bytes 25165824 | tf_op jit(solution)/shard_map/pallas_call | solution.py:595
  373.6 2.4 collective-permute-done.14
  376.0 2.3 add_convert_fusion
  384.9 9.8 %shard_map.318 = (bf16[640,1024]{1,0:T(8,128)(2,1)}, bf16[640,1024]{1,0:T(8,128)(2,1)}, f32[2,1024]{1,0:T(2,128)}) custom-call(bf16[3,1280,512]{2,1,0:T(8,128)(2,1)} %get-tuple-element.164.refs_3_.dl, bf16[1280,512]{1,0:T(8,128)(2,1)} %get-tuple-element.153.refs_5_.ctx, bf16[1024,1536]{1,0:T(8,128)(2,1)} %pad_maximum_fusion.1.refs_6_.refs_7_.refs_8_.wqkv, ...), custom_call_target="tpu_custom_call" | custom-call | flops 2684354560 | bytes 13369344 | tf_op jit(solution)/shard_map/pallas_call | solution.py:680
  394.7 9.8 %shard_map.317 = (bf16[640,1024]{1,0:T(8,128)(2,1)}, bf16[640,1024]{1,0:T(8,128)(2,1)}, f32[2,1024]{1,0:T(2,128)}) custom-call(bf16[3,1280,512]{2,1,0:T(8,128)(2,1)} %get-tuple-element.158.refs_2_.dl, bf16[1280,512]{1,0:T(8,128)(2,1)} %get-tuple-element.152.refs_4_.ctx, bf16[1024,1536]{1,0:T(8,128)(2,1)} %pad_maximum_fusion.1.refs_6_.refs_7_.refs_8_.wqkv, ...), custom_call_target="tpu_custom_call" | custom-call | flops 2684354560 | bytes 13369344 | tf_op jit(solution)/shard_map/pallas_call | solution.py:680
  404.5 4.5 collective-permute-done.15
  409.1 2.0 add_convert_fusion.4
  411.1 4.9 collective-permute-start.17
  416.0 2.2 add_convert_fusion.6
  418.1 2.7 collective-permute-start.16
  422.9 18.7 %collective-permute-done.19.refs_5_ = bf16[640,1024]{1,0:T(8,128)(2,1)} collective-permute-done((bf16[640,1024]{1,0:T(8,128)(2,1)}, bf16[640,1024]{1,0:T(8,128)(2,1)}, u32[]{:S(2)}, u32[]{:S(2)}) %collective-permute-start.19) | collective-permute-done | bytes 1310752 | tf_op jit(solution)/shard_map/ppermute | solution.py:747
  444.1 2.8 collective-permute-start.20
  462.4 6.7 %shard_map.319 = (bf16[2,512,1024]{2,1,0:T(8,128)(2,1)}, bf16[2,128,1024]{2,1,0:T(8,128)(2,1)}, f32[2,512,1024]{2,1,0:T(8,128)}, f32[2,128,1024]{2,1,0:T(8,128)}) custom-call(bf16[640,1024]{1,0:T(8,128)(2,1)S(1)} %copy-done.3, bf16[640,1024]{1,0:T(8,128)(2,1)} %pad_maximum_fusion.5.dy_ref.refs_3_.refs_2_.refs_6_.refs_1_, bf16[640,1024]{1,0:T(8,128)(2,1)S(1)} %copy-done.12, ...), custom_call_target="tpu_custom_call" | custom-call | flops 13107200 | bytes 11796480 | tf_op jit(solution)/shard_map/pallas_call | solution.py:734
  473.1 7.9 %collective-permute-done.28 = bf16[2,128,512]{2,1,0:T(8,128)(2,1)} collective-permute-done((bf16[2,128,512]{2,1,0:T(8,128)(2,1)}, bf16[2,128,512]{2,1,0:T(8,128)(2,1)}, u32[]{:S(2)}, u32[]{:S(2)}) %collective-permute-start.28) | collective-permute-done | bytes 262176 | tf_op jit(solution)/shard_map/ppermute | solution.py:763
  480.9 1.8 pad_maximum_fusion.13
  483.6 2.2 collective-permute-start.27
  487.4 10.1 %collective-permute-done.31 = f32[24,512]{1,0:T(8,128)S(1)} collective-permute-done((f32[24,512]{1,0:T(8,128)S(1)}, f32[24,512]{1,0:T(8,128)S(1)}, u32[]{:S(2)}, u32[]{:S(2)}) %collective-permute-start.31) | collective-permute-done | bytes 49184 | tf_op jit(solution)/shard_map/ppermute | solution.py:763
  497.6 1.8 collective-permute-start.32
  499.4 2.3 collective-permute-done.32
  501.8 5.0 collective-permute-done.33
  510.8 6.1 %shard_map.320 = (bf16[2,512,1024]{2,1,0:T(8,128)(2,1)}, bf16[2,128,1024]{2,1,0:T(8,128)(2,1)}, f32[2,512,1024]{2,1,0:T(8,128)}, f32[2,128,1024]{2,1,0:T(8,128)}) custom-call(bf16[640,1024]{1,0:T(8,128)(2,1)S(1)} %copy-done.1, bf16[640,1024]{1,0:T(8,128)(2,1)S(1)} %copy-done.5, ...), custom_call_target="tpu_custom_call", output_to_operand_aliasing={{0}: (7, {}), {1}: (8, {}), {2}: (9, {}), {3}: (10, {})} | custom-call | flops 13107200 | bytes 11796480 | tf_op jit(solution)/shard_map/pallas_call | solution.py:734
  516.9 3.4 copy-done.4
  520.2 6.1 %shard_map.321 = (f32[2048,1024]{1,0:T(8,128)}, f32[512,4096]{1,0:T(8,128)}) custom-call(bf16[16,256,1024]{2,1,0:T(8,128)(2,1)S(1)} %bitcast.74), custom_call_target="tpu_custom_call" | custom-call | bytes 25165824 | tf_op jit(solution)/shard_map/pallas_call | solution.py:533
  530.7 2.8 collective-permute-done.34
  535.4 6.4 %shard_map.322 = (f32[512,1024]{1,0:T(8,128)}, f32[512,3072]{1,0:T(8,128)}) custom-call(s32[2]{0:T(128)S(1)} %copy-done.14, bf16[8,128,512]{2,1,0:T(8,128)(2,1)S(1)} %pad_maximum_fusion.9.refs_0_.refs_1_.refs_2_.refs_3_, bf16[8,128,512]{2,1,0:T(8,128)(2,1)S(1)} %pad_maximum_fusion.9.refs_0_.refs_1_.refs_2_.refs_3_, ...), custom_call_target="tpu_custom_call" | custom-call | bytes 12582912 | tf_op jit(solution)/shard_map/pallas_call | solution.py:645
  (238 shorter events, 76.5 us)
Async XLA Ops:
  7.2 213.3 %all-gather.5.cloned.1.call-start = ((), (), s32[]{:S(2)}) async-start(), calls=%async_computation.2 | async-start | bytes 1671168 | tf_op jit(solution)/shard_map/all_gather | solution.py:804
  8.4 15.9 %collective-permute-start.2 = (bf16[128,2048]{1,0:T(8,128)(2,1)S(1)}, bf16[128,2048]{1,0:T(8,128)(2,1)}, u32[]{:S(2)}, u32[]{:S(2)}) collective-permute-start(bf16[128,2048]{1,0:T(8,128)(2,1)S(1)} %dynamic_slice.80), channel_id=1, source_target_pairs={{0,1},{1,0},{2,3},{3,2},{4,5},{5,4},{6,7},{7,6},{8,9},{9,8},{10,11... | collective-permute-start | bytes 1572872 | tf_op jit(solution)/shard_map/ppermute | solution.py:747
  16.3 27.0 %collective-permute-start.5 = (f32[9,512]{1,0:T(8,128)S(1)}, f32[9,512]{1,0:T(8,128)}, u32[]{:S(2)}, u32[]{:S(2)}) collective-permute-start(f32[9,512]{1,0:T(8,128)S(1)} %concatenate.76), channel_id=1, source_target_pairs={{0,1},{1,0},{2,3},{3,2},{4,5},{5,4},{6,7},{7,6},{8,9},{9,8},{10,11... | collective-permute-start | bytes 55304 | tf_op jit(solution)/shard_map/ppermute | solution.py:747
  20.6 110.7 %collective-permute-start.1 = (bf16[640,1024]{1,0:T(8,128)(2,1)}, bf16[640,1024]{1,0:T(8,128)(2,1)}, u32[]{:S(2)}, u32[]{:S(2)}) collective-permute-start(bf16[640,1024]{1,0:T(8,128)(2,1)} %pad_maximum_fusion.5.dy_ref.refs_3_.refs_2_.refs_6_.refs_1_), channel_id=1, source_target_pairs={{0,1},{1,0},{2,3},{3,2},{4,5},{5,4},{6,7},{7,6},{8,9},{9,8},{10,11... | collective-permute-start | bytes 3932168 | tf_op jit(solution)/shard_map/ppermute | solution.py:747
  24.2 12.6 %collective-permute-start.3 = (bf16[128,2048]{1,0:T(8,128)(2,1)}, bf16[128,2048]{1,0:T(8,128)(2,1)}, u32[]{:S(2)}, u32[]{:S(2)}) collective-permute-start(bf16[128,2048]{1,0:T(8,128)(2,1)} %collective-permute-done.2), channel_id=1, source_target_pairs={{0,4},{2,6},{4,0},{6,2},{8,12},{10,14},{12,8},{14,10},{16,20},{18,... | collective-permute-start | bytes 1572872 | tf_op jit(solution)/shard_map/ppermute | solution.py:763
  27.5 103.8 %collective-permute-start = (bf16[640,1024]{1,0:T(8,128)(2,1)S(1)}, bf16[640,1024]{1,0:T(8,128)(2,1)}, u32[]{:S(2)}, u32[]{:S(2)}) collective-permute-start(bf16[640,1024]{1,0:T(8,128)(2,1)S(1)} %pad_maximum_fusion.4.x_ref.refs_0_.x), channel_id=1, source_target_pairs={{0,1},{1,0},{2,3},{3,2},{4,5},{5,4},{6,7},{7,6},{8,9},{9,8},{10,11... | collective-permute-start | bytes 3932168 | tf_op jit(solution)/shard_map/ppermute | solution.py:747
  39.2 45.9 %collective-permute-start.4 = (bf16[256,2048]{1,0:T(8,128)(2,1)}, bf16[256,2048]{1,0:T(8,128)(2,1)}, u32[]{:S(2)}, u32[]{:S(2)}) collective-permute-start(bf16[256,2048]{1,0:T(8,128)(2,1)} %pad_maximum_fusion.8), channel_id=1, source_target_pairs={{0,2},{2,0},{4,6},{6,4},{8,10},{10,8},{12,14},{14,12},{16,18},{18,... | collective-permute-start | bytes 3145736 | tf_op jit(solution)/shard_map/ppermute | solution.py:763
  39.9 42.4 %collective-permute-start.6 = (bf16[32,1536]{1,0:T(8,128)(2,1)}, bf16[32,1536]{1,0:T(8,128)(2,1)S(1)}, u32[]{:S(2)}, u32[]{:S(2)}) collective-permute-start(bf16[32,1536]{1,0:T(8,128)(2,1)} %pad_maximum_fusion.16), channel_id=1, source_target_pairs={{0,1},{1,0},{2,3},{3,2},{4,5},{5,4},{6,7},{7,6},{8,9},{9,8},{10,11... | collective-permute-start | bytes 294920 | tf_op jit(solution)/shard_map/ppermute | solution.py:747
  42.6 44.3 %copy-start = (bf16[640,1024]{1,0:T(8,128)(2,1)}, bf16[640,1024]{1,0:T(8,128)(2,1)S(1)}, u32[]{:S(2)}) copy-start(bf16[640,1024]{1,0:T(8,128)(2,1)S(1)} %pad_maximum_fusion.6.x_ref.refs_0_.x) | copy-start | bytes 3932164
  82.9 257.0 %reduce-scatter.2.cloned.1.call-start = ((), (), s32[]{:S(2)}) async-start(), calls=%async_computation.1 | async-start | bytes 8912896 | tf_op jit(solution)/shard_map/reduce_scatter | solution.py:991
  83.0 96.9 %collective-permute-start.7 = (bf16[640,1024]{1,0:T(8,128)(2,1)S(1)}, bf16[640,1024]{1,0:T(8,128)(2,1)}, u32[]{:S(2)}, u32[]{:S(2)}) collective-permute-start(bf16[640,1024]{1,0:T(8,128)(2,1)S(1)} %pad_maximum_fusion.6.x_ref.refs_0_.x), channel_id=1, source_target_pairs={{0,1},{1,0},{2,3},{3,2},{4,5},{5,4},{6,7},{7,6},{8,9},{9,8},{10,11... | collective-permute-start | bytes 3932168 | tf_op jit(solution)/shard_map/ppermute | solution.py:747
  84.8 95.1 %collective-permute-start.8 = (bf16[640,1024]{1,0:T(8,128)(2,1)}, bf16[640,1024]{1,0:T(8,128)(2,1)}, u32[]{:S(2)}, u32[]{:S(2)}) collective-permute-start(bf16[640,1024]{1,0:T(8,128)(2,1)} %pad_maximum_fusion.7.dy_ref.refs_5_.refs_2_.refs_8_.refs_1_), channel_id=1, source_target_pairs={{0,1},{1,0},{2,3},{3,2},{4,5},{5,4},{6,7},{7,6},{8,9},{9,8},{10,11... | collective-permute-start | bytes 3932168 | tf_op jit(solution)/shard_map/ppermute | solution.py:747
  218.2 298.6 %all-gather.7.cloned.1.call-start = ((), (), s32[]{:S(2)}) async-start(), calls=%async_computation.3 | async-start | bytes 8912896 | tf_op jit(solution)/shard_map/all_gather | solution.py:1013
  281.3 66.4 %collective-permute-start.10 = (bf16[640,1024]{1,0:T(8,128)(2,1)}, bf16[640,1024]{1,0:T(8,128)(2,1)S(1)}, u32[]{:S(2)}, u32[]{:S(2)}) collective-permute-start(bf16[640,1024]{1,0:T(8,128)(2,1)} %get-tuple-element.147), channel_id=1, source_target_pairs={{0,1},{1,0},{2,3},{3,2},{4,5},{5,4},{6,7},{7,6},{8,9},{9,8},{10,11... | collective-permute-start | bytes 3932168 | tf_op jit(solution)/shard_map/ppermute | solution.py:747
  283.1 64.6 %collective-permute-start.9 = (bf16[640,1024]{1,0:T(8,128)(2,1)}, bf16[640,1024]{1,0:T(8,128)(2,1)}, u32[]{:S(2)}, u32[]{:S(2)}) collective-permute-start(bf16[640,1024]{1,0:T(8,128)(2,1)} %get-tuple-element.146), channel_id=1, source_target_pairs={{0,1},{1,0},{2,3},{3,2},{4,5},{5,4},{6,7},{7,6},{8,9},{9,8},{10,11... | collective-permute-start | bytes 3932168 | tf_op jit(solution)/shard_map/ppermute | solution.py:747
  340.9 5.0 collective-permute-start.11
  373.1 2.9 collective-permute-start.14
  373.1 6.9 %collective-permute-start.12 = (bf16[8,128,512]{2,1,0:T(8,128)(2,1)}, bf16[8,128,512]{2,1,0:T(8,128)(2,1)S(1)}, u32[]{:S(2)}, u32[]{:S(2)}) collective-permute-start(bf16[8,128,512]{2,1,0:T(8,128)(2,1)} %get-tuple-element.155), channel_id=1, source_target_pairs={{0,2},{2,0},{4,6},{6,4},{8,10},{10,8},{12,14},{14,12},{16,18},{18,... | collective-permute-start | bytes 3145736 | tf_op jit(solution)/shard_map/ppermute | solution.py:763
  378.3 30.7 %collective-permute-start.15 = (bf16[4,128,512]{2,1,0:T(8,128)(2,1)}, bf16[4,128,512]{2,1,0:T(8,128)(2,1)}, u32[]{:S(2)}, u32[]{:S(2)}) collective-permute-start(bf16[4,128,512]{2,1,0:T(8,128)(2,1)} %get-tuple-element.265), channel_id=1, source_target_pairs={{0,8},{2,10},{4,12},{6,14},{8,0},{10,2},{12,4},{14,6},{16,24},{18,... | collective-permute-start | bytes 1572872 | tf_op jit(solution)/shard_map/ppermute | solution.py:763
  381.4 27.7 %collective-permute-start.13 = (bf16[4,128,512]{2,1,0:T(8,128)(2,1)}, bf16[4,128,512]{2,1,0:T(8,128)(2,1)}, u32[]{:S(2)}, u32[]{:S(2)}) collective-permute-start(bf16[4,128,512]{2,1,0:T(8,128)(2,1)} %get-tuple-element.266), channel_id=1, source_target_pairs={{0,4},{2,6},{4,0},{6,2},{8,12},{10,14},{12,8},{14,10},{16,20},{18,... | collective-permute-start | bytes 1572872 | tf_op jit(solution)/shard_map/ppermute | solution.py:763
  382.9 40.0 %collective-permute-start.18 = (bf16[640,1024]{1,0:T(8,128)(2,1)}, bf16[640,1024]{1,0:T(8,128)(2,1)S(1)}, u32[]{:S(2)}, u32[]{:S(2)}) collective-permute-start(bf16[640,1024]{1,0:T(8,128)(2,1)} %get-tuple-element.172), channel_id=1, source_target_pairs={{0,1},{1,0},{2,3},{3,2},{4,5},{5,4},{6,7},{7,6},{8,9},{9,8},{10,11... | collective-permute-start | bytes 3932168 | tf_op jit(solution)/shard_map/ppermute | solution.py:747
  384.4 57.1 %collective-permute-start.19 = (bf16[640,1024]{1,0:T(8,128)(2,1)}, bf16[640,1024]{1,0:T(8,128)(2,1)}, u32[]{:S(2)}, u32[]{:S(2)}) collective-permute-start(bf16[640,1024]{1,0:T(8,128)(2,1)} %get-tuple-element.173), channel_id=1, source_target_pairs={{0,1},{1,0},{2,3},{3,2},{4,5},{5,4},{6,7},{7,6},{8,9},{9,8},{10,11... | collective-permute-start | bytes 3932168 | tf_op jit(solution)/shard_map/ppermute | solution.py:747
  411.1 30.5 %collective-permute-start.17 = (bf16[2,128,512]{2,1,0:T(8,128)(2,1)}, bf16[2,128,512]{2,1,0:T(8,128)(2,1)}, u32[]{:S(2)}, u32[]{:S(2)}) collective-permute-start(bf16[2,128,512]{2,1,0:T(8,128)(2,1)} %get-tuple-element.275), channel_id=1, source_target_pairs={{0,16},{2,18},{4,20},{6,22},{8,24},{10,26},{12,28},{14,30},{16,0},... | collective-permute-start | bytes 786440 | tf_op jit(solution)/shard_map/ppermute | solution.py:763
  418.1 23.4 %collective-permute-start.16 = (bf16[2,128,512]{2,1,0:T(8,128)(2,1)}, bf16[2,128,512]{2,1,0:T(8,128)(2,1)}, u32[]{:S(2)}, u32[]{:S(2)}) collective-permute-start(bf16[2,128,512]{2,1,0:T(8,128)(2,1)} %get-tuple-element.276), channel_id=1, source_target_pairs={{0,8},{2,10},{4,12},{6,14},{8,0},{10,2},{12,4},{14,6},{16,24},{18,... | collective-permute-start | bytes 786440 | tf_op jit(solution)/shard_map/ppermute | solution.py:763
  422.6 35.7 %copy-start.30 = (f32[2,1024]{1,0:T(2,128)S(1)}, f32[2,1024]{1,0:T(2,128)}, u32[]{:S(2)}) copy-start(f32[2,1024]{1,0:T(2,128)} %get-tuple-element.200) | copy-start | bytes 24580
  422.6 35.7 %copy-start.31 = (f32[2,1024]{1,0:T(2,128)S(1)}, f32[2,1024]{1,0:T(2,128)}, u32[]{:S(2)}) copy-start(f32[2,1024]{1,0:T(2,128)} %get-tuple-element.198) | copy-start | bytes 24580
  422.6 35.7 %copy-start.32 = (f32[2,1024]{1,0:T(2,128)S(1)}, f32[2,1024]{1,0:T(2,128)}, u32[]{:S(2)}) copy-start(f32[2,1024]{1,0:T(2,128)} %get-tuple-element.199) | copy-start | bytes 24580
  422.7 35.7 %copy-start.33 = (f32[2,1024]{1,0:T(2,128)S(1)}, f32[2,1024]{1,0:T(2,128)}, u32[]{:S(2)}) copy-start(f32[2,1024]{1,0:T(2,128)} %get-tuple-element.201) | copy-start | bytes 24580
  422.7 35.8 %copy-start.3 = (bf16[640,1024]{1,0:T(8,128)(2,1)S(1)}, bf16[640,1024]{1,0:T(8,128)(2,1)}, u32[]{:S(2)}) copy-start(bf16[640,1024]{1,0:T(8,128)(2,1)} %copy-done.2) | copy-start | bytes 3932164
  442.5 5.0 collective-permute-start.23
  444.1 7.5 %collective-permute-start.20 = (bf16[1,128,512]{2,1,0:T(8,128)(2,1)S(1)}, bf16[1,128,512]{2,1,0:T(8,128)(2,1)S(1)}, u32[]{:S(2)}, u32[]{:S(2)}) collective-permute-start(bf16[1,128,512]{2,1,0:T(8,128)(2,1)S(1)} %add_convert_fusion.12), channel_id=1, source_target_pairs={{0,16},{2,18},{4,20},{6,22},{8,24},{10,26},{12,28},{14,30},{16,0},... | collective-permute-start | bytes 393224 | tf_op jit(solution)/shard_map/ppermute | solution.py:763
  448.6 5.6 %collective-permute-start.24 = (bf16[32,512]{1,0:T(8,128)(2,1)S(1)}, bf16[32,512]{1,0:T(8,128)(2,1)S(1)}, u32[]{:S(2)}, u32[]{:S(2)}) collective-permute-start(bf16[32,512]{1,0:T(8,128)(2,1)S(1)} %dynamic-slice_bitcast_fusion.2), channel_id=1, source_target_pairs={{0,1},{1,0},{2,3},{3,2},{4,5},{5,4},{6,7},{7,6},{8,9},{9,8},{10,11... | collective-permute-start | bytes 98312 | tf_op jit(solution)/shard_map/ppermute | solution.py:747
  452.6 4.3 collective-permute-start.21
  454.3 14.9 %collective-permute-start.25 = (bf16[1,128,512]{2,1,0:T(8,128)(2,1)S(1)}, bf16[1,128,512]{2,1,0:T(8,128)(2,1)S(1)}, u32[]{:S(2)}, u32[]{:S(2)}) collective-permute-start(bf16[1,128,512]{2,1,0:T(8,128)(2,1)S(1)} %maximum_bitcast_fusion.1), channel_id=1, source_target_pairs={{0,4},{2,6},{4,0},{6,2},{8,12},{10,14},{12,8},{14,10},{16,20},{18,... | collective-permute-start | bytes 393224 | tf_op jit(solution)/shard_map/ppermute | solution.py:763
  457.0 12.1 %collective-permute-start.22 = (bf16[1,128,512]{2,1,0:T(8,128)(2,1)S(1)}, bf16[1,128,512]{2,1,0:T(8,128)(2,1)S(1)}, u32[]{:S(2)}, u32[]{:S(2)}) collective-permute-start(bf16[1,128,512]{2,1,0:T(8,128)(2,1)S(1)} %maximum_bitcast_fusion), channel_id=1, source_target_pairs={{0,16},{2,18},{4,20},{6,22},{8,24},{10,26},{12,28},{14,30},{16,0},... | collective-permute-start | bytes 393224 | tf_op jit(solution)/shard_map/ppermute | solution.py:763
  469.1 37.7 %copy-start.1 = (bf16[640,1024]{1,0:T(8,128)(2,1)S(1)}, bf16[640,1024]{1,0:T(8,128)(2,1)}, u32[]{:S(2)}) copy-start(bf16[640,1024]{1,0:T(8,128)(2,1)} %copy-done) | copy-start | bytes 3932164
  469.1 37.7 %copy-start.5 = (bf16[640,1024]{1,0:T(8,128)(2,1)S(1)}, bf16[640,1024]{1,0:T(8,128)(2,1)}, u32[]{:S(2)}) copy-start(bf16[640,1024]{1,0:T(8,128)(2,1)} %pad_maximum_fusion.7.dy_ref.refs_5_.refs_2_.refs_8_.refs_1_) | copy-start | bytes 3932164
  469.9 11.1 %collective-permute-start.28 = (bf16[2,128,512]{2,1,0:T(8,128)(2,1)}, bf16[2,128,512]{2,1,0:T(8,128)(2,1)}, u32[]{:S(2)}, u32[]{:S(2)}) collective-permute-start(bf16[2,128,512]{2,1,0:T(8,128)(2,1)} %pad_maximum_fusion.15), channel_id=1, source_target_pairs={{0,16},{2,18},{4,20},{6,22},{8,24},{10,26},{12,28},{14,30},{16,0},... | collective-permute-start | bytes 786440 | tf_op jit(solution)/shard_map/ppermute | solution.py:763
  472.2 10.5 %collective-permute-start.26 = (bf16[2,128,512]{2,1,0:T(8,128)(2,1)}, bf16[2,128,512]{2,1,0:T(8,128)(2,1)S(1)}, u32[]{:S(2)}, u32[]{:S(2)}) collective-permute-start(bf16[2,128,512]{2,1,0:T(8,128)(2,1)} %pad_maximum_fusion.14), channel_id=1, source_target_pairs={{0,8},{2,10},{4,12},{6,14},{8,0},{10,2},{12,4},{14,6},{16,24},{18,... | collective-permute-start | bytes 786440 | tf_op jit(solution)/shard_map/ppermute | solution.py:763
  482.7 43.6 %collective-permute-start.29 = (bf16[4,128,512]{2,1,0:T(8,128)(2,1)}, bf16[4,128,512]{2,1,0:T(8,128)(2,1)}, u32[]{:S(2)}, u32[]{:S(2)}) collective-permute-start(bf16[4,128,512]{2,1,0:T(8,128)(2,1)} %pad_maximum_fusion.13), channel_id=1, source_target_pairs={{0,8},{2,10},{4,12},{6,14},{8,0},{10,2},{12,4},{14,6},{16,24},{18,... | collective-permute-start | bytes 1572872 | tf_op jit(solution)/shard_map/ppermute | solution.py:763
  483.6 42.7 %collective-permute-start.27 = (bf16[4,128,512]{2,1,0:T(8,128)(2,1)}, bf16[4,128,512]{2,1,0:T(8,128)(2,1)}, u32[]{:S(2)}, u32[]{:S(2)}) collective-permute-start(bf16[4,128,512]{2,1,0:T(8,128)(2,1)} %pad_maximum_fusion.12), channel_id=1, source_target_pairs={{0,4},{2,6},{4,0},{6,2},{8,12},{10,14},{12,8},{14,10},{16,20},{18,... | collective-permute-start | bytes 1572872 | tf_op jit(solution)/shard_map/ppermute | solution.py:763
  486.0 1.3 collective-permute-start.30
  487.3 10.2 %collective-permute-start.31 = (f32[24,512]{1,0:T(8,128)S(1)}, f32[24,512]{1,0:T(8,128)S(1)}, u32[]{:S(2)}, u32[]{:S(2)}) collective-permute-start(f32[24,512]{1,0:T(8,128)S(1)} %add.325), channel_id=1, source_target_pairs={{0,4},{2,6},{4,0},{6,2},{8,12},{10,14},{12,8},{14,10},{16,20},{18,... | collective-permute-start | bytes 147464 | tf_op jit(solution)/shard_map/ppermute | solution.py:763
  497.6 4.2 collective-permute-start.32
  501.7 5.1 collective-permute-start.33
  527.6 7.7 %collective-permute-start.36 = (bf16[8,128,512]{2,1,0:T(8,128)(2,1)S(1)}, bf16[8,128,512]{2,1,0:T(8,128)(2,1)S(1)}, u32[]{:S(2)}, u32[]{:S(2)}) collective-permute-start(bf16[8,128,512]{2,1,0:T(8,128)(2,1)S(1)} %pad_maximum_fusion.10.refs_8_.refs_9_.refs_10_.refs_11_), channel_id=1, source_target_pairs={{0,2},{2,0},{4,6},{6,4},{8,10},{10,8},{12,14},{14,12},{16,18},{18,... | collective-permute-start | bytes 3145736 | tf_op jit(solution)/shard_map/ppermute | solution.py:763
  528.9 6.5 %collective-permute-start.35 = (bf16[8,128,512]{2,1,0:T(8,128)(2,1)S(1)}, bf16[8,128,512]{2,1,0:T(8,128)(2,1)}, u32[]{:S(2)}, u32[]{:S(2)}) collective-permute-start(bf16[8,128,512]{2,1,0:T(8,128)(2,1)S(1)} %pad_maximum_fusion.9.refs_0_.refs_1_.refs_2_.refs_3_), channel_id=1, source_target_pairs={{0,2},{2,0},{4,6},{6,4},{8,10},{10,8},{12,14},{14,12},{16,18},{18,... | collective-permute-start | bytes 3145736 | tf_op jit(solution)/shard_map/ppermute | solution.py:763
  529.4 4.1 collective-permute-start.34
  (38 other events, 371.3 us)
Sparse Core Ops, SparseCore 0:
  83.1 41.1 all-gather.4
  218.4 106.1 reduce-scatter.1
  347.9 92.8 all-gather.6
